TPU v7x, 32 devices: a whole 2x2x4 slice. The times are simulated.
32 devices in a mesh: dp: 4 (over x, core), seq: 2 (over y), vocab: 4 (over z).
Axes of the slice: x: 2, y: 2, z: 4, core: 2. Of those that a mesh axis runs over, the one named last changes fastest.
Arguments:
- queries: bfloat16 [4, 64, 4096], P('dp', 'seq', 'vocab'), may hold values from -64 to 64
- enc_keys: bfloat16 [4, 256, 4096], P('dp', 'seq', 'vocab'), may hold values from -6 to 6
- enc_values: bfloat16 [4, 256, 4096], P('dp', 'seq', 'vocab'), may hold values from -6 to 6
- enc_lengths: int32 [4], P('dp'), may hold values from 64 to 256, as said below
- out_proj: bfloat16 [4096, 4096], P('vocab', 'seq'), may hold values from -0.375 to 0.375
- residual: bfloat16 [4, 64, 4096], P('dp', None, 'seq'), may hold values from -270 to 270
- norm_gain: float32 [4096], P('seq'), may hold values from 0.4 to 1.6
- head_weight: bfloat16 [4096, 32128], P('seq', 'vocab'), may hold values from -1 to 1
- targets: int32 [4, 64], P('dp', 'seq'), may hold values from 0 to 32127
Outputs:
- mean_loss: float32 [], replicated
- head_grad: bfloat16 [4096, 32128], P('seq', 'vocab')
- key_grad: float32 [4, 256, 4096], P('dp', 'seq', 'vocab')
- value_grad: float32 [4, 256, 4096], P('dp', 'seq', 'vocab')
Inputs may be any that keep to these rules, and one draw needn't show every extreme that they name: `enc_lengths`: each example has at least 64 unpadded positions; some example has none padded.
All inputs are finite; a program needn't handle non-finite values.
Results may differ from a plain program's by a relative error of at most 0.02.
Values may be sent and summed in bfloat16 or wider, within the bound.
No kernel may reach another device: no remote copies, remote signals or barrier semaphores. Data moves between devices by JAX's collectives and lax.ppermute only.
A program may use at most 192 MiB of HBM per device.

v0:
```python
import jax
import jax.numpy as jnp
from jax import lax
from jax.sharding import PartitionSpec as P

D = 4096
HDIM = 256


zloss_weight = 0.0001
norm_epsilon = 1e-06


def body(
    queries, enc_keys, enc_values, enc_lengths, out_proj, residual, norm_gain, head_weight, targets
):
    examples, tgt_rows, features = queries.shape
    heads_here = features // HDIM
    vocab_cols = head_weight.shape[1]
    all_targets = tgt_rows * lax.axis_size("seq")
    score_scale = HDIM ** (-0.5)
    key_all, value_all = (
        lax.all_gather(enc_keys, "seq", axis=1, tiled=True),
        lax.all_gather(enc_values, "seq", axis=1, tiled=True),
    )
    enc_rows = key_all.shape[1]
    query_heads = queries.reshape(examples, tgt_rows, heads_here, HDIM)
    key_heads = key_all.reshape(examples, enc_rows, heads_here, HDIM)
    value_heads = value_all.reshape(examples, enc_rows, heads_here, HDIM)
    scores = (
        jnp.einsum("bthd,bjhd->bhtj", query_heads, key_heads, preferred_element_type=jnp.float32)
        * score_scale
    )
    valid_keys = lax.broadcasted_iota(jnp.int32, (examples, enc_rows), 1) < enc_lengths[:, None]
    scores = jnp.where(valid_keys[:, None, None, :], scores, -jnp.inf)
    score_peak = jnp.max(scores, axis=-1, keepdims=True)
    score_exp = jnp.exp(scores - score_peak)
    weights_full = score_exp / jnp.sum(score_exp, axis=-1, keepdims=True)
    weights_half = weights_full.astype(jnp.bfloat16)
    attended = jnp.einsum(
        "bhtj,bjhd->tbhd", weights_half, value_heads, preferred_element_type=jnp.float32
    )
    attended = attended.astype(jnp.bfloat16).reshape(tgt_rows, examples, features)
    attended_all = lax.all_gather(attended, "seq", axis=0, tiled=True)
    mixed_part = jnp.einsum(
        "tbf,fd->tbd", attended_all, out_proj, preferred_element_type=jnp.float32
    )
    mixed_rows = lax.psum(mixed_part, "vocab") + jnp.swapaxes(residual, 0, 1).astype(jnp.float32)
    square_sum = lax.psum(jnp.sum(mixed_rows * mixed_rows, axis=-1), "seq")
    inverse_rms = lax.rsqrt(square_sum / D + norm_epsilon)
    normed = (mixed_rows * inverse_rms[..., None] * norm_gain).astype(jnp.bfloat16)
    row_block = normed
    logits = lax.psum_scatter(
        jnp.einsum("tbd,dv->tbv", row_block, head_weight, preferred_element_type=jnp.float32),
        "seq",
        scatter_dimension=0,
        tiled=True,
    )
    column_ids = (
        lax.broadcasted_iota(jnp.int32, (1, 1, vocab_cols), 2)
        + lax.axis_index("vocab") * vocab_cols
    )
    target_hit = column_ids == jnp.swapaxes(targets, 0, 1)[..., None]
    local_target = jnp.sum(jnp.where(target_hit, logits, 0.0), axis=-1)
    row_peak = lax.pmax(jnp.max(logits, axis=-1), "vocab")
    exp_total, target_logit = lax.psum(
        (jnp.sum(jnp.exp(logits - row_peak[..., None]), axis=-1), local_target), "vocab"
    )
    log_total = row_peak + jnp.log(exp_total)
    token_loss = log_total - target_logit + zloss_weight * log_total * log_total
    mean_loss = lax.psum(jnp.sum(token_loss), ("dp", "seq")) / (
        examples * lax.axis_size("dp") * all_targets
    )
    logit_grad = (
        jnp.exp(logits - log_total[..., None]) * (1.0 + 2.0 * zloss_weight * log_total)[..., None]
        - target_hit.astype(jnp.float32)
    ).astype(jnp.bfloat16)
    grad_piece = lax.all_gather(logit_grad, "seq", axis=0, tiled=True)
    row_block = normed
    weight_acc = jnp.einsum(
        "tbd,tbv->dv", row_block, grad_piece, preferred_element_type=jnp.float32
    )
    hidden_part = jnp.einsum(
        "tbv,dv->tbd", grad_piece, head_weight, preferred_element_type=jnp.float32
    )
    head_total = lax.psum(weight_acc.astype(jnp.bfloat16), "dp")
    summed_grad = lax.psum(hidden_part, "vocab")
    gated = summed_grad * norm_gain
    dot_row = lax.psum(jnp.sum(gated * mixed_rows, axis=-1), "seq")
    mixed_grad = (
        gated * inverse_rms[..., None] - mixed_rows * (inverse_rms**3 * dot_row / D)[..., None]
    ).astype(jnp.bfloat16)
    row_block = mixed_grad
    attended_grad = lax.psum_scatter(
        jnp.einsum("tbd,fd->tbf", row_block, out_proj, preferred_element_type=jnp.float32),
        "seq",
        scatter_dimension=0,
        tiled=True,
    ).astype(jnp.bfloat16)
    grad_heads = attended_grad.reshape(tgt_rows, examples, heads_here, HDIM)
    prob_grad = jnp.einsum(
        "tbhd,bjhd->bhtj", grad_heads, value_heads, preferred_element_type=jnp.float32
    )
    score_grad = weights_full * (
        prob_grad - jnp.sum(weights_full * prob_grad, axis=-1, keepdims=True)
    )
    score_half = (score_grad * score_scale).astype(jnp.bfloat16)
    value_part = jnp.einsum(
        "bhtj,tbhd->bjhd", weights_half, grad_heads, preferred_element_type=jnp.float32
    )
    key_part = jnp.einsum(
        "bhtj,bthd->bjhd", score_half, query_heads, preferred_element_type=jnp.float32
    )
    key_grad, value_grad = (
        lax.psum_scatter(
            key_part.reshape(examples, enc_rows, features).astype(jnp.bfloat16),
            "seq",
            scatter_dimension=1,
            tiled=True,
        ).astype(jnp.float32),
        lax.psum_scatter(
            value_part.reshape(examples, enc_rows, features).astype(jnp.bfloat16),
            "seq",
            scatter_dimension=1,
            tiled=True,
        ).astype(jnp.float32),
    )
    return (mean_loss, head_total, key_grad, value_grad)


def solution(mesh):
    placed = (
        P("dp", "seq", "vocab"),
        P("dp", "seq", "vocab"),
        P("dp", "seq", "vocab"),
        P("dp"),
        P("vocab", "seq"),
        P("dp", None, "seq"),
        P("seq"),
        P("seq", "vocab"),
        P("dp", "seq"),
    )
    return jax.shard_map(
        body,
        mesh=mesh,
        in_specs=placed,
        out_specs=(P(), P("seq", "vocab"), P("dp", "seq", "vocab"), P("dp", "seq", "vocab")),
        check_vma=False,
    )
```

profile of v0, /device:TPU:0, one launch (start us, length us, event | category | flops | bytes accessed | tf_op | source)
XLA Modules:
  0.0 859.8 jit_solution(10295888151169076250)
XLA Ops:
  8.8 1.1 copy.19
  9.9 10.0 %all_gather.12 = bf16[1,256,1024]{1,2,0:T(8,128)(2,1)S(1)} all-gather(bf16[1,128,1024]{1,2,0:T(8,128)(2,1)S(1)} %copy.19), channel_id=1, replica_groups=mesh['dp'=4,'seq'=2,'vocab'=4] {'seq'}, dimensions={1}, use_global_device_ids=true | all-gather | bytes 786432 | tf_op jit(solution)/shard_map/all_gather | solution.py:23
  20.8 1.1 copy.22
  21.9 8.2 all_gather.13
  30.4 4.9 all_gather.14
  35.3 3.8 convolution_bitcast_fusion.1
  39.2 39.6 %all-reduce.5.cloned.1.call-done = f32[64,1,2048]{2,0,1:T(8,128)} async-done(((f32[64,1,2048]{2,0,1:T(8,128)}), f32[64,1,2048]{2,0,1:T(8,128)}) %all-reduce.5.cloned.1.call-update) | async-done | bytes 524304 | tf_op jit(solution)/shard_map/psum | solution.py:48
  78.8 1.3 multiply_reduce_fusion.1
  80.1 4.9 psum.57
  85.1 1.2 fusion.15
  86.3 15.9 %convolution_bitcast_fusion = f32[64,1,8032]{2,0,1:T(8,128)} fusion(bf16[64,2048]{1,0:T(8,128)(2,1)S(1)} %fusion.15, bf16[2048,8032]{0,1:T(8,128)(2,1)} %param.16), kind=kOutput, calls=%fused_computation.3 | convolution fusion | flops 2105540608 | bytes 35217408 | tf_op jit(solution)/shard_map/tbd,dv->tbv/dot_general | solution.py:54
  102.3 31.5 %reduce-scatter.5.cloned.1.call-done = f32[32,1,8032]{2,0,1:T(8,128)} async-done(((f32[64,1,8032]{2,0,1:T(8,128)}), f32[32,1,8032]{2,0,1:T(8,128)}) %reduce-scatter.5.cloned.1.call-update) | async-done | bytes 1028112 | tf_op jit(solution)/shard_map/reduce_scatter | solution.py:53
  133.9 1.4 reduce_max.21
  135.3 11.7 %pmax.7 = f32[32,1]{0,1:T(1,128)S(1)} all-reduce(f32[32,1]{0,1:T(1,128)S(1)} %bitcast.97), channel_id=1, replica_groups=mesh['dp'=4,'seq'=2,'vocab'=4] {'vocab'}, use_global_device_ids=true, to_apply=%region_7.8 | all-reduce | flops 32 | bytes 256 | tf_op jit(solution)/shard_map/pmax | solution.py:65
  146.9 1.6 exponential_reduce_fusion
  148.6 8.4 all-reduce
  157.6 1.5 fusion.12
  159.1 10.4 %all_gather.15 = bf16[64,1,8032]{2,0,1:T(8,128)(2,1)S(1)} all-gather(bf16[32,1,8032]{2,0,1:T(8,128)(2,1)S(1)} %fusion.12), channel_id=1, replica_groups=mesh['dp'=4,'seq'=2,'vocab'=4] {'seq'}, dimensions={0}, use_global_device_ids=true | all-gather | bytes 1542144 | tf_op jit(solution)/shard_map/all_gather | solution.py:78
  169.5 14.2 %convolution_bitcast_fusion.2 = f32[64,1,2048]{2,0,1:T(8,128)} fusion(bf16[2048,8032]{0,1:T(8,128)(2,1)} %param.16, bf16[64,1,8032]{2,0,1:T(8,128)(2,1)S(1)} %all_gather.15), kind=kOutput, calls=%fused_computation.5 | convolution fusion | flops 2105540608 | bytes 34451456 | tf_op jit(solution)/shard_map/tbv,dv->tbd/dot_general | solution.py:83
  183.8 37.1 %all-reduce.9.cloned.1.call-done = f32[64,1,2048]{2,0,1:T(8,128)} async-done(((f32[64,1,2048]{2,0,1:T(8,128)}), f32[64,1,2048]{2,0,1:T(8,128)}) %all-reduce.9.cloned.1.call-update) | async-done | bytes 524304 | tf_op jit(solution)/shard_map/psum | solution.py:87
  220.9 1.2 multiply_reduce_fusion
  222.1 4.9 psum.63
  227.1 4.5 convolution_bitcast_fusion.3
  231.6 11.8 %reduce-scatter.7.cloned.1.call-done = f32[32,1,1024]{2,0,1:T(8,128)} async-done(((f32[64,1,1024]{2,0,1:T(8,128)}), f32[32,1,1024]{2,0,1:T(8,128)}) %reduce-scatter.7.cloned.1.call-update) | async-done | bytes 131088 | tf_op jit(solution)/shard_map/reduce_scatter | solution.py:94
  245.1 1.0 copy.28
  246.7 1.0 copy.30
  247.7 14.6 %convolution_convert_fusion = bf16[2048,8032]{0,1:T(8,128)(2,1)} fusion(bf16[64,2048]{1,0:T(8,128)(2,1)S(1)} %fusion.15, bf16[64,1,8032]{2,0,1:T(8,128)(2,1)S(1)} %all_gather.15), kind=kOutput, calls=%fused_computation.2 | convolution fusion | flops 2121990144 | bytes 34189312 | tf_op jit(solution)/shard_map/tbd,tbv->dv/dot_general | solution.py:80
  262.4 13.6 %psum.60 = f32[]{:T(128)} all-reduce(f32[]{:T(128)} %get-tuple-element.10), channel_id=1, replica_groups=mesh['dp'=4,'seq'=2,'vocab'=4] {'dp','seq'}, use_global_device_ids=true, to_apply=%region_13.14 | all-reduce | flops 1 | bytes 8 | tf_op jit(solution)/shard_map/psum | solution.py:71
  276.7 1.8 convert_element_type.128
  278.5 1.8 convert_element_type.133
  280.2 548.4 %all-reduce.7.cloned.1.call-done = bf16[2048,8032]{0,1:T(8,128)(2,1)} async-done(((bf16[2048,8032]{0,1:T(8,128)(2,1)}), bf16[2048,8032]{0,1:T(8,128)(2,1)}) %all-reduce.7.cloned.1.call-update) | async-done | bytes 32899088 | tf_op jit(solution)/shard_map/psum | solution.py:86
  828.6 23.2 %copy.47 = bf16[2048,8032]{0,1:T(8,128)(2,1)} copy(bf16[2048,8032]{0,1:T(8,128)(2,1)} %all-reduce.7.cloned.1.call-done) | data formatting | bytes 65798144
  (39 shorter events, 5.3 us)
Async XLA Ops:
  7.2 139.8 %copy-start.3 = (s32[1,32]{1,0:T(1,128)S(1)}, s32[1,32]{1,0:T(1,128)}, u32[]{:S(2)}) copy-start(s32[1,32]{1,0:T(1,128)} %param.17) | copy-start | bytes 388
  7.2 71.7 %all-reduce.5.cloned.1.call-start = ((), (), s32[]{:S(2)}) async-start(), calls=%async_computation.4 | async-start | bytes 1048576 | tf_op jit(solution)/shard_map/psum | solution.py:48
  39.2 94.7 %reduce-scatter.5.cloned.1.call-start = ((), (), s32[]{:S(2)}) async-start(), calls=%async_computation.5 | async-start | bytes 3096576 | tf_op jit(solution)/shard_map/reduce_scatter | solution.py:53
  102.2 118.7 %copy-start = (f32[64,1,2048]{2,0,1:T(8,128)S(1)}, f32[64,1,2048]{2,0,1:T(8,128)}, u32[]{:S(2)}) copy-start(f32[64,1,2048]{2,0,1:T(8,128)} %all-reduce.5.cloned.1.call-done) | copy-start | bytes 1572868
  102.2 118.7 %copy-start.1 = (bf16[1,64,2048]{2,1,0:T(8,128)(2,1)S(1)}, bf16[1,64,2048]{2,1,0:T(8,128)(2,1)}, u32[]{:S(2)}) copy-start(bf16[1,64,2048]{2,1,0:T(8,128)(2,1)} %param.14) | copy-start | bytes 786436
  102.2 118.7 %copy-start.2 = (f32[2048]{0:T(1024)S(1)}, f32[2048]{0:T(1024)}, u32[]{:S(2)}) copy-start(f32[2048]{0:T(1024)} %param.15) | copy-start | bytes 24580
  102.3 118.6 %all-reduce.9.cloned.1.call-start = ((), (), s32[]{:S(2)}) async-start(), calls=%async_computation.7 | async-start | bytes 1048576 | tf_op jit(solution)/shard_map/psum | solution.py:87
  183.7 59.6 %reduce-scatter.7.cloned.1.call-start = ((), (), s32[]{:S(2)}) async-start(), calls=%async_computation.8 | async-start | bytes 393216 | tf_op jit(solution)/shard_map/reduce_scatter | solution.py:94
  231.6 45.1 %reduce-scatter.9.cloned.1.call-start = ((), (), s32[]{:S(2)}) async-start(), calls=%async_computation.9 | async-start | bytes 786432 | tf_op jit(solution)/shard_map/reduce_scatter | solution.py:115
  246.1 32.3 %reduce-scatter.11.cloned.1.call-start = ((), (), s32[]{:S(2)}) async-start(), calls=%async_computation.10 | async-start | bytes 786432 | tf_op jit(solution)/shard_map/reduce_scatter | solution.py:121
  247.7 580.9 %all-reduce.7.cloned.1.call-start = ((), (), s32[]{:S(2)}) async-start(), calls=%async_computation.6 | async-start | bytes 65798144 | tf_op jit(solution)/shard_map/psum | solution.py:86
Sparse Core Ops, SparseCore 0:
  39.3 39.4 all-reduce.4
  102.4 31.4 reduce-scatter.4
  183.9 36.9 all-reduce.8
  231.7 11.6 reduce-scatter.6
  246.3 14.5 reduce-scatter.8
  262.9 14.7 reduce-scatter.10
  281.0 547.5 all-reduce.6
where the time goes:
time: 861 us; the launch traced here: 860 us
  waiting for transfers between devices  668 us (78%)
  blocking collectives  77.1 us (9%)
  matrix products  54.7 us (6%)
  local copies, waits for them, and re-layouts  28.4 us (3%)
  between operations  16.7 us (2%)
  other arithmetic  14.2 us (2%)
    psum x1, waiting for transfers between devices, body(): head_total = lax.psum(weight_acc.astype(jnp.bfloat16), 'dp')  548 us
    psum x1, waiting for transfers between devices, body(): lax.psum(mixed_part, 'vocab')  39.6 us
    psum x1, waiting for transfers between devices, body(): summed_grad = lax.psum(hidden_part, 'vocab')  37.1 us
    reduce_scatter x1, waiting for transfers between devices, body(): lax.psum_scatter(jnp.einsum('tbd,dv->tbv', row_block, head_weight, prefer...  31.5 us
    unnamed x11, local copies, waits for them, and re-layouts  25.5 us
  transfers between devices with their start and end apart: 7, of which 5 were waited for; matrix products, arithmetic and copies ran while one was open for 2% of the time, Pallas kernels for 0%

commit v1 on v0

v1 whole, which is shorter than its diff:
```python
import functools
import jax
import jax.numpy as jnp
from jax import lax
from jax.experimental import pallas as pl
from jax.experimental.pallas import tpu as pltpu
from jax.sharding import PartitionSpec as P

HDIM = 256
LANES = 128
TILE = 512
MAX_CHUNKS = 4
LOW = -1e30
CODE_TOP = 32767.0

zloss_weight = 0.0001
norm_epsilon = 1e-06
score_scale = HDIM ** (-0.5)
f32, bf16, i32 = jnp.float32, jnp.bfloat16, jnp.int32

VMEM = pl.BlockSpec(memory_space=pltpu.VMEM)
SMEM = pl.BlockSpec(memory_space=pltpu.SMEM)


def sds(shape, dtype):
    return jax.ShapeDtypeStruct(shape, dtype)


def params(mib=40):
    return pltpu.CompilerParams(vmem_limit_bytes=mib * 1024 * 1024)


def cost(flops, nbytes):
    return pl.CostEstimate(flops=int(flops), bytes_accessed=int(nbytes), transcendentals=0)


def dot(a, b, ca, cb):
    return lax.dot_general(a, b, (((ca,), (cb,)), ((), ())), preferred_element_type=f32)


def from_ahead(x, axis, k):
    n = lax.axis_size(axis)
    return lax.ppermute(x, axis, [((i + k) % n, i) for i in range(n)])


def gather_ring(x, axis):
    return [x] + [from_ahead(x, axis, k) for k in range(1, lax.axis_size(axis))]


def scatter_ring(x, axis, rows):
    n = lax.axis_size(axis)
    return [
        lax.ppermute(x[k * rows : (k + 1) * rows], axis, [(i, (i + k) % n) for i in range(n)])
        for k in range(1, n)
    ]


def swap(x, axis, bit):
    n = lax.axis_size(axis)
    return lax.ppermute(x, axis, [(i, i ^ bit) for i in range(n)])


def gather_swaps(x, axis):
    held = [x]
    bit = lax.axis_size(axis) // 2
    while bit:
        held = held + [swap(h, axis, bit) for h in held]
        bit //= 2
    return held


def tree(terms, op=jnp.add):
    while len(terms) > 1:
        half = len(terms) // 2
        rest = terms[2 * half :]
        terms = [op(terms[i], terms[i + half]) for i in range(half)] + rest
    return terms[0]


def three_parts(x):
    hi = x.astype(bf16).astype(f32)
    mid = (x - hi).astype(bf16).astype(f32)
    return hi, mid, x - hi - mid


def lanes(rows):
    return lax.broadcasted_iota(i32, (rows, LANES), 1)


def attend_kernel(n_seq, scal, *refs):
    q_refs = refs[:n_seq]
    k_ref, v_ref, o_ref, q_out, q_twice = refs[n_seq:]
    tgt_rows = q_refs[0].shape[1]
    rows = tgt_rows * n_seq
    enc, features = k_ref.shape[1:]
    for i, r in enumerate(q_refs):
        for at in (i * tgt_rows, rows + i * tgt_rows):
            q_twice[at : at + tgt_rows, :] = r[0]
    q = q_twice[pl.ds(pl.multiple_of(scal[0], 16), rows), :]
    q_out[...] = q
    valid = lax.broadcasted_iota(i32, (rows, enc), 1) < scal[1]
    lane = lanes(rows)
    stat = jnp.zeros((rows, LANES), f32)
    for h in range(features // HDIM):
        at = slice(h * HDIM, (h + 1) * HDIM)
        scores = dot(q[:, at], k_ref[0, :, at], 1, 1) * score_scale
        scores = jnp.where(valid, scores, LOW)
        peak = jnp.max(scores, axis=1, keepdims=True)
        e = jnp.where(valid, jnp.exp(scores - peak), 0.0)
        total = jnp.sum(e, axis=1, keepdims=True)
        some = total > 0.0
        safe = jnp.where(some, total, 1.0)
        o = dot(e.astype(bf16), v_ref[0, :, at], 1, 0) / safe
        o_ref[:, at] = o.astype(bf16)
        lse = jnp.where(some, peak + jnp.log(safe), LOW)
        for i, part in enumerate(three_parts(lse)):
            stat = jnp.where(lane == 3 * h + i, part, stat)
    o_ref[:, features:] = stat.astype(bf16)


def project_kernel(n_seq, own_rows, *refs):
    o_refs = refs[:n_seq]
    p_ref, mixed_ref, own_ref, att_ref, lse_ref, att = refs[n_seq:]
    rows, features = att.shape

    @pl.when(pl.program_id(0) == 0)
    def _():
        stats = [r[:, features:].astype(f32) for r in o_refs]
        lane = lanes(rows)
        lse_all = jnp.zeros((rows, LANES), f32)
        for h in range(features // HDIM):
            at = slice(h * HDIM, (h + 1) * HDIM)
            lses = [
                s[:, 3 * h : 3 * h + 1] + s[:, 3 * h + 1 : 3 * h + 2] + s[:, 3 * h + 2 : 3 * h + 3]
                for s in stats
            ]
            top = tree(lses, jnp.maximum)
            lse = top + jnp.log(tree([jnp.exp(x - top) for x in lses]))
            o = tree([jnp.exp(x - lse) * r[:, at].astype(f32) for x, r in zip(lses, o_refs)])
            att[:, at] = o.astype(bf16)
            lse_all = jnp.where(lane == h, lse, lse_all)
        att_ref[...] = att[...]
        lse_ref[...] = lse_all

    part = dot(att[...], p_ref[...], 1, 0)
    mixed_ref[...] = part.astype(bf16)
    own_ref[...] = part[:own_rows]


def norm_kernel(n_got, scal, *refs):
    own_ref, got_refs = refs[0], refs[1 : 1 + n_got]
    residual_ref, gain_ref, mixed_ref, ng_ref = refs[1 + n_got :]
    rows, width = own_ref.shape
    res = residual_ref[0, pl.ds(pl.multiple_of(scal[2], 16), rows), :].astype(f32)
    mixed = own_ref[...] + res
    for r in got_refs:
        mixed = mixed + r[...].astype(f32)
    mixed_ref[...] = mixed
    ng_ref[:, :width] = (mixed * gain_ref[...]).astype(bf16)
    square = jnp.sum(mixed * mixed, axis=1, keepdims=True)
    lane = lanes(rows)
    stat = jnp.zeros((rows, LANES), f32)
    for i, part in enumerate(three_parts(square)):
        stat = jnp.where(lane == i, part, stat)
    ng_ref[:, width:] = stat.astype(bf16)


def logits_kernel(first, cols, ng_ref, w_ref, code_ref, stat_ref, z):
    j = pl.program_id(0)
    rows, width = z.shape[0], w_ref.shape[0]
    part = dot(ng_ref[:, :width], w_ref[...], 1, 0)
    if first + z.shape[1] > cols:
        at = first + j * TILE + lax.broadcasted_iota(i32, part.shape, 1)
        part = jnp.where(at < cols, part, 0.0)
    z[:, pl.ds(pl.multiple_of(j * TILE, TILE), TILE)] = part

    @pl.when(j == pl.num_programs(0) - 1)
    def _():
        val = z[...]
        peak = jnp.maximum(jnp.max(jnp.abs(val), axis=1, keepdims=True), 1e-30)
        code_ref[...] = jnp.round(val * (CODE_TOP / peak)).astype(i32).astype(jnp.int16)
        s = ng_ref[:, width:].astype(f32)
        square = s[:, 0:1] + s[:, 1:2] + s[:, 2:3]
        lane = lanes(rows)
        stat_ref[...] = jnp.where(lane == 0, peak / CODE_TOP, jnp.where(lane == 1, square, 0.0))


def hidden_kernel(chunk, first, cols, n_seq, features, scal, *refs):
    code_refs, sc_refs = refs[:n_seq], refs[n_seq : 2 * n_seq]
    refs = refs[2 * n_seq :]
    if chunk:
        tgt_ref, w_ref, acc_prev, st_prev, acc_ref, e_ref, st_ref, lhs = refs
    else:
        tgt_ref, w_ref, acc_ref, e_ref, st_ref, lhs = refs
    j = pl.program_id(0)
    rows, size = e_ref.shape
    partial_cols = first + size > cols

    @pl.when(j == 0)
    def _():
        z = tree([c[...].astype(i32).astype(f32) * s[:, 0:1] for c, s in zip(code_refs, sc_refs)])
        square = tree([s[:, 1:2] for s in sc_refs])
        inv = lax.rsqrt(square / features + norm_epsilon)
        z = z * inv
        at = first + lax.broadcasted_iota(i32, (rows, size), 1)
        hit = at == tgt_ref[:, 0:1]
        if partial_cols:
            z = jnp.where(at < cols, z, LOW)
            hit = hit & (at < cols)
        here = jnp.sum(jnp.where(hit, z, 0.0), axis=1, keepdims=True)
        peak = jnp.max(z, axis=1, keepdims=True)
        if chunk:
            old = st_prev[...]
            peak = jnp.maximum(peak, old[:, 0:1])
            fade = jnp.exp(old[:, 0:1] - peak)
            acc_ref[:rows, :] = acc_prev[:rows, :] * fade
            acc_ref[rows:, :] = acc_prev[rows:, :]
        else:
            old = jnp.zeros((rows, LANES), f32)
            fade = 0.0
            acc_ref[...] = jnp.zeros_like(acc_ref)
        e = jnp.exp(z - peak)
        total = jnp.sum(e, axis=1, keepdims=True) + old[:, 1:2] * fade
        eh = e.astype(bf16)
        e_ref[...] = eh
        lhs[:rows, :] = eh
        lhs[rows:, :] = hit.astype(f32).astype(bf16)
        lane = lanes(rows)
        st = jnp.where(lane == 0, peak, old)
        st = jnp.where(lane == 1, total, st)
        st = jnp.where(lane == 2, here + old[:, 2:3], st)
        st = jnp.where(lane == 3, inv, st)
        st_ref[...] = jnp.where(lane == 8 + chunk, peak, st)

    w = w_ref[...]
    if partial_cols:
        at = first + j * TILE + lax.broadcasted_iota(i32, (1, TILE), 1)
        w = jnp.where(at < cols, w, jnp.zeros_like(w))
    left = lhs[:, pl.ds(pl.multiple_of(j * TILE, TILE), TILE)]
    acc_ref[...] += dot(left, w, 1, 1)


def total_kernel(n_vocab, own_rows, *refs):
    st_refs = refs[:n_vocab]
    acc_ref, part_ref, own_ref, coef_ref, loss_ref = refs[n_vocab:]
    rows = coef_ref.shape[0]
    mine = st_refs[0][...]
    stats = [mine]
    for k in range(1, n_vocab):
        s = st_refs[k][...]
        cut = rows - k * own_rows
        stats.append(jnp.concatenate([s[cut:], s[:cut]], axis=0))
    top = tree([s[:, 0:1] for s in stats], jnp.maximum)
    total = tree([s[:, 1:2] * jnp.exp(s[:, 0:1] - top) for s in stats])
    hit_logit = tree([s[:, 2:3] for s in stats])
    log_total = top + jnp.log(total)
    loss = log_total - hit_logit + zloss_weight * log_total * log_total
    loss_ref[...] = jnp.broadcast_to(jnp.sum(loss, axis=0, keepdims=True), loss_ref.shape)
    lift = 1.0 + 2.0 * zloss_weight * log_total
    inv = mine[:, 3:4]
    lane = lanes(rows)
    coef_ref[...] = jnp.where(lane >= 8, jnp.exp(jnp.minimum(mine - log_total, 30.0)) * lift * inv, inv)
    scale = jnp.exp(mine[:, 0:1] - log_total) * lift
    part = acc_ref[:rows, :] * scale - acc_ref[rows:, :]
    part_ref[...] = part.astype(bf16)
    own_ref[...] = part[:own_rows]


def grad_kernel(firsts, cols, coef_ref, tgt_ref, *refs):
    n = len(firsts)
    for c, first in enumerate(firsts):
        e_ref, g_ref = refs[c], refs[n + c]
        at = first + lax.broadcasted_iota(i32, e_ref.shape, 1)
        hit = at == tgt_ref[:, 0:1]
        inv = coef_ref[:, 0:1]
        g = e_ref[...].astype(f32) * coef_ref[:, 8 + c : 9 + c] - jnp.where(hit, inv, 0.0)
        g_ref[...] = g.astype(bf16)


def head_kernel(n_dp, has_prev, ng_ref, *refs):
    g_refs = refs[:n_dp]
    out_ref = refs[-1]
    g = jnp.concatenate([r[...] for r in g_refs], axis=0)
    width = out_ref.shape[0]
    step = min(width, 512)
    for at in range(0, width, step):
        out_ref[at : at + step, :] = dot(ng_ref[at : at + step, :], g, 1, 0).astype(bf16)


def gate_kernel(n_got, *refs):
    own_ref, got_refs = refs[0], refs[1 : 1 + n_got]
    mixed_ref, gain_ref, gated_ref, dot_ref = refs[1 + n_got :]
    total = own_ref[...]
    for r in got_refs:
        total = total + r[...].astype(f32)
    gated = total * gain_ref[...]
    gated_ref[...] = gated
    inner = jnp.sum(gated * mixed_ref[...], axis=1, keepdims=True)
    dot_ref[...] = jnp.broadcast_to(inner, dot_ref.shape)


def mixed_grad_kernel(n_seq, features, gated_ref, mixed_ref, coef_ref, *refs):
    dot_refs, out_ref = refs[:n_seq], refs[n_seq]
    rows = out_ref.shape[0]
    inner = tree([r[:, 0:1] for r in dot_refs])
    inv = coef_ref[:rows, 0:1]
    out = gated_ref[...] * inv - mixed_ref[...] * (inv * inv * inv * inner / features)
    out_ref[...] = out.astype(bf16)


def back_project_kernel(mg_ref, p_ref, out_ref):
    out_ref[...] = dot(mg_ref[...], p_ref[...], 1, 1).astype(bf16)


def attend_back_kernel(n_seq, scal, *refs):
    a_refs = refs[:n_seq]
    q_ref, k_ref, v_ref, att_ref, lse_ref, kg_ref, vg_ref = refs[n_seq:]
    enc, features = k_ref.shape[1:]
    rows = q_ref.shape[0]
    valid = lax.broadcasted_iota(i32, (rows, enc), 1) < scal[1]
    for h in range(features // HDIM):
        at = slice(h * HDIM, (h + 1) * HDIM)
        grad = tree([r[:, at].astype(f32) for r in a_refs]).astype(bf16)
        q = q_ref[:, at]
        scores = dot(q, k_ref[0, :, at], 1, 1) * score_scale
        w = jnp.where(valid, jnp.exp(jnp.minimum(scores - lse_ref[:, h : h + 1], 0.5)), 0.0)
        prob_grad = dot(grad, v_ref[0, :, at], 1, 1)
        inner = jnp.sum(grad.astype(f32) * att_ref[:, at].astype(f32), axis=1, keepdims=True)
        sg = (w * (prob_grad - inner) * score_scale).astype(bf16)
        vg_ref[0, :, at] = dot(w.astype(bf16), grad, 0, 0)
        kg_ref[0, :, at] = dot(sg, q, 0, 0)


def body(
    queries, enc_keys, enc_values, enc_lengths, out_proj, residual, norm_gain, head_weight, targets
):
    n_seq, n_vocab, n_dp = lax.axis_size("seq"), lax.axis_size("vocab"), lax.axis_size("dp")
    seq, voc = lax.axis_index("seq"), lax.axis_index("vocab")
    tgt_rows, features = queries.shape[1:]
    enc = enc_keys.shape[1]
    rows = tgt_rows * n_seq
    own_rows = rows // n_vocab
    width, cols = head_weight.shape
    full_width = width * n_seq
    tiles = -(-cols // TILE)
    per = -(-tiles // MAX_CHUNKS)
    chunks = [(t, min(per, tiles - t)) for t in range(0, tiles, per)]
    firsts = [t * TILE for t, _ in chunks]
    gain = norm_gain.reshape(1, width)

    start = lax.rem(voc * own_rows - seq * tgt_rows + rows, rows).astype(i32)
    scal = jnp.stack(
        [start, enc_lengths[0] - seq * enc, voc * own_rows, voc * cols]
    ).astype(i32)

    q_parts = gather_ring(queries, "seq")
    tgt_parts = gather_ring(targets.reshape(tgt_rows), "seq")
    tgt_twice = jnp.concatenate(tgt_parts + tgt_parts)
    tgt = lax.dynamic_slice(tgt_twice, (start,), (rows,)) - voc * cols
    tgt = jnp.broadcast_to(tgt[:, None], (rows, LANES))

    o_part, q_all = pl.pallas_call(
        functools.partial(attend_kernel, n_seq),
        out_shape=[sds((rows, features + LANES), bf16), sds((rows, features), bf16)],
        in_specs=[SMEM] + [VMEM] * (n_seq + 2),
        out_specs=[VMEM, VMEM],
        scratch_shapes=[pltpu.VMEM((2 * rows, features), bf16)],
        compiler_params=params(),
        name="attend",
    )(scal, *q_parts, enc_keys, enc_values)

    o_all = gather_ring(o_part, "seq")
    ptile = min(TILE, width)
    whole = lambda shape: pl.BlockSpec(shape, lambda j: (0, 0))
    mixed_part, mixed_own, att, lse = pl.pallas_call(
        functools.partial(project_kernel, n_seq, own_rows),
        grid=(width // ptile,),
        out_shape=[
            sds((rows, width), bf16),
            sds((own_rows, width), f32),
            sds((rows, features), bf16),
            sds((rows, LANES), f32),
        ],
        in_specs=[whole((rows, features + LANES))] * n_seq
        + [pl.BlockSpec((features, ptile), lambda j: (0, j))],
        out_specs=[
            pl.BlockSpec((rows, ptile), lambda j: (0, j)),
            pl.BlockSpec((own_rows, ptile), lambda j: (0, j)),
            whole((rows, features)),
            whole((rows, LANES)),
        ],
        scratch_shapes=[pltpu.VMEM((rows, features), bf16)],
        compiler_params=params(),
        name="project",
    )(*o_all, out_proj)

    got = scatter_ring(mixed_part, "vocab", own_rows)
    mixed, ng_own = pl.pallas_call(
        functools.partial(norm_kernel, len(got)),
        out_shape=[sds((own_rows, width), f32), sds((own_rows, width + LANES), bf16)],
        in_specs=[SMEM] + [VMEM] * (len(got) + 3),
        out_specs=[VMEM, VMEM],
        compiler_params=params(),
        name="norm",
    )(scal, mixed_own, *got, residual, gain)
    ng = jnp.concatenate(gather_ring(ng_own, "vocab"), axis=0)

    ng_dp = gather_swaps(ng[:, :width], "dp")
    ng_turned = jnp.concatenate(ng_dp, axis=0).T

    codes, stats = [], []
    for tile0, n in chunks:
        size = n * TILE
        code, stat = pl.pallas_call(
            functools.partial(logits_kernel, tile0 * TILE, cols),
            grid=(n,),
            out_shape=[sds((rows, size), jnp.int16), sds((rows, LANES), f32)],
            in_specs=[
                whole((rows, width + LANES)),
                pl.BlockSpec((width, TILE), lambda j, t=tile0: (0, t + j)),
            ],
            out_specs=[whole((rows, size)), whole((rows, LANES))],
            scratch_shapes=[pltpu.VMEM((rows, size), f32)],
            compiler_params=params(),
            cost_estimate=cost(2 * 256 * width * size, 2 * width * size),
            name="logits",
        )(ng, head_weight)
        codes.append(gather_ring(code, "seq"))
        stats.append(gather_ring(stat, "seq"))

    acc = st = None
    exps = []
    for c, (tile0, n) in enumerate(chunks):
        size = n * TILE
        prev = [acc, st] if c else []
        acc, e, st = pl.pallas_call(
            functools.partial(hidden_kernel, c, tile0 * TILE, cols, n_seq, full_width),
            grid=(n,),
            out_shape=[sds((2 * rows, width), f32), sds((rows, size), bf16), sds((rows, LANES), f32)],
            in_specs=[SMEM]
            + [whole((rows, size))] * n_seq
            + [whole((rows, LANES))] * (n_seq + 1)
            + [pl.BlockSpec((width, TILE), lambda j, t=tile0: (0, t + j))]
            + ([whole((2 * rows, width)), whole((rows, LANES))] if c else []),
            out_specs=[whole((2 * rows, width)), whole((rows, size)), whole((rows, LANES))],
            scratch_shapes=[pltpu.VMEM((2 * rows, size), bf16)],
            compiler_params=params(),
            cost_estimate=cost(2 * 256 * width * size, 2 * width * size),
            name="hidden",
        )(scal, *codes[c], *stats[c], tgt, head_weight, *prev)
        exps.append(e)

    st_all = gather_ring(st, "vocab")
    hidden_part, hidden_own, coef, loss = pl.pallas_call(
        functools.partial(total_kernel, n_vocab, own_rows),
        out_shape=[
            sds((rows, width), bf16),
            sds((own_rows, width), f32),
            sds((rows, LANES), f32),
            sds((8, LANES), f32),
        ],
        in_specs=[VMEM] * (n_vocab + 1),
        out_specs=[VMEM] * 4,
        compiler_params=params(),
        name="total",
    )(*st_all, acc)
    got = scatter_ring(hidden_part, "vocab", own_rows)

    grads = pl.pallas_call(
        functools.partial(grad_kernel, firsts, cols),
        out_shape=[sds(e.shape, bf16) for e in exps],
        in_specs=[VMEM] * (2 + len(exps)),
        out_specs=[VMEM] * len(exps),
        compiler_params=params(),
        name="logit_grad",
    )(coef, tgt, *exps)
    bit = n_dp // 2
    while bit:
        loss = loss + swap(loss, "dp", bit)
        bit //= 2
    mean_loss = loss[0, 0] / (n_dp * rows)

    gated, inner = pl.pallas_call(
        functools.partial(gate_kernel, len(got)),
        out_shape=[sds((own_rows, width), f32), sds((own_rows, LANES), f32)],
        in_specs=[VMEM] * (len(got) + 3),
        out_specs=[VMEM, VMEM],
        compiler_params=params(),
        name="gate",
    )(hidden_own, *got, mixed, gain)
    inner_all = gather_ring(inner, "seq")
    mixed_grad = pl.pallas_call(
        functools.partial(mixed_grad_kernel, n_seq, full_width),
        out_shape=sds((own_rows, width), bf16),
        in_specs=[VMEM] * (3 + n_seq),
        out_specs=VMEM,
        compiler_params=params(),
        name="mixed_grad",
    )(gated, mixed, coef, *inner_all)
    mg = jnp.concatenate(gather_ring(mixed_grad, "vocab"), axis=0)

    ftile = min(256, features)
    back_part = pl.pallas_call(
        back_project_kernel,
        grid=(features // ftile,),
        out_shape=sds((rows, features), bf16),
        in_specs=[whole((rows, width)), pl.BlockSpec((ftile, width), lambda j: (j, 0))],
        out_specs=pl.BlockSpec((rows, ftile), lambda j: (0, j)),
        compiler_params=params(),
        name="back_project",
    )(mg, out_proj)
    back_all = gather_ring(back_part, "seq")
    key_grad, value_grad = pl.pallas_call(
        functools.partial(attend_back_kernel, n_seq),
        out_shape=[sds(enc_keys.shape, f32), sds(enc_values.shape, f32)],
        in_specs=[SMEM] + [VMEM] * (n_seq + 5),
        out_specs=[VMEM, VMEM],
        compiler_params=params(),
        name="attend_back",
    )(scal, *back_all, q_all, enc_keys, enc_values, att, lse)

    head = None
    for c, (tile0, n) in enumerate(chunks):
        g_all = gather_swaps(grads[c], "dp")
        place = pl.BlockSpec((width, TILE), lambda j, t=tile0: (0, t + j))
        prev = [head] if c else []
        head = pl.pallas_call(
            functools.partial(head_kernel, n_dp, bool(c)),
            grid=(n,),
            out_shape=sds((width, cols), bf16),
            in_specs=[whole((width, n_dp * rows))]
            + [pl.BlockSpec((rows, TILE), lambda j: (0, j))] * n_dp
            + [pl.BlockSpec(memory_space=pl.ANY)] * len(prev),
            out_specs=place,
            input_output_aliases={1 + n_dp: 0} if c else {},
            compiler_params=params(),
            cost_estimate=cost(2 * n_dp * rows * width * n * TILE, 2 * width * n * TILE),
            name="head_grad",
        )(ng_turned, *g_all, *prev)
    return (mean_loss, head, key_grad, value_grad)


def solution(mesh):
    placed = (
        P("dp", "seq", "vocab"),
        P("dp", "seq", "vocab"),
        P("dp", "seq", "vocab"),
        P("dp"),
        P("vocab", "seq"),
        P("dp", None, "seq"),
        P("seq"),
        P("seq", "vocab"),
        P("dp", "seq"),
    )
    return jax.shard_map(
        body,
        mesh=mesh,
        in_specs=placed,
        out_specs=(P(), P("seq", "vocab"), P("dp", "seq", "vocab"), P("dp", "seq", "vocab")),
        check_vma=False,
    )
```

time: 861 us -> 244 us (0.28)
  waiting for transfers between devices: 668 us -> 25.5 us
  blocking collectives: 77.1 us -> 0 us
  Pallas kernels: 0 us -> 75.9 us
  local copies, waits for them, and re-layouts: 28.4 us -> 88.5 us
  matrix products: 54.7 us -> 0 us
  starting transfers between devices: 0.29 us -> 46.2 us
  between operations: 16.7 us -> 3.36 us
  other arithmetic: 14.2 us -> 1.69 us
    psum x3 -> x0, waiting for transfers between devices: 625 us -> none  [the longest x1 548 us: body(): head_total = lax.psum(weight_acc.astype(jnp.bfloat16), 'dp')]
    pallas_call x0 -> x21, Pallas kernels: none -> 75.9 us  [the longest x4 25.4 us: body(): pl.pallas_call(functools.partial(hidden_kernel, c, tile0 * TILE, cols, n_...]
    unnamed x11 -> x22, local copies, waits for them, and re-layouts: 25.5 us -> 86.3 us
    dot_general x10 -> x0, matrix products: 54.7 us -> none  [the longest x1 15.9 us: body(): jnp.einsum('tbd,dv->tbv', row_block, head_weight, preferred_element_type=...]
    ppermute x0 -> x45, starting transfers between devices: none -> 46.2 us  [the longest x22 26.4 us: from_ahead(): return lax.ppermute(x, axis, [((i + k) % n, i) for i in range(n)])]
    reduce_scatter x4 -> x0, waiting for transfers between devices: 43.3 us -> none  [the longest x1 31.5 us: body(): lax.psum_scatter(jnp.einsum('tbd,dv->tbv', row_block, head_weight, prefer...]
    all_gather x4 -> x0, blocking collectives: 33.6 us -> none  [the longest x1 10.4 us: body(): grad_piece = lax.all_gather(logit_grad, 'seq', axis=0, tiled=True)]
    psum x4 -> x0, blocking collectives: 31.9 us -> none  [the longest x1 13.6 us: body(): lax.psum(jnp.sum(token_loss), ('dp', 'seq'))]
  transfers between devices with their start and end apart: 7 -> 45, of which waited for: 5 -> 16; matrix products, arithmetic and copies ran while one was open for 2% -> 17% of each run, Pallas kernels for 0% -> 22%
where the time goes in v1:
time: 244 us; the launch traced here: 241 us
  local copies, waits for them, and re-layouts  88.5 us (36%)
  Pallas kernels  75.9 us (31%)
  starting transfers between devices  46.2 us (19%)
  waiting for transfers between devices  25.5 us (10%)
  between operations  3.36 us (1%)
    unnamed x22, local copies, waits for them, and re-layouts  86.3 us
    ppermute x22, starting transfers between devices, from_ahead(): return lax.ppermute(x, axis, [((i + k) % n, i) for i in range(n)])  26.4 us
    pallas_call x4, Pallas kernels, body(): pl.pallas_call(functools.partial(hidden_kernel, c, tile0 * TILE, cols, n_...  25.4 us
    pallas_call x4, Pallas kernels, body(): pl.pallas_call(functools.partial(head_kernel, n_dp, bool(c)), grid=(n,),...  20.4 us
    pallas_call x4, Pallas kernels, body(): pl.pallas_call(functools.partial(logits_kernel, tile0 * TILE, cols), grid...  20.4 us
    ppermute x22, waiting for transfers between devices, from_ahead(): return lax.ppermute(x, axis, [((i + k) % n, i) for i in range(n)])  10.5 us
    ppermute x17, starting transfers between devices, swap(): return lax.ppermute(x, axis, [(i, i ^ bit) for i in range(n)])  9.95 us
    ppermute x6, starting transfers between devices, scatter_ring(): lax.ppermute(x[k * rows:(k + 1) * rows], axis, [(i, (i + k) % n) for i in...  9.87 us
  transfers between devices with their start and end apart: 45, of which 16 were waited for; matrix products, arithmetic and copies ran while one was open for 17% of the time, Pallas kernels for 22%

profile of v1, /device:TPU:0, one launch (start us, length us, event | category | flops | bytes accessed | tf_op | source)
XLA Modules:
  0.0 241.1 jit_solution(15298706875350749830)
XLA Ops:
  0.6 3.0 %collective-permute-start = (bf16[1,32,1024]{2,1,0:T(8,128)(2,1)}, bf16[1,32,1024]{2,1,0:T(8,128)(2,1)S(1)}, u32[]{:S(2)}, u32[]{:S(2)}) collective-permute-start(bf16[1,32,1024]{2,1,0:T(8,128)(2,1)} %refs_0_.1), channel_id=1, source_target_pairs={{4,0},{0,4},{5,1},{1,5},{6,2},{2,6},{7,3},{3,7},{12,8},{8,12},{13,... | collective-permute-start | bytes 196616 | tf_op jit(solution)/shard_map/ppermute | solution.py:43
  10.5 2.1 collective-permute-start.1
  12.6 38.8 %copy.38.w_ref.refs_5_ = bf16[2048,8032]{1,0:T(8,128)(2,1)} copy(bf16[2048,8032]{0,1:T(8,128)(2,1)} %param.16) | data formatting | bytes 65798144 | tf_op args[7]
  51.5 2.2 copy-done
  53.7 1.9 project.1
  55.6 2.1 collective-permute-start.2
  57.6 2.6 %collective-permute-start.3 = (bf16[16,2048]{1,0:T(8,128)(2,1)S(1)}, bf16[16,2048]{1,0:T(8,128)(2,1)S(1)}, u32[]{:S(2)}, u32[]{:S(2)}) collective-permute-start(bf16[16,2048]{1,0:T(8,128)(2,1)S(1)} %get-tuple-element.96), channel_id=1, source_target_pairs={{0,2},{1,3},{2,0},{3,1},{4,6},{5,7},{6,4},{7,5},{8,10},{9,11},{10,... | collective-permute-start | bytes 196616 | tf_op jit(solution)/shard_map/ppermute | solution.py:53
  62.9 2.0 collective-permute-done.4.refs_3_
  65.6 2.8 %collective-permute-start.5 = (bf16[16,2176]{1,0:T(8,128)(2,1)S(1)}, bf16[16,2176]{1,0:T(8,128)(2,1)S(1)}, u32[]{:S(2)}, u32[]{:S(2)}) collective-permute-start(bf16[16,2176]{1,0:T(8,128)(2,1)S(1)} %get-tuple-element.47), channel_id=1, source_target_pairs={{1,0},{2,1},{3,2},{0,3},{5,4},{6,5},{7,6},{4,7},{9,8},{10,9},{11,1... | collective-permute-start | bytes 208904 | tf_op jit(solution)/shard_map/ppermute | solution.py:43
  71.1 2.4 %collective-permute-done.6 = bf16[16,2176]{1,0:T(8,128)(2,1)S(1)} collective-permute-done((bf16[16,2176]{1,0:T(8,128)(2,1)S(1)}, bf16[16,2176]{1,0:T(8,128)(2,1)S(1)}, u32[]{:S(2)}, u32[]{:S(2)}) %collective-permute-start.6) | collective-permute-done | bytes 69664 | tf_op jit(solution)/shard_map/ppermute | solution.py:43
  75.8 5.1 %logits.7 = (s16[64,2048]{1,0:T(8,128)(2,1)S(1)}, f32[64,128]{1,0:T(8,128)S(1)}) custom-call(bf16[64,2176]{1,0:T(8,128)(2,1)S(1)} %copy.37.ng_ref, bf16[2048,8032]{1,0:T(8,128)(2,1)} %copy.38.w_ref.refs_5_), custom_call_target="tpu_custom_call" | custom-call | flops 2147483648 | bytes 8388608 | tf_op jit(solution)/shard_map/logits/pallas_call | solution.py:414
  80.9 5.1 %logits.6 = (s16[64,2048]{1,0:T(8,128)(2,1)S(1)}, f32[64,128]{1,0:T(8,128)S(1)}) custom-call(bf16[64,2176]{1,0:T(8,128)(2,1)S(1)} %copy.37.ng_ref, bf16[2048,8032]{1,0:T(8,128)(2,1)} %copy.38.w_ref.refs_5_), custom_call_target="tpu_custom_call" | custom-call | flops 2147483648 | bytes 8388608 | tf_op jit(solution)/shard_map/logits/pallas_call | solution.py:414
  87.7 5.1 %logits.5 = (s16[64,2048]{1,0:T(8,128)(2,1)S(1)}, f32[64,128]{1,0:T(8,128)S(1)}) custom-call(bf16[64,2176]{1,0:T(8,128)(2,1)S(1)} %copy.37.ng_ref, bf16[2048,8032]{1,0:T(8,128)(2,1)} %copy.38.w_ref.refs_5_), custom_call_target="tpu_custom_call" | custom-call | flops 2147483648 | bytes 8388608 | tf_op jit(solution)/shard_map/logits/pallas_call | solution.py:414
  94.9 4.9 %logits.4 = (s16[64,2048]{1,0:T(8,128)(2,1)S(1)}, f32[64,128]{1,0:T(8,128)S(1)}) custom-call(bf16[64,2176]{1,0:T(8,128)(2,1)S(1)} %copy.37.ng_ref, bf16[2048,8032]{1,0:T(8,128)(2,1)} %copy.38.w_ref.refs_5_), custom_call_target="tpu_custom_call" | custom-call | flops 2147483648 | bytes 8388608 | tf_op jit(solution)/shard_map/logits/pallas_call | solution.py:414
  104.0 6.4 %hidden.4 = (f32[128,2048]{1,0:T(8,128)S(1)}, bf16[64,2048]{1,0:T(8,128)(2,1)S(1)}, f32[64,128]{1,0:T(8,128)S(1)}) custom-call(s32[4]{0:T(128)S(1)} %pad_add_fusion.scal, s16[64,2048]{1,0:T(8,128)(2,1)S(1)} %get-tuple-element.54.refs_0_, s16[64,2048]{1,0:T(8,128)(2,1)S(1)} %collective-permute-done.15.refs_1_, f32[64,128]{1,0:T(8,128)S(1)} %get-tuple-element.55.refs_2_, ...), custom_call_target="tpu_custom_call" | custom-call | flops 2147483648 | bytes 8388608 | tf_op jit(solution)/shard_map/hidden/pallas_call | solution.py:436
  111.0 6.4 %hidden.5 = (f32[128,2048]{1,0:T(8,128)S(1)}, bf16[64,2048]{1,0:T(8,128)(2,1)S(1)}, f32[64,128]{1,0:T(8,128)S(1)}) custom-call(s32[4]{0:T(128)S(1)} %pad_add_fusion.scal, s16[64,2048]{1,0:T(8,128)(2,1)S(1)} %get-tuple-element.52.refs_0_, s16[64,2048]{1,0:T(8,128)(2,1)S(1)} %collective-permute-done.13.refs_1_, f32[64,128]{1,0:T(8,128)S(1)} %get-tuple-element.53.refs_2_, ...), custom_call_target="tpu_custom_call" | custom-call | flops 2147483648 | bytes 8388608 | tf_op jit(solution)/shard_map/hidden/pallas_call | solution.py:436
  117.4 6.4 %hidden.6 = (f32[128,2048]{1,0:T(8,128)S(1)}, bf16[64,2048]{1,0:T(8,128)(2,1)S(1)}, f32[64,128]{1,0:T(8,128)S(1)}) custom-call(s32[4]{0:T(128)S(1)} %pad_add_fusion.scal, s16[64,2048]{1,0:T(8,128)(2,1)S(1)} %get-tuple-element.50.refs_0_, s16[64,2048]{1,0:T(8,128)(2,1)S(1)} %collective-permute-done.11.refs_1_, f32[64,128]{1,0:T(8,128)S(1)} %get-tuple-element.51.refs_2_, ...), custom_call_target="tpu_custom_call" | custom-call | flops 2147483648 | bytes 8388608 | tf_op jit(solution)/shard_map/hidden/pallas_call | solution.py:436
  123.9 6.2 %hidden.7 = (f32[128,2048]{1,0:T(8,128)S(1)}, bf16[64,2048]{1,0:T(8,128)(2,1)S(1)}, f32[64,128]{1,0:T(8,128)S(1)}) custom-call(s32[4]{0:T(128)S(1)} %pad_add_fusion.scal, s16[64,2048]{1,0:T(8,128)(2,1)S(1)} %get-tuple-element.48.refs_0_, s16[64,2048]{1,0:T(8,128)(2,1)S(1)} %collective-permute-done.8.refs_1_, f32[64,128]{1,0:T(8,128)S(1)} %get-tuple-element.49.refs_2_, ...), custom_call_target="tpu_custom_call" | custom-call | flops 2147483648 | bytes 8388608 | tf_op jit(solution)/shard_map/hidden/pallas_call | solution.py:436
  131.4 1.9 collective-permute-start.19
  139.4 1.9 collective-permute-start.39
  141.3 2.4 collective-permute-done.37.refs_1_
  146.6 2.1 collective-permute-done.40.refs_1_
  148.8 2.5 %collective-permute-start.41 = (bf16[16,2048]{1,0:T(8,128)(2,1)S(1)}, bf16[16,2048]{1,0:T(8,128)(2,1)S(1)}, u32[]{:S(2)}, u32[]{:S(2)}) collective-permute-start(bf16[16,2048]{1,0:T(8,128)(2,1)S(1)} %mixed_grad.1), channel_id=1, source_target_pairs={{1,0},{2,1},{3,2},{0,3},{5,4},{6,5},{7,6},{4,7},{9,8},{10,9},{11,1... | collective-permute-start | bytes 196616 | tf_op jit(solution)/shard_map/ppermute | solution.py:43
  158.0 1.9 back_project.1.refs_0_
  162.9 1.8 collective-permute-done.34.refs_1_
  166.5 3.9 %collective-permute-done.31.refs_1_ = bf16[64,2048]{1,0:T(8,128)(2,1)S(1)} collective-permute-done((bf16[64,2048]{1,0:T(8,128)(2,1)S(1)}, bf16[64,2048]{1,0:T(8,128)(2,1)S(1)}, u32[]{:S(2)}, u32[]{:S(2)}) %collective-permute-start.31) | collective-permute-done | bytes 262176 | tf_op jit(solution)/shard_map/ppermute | solution.py:60
  172.6 2.6 %attend_back.1 = (f32[1,128,1024]{2,1,0:T(8,128)}, f32[1,128,1024]{2,1,0:T(8,128)}) custom-call(s32[4]{0:T(128)S(1)} %pad_add_fusion.scal, bf16[64,1024]{1,0:T(8,128)(2,1)S(1)} %back_project.1.refs_0_, bf16[64,1024]{1,0:T(8,128)(2,1)S(1)} %collective-permute-done.44.refs_1_, bf16[64,1024]{1,0:T(8,128)(2,1)S(1)} %get-tuple-element.79.refs_2_, ...), custom_call_target="tpu_custom_call" | custom-call | tf_op jit(solution)/shard_map/attend_back/pallas_call | solution.py:513
  176.5 5.2 %head_grad.4.refs_4_ = bf16[2048,8032]{1,0:T(8,128)(2,1)} custom-call(bf16[2048,256]{1,0:T(8,128)(2,1)S(1)} %maximum_bitcast_fusion.ng_ref, bf16[64,2048]{1,0:T(8,128)(2,1)S(1)} %get-tuple-element.73.refs_0_, bf16[64,2048]{1,0:T(8,128)(2,1)S(1)} %collective-permute-done.34.refs_1_, bf16[64,2048]{1,0:T(8,128)(2,1)S(1)} %collective-permute-done.35.refs_2_, ...), custom_call_target="tpu_custom_call" | custom-call | flops 2147483648 | bytes 8388608 | tf_op jit(solution)/shard_map/head_grad/pallas_call | solution.py:527
  182.2 5.1 %head_grad.5.refs_4_ = bf16[2048,8032]{1,0:T(8,128)(2,1)} custom-call(bf16[2048,256]{1,0:T(8,128)(2,1)S(1)} %maximum_bitcast_fusion.ng_ref, bf16[64,2048]{1,0:T(8,128)(2,1)S(1)} %get-tuple-element.72.refs_0_, bf16[64,2048]{1,0:T(8,128)(2,1)S(1)} %collective-permute-done.31.refs_1_, ...), custom_call_target="tpu_custom_call", output_to_operand_aliasing={{}: (5, {})} | custom-call | flops 2147483648 | bytes 8388608 | tf_op jit(solution)/shard_map/head_grad/pallas_call | solution.py:527
  187.3 5.2 %head_grad.6.refs_4_ = bf16[2048,8032]{1,0:T(8,128)(2,1)} custom-call(bf16[2048,256]{1,0:T(8,128)(2,1)S(1)} %maximum_bitcast_fusion.ng_ref, bf16[64,2048]{1,0:T(8,128)(2,1)S(1)} %get-tuple-element.71.refs_0_, bf16[64,2048]{1,0:T(8,128)(2,1)S(1)} %collective-permute-done.28.refs_1_, ...), custom_call_target="tpu_custom_call", output_to_operand_aliasing={{}: (5, {})} | custom-call | flops 2147483648 | bytes 8388608 | tf_op jit(solution)/shard_map/head_grad/pallas_call | solution.py:527
  192.5 4.9 %head_grad.7 = bf16[2048,8032]{1,0:T(8,128)(2,1)} custom-call(bf16[2048,256]{1,0:T(8,128)(2,1)S(1)} %maximum_bitcast_fusion.ng_ref, bf16[64,2048]{1,0:T(8,128)(2,1)S(1)} %get-tuple-element.70.refs_0_, bf16[64,2048]{1,0:T(8,128)(2,1)S(1)} %collective-permute-done.25.refs_1_, ...), custom_call_target="tpu_custom_call", output_to_operand_aliasing={{}: (5, {})} | custom-call | flops 2147483648 | bytes 8388608 | tf_op jit(solution)/shard_map/head_grad/pallas_call | solution.py:527
  197.4 42.6 %copy.49 = bf16[2048,8032]{0,1:T(8,128)(2,1)} copy(bf16[2048,8032]{1,0:T(8,128)(2,1)} %head_grad.7) | data formatting | bytes 65798144
  (119 shorter events, 48.2 us)
Async XLA Ops:
  10.5 41.0 %collective-permute-start.1 = (bf16[64,1152]{1,0:T(8,128)(2,1)S(1)}, bf16[64,1152]{1,0:T(8,128)(2,1)S(1)}, u32[]{:S(2)}, u32[]{:S(2)}) collective-permute-start(bf16[64,1152]{1,0:T(8,128)(2,1)S(1)} %get-tuple-element.44.refs_0_), channel_id=1, source_target_pairs={{4,0},{0,4},{5,1},{1,5},{6,2},{2,6},{7,3},{3,7},{12,8},{8,12},{13,... | collective-permute-start | bytes 442376 | tf_op jit(solution)/shard_map/ppermute | solution.py:43
  12.6 49.0 %collective-permute-start.10 = (s32[32]{0:T(128)}, s32[32]{0:T(128)S(1)}, u32[]{:S(2)}, u32[]{:S(2)}) collective-permute-start(s32[32]{0:T(128)} %bitcast.13), channel_id=1, source_target_pairs={{4,0},{0,4},{5,1},{1,5},{6,2},{2,6},{7,3},{3,7},{12,8},{8,12},{13,... | collective-permute-start | bytes 392 | tf_op jit(solution)/shard_map/ppermute | solution.py:43
  55.6 6.6 %collective-permute-start.2 = (bf16[16,2048]{1,0:T(8,128)(2,1)S(1)}, bf16[16,2048]{1,0:T(8,128)(2,1)S(1)}, u32[]{:S(2)}, u32[]{:S(2)}) collective-permute-start(bf16[16,2048]{1,0:T(8,128)(2,1)S(1)} %get-tuple-element.97), channel_id=1, source_target_pairs={{0,1},{1,2},{2,3},{3,0},{4,5},{5,6},{6,7},{7,4},{8,9},{9,10},{10,1... | collective-permute-start | bytes 196616 | tf_op jit(solution)/shard_map/ppermute | solution.py:53
  68.3 6.1 %collective-permute-start.7 = (bf16[16,2176]{1,0:T(8,128)(2,1)S(1)}, bf16[16,2176]{1,0:T(8,128)(2,1)S(1)}, u32[]{:S(2)}, u32[]{:S(2)}) collective-permute-start(bf16[16,2176]{1,0:T(8,128)(2,1)S(1)} %get-tuple-element.47), channel_id=1, source_target_pairs={{3,0},{0,1},{1,2},{2,3},{7,4},{4,5},{5,6},{6,7},{11,8},{8,9},{9,10... | collective-permute-start | bytes 208904 | tf_op jit(solution)/shard_map/ppermute | solution.py:43
  86.1 16.4 %collective-permute-start.15 = (s16[64,2048]{1,0:T(8,128)(2,1)S(1)}, s16[64,2048]{1,0:T(8,128)(2,1)S(1)}, u32[]{:S(2)}, u32[]{:S(2)}) collective-permute-start(s16[64,2048]{1,0:T(8,128)(2,1)S(1)} %get-tuple-element.54.refs_0_), channel_id=1, source_target_pairs={{4,0},{0,4},{5,1},{1,5},{6,2},{2,6},{7,3},{3,7},{12,8},{8,12},{13,... | collective-permute-start | bytes 786440 | tf_op jit(solution)/shard_map/ppermute | solution.py:43
  92.8 9.1 %collective-permute-start.16 = (f32[64,128]{1,0:T(8,128)S(1)}, f32[64,128]{1,0:T(8,128)S(1)}, u32[]{:S(2)}, u32[]{:S(2)}) collective-permute-start(f32[64,128]{1,0:T(8,128)S(1)} %get-tuple-element.55.refs_2_), channel_id=1, source_target_pairs={{4,0},{0,4},{5,1},{1,5},{6,2},{2,6},{7,3},{3,7},{12,8},{8,12},{13,... | collective-permute-start | bytes 98312 | tf_op jit(solution)/shard_map/ppermute | solution.py:43
  93.4 17.6 %collective-permute-start.13 = (s16[64,2048]{1,0:T(8,128)(2,1)S(1)}, s16[64,2048]{1,0:T(8,128)(2,1)S(1)}, u32[]{:S(2)}, u32[]{:S(2)}) collective-permute-start(s16[64,2048]{1,0:T(8,128)(2,1)S(1)} %get-tuple-element.52.refs_0_), channel_id=1, source_target_pairs={{4,0},{0,4},{5,1},{1,5},{6,2},{2,6},{7,3},{3,7},{12,8},{8,12},{13,... | collective-permute-start | bytes 786440 | tf_op jit(solution)/shard_map/ppermute | solution.py:43
  99.8 10.6 %collective-permute-start.14 = (f32[64,128]{1,0:T(8,128)S(1)}, f32[64,128]{1,0:T(8,128)S(1)}, u32[]{:S(2)}, u32[]{:S(2)}) collective-permute-start(f32[64,128]{1,0:T(8,128)S(1)} %get-tuple-element.53.refs_2_), channel_id=1, source_target_pairs={{4,0},{0,4},{5,1},{1,5},{6,2},{2,6},{7,3},{3,7},{12,8},{8,12},{13,... | collective-permute-start | bytes 98312 | tf_op jit(solution)/shard_map/ppermute | solution.py:43
  100.4 17.0 %collective-permute-start.11 = (s16[64,2048]{1,0:T(8,128)(2,1)S(1)}, s16[64,2048]{1,0:T(8,128)(2,1)S(1)}, u32[]{:S(2)}, u32[]{:S(2)}) collective-permute-start(s16[64,2048]{1,0:T(8,128)(2,1)S(1)} %get-tuple-element.50.refs_0_), channel_id=1, source_target_pairs={{4,0},{0,4},{5,1},{1,5},{6,2},{2,6},{7,3},{3,7},{12,8},{8,12},{13,... | collective-permute-start | bytes 786440 | tf_op jit(solution)/shard_map/ppermute | solution.py:43
  101.9 15.5 %collective-permute-start.12 = (f32[64,128]{1,0:T(8,128)S(1)}, f32[64,128]{1,0:T(8,128)S(1)}, u32[]{:S(2)}, u32[]{:S(2)}) collective-permute-start(f32[64,128]{1,0:T(8,128)S(1)} %get-tuple-element.51.refs_2_), channel_id=1, source_target_pairs={{4,0},{0,4},{5,1},{1,5},{6,2},{2,6},{7,3},{3,7},{12,8},{8,12},{13,... | collective-permute-start | bytes 98312 | tf_op jit(solution)/shard_map/ppermute | solution.py:43
  102.4 21.4 %collective-permute-start.8 = (s16[64,2048]{1,0:T(8,128)(2,1)S(1)}, s16[64,2048]{1,0:T(8,128)(2,1)S(1)}, u32[]{:S(2)}, u32[]{:S(2)}) collective-permute-start(s16[64,2048]{1,0:T(8,128)(2,1)S(1)} %get-tuple-element.48.refs_0_), channel_id=1, source_target_pairs={{4,0},{0,4},{5,1},{1,5},{6,2},{2,6},{7,3},{3,7},{12,8},{8,12},{13,... | collective-permute-start | bytes 786440 | tf_op jit(solution)/shard_map/ppermute | solution.py:43
  110.4 13.4 %collective-permute-start.9 = (f32[64,128]{1,0:T(8,128)S(1)}, f32[64,128]{1,0:T(8,128)S(1)}, u32[]{:S(2)}, u32[]{:S(2)}) collective-permute-start(f32[64,128]{1,0:T(8,128)S(1)} %get-tuple-element.49.refs_2_), channel_id=1, source_target_pairs={{4,0},{0,4},{5,1},{1,5},{6,2},{2,6},{7,3},{3,7},{12,8},{8,12},{13,... | collective-permute-start | bytes 98312 | tf_op jit(solution)/shard_map/ppermute | solution.py:43
  133.4 18.6 %collective-permute-start.22 = (bf16[64,2048]{0,1:T(8,128)(2,1)S(1)}, bf16[64,2048]{0,1:T(8,128)(2,1)S(1)}, u32[]{:S(2)}, u32[]{:S(2)}) collective-permute-start(bf16[64,2048]{0,1:T(8,128)(2,1)S(1)} %slice.32), channel_id=1, source_target_pairs={{0,16},{8,24},{16,0},{24,8},{1,17},{9,25},{17,1},{25,9},{2,18},{10... | collective-permute-start | bytes 786440 | tf_op jit(solution)/shard_map/ppermute | solution.py:60
  134.9 20.6 %collective-permute-start.23 = (bf16[64,2048]{0,1:T(8,128)(2,1)S(1)}, bf16[64,2048]{0,1:T(8,128)(2,1)S(1)}, u32[]{:S(2)}, u32[]{:S(2)}) collective-permute-start(bf16[64,2048]{0,1:T(8,128)(2,1)S(1)} %slice.32), channel_id=1, source_target_pairs={{0,8},{8,0},{16,24},{24,16},{1,9},{9,1},{17,25},{25,17},{2,10},{10... | collective-permute-start | bytes 786440 | tf_op jit(solution)/shard_map/ppermute | solution.py:60
  137.4 6.2 %collective-permute-start.37 = (bf16[16,2048]{1,0:T(8,128)(2,1)S(1)}, bf16[16,2048]{1,0:T(8,128)(2,1)S(1)}, u32[]{:S(2)}, u32[]{:S(2)}) collective-permute-start(bf16[16,2048]{1,0:T(8,128)(2,1)S(1)} %get-tuple-element.94), channel_id=1, source_target_pairs={{0,1},{1,2},{2,3},{3,0},{4,5},{5,6},{6,7},{7,4},{8,9},{9,10},{10,1... | collective-permute-start | bytes 196616 | tf_op jit(solution)/shard_map/ppermute | solution.py:53
  137.6 7.3 %collective-permute-start.38 = (bf16[16,2048]{1,0:T(8,128)(2,1)S(1)}, bf16[16,2048]{1,0:T(8,128)(2,1)S(1)}, u32[]{:S(2)}, u32[]{:S(2)}) collective-permute-start(bf16[16,2048]{1,0:T(8,128)(2,1)S(1)} %get-tuple-element.93), channel_id=1, source_target_pairs={{0,2},{1,3},{2,0},{3,1},{4,6},{5,7},{6,4},{7,5},{8,10},{9,11},{10,... | collective-permute-start | bytes 196616 | tf_op jit(solution)/shard_map/ppermute | solution.py:53
  148.8 8.3 %collective-permute-start.41 = (bf16[16,2048]{1,0:T(8,128)(2,1)S(1)}, bf16[16,2048]{1,0:T(8,128)(2,1)S(1)}, u32[]{:S(2)}, u32[]{:S(2)}) collective-permute-start(bf16[16,2048]{1,0:T(8,128)(2,1)S(1)} %mixed_grad.1), channel_id=1, source_target_pairs={{1,0},{2,1},{3,2},{0,3},{5,4},{6,5},{7,6},{4,7},{9,8},{10,9},{11,1... | collective-permute-start | bytes 196616 | tf_op jit(solution)/shard_map/ppermute | solution.py:43
  151.3 6.0 %collective-permute-start.42 = (bf16[16,2048]{1,0:T(8,128)(2,1)S(1)}, bf16[16,2048]{1,0:T(8,128)(2,1)S(1)}, u32[]{:S(2)}, u32[]{:S(2)}) collective-permute-start(bf16[16,2048]{1,0:T(8,128)(2,1)S(1)} %mixed_grad.1), channel_id=1, source_target_pairs={{2,0},{3,1},{0,2},{1,3},{6,4},{7,5},{4,6},{5,7},{10,8},{11,9},{8,1... | collective-permute-start | bytes 196616 | tf_op jit(solution)/shard_map/ppermute | solution.py:43
  151.7 6.3 %collective-permute-start.43 = (bf16[16,2048]{1,0:T(8,128)(2,1)S(1)}, bf16[16,2048]{1,0:T(8,128)(2,1)S(1)}, u32[]{:S(2)}, u32[]{:S(2)}) collective-permute-start(bf16[16,2048]{1,0:T(8,128)(2,1)S(1)} %mixed_grad.1), channel_id=1, source_target_pairs={{3,0},{0,1},{1,2},{2,3},{7,4},{4,5},{5,6},{6,7},{11,8},{8,9},{9,10... | collective-permute-start | bytes 196616 | tf_op jit(solution)/shard_map/ppermute | solution.py:43
  155.6 9.2 %collective-permute-start.34 = (bf16[64,2048]{1,0:T(8,128)(2,1)S(1)}, bf16[64,2048]{1,0:T(8,128)(2,1)S(1)}, u32[]{:S(2)}, u32[]{:S(2)}) collective-permute-start(bf16[64,2048]{1,0:T(8,128)(2,1)S(1)} %get-tuple-element.73.refs_0_), channel_id=1, source_target_pairs={{0,16},{8,24},{16,0},{24,8},{1,17},{9,25},{17,1},{25,9},{2,18},{10... | collective-permute-start | bytes 786440 | tf_op jit(solution)/shard_map/ppermute | solution.py:60
  157.1 8.8 %collective-permute-start.35 = (bf16[64,2048]{1,0:T(8,128)(2,1)S(1)}, bf16[64,2048]{1,0:T(8,128)(2,1)S(1)}, u32[]{:S(2)}, u32[]{:S(2)}) collective-permute-start(bf16[64,2048]{1,0:T(8,128)(2,1)S(1)} %get-tuple-element.73.refs_0_), channel_id=1, source_target_pairs={{0,8},{8,0},{16,24},{24,16},{1,9},{9,1},{17,25},{25,17},{2,10},{10... | collective-permute-start | bytes 786440 | tf_op jit(solution)/shard_map/ppermute | solution.py:60
  157.3 13.1 %collective-permute-start.31 = (bf16[64,2048]{1,0:T(8,128)(2,1)S(1)}, bf16[64,2048]{1,0:T(8,128)(2,1)S(1)}, u32[]{:S(2)}, u32[]{:S(2)}) collective-permute-start(bf16[64,2048]{1,0:T(8,128)(2,1)S(1)} %get-tuple-element.72.refs_0_), channel_id=1, source_target_pairs={{0,16},{8,24},{16,0},{24,8},{1,17},{9,25},{17,1},{25,9},{2,18},{10... | collective-permute-start | bytes 786440 | tf_op jit(solution)/shard_map/ppermute | solution.py:60
  159.9 12.0 %collective-permute-start.44 = (bf16[64,1024]{1,0:T(8,128)(2,1)S(1)}, bf16[64,1024]{1,0:T(8,128)(2,1)S(1)}, u32[]{:S(2)}, u32[]{:S(2)}) collective-permute-start(bf16[64,1024]{1,0:T(8,128)(2,1)S(1)} %back_project.1.refs_0_), channel_id=1, source_target_pairs={{4,0},{0,4},{5,1},{1,5},{6,2},{2,6},{7,3},{3,7},{12,8},{8,12},{13,... | collective-permute-start | bytes 393224 | tf_op jit(solution)/shard_map/ppermute | solution.py:43
  161.5 14.5 %collective-permute-start.28 = (bf16[64,2048]{1,0:T(8,128)(2,1)S(1)}, bf16[64,2048]{1,0:T(8,128)(2,1)S(1)}, u32[]{:S(2)}, u32[]{:S(2)}) collective-permute-start(bf16[64,2048]{1,0:T(8,128)(2,1)S(1)} %get-tuple-element.71.refs_0_), channel_id=1, source_target_pairs={{0,16},{8,24},{16,0},{24,8},{1,17},{9,25},{17,1},{25,9},{2,18},{10... | collective-permute-start | bytes 786440 | tf_op jit(solution)/shard_map/ppermute | solution.py:60
  164.7 11.2 %collective-permute-start.36 = (bf16[64,2048]{1,0:T(8,128)(2,1)S(1)}, bf16[64,2048]{1,0:T(8,128)(2,1)S(1)}, u32[]{:S(2)}, u32[]{:S(2)}) collective-permute-start(bf16[64,2048]{1,0:T(8,128)(2,1)S(1)} %collective-permute-done.34.refs_1_), channel_id=1, source_target_pairs={{0,8},{8,0},{16,24},{24,16},{1,9},{9,1},{17,25},{25,17},{2,10},{10... | collective-permute-start | bytes 786440 | tf_op jit(solution)/shard_map/ppermute | solution.py:60
  165.9 15.8 %collective-permute-start.32 = (bf16[64,2048]{1,0:T(8,128)(2,1)S(1)}, bf16[64,2048]{1,0:T(8,128)(2,1)S(1)}, u32[]{:S(2)}, u32[]{:S(2)}) collective-permute-start(bf16[64,2048]{1,0:T(8,128)(2,1)S(1)} %get-tuple-element.72.refs_0_), channel_id=1, source_target_pairs={{0,8},{8,0},{16,24},{24,16},{1,9},{9,1},{17,25},{25,17},{2,10},{10... | collective-permute-start | bytes 786440 | tf_op jit(solution)/shard_map/ppermute | solution.py:60
  170.4 11.4 %collective-permute-start.25 = (bf16[64,2048]{1,0:T(8,128)(2,1)S(1)}, bf16[64,2048]{1,0:T(8,128)(2,1)S(1)}, u32[]{:S(2)}, u32[]{:S(2)}) collective-permute-start(bf16[64,2048]{1,0:T(8,128)(2,1)S(1)} %get-tuple-element.70.refs_0_), channel_id=1, source_target_pairs={{0,16},{8,24},{16,0},{24,8},{1,17},{9,25},{17,1},{25,9},{2,18},{10... | collective-permute-start | bytes 786440 | tf_op jit(solution)/shard_map/ppermute | solution.py:60
  171.9 10.4 %collective-permute-start.33 = (bf16[64,2048]{1,0:T(8,128)(2,1)S(1)}, bf16[64,2048]{1,0:T(8,128)(2,1)S(1)}, u32[]{:S(2)}, u32[]{:S(2)}) collective-permute-start(bf16[64,2048]{1,0:T(8,128)(2,1)S(1)} %collective-permute-done.31.refs_1_), channel_id=1, source_target_pairs={{0,8},{8,0},{16,24},{24,16},{1,9},{9,1},{17,25},{25,17},{2,10},{10... | collective-permute-start | bytes 786440 | tf_op jit(solution)/shard_map/ppermute | solution.py:60
  176.0 11.3 %collective-permute-start.29 = (bf16[64,2048]{1,0:T(8,128)(2,1)S(1)}, bf16[64,2048]{1,0:T(8,128)(2,1)S(1)}, u32[]{:S(2)}, u32[]{:S(2)}) collective-permute-start(bf16[64,2048]{1,0:T(8,128)(2,1)S(1)} %get-tuple-element.71.refs_0_), channel_id=1, source_target_pairs={{0,8},{8,0},{16,24},{24,16},{1,9},{9,1},{17,25},{25,17},{2,10},{10... | collective-permute-start | bytes 786440 | tf_op jit(solution)/shard_map/ppermute | solution.py:60
  176.0 11.3 %collective-permute-start.30 = (bf16[64,2048]{1,0:T(8,128)(2,1)S(1)}, bf16[64,2048]{1,0:T(8,128)(2,1)S(1)}, u32[]{:S(2)}, u32[]{:S(2)}) collective-permute-start(bf16[64,2048]{1,0:T(8,128)(2,1)S(1)} %collective-permute-done.28.refs_1_), channel_id=1, source_target_pairs={{0,8},{8,0},{16,24},{24,16},{1,9},{9,1},{17,25},{25,17},{2,10},{10... | collective-permute-start | bytes 786440 | tf_op jit(solution)/shard_map/ppermute | solution.py:60
  181.7 10.8 %collective-permute-start.26 = (bf16[64,2048]{1,0:T(8,128)(2,1)S(1)}, bf16[64,2048]{1,0:T(8,128)(2,1)S(1)}, u32[]{:S(2)}, u32[]{:S(2)}) collective-permute-start(bf16[64,2048]{1,0:T(8,128)(2,1)S(1)} %get-tuple-element.70.refs_0_), channel_id=1, source_target_pairs={{0,8},{8,0},{16,24},{24,16},{1,9},{9,1},{17,25},{25,17},{2,10},{10... | collective-permute-start | bytes 786440 | tf_op jit(solution)/shard_map/ppermute | solution.py:60
  181.7 10.8 %collective-permute-start.27 = (bf16[64,2048]{1,0:T(8,128)(2,1)S(1)}, bf16[64,2048]{1,0:T(8,128)(2,1)S(1)}, u32[]{:S(2)}, u32[]{:S(2)}) collective-permute-start(bf16[64,2048]{1,0:T(8,128)(2,1)S(1)} %collective-permute-done.25.refs_1_), channel_id=1, source_target_pairs={{0,8},{8,0},{16,24},{24,16},{1,9},{9,1},{17,25},{25,17},{2,10},{10... | collective-permute-start | bytes 786440 | tf_op jit(solution)/shard_map/ppermute | solution.py:60
  (23 other events, 147.2 us)

commit v2 on v1

--- a/solution.py
+++ b/solution.py
@@ -9,7 +9,7 @@
 HDIM = 256
 LANES = 128
 TILE = 512
-MAX_CHUNKS = 4
+MAX_CHUNKS = 3
 LOW = -1e30
 CODE_TOP = 32767.0
 
@@ -47,12 +47,12 @@
     return [x] + [from_ahead(x, axis, k) for k in range(1, lax.axis_size(axis))]
 
 
-def scatter_ring(x, axis, rows):
-    n = lax.axis_size(axis)
-    return [
-        lax.ppermute(x[k * rows : (k + 1) * rows], axis, [(i, (i + k) % n) for i in range(n)])
-        for k in range(1, n)
-    ]
+def gather_rows(x, axis):
+    return lax.all_gather(x, axis, axis=0, tiled=True)
+
+
+def exchange_rows(x, axis):
+    return lax.all_to_all(x, axis, split_axis=0, concat_axis=0, tiled=True)
 
 
 def swap(x, axis, bit):
@@ -118,9 +118,9 @@
     o_ref[:, features:] = stat.astype(bf16)
 
 
-def project_kernel(n_seq, own_rows, *refs):
+def project_kernel(n_seq, *refs):
     o_refs = refs[:n_seq]
-    p_ref, mixed_ref, own_ref, att_ref, lse_ref, att = refs[n_seq:]
+    p_ref, mixed_ref, att_ref, lse_ref, att = refs[n_seq:]
     rows, features = att.shape
 
     @pl.when(pl.program_id(0) == 0)
@@ -142,19 +142,18 @@
         att_ref[...] = att[...]
         lse_ref[...] = lse_all
 
-    part = dot(att[...], p_ref[...], 1, 0)
-    mixed_ref[...] = part.astype(bf16)
-    own_ref[...] = part[:own_rows]
-
-
-def norm_kernel(n_got, scal, *refs):
-    own_ref, got_refs = refs[0], refs[1 : 1 + n_got]
-    residual_ref, gain_ref, mixed_ref, ng_ref = refs[1 + n_got :]
-    rows, width = own_ref.shape
+    mixed_ref[...] = dot(att[...], p_ref[...], 1, 0).astype(bf16)
+
+
+def block_sum(ref, rows):
+    n = ref.shape[0] // rows
+    return tree([ref[i * rows : (i + 1) * rows, :].astype(f32) for i in range(n)])
+
+
+def norm_kernel(scal, got_ref, residual_ref, gain_ref, mixed_ref, ng_ref):
+    rows, width = mixed_ref.shape
     res = residual_ref[0, pl.ds(pl.multiple_of(scal[2], 16), rows), :].astype(f32)
-    mixed = own_ref[...] + res
-    for r in got_refs:
-        mixed = mixed + r[...].astype(f32)
+    mixed = res + block_sum(got_ref, rows)
     mixed_ref[...] = mixed
     ng_ref[:, :width] = (mixed * gain_ref[...]).astype(bf16)
     square = jnp.sum(mixed * mixed, axis=1, keepdims=True)
@@ -167,8 +166,8 @@
 
 def logits_kernel(first, cols, ng_ref, w_ref, code_ref, stat_ref, z):
     j = pl.program_id(0)
-    rows, width = z.shape[0], w_ref.shape[0]
-    part = dot(ng_ref[:, :width], w_ref[...], 1, 0)
+    rows, width = z.shape[0], w_ref.shape[1]
+    part = dot(ng_ref[:, :width], w_ref[...], 1, 1)
     if first + z.shape[1] > cols:
         at = first + j * TILE + lax.broadcasted_iota(i32, part.shape, 1)
         part = jnp.where(at < cols, part, 0.0)
@@ -234,36 +233,30 @@
 
     w = w_ref[...]
     if partial_cols:
-        at = first + j * TILE + lax.broadcasted_iota(i32, (1, TILE), 1)
+        at = first + j * TILE + lax.broadcasted_iota(i32, (TILE, 1), 0)
         w = jnp.where(at < cols, w, jnp.zeros_like(w))
     left = lhs[:, pl.ds(pl.multiple_of(j * TILE, TILE), TILE)]
-    acc_ref[...] += dot(left, w, 1, 1)
-
-
-def total_kernel(n_vocab, own_rows, *refs):
-    st_refs = refs[:n_vocab]
-    acc_ref, part_ref, own_ref, coef_ref, loss_ref = refs[n_vocab:]
+    acc_ref[...] += dot(left, w, 1, 0)
+
+
+def total_kernel(n_vocab, st_ref, st_all_ref, acc_ref, part_ref, coef_ref):
     rows = coef_ref.shape[0]
-    mine = st_refs[0][...]
-    stats = [mine]
-    for k in range(1, n_vocab):
-        s = st_refs[k][...]
-        cut = rows - k * own_rows
-        stats.append(jnp.concatenate([s[cut:], s[:cut]], axis=0))
+    mine = st_ref[...]
+    stats = [st_all_ref[k * rows : (k + 1) * rows, :] for k in range(n_vocab)]
     top = tree([s[:, 0:1] for s in stats], jnp.maximum)
     total = tree([s[:, 1:2] * jnp.exp(s[:, 0:1] - top) for s in stats])
     hit_logit = tree([s[:, 2:3] for s in stats])
     log_total = top + jnp.log(total)
     loss = log_total - hit_logit + zloss_weight * log_total * log_total
-    loss_ref[...] = jnp.broadcast_to(jnp.sum(loss, axis=0, keepdims=True), loss_ref.shape)
     lift = 1.0 + 2.0 * zloss_weight * log_total
     inv = mine[:, 3:4]
     lane = lanes(rows)
-    coef_ref[...] = jnp.where(lane >= 8, jnp.exp(jnp.minimum(mine - log_total, 30.0)) * lift * inv, inv)
+    coef = jnp.exp(jnp.minimum(mine - log_total, 30.0)) * lift * inv
+    coef = jnp.where(lane >= 8, coef, inv)
+    coef_ref[...] = jnp.where(lane == 1, loss, coef)
     scale = jnp.exp(mine[:, 0:1] - log_total) * lift
     part = acc_ref[:rows, :] * scale - acc_ref[rows:, :]
     part_ref[...] = part.astype(bf16)
-    own_ref[...] = part[:own_rows]
 
 
 def grad_kernel(firsts, cols, coef_ref, tgt_ref, *refs):
@@ -275,35 +268,50 @@
         inv = coef_ref[:, 0:1]
         g = e_ref[...].astype(f32) * coef_ref[:, 8 + c : 9 + c] - jnp.where(hit, inv, 0.0)
         g_ref[...] = g.astype(bf16)
-
-
-def head_kernel(n_dp, has_prev, ng_ref, *refs):
-    g_refs = refs[:n_dp]
-    out_ref = refs[-1]
+    last = refs[-1]
+    rows, size = last.shape
+    lane = lanes(rows)
+    stat = last[:, size - LANES :].astype(f32)
+    for i, part in enumerate(three_parts(coef_ref[:, 1:2])):
+        stat = jnp.where(lane == LANES - 3 + i, part, stat)
+    last[:, size - LANES :] = stat.astype(bf16)
+
+
+def loss_kernel(rows_all, *refs):
+    sums = []
+    for r in refs[:-1]:
+        s = r[...].astype(f32)
+        sums.append(jnp.sum(s[:, -3:-2] + s[:, -2:-1] + s[:, -1:], axis=0, keepdims=True))
+    refs[-1][...] = jnp.broadcast_to(tree(sums) / rows_all, refs[-1].shape)
+
+
+def head_kernel(n_dp, *refs):
+    ng_refs, g_refs = refs[:n_dp], refs[n_dp : 2 * n_dp]
+    out_ref, ng = refs[-2], refs[-1]
+    rows, width = ng_refs[0].shape[0], out_ref.shape[1]
+
+    @pl.when(pl.program_id(0) == 0)
+    def _():
+        for i, r in enumerate(ng_refs):
+            ng[i * rows : (i + 1) * rows, :] = r[:, :width]
+
     g = jnp.concatenate([r[...] for r in g_refs], axis=0)
-    width = out_ref.shape[0]
-    step = min(width, 512)
-    for at in range(0, width, step):
-        out_ref[at : at + step, :] = dot(ng_ref[at : at + step, :], g, 1, 0).astype(bf16)
-
-
-def gate_kernel(n_got, *refs):
-    own_ref, got_refs = refs[0], refs[1 : 1 + n_got]
-    mixed_ref, gain_ref, gated_ref, dot_ref = refs[1 + n_got :]
-    total = own_ref[...]
-    for r in got_refs:
-        total = total + r[...].astype(f32)
-    gated = total * gain_ref[...]
+    for at in range(0, TILE, 256):
+        out_ref[at : at + 256, :] = dot(g[:, at : at + 256], ng[...], 0, 0).astype(bf16)
+
+
+def gate_kernel(got_ref, mixed_ref, gain_ref, gated_ref, dot_ref):
+    gated = block_sum(got_ref, mixed_ref.shape[0]) * gain_ref[...]
     gated_ref[...] = gated
     inner = jnp.sum(gated * mixed_ref[...], axis=1, keepdims=True)
     dot_ref[...] = jnp.broadcast_to(inner, dot_ref.shape)
 
 
-def mixed_grad_kernel(n_seq, features, gated_ref, mixed_ref, coef_ref, *refs):
+def mixed_grad_kernel(n_seq, features, scal, gated_ref, mixed_ref, coef_ref, *refs):
     dot_refs, out_ref = refs[:n_seq], refs[n_seq]
     rows = out_ref.shape[0]
     inner = tree([r[:, 0:1] for r in dot_refs])
-    inv = coef_ref[:rows, 0:1]
+    inv = coef_ref[pl.ds(pl.multiple_of(scal[2], 16), rows), :][:, 0:1]
     out = gated_ref[...] * inv - mixed_ref[...] * (inv * inv * inv * inner / features)
     out_ref[...] = out.astype(bf16)
 
@@ -347,8 +355,9 @@
     chunks = [(t, min(per, tiles - t)) for t in range(0, tiles, per)]
     firsts = [t * TILE for t, _ in chunks]
     gain = norm_gain.reshape(1, width)
-
-    start = lax.rem(voc * own_rows - seq * tgt_rows + rows, rows).astype(i32)
+    weight = head_weight.T
+
+    start = lax.rem(rows - seq * tgt_rows, rows).astype(i32)
     scal = jnp.stack(
         [start, enc_lengths[0] - seq * enc, voc * own_rows, voc * cols]
     ).astype(i32)
@@ -372,12 +381,11 @@
     o_all = gather_ring(o_part, "seq")
     ptile = min(TILE, width)
     whole = lambda shape: pl.BlockSpec(shape, lambda j: (0, 0))
-    mixed_part, mixed_own, att, lse = pl.pallas_call(
-        functools.partial(project_kernel, n_seq, own_rows),
+    mixed_part, att, lse = pl.pallas_call(
+        functools.partial(project_kernel, n_seq),
         grid=(width // ptile,),
         out_shape=[
             sds((rows, width), bf16),
-            sds((own_rows, width), f32),
             sds((rows, features), bf16),
             sds((rows, LANES), f32),
         ],
@@ -385,7 +393,6 @@
         + [pl.BlockSpec((features, ptile), lambda j: (0, j))],
         out_specs=[
             pl.BlockSpec((rows, ptile), lambda j: (0, j)),
-            pl.BlockSpec((own_rows, ptile), lambda j: (0, j)),
             whole((rows, features)),
             whole((rows, LANES)),
         ],
@@ -394,19 +401,16 @@
         name="project",
     )(*o_all, out_proj)
 
-    got = scatter_ring(mixed_part, "vocab", own_rows)
     mixed, ng_own = pl.pallas_call(
-        functools.partial(norm_kernel, len(got)),
+        norm_kernel,
         out_shape=[sds((own_rows, width), f32), sds((own_rows, width + LANES), bf16)],
-        in_specs=[SMEM] + [VMEM] * (len(got) + 3),
+        in_specs=[SMEM] + [VMEM] * 3,
         out_specs=[VMEM, VMEM],
         compiler_params=params(),
         name="norm",
-    )(scal, mixed_own, *got, residual, gain)
-    ng = jnp.concatenate(gather_ring(ng_own, "vocab"), axis=0)
-
-    ng_dp = gather_swaps(ng[:, :width], "dp")
-    ng_turned = jnp.concatenate(ng_dp, axis=0).T
+    )(scal, exchange_rows(mixed_part, "vocab"), residual, gain)
+    ng = gather_rows(ng_own, "vocab")
+    ng_dp = gather_swaps(ng, "dp")
 
     codes, stats = [], []
     for tile0, n in chunks:
@@ -417,14 +421,14 @@
             out_shape=[sds((rows, size), jnp.int16), sds((rows, LANES), f32)],
             in_specs=[
                 whole((rows, width + LANES)),
-                pl.BlockSpec((width, TILE), lambda j, t=tile0: (0, t + j)),
+                pl.BlockSpec((TILE, width), lambda j, t=tile0: (t + j, 0)),
             ],
             out_specs=[whole((rows, size)), whole((rows, LANES))],
             scratch_shapes=[pltpu.VMEM((rows, size), f32)],
             compiler_params=params(),
             cost_estimate=cost(2 * 256 * width * size, 2 * width * size),
             name="logits",
-        )(ng, head_weight)
+        )(ng, weight)
         codes.append(gather_ring(code, "seq"))
         stats.append(gather_ring(stat, "seq"))
 
@@ -440,32 +444,28 @@
             in_specs=[SMEM]
             + [whole((rows, size))] * n_seq
             + [whole((rows, LANES))] * (n_seq + 1)
-            + [pl.BlockSpec((width, TILE), lambda j, t=tile0: (0, t + j))]
+            + [pl.BlockSpec((TILE, width), lambda j, t=tile0: (t + j, 0))]
             + ([whole((2 * rows, width)), whole((rows, LANES))] if c else []),
             out_specs=[whole((2 * rows, width)), whole((rows, size)), whole((rows, LANES))],
             scratch_shapes=[pltpu.VMEM((2 * rows, size), bf16)],
             compiler_params=params(),
             cost_estimate=cost(2 * 256 * width * size, 2 * width * size),
             name="hidden",
-        )(scal, *codes[c], *stats[c], tgt, head_weight, *prev)
+        )(scal, *codes[c], *stats[c], tgt, weight, *prev)
         exps.append(e)
 
-    st_all = gather_ring(st, "vocab")
-    hidden_part, hidden_own, coef, loss = pl.pallas_call(
-        functools.partial(total_kernel, n_vocab, own_rows),
-        out_shape=[
-            sds((rows, width), bf16),
-            sds((own_rows, width), f32),
-            sds((rows, LANES), f32),
-            sds((8, LANES), f32),
-        ],
-        in_specs=[VMEM] * (n_vocab + 1),
-        out_specs=[VMEM] * 4,
+    st_all = gather_rows(st, "vocab")
+    hidden_part, coef = pl.pallas_call(
+        functools.partial(total_kernel, n_vocab),
+        out_shape=[sds((rows, width), bf16), sds((rows, LANES), f32)],
+        in_specs=[VMEM] * 3,
+        out_specs=[VMEM] * 2,
         compiler_params=params(),
         name="total",
-    )(*st_all, acc)
-    got = scatter_ring(hidden_part, "vocab", own_rows)
-
+    )(st, st_all, acc)
+    got = exchange_rows(hidden_part, "vocab")
+
+    assert cols + 3 <= tiles * TILE
     grads = pl.pallas_call(
         functools.partial(grad_kernel, firsts, cols),
         out_shape=[sds(e.shape, bf16) for e in exps],
@@ -474,30 +474,37 @@
         compiler_params=params(),
         name="logit_grad",
     )(coef, tgt, *exps)
-    bit = n_dp // 2
-    while bit:
-        loss = loss + swap(loss, "dp", bit)
-        bit //= 2
-    mean_loss = loss[0, 0] / (n_dp * rows)
+    grads_dp = [gather_swaps(g, "dp") for g in grads]
+    last = chunks[-1][1] * TILE
+    loss = pl.pallas_call(
+        functools.partial(loss_kernel, n_dp * rows),
+        grid=(1,),
+        out_shape=sds((8, LANES), f32),
+        in_specs=[pl.BlockSpec((rows, LANES), lambda j: (0, last // LANES - 1))] * n_dp,
+        out_specs=whole((8, LANES)),
+        compiler_params=params(),
+        name="loss",
+    )(*grads_dp[-1])
+    mean_loss = loss[0, 0]
 
     gated, inner = pl.pallas_call(
-        functools.partial(gate_kernel, len(got)),
+        gate_kernel,
         out_shape=[sds((own_rows, width), f32), sds((own_rows, LANES), f32)],
-        in_specs=[VMEM] * (len(got) + 3),
+        in_specs=[VMEM] * 3,
         out_specs=[VMEM, VMEM],
         compiler_params=params(),
         name="gate",
-    )(hidden_own, *got, mixed, gain)
+    )(got, mixed, gain)
     inner_all = gather_ring(inner, "seq")
     mixed_grad = pl.pallas_call(
         functools.partial(mixed_grad_kernel, n_seq, full_width),
         out_shape=sds((own_rows, width), bf16),
-        in_specs=[VMEM] * (3 + n_seq),
+        in_specs=[SMEM] + [VMEM] * (3 + n_seq),
         out_specs=VMEM,
         compiler_params=params(),
         name="mixed_grad",
-    )(gated, mixed, coef, *inner_all)
-    mg = jnp.concatenate(gather_ring(mixed_grad, "vocab"), axis=0)
+    )(scal, gated, mixed, coef, *inner_all)
+    mg = gather_rows(mixed_grad, "vocab")
 
     ftile = min(256, features)
     back_part = pl.pallas_call(
@@ -521,23 +528,22 @@
 
     head = None
     for c, (tile0, n) in enumerate(chunks):
-        g_all = gather_swaps(grads[c], "dp")
-        place = pl.BlockSpec((width, TILE), lambda j, t=tile0: (0, t + j))
         prev = [head] if c else []
         head = pl.pallas_call(
-            functools.partial(head_kernel, n_dp, bool(c)),
+            functools.partial(head_kernel, n_dp),
             grid=(n,),
-            out_shape=sds((width, cols), bf16),
-            in_specs=[whole((width, n_dp * rows))]
+            out_shape=sds((cols, width), bf16),
+            in_specs=[whole((rows, width + LANES))] * n_dp
             + [pl.BlockSpec((rows, TILE), lambda j: (0, j))] * n_dp
             + [pl.BlockSpec(memory_space=pl.ANY)] * len(prev),
-            out_specs=place,
-            input_output_aliases={1 + n_dp: 0} if c else {},
+            out_specs=pl.BlockSpec((TILE, width), lambda j, t=tile0: (t + j, 0)),
+            scratch_shapes=[pltpu.VMEM((n_dp * rows, width), bf16)],
+            input_output_aliases={2 * n_dp: 0} if c else {},
             compiler_params=params(),
             cost_estimate=cost(2 * n_dp * rows * width * n * TILE, 2 * width * n * TILE),
             name="head_grad",
-        )(ng_turned, *g_all, *prev)
-    return (mean_loss, head, key_grad, value_grad)
+        )(*ng_dp, *grads_dp[c], *prev)
+    return (mean_loss, head.T, key_grad, value_grad)
 
 
 def solution(mesh):

time: 244 us -> 184 us (0.75)
  local copies, waits for them, and re-layouts: 88.5 us -> 10.3 us
  blocking collectives: 0 us -> 41.7 us
  starting transfers between devices: 46.2 us -> 30.1 us
  waiting for transfers between devices: 25.5 us -> 22.2 us
    unnamed x22 -> x24, local copies, waits for them, and re-layouts: 86.3 us -> 9.69 us
    all_gather x0 -> x3, blocking collectives: none -> 41.7 us  [gather_rows(): return lax.all_gather(x, axis, axis=0, tiled=True)]
    ppermute x22 -> x11, starting transfers between devices: 26.4 us -> 16 us  [from_ahead(): return lax.ppermute(x, axis, [((i + k) % n, i) for i in range(n)])]
    ppermute x6 -> x0, starting transfers between devices: 9.87 us -> none  [scatter_ring(): lax.ppermute(x[k * rows:(k + 1) * rows], axis, [(i, (i + k) % n) for i in...]
    all_to_all x0 -> x2, starting transfers between devices: none -> 8.8 us  [exchange_rows(): return lax.all_to_all(x, axis, split_axis=0, concat_axis=0, tiled=True)]
    ppermute x6 -> x0, waiting for transfers between devices: 6.87 us -> none  [scatter_ring(): lax.ppermute(x[k * rows:(k + 1) * rows], axis, [(i, (i + k) % n) for i in...]
    ppermute x17 -> x12, starting transfers between devices: 9.95 us -> 5.28 us  [swap(): return lax.ppermute(x, axis, [(i, i ^ bit) for i in range(n)])]
    pallas_call x4 -> x3, Pallas kernels: 25.4 us -> 21 us  [body(): pl.pallas_call(functools.partial(hidden_kernel, c, tile0 * TILE, cols, n_...]
  transfers between devices with their start and end apart: 45 -> 25, of which waited for: 16 -> 9; matrix products, arithmetic and copies ran while one was open for 17% -> 1% of each run, Pallas kernels for 22% -> 27%
where the time goes in v2:
time: 184 us; the launch traced here: 183 us
  Pallas kernels  76.5 us (42%)
  blocking collectives  41.7 us (23%)
  starting transfers between devices  30.1 us (16%)
  waiting for transfers between devices  22.2 us (12%)
  local copies, waits for them, and re-layouts  10.3 us (6%)
    all_gather x3, blocking collectives, gather_rows(): return lax.all_gather(x, axis, axis=0, tiled=True)  41.7 us
    pallas_call x3, Pallas kernels, body(): pl.pallas_call(functools.partial(logits_kernel, tile0 * TILE, cols), grid...  22.3 us
    pallas_call x3, Pallas kernels, body(): pl.pallas_call(functools.partial(head_kernel, n_dp), grid=(n,), out_shape...  21.2 us
    pallas_call x3, Pallas kernels, body(): pl.pallas_call(functools.partial(hidden_kernel, c, tile0 * TILE, cols, n_...  21 us
    ppermute x11, starting transfers between devices, from_ahead(): return lax.ppermute(x, axis, [((i + k) % n, i) for i in range(n)])  16 us
    ppermute x11, waiting for transfers between devices, from_ahead(): return lax.ppermute(x, axis, [((i + k) % n, i) for i in range(n)])  12.5 us
    unnamed x24, local copies, waits for them, and re-layouts  9.69 us
    all_to_all x2, starting transfers between devices, exchange_rows(): return lax.all_to_all(x, axis, split_axis=0, concat_axis=0, tiled=True)  8.8 us
  transfers between devices with their start and end apart: 25, of which 9 were waited for; matrix products, arithmetic and copies ran while one was open for 1% of the time, Pallas kernels for 27%

profile of v2, /device:TPU:0, one launch (start us, length us, event | category | flops | bytes accessed | tf_op | source)
XLA Modules:
  0.0 183.2 jit_solution(2839922779912485276)
XLA Ops:
  0.6 3.0 %collective-permute-start = (bf16[1,32,1024]{2,1,0:T(8,128)(2,1)}, bf16[1,32,1024]{2,1,0:T(8,128)(2,1)S(1)}, u32[]{:S(2)}, u32[]{:S(2)}) collective-permute-start(bf16[1,32,1024]{2,1,0:T(8,128)(2,1)} %refs_0_.1), channel_id=1, source_target_pairs={{4,0},{0,4},{5,1},{1,5},{6,2},{2,6},{7,3},{3,7},{12,8},{8,12},{13,... | collective-permute-start | bytes 196616 | tf_op jit(solution)/shard_map/ppermute | solution.py:43
  4.4 1.7 collective-permute-done.refs_1_
  10.5 2.1 %collective-permute-start.1 = (bf16[64,1152]{1,0:T(8,128)(2,1)S(1)}, bf16[64,1152]{1,0:T(8,128)(2,1)S(1)}, u32[]{:S(2)}, u32[]{:S(2)}) collective-permute-start(bf16[64,1152]{1,0:T(8,128)(2,1)S(1)} %get-tuple-element.35.refs_0_), channel_id=1, source_target_pairs={{4,0},{0,4},{5,1},{1,5},{6,2},{2,6},{7,3},{3,7},{12,8},{8,12},{13,... | collective-permute-start | bytes 442376 | tf_op jit(solution)/shard_map/ppermute | solution.py:43
  12.6 3.1 %collective-permute-done.1.refs_1_ = bf16[64,1152]{1,0:T(8,128)(2,1)S(1)} collective-permute-done((bf16[64,1152]{1,0:T(8,128)(2,1)S(1)}, bf16[64,1152]{1,0:T(8,128)(2,1)S(1)}, u32[]{:S(2)}, u32[]{:S(2)}) %collective-permute-start.1) | collective-permute-done | bytes 147488 | tf_op jit(solution)/shard_map/ppermute | solution.py:43
  15.7 2.2 %copy-done = bf16[1024,2048]{1,0:T(8,128)(2,1)S(1)} copy-done((bf16[1024,2048]{1,0:T(8,128)(2,1)S(1)}, bf16[1024,2048]{1,0:T(8,128)(2,1)}, u32[]{:S(2)}) %copy-start) | copy-done | bytes 4194328
  17.9 2.7 %project.1 = (bf16[64,2048]{1,0:T(8,128)(2,1)}, bf16[64,1024]{1,0:T(8,128)(2,1)S(1)}, f32[64,128]{1,0:T(8,128)S(1)}) custom-call(bf16[64,1152]{1,0:T(8,128)(2,1)S(1)} %get-tuple-element.35.refs_0_, bf16[64,1152]{1,0:T(8,128)(2,1)S(1)} %collective-permute-done.1.refs_1_, bf16[1024,2048]{1,0:T(8,128)(2,1)S(1)} %copy-done), custom_call_target="tpu_custom_call" | custom-call | tf_op jit(solution)/shard_map/project/pallas_call | solution.py:384
  20.6 5.4 %all-to-all-start = ((bf16[4,16,2048]{2,1,0:T(8,128)(2,1)}), bf16[4,16,2048]{2,1,0:T(8,128)(2,1)S(1)}, u32[]{:S(2)}, u32[]{:S(2)}) async-start(bf16[4,16,2048]{2,1,0:T(8,128)(2,1)} %bitcast.5), calls=%async_computation | async-start | bytes 524288 | tf_op jit(solution)/shard_map/all_to_all | solution.py:55
  27.5 2.2 %collective-permute-done.4 = s32[32]{0:T(128)S(1)} collective-permute-done((s32[32]{0:T(128)}, s32[32]{0:T(128)S(1)}, u32[]{:S(2)}, u32[]{:S(2)}) %collective-permute-start.4) | collective-permute-done | bytes 160 | tf_op jit(solution)/shard_map/ppermute | solution.py:43
  30.5 2.2 %all-to-all-done = bf16[4,16,2048]{2,1,0:T(8,128)(2,1)S(1)} async-done(((bf16[4,16,2048]{2,1,0:T(8,128)(2,1)}), bf16[4,16,2048]{2,1,0:T(8,128)(2,1)S(1)}, u32[]{:S(2)}, u32[]{:S(2)}) %all-to-all-start) | async-done | bytes 262176 | tf_op jit(solution)/shard_map/all_to_all | solution.py:55
  35.0 14.0 %all_gather.9.ng_ref.refs_0_ = bf16[64,2176]{1,0:T(8,128)(2,1)S(1)} all-gather(bf16[16,2176]{1,0:T(8,128)(2,1)S(1)} %get-tuple-element.37), channel_id=1, replica_groups=mesh['dp'=4,'seq'=2,'vocab'=4] {'vocab'}, dimensions={0}, use_global_device_ids=true | all-gather | bytes 348160 | tf_op jit(solution)/shard_map/all_gather | solution.py:51
  49.0 8.3 %logits.5 = (s16[64,3072]{1,0:T(8,128)(2,1)S(1)}, f32[64,128]{1,0:T(8,128)S(1)}) custom-call(bf16[64,2176]{1,0:T(8,128)(2,1)S(1)} %all_gather.9.ng_ref.refs_0_, bf16[8032,2048]{1,0:T(8,128)(2,1)} %bitcast.19), custom_call_target="tpu_custom_call" | custom-call | flops 3221225472 | bytes 12582912 | tf_op jit(solution)/shard_map/logits/pallas_call | solution.py:418
  59.5 8.3 %logits.4 = (s16[64,3072]{1,0:T(8,128)(2,1)S(1)}, f32[64,128]{1,0:T(8,128)S(1)}) custom-call(bf16[64,2176]{1,0:T(8,128)(2,1)S(1)} %all_gather.9.ng_ref.refs_0_, bf16[8032,2048]{1,0:T(8,128)(2,1)} %bitcast.20), custom_call_target="tpu_custom_call" | custom-call | flops 3221225472 | bytes 12582912 | tf_op jit(solution)/shard_map/logits/pallas_call | solution.py:418
  69.4 5.6 %logits.3 = (s16[64,2048]{1,0:T(8,128)(2,1)S(1)}, f32[64,128]{1,0:T(8,128)S(1)}) custom-call(bf16[64,2176]{1,0:T(8,128)(2,1)S(1)} %all_gather.9.ng_ref.refs_0_, bf16[8032,2048]{1,0:T(8,128)(2,1)} %bitcast.21), custom_call_target="tpu_custom_call" | custom-call | flops 2147483648 | bytes 8388608 | tf_op jit(solution)/shard_map/logits/pallas_call | solution.py:418
  79.2 7.8 %hidden.3 = (f32[128,2048]{1,0:T(8,128)S(1)}, bf16[64,3072]{1,0:T(8,128)(2,1)S(1)}, f32[64,128]{1,0:T(8,128)S(1)}) custom-call(s32[4]{0:T(128)S(1)} %pad_add_fusion.scal, s16[64,3072]{1,0:T(8,128)(2,1)S(1)} %get-tuple-element.42.refs_0_, s16[64,3072]{1,0:T(8,128)(2,1)S(1)} %collective-permute-done.7.refs_1_, f32[64,128]{1,0:T(8,128)S(1)} %get-tuple-element.43.refs_2_, ...), custom_call_target="tpu_custom_call" | custom-call | flops 3221225472 | bytes 12582912 | tf_op jit(solution)/shard_map/hidden/pallas_call | solution.py:440
  87.1 7.9 %hidden.4 = (f32[128,2048]{1,0:T(8,128)S(1)}, bf16[64,3072]{1,0:T(8,128)(2,1)S(1)}, f32[64,128]{1,0:T(8,128)S(1)}) custom-call(s32[4]{0:T(128)S(1)} %pad_add_fusion.scal, s16[64,3072]{1,0:T(8,128)(2,1)S(1)} %get-tuple-element.40.refs_0_, s16[64,3072]{1,0:T(8,128)(2,1)S(1)} %collective-permute-done.5.refs_1_, f32[64,128]{1,0:T(8,128)S(1)} %get-tuple-element.41.refs_2_, ...), custom_call_target="tpu_custom_call" | custom-call | flops 3221225472 | bytes 12582912 | tf_op jit(solution)/shard_map/hidden/pallas_call | solution.py:440
  95.0 5.3 %hidden.5 = (f32[128,2048]{1,0:T(8,128)S(1)}, bf16[64,2048]{1,0:T(8,128)(2,1)S(1)}, f32[64,128]{1,0:T(8,128)S(1)}) custom-call(s32[4]{0:T(128)S(1)} %pad_add_fusion.scal, s16[64,2048]{1,0:T(8,128)(2,1)S(1)} %get-tuple-element.38.refs_0_, s16[64,2048]{1,0:T(8,128)(2,1)S(1)} %collective-permute-done.2.refs_1_, f32[64,128]{1,0:T(8,128)S(1)} %get-tuple-element.39.refs_2_, ...), custom_call_target="tpu_custom_call" | custom-call | flops 2147483648 | bytes 8388608 | tf_op jit(solution)/shard_map/hidden/pallas_call | solution.py:440
  100.3 13.7 %all_gather.10.st_all_ref = f32[256,128]{1,0:T(8,128)S(1)} all-gather(f32[64,128]{1,0:T(8,128)S(1)} %get-tuple-element.48.st_ref), channel_id=1, replica_groups=mesh['dp'=4,'seq'=2,'vocab'=4] {'vocab'}, dimensions={0}, use_global_device_ids=true | all-gather | bytes 163840 | tf_op jit(solution)/shard_map/all_gather | solution.py:51
  116.1 3.4 %all-to-all-start.1 = ((bf16[4,16,2048]{2,1,0:T(8,128)(2,1)}), bf16[4,16,2048]{2,1,0:T(8,128)(2,1)S(1)}, u32[]{:S(2)}, u32[]{:S(2)}) async-start(bf16[4,16,2048]{2,1,0:T(8,128)(2,1)} %bitcast.12), calls=%async_computation.1 | async-start | bytes 524288 | tf_op jit(solution)/shard_map/all_to_all | solution.py:55
  119.6 1.7 collective-permute-start.9
  122.2 2.1 %collective-permute-done.18.refs_5_ = bf16[64,3072]{1,0:T(8,128)(2,1)} collective-permute-done((bf16[64,3072]{1,0:T(8,128)(2,1)S(1)}, bf16[64,3072]{1,0:T(8,128)(2,1)}, u32[]{:S(2)}, u32[]{:S(2)}) %collective-permute-start.18) | collective-permute-done | bytes 393248 | tf_op jit(solution)/shard_map/ppermute | solution.py:60
  124.3 2.0 %all-to-all-done.1 = bf16[4,16,2048]{2,1,0:T(8,128)(2,1)S(1)} async-done(((bf16[4,16,2048]{2,1,0:T(8,128)(2,1)}), bf16[4,16,2048]{2,1,0:T(8,128)(2,1)S(1)}, u32[]{:S(2)}, u32[]{:S(2)}) %all-to-all-start.1) | async-done | bytes 262176 | tf_op jit(solution)/shard_map/all_to_all | solution.py:55
  126.4 3.3 %collective-permute-done.9.refs_1_.refs_5_ = bf16[64,2048]{1,0:T(8,128)(2,1)S(1)} collective-permute-done((bf16[64,2048]{1,0:T(8,128)(2,1)S(1)}, bf16[64,2048]{1,0:T(8,128)(2,1)S(1)}, u32[]{:S(2)}, u32[]{:S(2)}) %collective-permute-start.9) | collective-permute-done | bytes 262176 | tf_op jit(solution)/shard_map/ppermute | solution.py:60
  131.3 2.1 %collective-permute-done.21.refs_1_ = f32[16,128]{1,0:T(8,128)S(1)} collective-permute-done((f32[16,128]{1,0:T(8,128)S(1)}, f32[16,128]{1,0:T(8,128)S(1)}, u32[]{:S(2)}, u32[]{:S(2)}) %collective-permute-start.21) | collective-permute-done | bytes 8224 | tf_op jit(solution)/shard_map/ppermute | solution.py:43
  134.6 14.0 %all_gather.11.mg_ref = bf16[64,2048]{1,0:T(8,128)(2,1)S(1)} all-gather(bf16[16,2048]{1,0:T(8,128)(2,1)S(1)} %mixed_grad.1), channel_id=1, replica_groups=mesh['dp'=4,'seq'=2,'vocab'=4] {'vocab'}, dimensions={0}, use_global_device_ids=true | all-gather | bytes 327680 | tf_op jit(solution)/shard_map/all_gather | solution.py:51
  148.6 2.2 %copy-done.1 = bf16[1024,2048]{1,0:T(8,128)(2,1)S(1)} copy-done((bf16[1024,2048]{1,0:T(8,128)(2,1)S(1)}, bf16[1024,2048]{1,0:T(8,128)(2,1)}, u32[]{:S(2)}) %copy-start.1) | copy-done | bytes 4194328
  150.8 1.8 back_project.1.refs_0_
  152.7 1.6 collective-permute-start.22
  154.3 3.4 %collective-permute-done.22.refs_1_ = bf16[64,1024]{1,0:T(8,128)(2,1)S(1)} collective-permute-done((bf16[64,1024]{1,0:T(8,128)(2,1)S(1)}, bf16[64,1024]{1,0:T(8,128)(2,1)S(1)}, u32[]{:S(2)}, u32[]{:S(2)}) %collective-permute-start.22) | collective-permute-done | bytes 131104 | tf_op jit(solution)/shard_map/ppermute | solution.py:43
  159.3 2.6 %attend_back.1 = (f32[1,128,1024]{2,1,0:T(8,128)}, f32[1,128,1024]{2,1,0:T(8,128)}) custom-call(s32[4]{0:T(128)S(1)} %pad_add_fusion.scal, bf16[64,1024]{1,0:T(8,128)(2,1)S(1)} %back_project.1.refs_0_, bf16[64,1024]{1,0:T(8,128)(2,1)S(1)} %collective-permute-done.22.refs_1_, bf16[64,1024]{1,0:T(8,128)(2,1)S(1)} %get-tuple-element.61.refs_2_, ...), custom_call_target="tpu_custom_call" | custom-call | tf_op jit(solution)/shard_map/attend_back/pallas_call | solution.py:520
  162.0 8.3 %head_grad.3.refs_8_ = bf16[8032,2048]{1,0:T(8,128)(2,1)} custom-call(bf16[64,2176]{1,0:T(8,128)(2,1)S(1)} %all_gather.9.ng_ref.refs_0_, bf16[64,2176]{1,0:T(8,128)(2,1)S(1)} %collective-permute-done.12.refs_1_, bf16[64,2176]{1,0:T(8,128)(2,1)S(1)} %collective-permute-done.13.refs_2_, bf16[64,2176]{1,0:T(8,128)(2,1)S(1)} %collective-permute-done.14.refs_3_, ...), custom_call_target="tpu_custom_call" | custom-call | flops 3221225472 | bytes 12582912 | tf_op jit(solution)/shard_map/head_grad/pallas_call | solution.py:532
  170.3 8.0 %head_grad.4.refs_8_ = bf16[8032,2048]{1,0:T(8,128)(2,1)} custom-call(bf16[64,2176]{1,0:T(8,128)(2,1)S(1)} %all_gather.9.ng_ref.refs_0_, bf16[64,2176]{1,0:T(8,128)(2,1)S(1)} %collective-permute-done.12.refs_1_, bf16[64,2176]{1,0:T(8,128)(2,1)S(1)} %collective-permute-done.13.refs_2_, ...), custom_call_target="tpu_custom_call", output_to_operand_aliasing={{}: (8, {})} | custom-call | flops 3221225472 | bytes 12582912 | tf_op jit(solution)/shard_map/head_grad/pallas_call | solution.py:532
  178.3 4.8 %head_grad.5 = bf16[8032,2048]{1,0:T(8,128)(2,1)} custom-call(bf16[64,2176]{1,0:T(8,128)(2,1)S(1)} %all_gather.9.ng_ref.refs_0_, bf16[64,2176]{1,0:T(8,128)(2,1)S(1)} %collective-permute-done.12.refs_1_, bf16[64,2176]{1,0:T(8,128)(2,1)S(1)} %collective-permute-done.13.refs_2_, ...), custom_call_target="tpu_custom_call", output_to_operand_aliasing={{}: (8, {})} | custom-call | flops 2147483648 | bytes 8388608 | tf_op jit(solution)/shard_map/head_grad/pallas_call | solution.py:532
  (69 shorter events, 24.6 us)
Async XLA Ops:
  0.6 5.5 %collective-permute-start = (bf16[1,32,1024]{2,1,0:T(8,128)(2,1)}, bf16[1,32,1024]{2,1,0:T(8,128)(2,1)S(1)}, u32[]{:S(2)}, u32[]{:S(2)}) collective-permute-start(bf16[1,32,1024]{2,1,0:T(8,128)(2,1)} %refs_0_.1), channel_id=1, source_target_pairs={{4,0},{0,4},{5,1},{1,5},{6,2},{2,6},{7,3},{3,7},{12,8},{8,12},{13,... | collective-permute-start | bytes 196616 | tf_op jit(solution)/shard_map/ppermute | solution.py:43
  10.5 5.2 %collective-permute-start.1 = (bf16[64,1152]{1,0:T(8,128)(2,1)S(1)}, bf16[64,1152]{1,0:T(8,128)(2,1)S(1)}, u32[]{:S(2)}, u32[]{:S(2)}) collective-permute-start(bf16[64,1152]{1,0:T(8,128)(2,1)S(1)} %get-tuple-element.35.refs_0_), channel_id=1, source_target_pairs={{4,0},{0,4},{5,1},{1,5},{6,2},{2,6},{7,3},{3,7},{12,8},{8,12},{13,... | collective-permute-start | bytes 442376 | tf_op jit(solution)/shard_map/ppermute | solution.py:43
  15.7 2.2 %copy-start = (bf16[1024,2048]{1,0:T(8,128)(2,1)S(1)}, bf16[1024,2048]{1,0:T(8,128)(2,1)}, u32[]{:S(2)}) copy-start(bf16[1024,2048]{1,0:T(8,128)(2,1)} %p_ref.1) | copy-start | bytes 12582916
  20.6 12.2 %copy-start.7 = (bf16[64,1024]{1,0:T(8,128)(2,1)}, bf16[64,1024]{1,0:T(8,128)(2,1)S(1)}, u32[]{:S(2)}) copy-start(bf16[64,1024]{1,0:T(8,128)(2,1)S(1)} %get-tuple-element.62.refs_5_) | copy-start | bytes 393220
  20.6 12.1 %all-to-all-start = ((bf16[4,16,2048]{2,1,0:T(8,128)(2,1)}), bf16[4,16,2048]{2,1,0:T(8,128)(2,1)S(1)}, u32[]{:S(2)}, u32[]{:S(2)}) async-start(bf16[4,16,2048]{2,1,0:T(8,128)(2,1)} %bitcast.5), calls=%async_computation | async-start | bytes 524288 | tf_op jit(solution)/shard_map/all_to_all | solution.py:55
  26.0 3.7 %collective-permute-start.4 = (s32[32]{0:T(128)}, s32[32]{0:T(128)S(1)}, u32[]{:S(2)}, u32[]{:S(2)}) collective-permute-start(s32[32]{0:T(128)} %bitcast.26), channel_id=1, source_target_pairs={{4,0},{0,4},{5,1},{1,5},{6,2},{2,6},{7,3},{3,7},{12,8},{8,12},{13,... | collective-permute-start | bytes 392 | tf_op jit(solution)/shard_map/ppermute | solution.py:43
  32.7 1.0 copy-start.6
  57.4 21.3 %collective-permute-start.7 = (s16[64,3072]{1,0:T(8,128)(2,1)S(1)}, s16[64,3072]{1,0:T(8,128)(2,1)S(1)}, u32[]{:S(2)}, u32[]{:S(2)}) collective-permute-start(s16[64,3072]{1,0:T(8,128)(2,1)S(1)} %get-tuple-element.42.refs_0_), channel_id=1, source_target_pairs={{4,0},{0,4},{5,1},{1,5},{6,2},{2,6},{7,3},{3,7},{12,8},{8,12},{13,... | collective-permute-start | bytes 1179656 | tf_op jit(solution)/shard_map/ppermute | solution.py:43
  59.0 18.2 %collective-permute-start.8 = (f32[64,128]{1,0:T(8,128)S(1)}, f32[64,128]{1,0:T(8,128)S(1)}, u32[]{:S(2)}, u32[]{:S(2)}) collective-permute-start(f32[64,128]{1,0:T(8,128)S(1)} %get-tuple-element.43.refs_2_), channel_id=1, source_target_pairs={{4,0},{0,4},{5,1},{1,5},{6,2},{2,6},{7,3},{3,7},{12,8},{8,12},{13,... | collective-permute-start | bytes 98312 | tf_op jit(solution)/shard_map/ppermute | solution.py:43
  67.8 19.2 %collective-permute-start.5 = (s16[64,3072]{1,0:T(8,128)(2,1)S(1)}, s16[64,3072]{1,0:T(8,128)(2,1)S(1)}, u32[]{:S(2)}, u32[]{:S(2)}) collective-permute-start(s16[64,3072]{1,0:T(8,128)(2,1)S(1)} %get-tuple-element.40.refs_0_), channel_id=1, source_target_pairs={{4,0},{0,4},{5,1},{1,5},{6,2},{2,6},{7,3},{3,7},{12,8},{8,12},{13,... | collective-permute-start | bytes 1179656 | tf_op jit(solution)/shard_map/ppermute | solution.py:43
  75.0 46.6 %collective-permute-start.12 = (bf16[64,2176]{1,0:T(8,128)(2,1)S(1)}, bf16[64,2176]{1,0:T(8,128)(2,1)S(1)}, u32[]{:S(2)}, u32[]{:S(2)}) collective-permute-start(bf16[64,2176]{1,0:T(8,128)(2,1)S(1)} %all_gather.9.ng_ref.refs_0_), channel_id=1, source_target_pairs={{0,16},{8,24},{16,0},{24,8},{1,17},{9,25},{17,1},{25,9},{2,18},{10... | collective-permute-start | bytes 835592 | tf_op jit(solution)/shard_map/ppermute | solution.py:60
  76.6 10.4 %collective-permute-start.6 = (f32[64,128]{1,0:T(8,128)S(1)}, f32[64,128]{1,0:T(8,128)S(1)}, u32[]{:S(2)}, u32[]{:S(2)}) collective-permute-start(f32[64,128]{1,0:T(8,128)S(1)} %get-tuple-element.41.refs_2_), channel_id=1, source_target_pairs={{4,0},{0,4},{5,1},{1,5},{6,2},{2,6},{7,3},{3,7},{12,8},{8,12},{13,... | collective-permute-start | bytes 98312 | tf_op jit(solution)/shard_map/ppermute | solution.py:43
  77.1 17.9 %collective-permute-start.2 = (s16[64,2048]{1,0:T(8,128)(2,1)S(1)}, s16[64,2048]{1,0:T(8,128)(2,1)S(1)}, u32[]{:S(2)}, u32[]{:S(2)}) collective-permute-start(s16[64,2048]{1,0:T(8,128)(2,1)S(1)} %get-tuple-element.38.refs_0_), channel_id=1, source_target_pairs={{4,0},{0,4},{5,1},{1,5},{6,2},{2,6},{7,3},{3,7},{12,8},{8,12},{13,... | collective-permute-start | bytes 786440 | tf_op jit(solution)/shard_map/ppermute | solution.py:43
  78.6 16.4 %collective-permute-start.3 = (f32[64,128]{1,0:T(8,128)S(1)}, f32[64,128]{1,0:T(8,128)S(1)}, u32[]{:S(2)}, u32[]{:S(2)}) collective-permute-start(f32[64,128]{1,0:T(8,128)S(1)} %get-tuple-element.39.refs_2_), channel_id=1, source_target_pairs={{4,0},{0,4},{5,1},{1,5},{6,2},{2,6},{7,3},{3,7},{12,8},{8,12},{13,... | collective-permute-start | bytes 98312 | tf_op jit(solution)/shard_map/ppermute | solution.py:43
  87.0 39.3 %copy-start.11 = (f32[2048]{0:T(1024)S(1)}, f32[2048]{0:T(1024)}, u32[]{:S(2)}) copy-start(f32[2048]{0:T(1024)} %param.15) | copy-start | bytes 24580
  87.0 71.4 %copy-start.3 = (bf16[1,128,1024]{2,1,0:T(8,128)(2,1)S(1)}, bf16[1,128,1024]{2,1,0:T(8,128)(2,1)}, u32[]{:S(2)}) copy-start(bf16[1,128,1024]{2,1,0:T(8,128)(2,1)} %refs_3_.3) | copy-start | bytes 786436
  87.1 71.4 %copy-start.5 = (bf16[1,128,1024]{2,1,0:T(8,128)(2,1)S(1)}, bf16[1,128,1024]{2,1,0:T(8,128)(2,1)}, u32[]{:S(2)}) copy-start(bf16[1,128,1024]{2,1,0:T(8,128)(2,1)} %refs_4_.1) | copy-start | bytes 786436
  115.6 8.6 %collective-permute-start.18 = (bf16[64,3072]{1,0:T(8,128)(2,1)S(1)}, bf16[64,3072]{1,0:T(8,128)(2,1)}, u32[]{:S(2)}, u32[]{:S(2)}) collective-permute-start(bf16[64,3072]{1,0:T(8,128)(2,1)S(1)} %get-tuple-element.56.refs_4_), channel_id=1, source_target_pairs={{0,16},{8,24},{16,0},{24,8},{1,17},{9,25},{17,1},{25,9},{2,18},{10... | collective-permute-start | bytes 1179656 | tf_op jit(solution)/shard_map/ppermute | solution.py:60
  116.1 10.2 %all-to-all-start.1 = ((bf16[4,16,2048]{2,1,0:T(8,128)(2,1)}), bf16[4,16,2048]{2,1,0:T(8,128)(2,1)S(1)}, u32[]{:S(2)}, u32[]{:S(2)}) async-start(bf16[4,16,2048]{2,1,0:T(8,128)(2,1)} %bitcast.12), calls=%async_computation.1 | async-start | bytes 524288 | tf_op jit(solution)/shard_map/all_to_all | solution.py:55
  119.5 2.2 %collective-permute-start.13 = (bf16[64,2176]{1,0:T(8,128)(2,1)S(1)}, bf16[64,2176]{1,0:T(8,128)(2,1)S(1)}, u32[]{:S(2)}, u32[]{:S(2)}) collective-permute-start(bf16[64,2176]{1,0:T(8,128)(2,1)S(1)} %all_gather.9.ng_ref.refs_0_), channel_id=1, source_target_pairs={{0,8},{8,0},{16,24},{24,16},{1,9},{9,1},{17,25},{25,17},{2,10},{10... | collective-permute-start | bytes 835592 | tf_op jit(solution)/shard_map/ppermute | solution.py:60
  119.6 10.2 %collective-permute-start.9 = (bf16[64,2048]{1,0:T(8,128)(2,1)S(1)}, bf16[64,2048]{1,0:T(8,128)(2,1)S(1)}, u32[]{:S(2)}, u32[]{:S(2)}) collective-permute-start(bf16[64,2048]{1,0:T(8,128)(2,1)S(1)} %get-tuple-element.54.refs_0_.refs_4_), channel_id=1, source_target_pairs={{0,16},{8,24},{16,0},{24,8},{1,17},{9,25},{17,1},{25,9},{2,18},{10... | collective-permute-start | bytes 786440 | tf_op jit(solution)/shard_map/ppermute | solution.py:60
  121.3 31.4 %collective-permute-start.15 = (bf16[64,3072]{1,0:T(8,128)(2,1)S(1)}, bf16[64,3072]{1,0:T(8,128)(2,1)}, u32[]{:S(2)}, u32[]{:S(2)}) collective-permute-start(bf16[64,3072]{1,0:T(8,128)(2,1)S(1)} %get-tuple-element.55.refs_4_), channel_id=1, source_target_pairs={{0,16},{8,24},{16,0},{24,8},{1,17},{9,25},{17,1},{25,9},{2,18},{10... | collective-permute-start | bytes 1179656 | tf_op jit(solution)/shard_map/ppermute | solution.py:60
  121.7 12.4 %collective-permute-start.10 = (bf16[64,2048]{1,0:T(8,128)(2,1)S(1)}, bf16[64,2048]{1,0:T(8,128)(2,1)S(1)}, u32[]{:S(2)}, u32[]{:S(2)}) collective-permute-start(bf16[64,2048]{1,0:T(8,128)(2,1)S(1)} %get-tuple-element.54.refs_0_.refs_4_), channel_id=1, source_target_pairs={{0,8},{8,0},{16,24},{24,16},{1,9},{9,1},{17,25},{25,17},{2,10},{10... | collective-permute-start | bytes 786440 | tf_op jit(solution)/shard_map/ppermute | solution.py:60
  121.7 40.3 %collective-permute-start.19 = (bf16[64,3072]{1,0:T(8,128)(2,1)S(1)}, bf16[64,3072]{1,0:T(8,128)(2,1)}, u32[]{:S(2)}, u32[]{:S(2)}) collective-permute-start(bf16[64,3072]{1,0:T(8,128)(2,1)S(1)} %get-tuple-element.56.refs_4_), channel_id=1, source_target_pairs={{0,8},{8,0},{16,24},{24,16},{1,9},{9,1},{17,25},{25,17},{2,10},{10... | collective-permute-start | bytes 1179656 | tf_op jit(solution)/shard_map/ppermute | solution.py:60
  124.3 37.7 %collective-permute-start.20 = (bf16[64,3072]{1,0:T(8,128)(2,1)}, bf16[64,3072]{1,0:T(8,128)(2,1)}, u32[]{:S(2)}, u32[]{:S(2)}) collective-permute-start(bf16[64,3072]{1,0:T(8,128)(2,1)} %collective-permute-done.18.refs_5_), channel_id=1, source_target_pairs={{0,8},{8,0},{16,24},{24,16},{1,9},{9,1},{17,25},{25,17},{2,10},{10... | collective-permute-start | bytes 1179656 | tf_op jit(solution)/shard_map/ppermute | solution.py:60
  129.8 3.7 %collective-permute-start.21 = (f32[16,128]{1,0:T(8,128)S(1)}, f32[16,128]{1,0:T(8,128)S(1)}, u32[]{:S(2)}, u32[]{:S(2)}) collective-permute-start(f32[16,128]{1,0:T(8,128)S(1)} %get-tuple-element.60.refs_0_), channel_id=1, source_target_pairs={{4,0},{0,4},{5,1},{1,5},{6,2},{2,6},{7,3},{3,7},{12,8},{8,12},{13,... | collective-permute-start | bytes 24584 | tf_op jit(solution)/shard_map/ppermute | solution.py:43
  133.4 20.9 %collective-permute-start.11 = (bf16[64,2048]{1,0:T(8,128)(2,1)S(1)}, bf16[64,2048]{1,0:T(8,128)(2,1)S(1)}, u32[]{:S(2)}, u32[]{:S(2)}) collective-permute-start(bf16[64,2048]{1,0:T(8,128)(2,1)S(1)} %collective-permute-done.9.refs_1_.refs_5_), channel_id=1, source_target_pairs={{0,8},{8,0},{16,24},{24,16},{1,9},{9,1},{17,25},{25,17},{2,10},{10... | collective-permute-start | bytes 786440 | tf_op jit(solution)/shard_map/ppermute | solution.py:60
  134.1 27.9 %collective-permute-start.14 = (bf16[64,2176]{1,0:T(8,128)(2,1)S(1)}, bf16[64,2176]{1,0:T(8,128)(2,1)S(1)}, u32[]{:S(2)}, u32[]{:S(2)}) collective-permute-start(bf16[64,2176]{1,0:T(8,128)(2,1)S(1)} %collective-permute-done.12.refs_1_), channel_id=1, source_target_pairs={{0,8},{8,0},{16,24},{24,16},{1,9},{9,1},{17,25},{25,17},{2,10},{10... | collective-permute-start | bytes 835592 | tf_op jit(solution)/shard_map/ppermute | solution.py:60
  148.6 2.2 %copy-start.1 = (bf16[1024,2048]{1,0:T(8,128)(2,1)S(1)}, bf16[1024,2048]{1,0:T(8,128)(2,1)}, u32[]{:S(2)}) copy-start(bf16[1024,2048]{1,0:T(8,128)(2,1)} %p_ref.1) | copy-start | bytes 12582916
  152.7 5.0 %collective-permute-start.22 = (bf16[64,1024]{1,0:T(8,128)(2,1)S(1)}, bf16[64,1024]{1,0:T(8,128)(2,1)S(1)}, u32[]{:S(2)}, u32[]{:S(2)}) collective-permute-start(bf16[64,1024]{1,0:T(8,128)(2,1)S(1)} %back_project.1.refs_0_), channel_id=1, source_target_pairs={{4,0},{0,4},{5,1},{1,5},{6,2},{2,6},{7,3},{3,7},{12,8},{8,12},{13,... | collective-permute-start | bytes 393224 | tf_op jit(solution)/shard_map/ppermute | solution.py:43
  154.3 16.0 %collective-permute-start.16 = (bf16[64,3072]{1,0:T(8,128)(2,1)S(1)}, bf16[64,3072]{1,0:T(8,128)(2,1)S(1)}, u32[]{:S(2)}, u32[]{:S(2)}) collective-permute-start(bf16[64,3072]{1,0:T(8,128)(2,1)S(1)} %get-tuple-element.55.refs_4_), channel_id=1, source_target_pairs={{0,8},{8,0},{16,24},{24,16},{1,9},{9,1},{17,25},{25,17},{2,10},{10... | collective-permute-start | bytes 1179656 | tf_op jit(solution)/shard_map/ppermute | solution.py:60
  157.7 12.6 %collective-permute-start.17 = (bf16[64,3072]{1,0:T(8,128)(2,1)}, bf16[64,3072]{1,0:T(8,128)(2,1)S(1)}, u32[]{:S(2)}, u32[]{:S(2)}) collective-permute-start(bf16[64,3072]{1,0:T(8,128)(2,1)} %collective-permute-done.15.refs_5_), channel_id=1, source_target_pairs={{0,8},{8,0},{16,24},{24,16},{1,9},{9,1},{17,25},{25,17},{2,10},{10... | collective-permute-start | bytes 1179656 | tf_op jit(solution)/shard_map/ppermute | solution.py:60
  (5 other events, 4.3 us)

commit v3 on v2

--- a/solution.py
+++ b/solution.py
@@ -9,6 +9,9 @@
 HDIM = 256
 LANES = 128
 TILE = 512
+PARTS = 4
+PART = TILE // PARTS
+HEAD_TILE = 2 * TILE
 MAX_CHUNKS = 3
 LOW = -1e30
 CODE_TOP = 32767.0
@@ -45,10 +48,6 @@
 
 def gather_ring(x, axis):
     return [x] + [from_ahead(x, axis, k) for k in range(1, lax.axis_size(axis))]
-
-
-def gather_rows(x, axis):
-    return lax.all_gather(x, axis, axis=0, tiled=True)
 
 
 def exchange_rows(x, axis):
@@ -89,7 +88,7 @@
 
 def attend_kernel(n_seq, scal, *refs):
     q_refs = refs[:n_seq]
-    k_ref, v_ref, o_ref, q_out, q_twice = refs[n_seq:]
+    tgt_ref, k_ref, v_ref, o_ref, q_out, q_twice = refs[n_seq:]
     tgt_rows = q_refs[0].shape[1]
     rows = tgt_rows * n_seq
     enc, features = k_ref.shape[1:]
@@ -100,7 +99,11 @@
     q_out[...] = q
     valid = lax.broadcasted_iota(i32, (rows, enc), 1) < scal[1]
     lane = lanes(rows)
-    stat = jnp.zeros((rows, LANES), f32)
+    row = lax.broadcasted_iota(i32, (rows, LANES), 0)
+    mine = (row >= scal[4]) & (row < scal[4] + tgt_rows)
+    ids = jnp.concatenate([tgt_ref[...]] * n_seq, axis=0)
+    ids = jnp.where(lane == LANES - 2, ids >> 8, ids & 255).astype(f32)
+    stat = jnp.where(mine & (lane >= LANES - 2), ids, 0.0)
     for h in range(features // HDIM):
         at = slice(h * HDIM, (h + 1) * HDIM)
         scores = dot(q[:, at], k_ref[0, :, at], 1, 1) * score_scale
@@ -118,9 +121,9 @@
     o_ref[:, features:] = stat.astype(bf16)
 
 
-def project_kernel(n_seq, *refs):
+def project_kernel(n_seq, scal, *refs):
     o_refs = refs[:n_seq]
-    p_ref, mixed_ref, att_ref, lse_ref, att = refs[n_seq:]
+    p_ref, mixed_ref, att_ref, lse_ref, tgt_ref, att = refs[n_seq:]
     rows, features = att.shape
 
     @pl.when(pl.program_id(0) == 0)
@@ -141,6 +144,8 @@
             lse_all = jnp.where(lane == h, lse, lse_all)
         att_ref[...] = att[...]
         lse_ref[...] = lse_all
+        ids = tree([s[:, LANES - 2 : LANES - 1] * 256.0 + s[:, LANES - 1 :] for s in stats])
+        tgt_ref[...] = jnp.broadcast_to(ids.astype(i32), (rows, LANES)) - scal[3]
 
     mixed_ref[...] = dot(att[...], p_ref[...], 1, 0).astype(bf16)
 
@@ -150,28 +155,33 @@
     return tree([ref[i * rows : (i + 1) * rows, :].astype(f32) for i in range(n)])
 
 
-def norm_kernel(scal, got_ref, residual_ref, gain_ref, mixed_ref, ng_ref):
+def norm_kernel(got_ref, residual_ref, gain_ref, mixed_ref, ng_ref):
     rows, width = mixed_ref.shape
-    res = residual_ref[0, pl.ds(pl.multiple_of(scal[2], 16), rows), :].astype(f32)
-    mixed = res + block_sum(got_ref, rows)
+    mixed = residual_ref[...].astype(f32) + block_sum(got_ref, rows)
     mixed_ref[...] = mixed
-    ng_ref[:, :width] = (mixed * gain_ref[...]).astype(bf16)
+    ng = (mixed * gain_ref[...]).astype(bf16)
     square = jnp.sum(mixed * mixed, axis=1, keepdims=True)
     lane = lanes(rows)
     stat = jnp.zeros((rows, LANES), f32)
     for i, part in enumerate(three_parts(square)):
         stat = jnp.where(lane == i, part, stat)
-    ng_ref[:, width:] = stat.astype(bf16)
-
-
-def logits_kernel(first, cols, ng_ref, w_ref, code_ref, stat_ref, z):
+    for at in range(0, ng_ref.shape[0], rows):
+        ng_ref[at : at + rows, :width] = ng
+        ng_ref[at : at + rows, width:] = stat.astype(bf16)
+
+
+def logits_kernel(first, cols, ng_ref, *refs):
+    w_refs = refs[:PARTS]
+    code_ref, stat_ref, z = refs[PARTS:]
     j = pl.program_id(0)
-    rows, width = z.shape[0], w_ref.shape[1]
-    part = dot(ng_ref[:, :width], w_ref[...], 1, 1)
+    rows, width = z.shape[0], w_refs[0].shape[1]
+    w = jnp.concatenate([r[...] for r in w_refs], axis=0)
+    part = dot(w, ng_ref[:, :width], 1, 1).T
+    at = j * TILE
     if first + z.shape[1] > cols:
-        at = first + j * TILE + lax.broadcasted_iota(i32, part.shape, 1)
-        part = jnp.where(at < cols, part, 0.0)
-    z[:, pl.ds(pl.multiple_of(j * TILE, TILE), TILE)] = part
+        here = first + at + lax.broadcasted_iota(i32, part.shape, 1)
+        part = jnp.where(here < cols, part, 0.0)
+    z[:, pl.ds(pl.multiple_of(at, TILE), TILE)] = part
 
     @pl.when(j == pl.num_programs(0) - 1)
     def _():
@@ -188,9 +198,10 @@
     code_refs, sc_refs = refs[:n_seq], refs[n_seq : 2 * n_seq]
     refs = refs[2 * n_seq :]
     if chunk:
-        tgt_ref, w_ref, acc_prev, st_prev, acc_ref, e_ref, st_ref, lhs = refs
+        acc_prev, st_prev, acc_ref, e_ref, st_ref, lhs = refs[1 + PARTS :]
     else:
-        tgt_ref, w_ref, acc_ref, e_ref, st_ref, lhs = refs
+        acc_ref, e_ref, st_ref, lhs = refs[1 + PARTS :]
+    tgt_ref, w_refs = refs[0], refs[1 : 1 + PARTS]
     j = pl.program_id(0)
     rows, size = e_ref.shape
     partial_cols = first + size > cols
@@ -229,19 +240,21 @@
         st = jnp.where(lane == 1, total, st)
         st = jnp.where(lane == 2, here + old[:, 2:3], st)
         st = jnp.where(lane == 3, inv, st)
-        st_ref[...] = jnp.where(lane == 8 + chunk, peak, st)
-
-    w = w_ref[...]
+        st = jnp.where(lane == 8 + chunk, peak, st)
+        for at in range(0, st_ref.shape[0], rows):
+            st_ref[at : at + rows, :] = st
+
+    w = jnp.concatenate([r[...] for r in w_refs], axis=0)
+    at = j * TILE
     if partial_cols:
-        at = first + j * TILE + lax.broadcasted_iota(i32, (TILE, 1), 0)
-        w = jnp.where(at < cols, w, jnp.zeros_like(w))
-    left = lhs[:, pl.ds(pl.multiple_of(j * TILE, TILE), TILE)]
-    acc_ref[...] += dot(left, w, 1, 0)
-
-
-def total_kernel(n_vocab, st_ref, st_all_ref, acc_ref, part_ref, coef_ref):
+        here = first + at + lax.broadcasted_iota(i32, (TILE, 1), 0)
+        w = jnp.where(here < cols, w, jnp.zeros_like(w))
+    acc_ref[...] += dot(lhs[:, pl.ds(pl.multiple_of(at, TILE), TILE)], w, 1, 0)
+
+
+def total_kernel(n_vocab, st_rep_ref, st_all_ref, acc_ref, part_ref, coef_ref):
     rows = coef_ref.shape[0]
-    mine = st_ref[...]
+    mine = st_rep_ref[:rows, :]
     stats = [st_all_ref[k * rows : (k + 1) * rows, :] for k in range(n_vocab)]
     top = tree([s[:, 0:1] for s in stats], jnp.maximum)
     total = tree([s[:, 1:2] * jnp.exp(s[:, 0:1] - top) for s in stats])
@@ -287,7 +300,7 @@
 
 def head_kernel(n_dp, *refs):
     ng_refs, g_refs = refs[:n_dp], refs[n_dp : 2 * n_dp]
-    out_ref, ng = refs[-2], refs[-1]
+    out_ref, ng, turned = refs[-3:]
     rows, width = ng_refs[0].shape[0], out_ref.shape[1]
 
     @pl.when(pl.program_id(0) == 0)
@@ -295,9 +308,9 @@
         for i, r in enumerate(ng_refs):
             ng[i * rows : (i + 1) * rows, :] = r[:, :width]
 
-    g = jnp.concatenate([r[...] for r in g_refs], axis=0)
-    for at in range(0, TILE, 256):
-        out_ref[at : at + 256, :] = dot(g[:, at : at + 256], ng[...], 0, 0).astype(bf16)
+    turned[...] = jnp.concatenate([r[...] for r in g_refs], axis=0).T
+    for at in range(0, width, 256):
+        out_ref[:, at : at + 256] = dot(turned[...], ng[:, at : at + 256], 1, 0).astype(bf16)
 
 
 def gate_kernel(got_ref, mixed_ref, gain_ref, gated_ref, dot_ref):
@@ -309,11 +322,12 @@
 
 def mixed_grad_kernel(n_seq, features, scal, gated_ref, mixed_ref, coef_ref, *refs):
     dot_refs, out_ref = refs[:n_seq], refs[n_seq]
-    rows = out_ref.shape[0]
+    rows = gated_ref.shape[0]
     inner = tree([r[:, 0:1] for r in dot_refs])
     inv = coef_ref[pl.ds(pl.multiple_of(scal[2], 16), rows), :][:, 0:1]
     out = gated_ref[...] * inv - mixed_ref[...] * (inv * inv * inv * inner / features)
-    out_ref[...] = out.astype(bf16)
+    for at in range(0, out_ref.shape[0], rows):
+        out_ref[at : at + rows, :] = out.astype(bf16)
 
 
 def back_project_kernel(mg_ref, p_ref, out_ref):
@@ -339,6 +353,17 @@
         kg_ref[0, :, at] = dot(sg, q, 0, 0)
 
 
+def weight_specs(tile0, width, cols):
+    top = -(-cols // PART) - 1
+    return [
+        pl.BlockSpec(
+            (PART, width),
+            lambda j, i=i: (jnp.minimum(PARTS * (tile0 + j) + i, top), 0),
+        )
+        for i in range(PARTS)
+    ]
+
+
 def body(
     queries, enc_keys, enc_values, enc_lengths, out_proj, residual, norm_gain, head_weight, targets
 ):
@@ -351,7 +376,8 @@
     width, cols = head_weight.shape
     full_width = width * n_seq
     tiles = -(-cols // TILE)
-    per = -(-tiles // MAX_CHUNKS)
+    per = 2 * -(-tiles // (2 * MAX_CHUNKS))
+    assert tiles % 2 == 0
     chunks = [(t, min(per, tiles - t)) for t in range(0, tiles, per)]
     firsts = [t * TILE for t, _ in chunks]
     gain = norm_gain.reshape(1, width)
@@ -359,57 +385,60 @@
 
     start = lax.rem(rows - seq * tgt_rows, rows).astype(i32)
     scal = jnp.stack(
-        [start, enc_lengths[0] - seq * enc, voc * own_rows, voc * cols]
+        [start, enc_lengths[0] - seq * enc, voc * own_rows, voc * cols, seq * tgt_rows]
     ).astype(i32)
 
     q_parts = gather_ring(queries, "seq")
-    tgt_parts = gather_ring(targets.reshape(tgt_rows), "seq")
-    tgt_twice = jnp.concatenate(tgt_parts + tgt_parts)
-    tgt = lax.dynamic_slice(tgt_twice, (start,), (rows,)) - voc * cols
-    tgt = jnp.broadcast_to(tgt[:, None], (rows, LANES))
-
+    tgt_own = jnp.broadcast_to(targets.reshape(tgt_rows, 1), (tgt_rows, LANES))
+    res_own = lax.dynamic_slice(residual[0], (voc * own_rows, 0), (own_rows, width))
     o_part, q_all = pl.pallas_call(
         functools.partial(attend_kernel, n_seq),
         out_shape=[sds((rows, features + LANES), bf16), sds((rows, features), bf16)],
-        in_specs=[SMEM] + [VMEM] * (n_seq + 2),
+        in_specs=[SMEM] + [VMEM] * (n_seq + 3),
         out_specs=[VMEM, VMEM],
         scratch_shapes=[pltpu.VMEM((2 * rows, features), bf16)],
         compiler_params=params(),
+        cost_estimate=cost(0, 7 * 1024 * 1024),
         name="attend",
-    )(scal, *q_parts, enc_keys, enc_values)
+    )(scal, *q_parts, tgt_own, enc_keys, enc_values)
 
     o_all = gather_ring(o_part, "seq")
     ptile = min(TILE, width)
     whole = lambda shape: pl.BlockSpec(shape, lambda j: (0, 0))
-    mixed_part, att, lse = pl.pallas_call(
+    mixed_part, att, lse, tgt = pl.pallas_call(
         functools.partial(project_kernel, n_seq),
         grid=(width // ptile,),
         out_shape=[
             sds((rows, width), bf16),
             sds((rows, features), bf16),
             sds((rows, LANES), f32),
+            sds((rows, LANES), i32),
         ],
-        in_specs=[whole((rows, features + LANES))] * n_seq
+        in_specs=[SMEM]
+        + [whole((rows, features + LANES))] * n_seq
         + [pl.BlockSpec((features, ptile), lambda j: (0, j))],
         out_specs=[
             pl.BlockSpec((rows, ptile), lambda j: (0, j)),
             whole((rows, features)),
             whole((rows, LANES)),
+            whole((rows, LANES)),
         ],
         scratch_shapes=[pltpu.VMEM((rows, features), bf16)],
         compiler_params=params(),
+        cost_estimate=cost(0, 7 * 1024 * 1024),
         name="project",
-    )(*o_all, out_proj)
+    )(scal, *o_all, out_proj)
 
     mixed, ng_own = pl.pallas_call(
         norm_kernel,
-        out_shape=[sds((own_rows, width), f32), sds((own_rows, width + LANES), bf16)],
-        in_specs=[SMEM] + [VMEM] * 3,
+        out_shape=[sds((own_rows, width), f32), sds((rows, width + LANES), bf16)],
+        in_specs=[VMEM] * 3,
         out_specs=[VMEM, VMEM],
         compiler_params=params(),
+        cost_estimate=cost(0, 7 * 1024 * 1024),
         name="norm",
-    )(scal, exchange_rows(mixed_part, "vocab"), residual, gain)
-    ng = gather_rows(ng_own, "vocab")
+    )(exchange_rows(mixed_part, "vocab"), res_own, gain)
+    ng = exchange_rows(ng_own, "vocab")
     ng_dp = gather_swaps(ng, "dp")
 
     codes, stats = [], []
@@ -419,16 +448,13 @@
             functools.partial(logits_kernel, tile0 * TILE, cols),
             grid=(n,),
             out_shape=[sds((rows, size), jnp.int16), sds((rows, LANES), f32)],
-            in_specs=[
-                whole((rows, width + LANES)),
-                pl.BlockSpec((TILE, width), lambda j, t=tile0: (t + j, 0)),
-            ],
+            in_specs=[whole((rows, width + LANES))] + weight_specs(tile0, width, cols),
             out_specs=[whole((rows, size)), whole((rows, LANES))],
             scratch_shapes=[pltpu.VMEM((rows, size), f32)],
             compiler_params=params(),
             cost_estimate=cost(2 * 256 * width * size, 2 * width * size),
             name="logits",
-        )(ng, weight)
+        )(ng, *[weight] * PARTS)
         codes.append(gather_ring(code, "seq"))
         stats.append(gather_ring(stat, "seq"))
 
@@ -437,30 +463,32 @@
     for c, (tile0, n) in enumerate(chunks):
         size = n * TILE
         prev = [acc, st] if c else []
+        st_rows = rows * n_vocab if c == len(chunks) - 1 else rows
         acc, e, st = pl.pallas_call(
             functools.partial(hidden_kernel, c, tile0 * TILE, cols, n_seq, full_width),
             grid=(n,),
-            out_shape=[sds((2 * rows, width), f32), sds((rows, size), bf16), sds((rows, LANES), f32)],
+            out_shape=[sds((2 * rows, width), f32), sds((rows, size), bf16), sds((st_rows, LANES), f32)],
             in_specs=[SMEM]
             + [whole((rows, size))] * n_seq
             + [whole((rows, LANES))] * (n_seq + 1)
-            + [pl.BlockSpec((TILE, width), lambda j, t=tile0: (t + j, 0))]
+            + weight_specs(tile0, width, cols)
             + ([whole((2 * rows, width)), whole((rows, LANES))] if c else []),
-            out_specs=[whole((2 * rows, width)), whole((rows, size)), whole((rows, LANES))],
+            out_specs=[whole((2 * rows, width)), whole((rows, size)), whole((st_rows, LANES))],
             scratch_shapes=[pltpu.VMEM((2 * rows, size), bf16)],
             compiler_params=params(),
             cost_estimate=cost(2 * 256 * width * size, 2 * width * size),
             name="hidden",
-        )(scal, *codes[c], *stats[c], tgt, weight, *prev)
+        )(scal, *codes[c], *stats[c], tgt, *[weight] * PARTS, *prev)
         exps.append(e)
 
-    st_all = gather_rows(st, "vocab")
+    st_all = exchange_rows(st, "vocab")
     hidden_part, coef = pl.pallas_call(
         functools.partial(total_kernel, n_vocab),
         out_shape=[sds((rows, width), bf16), sds((rows, LANES), f32)],
         in_specs=[VMEM] * 3,
         out_specs=[VMEM] * 2,
         compiler_params=params(),
+        cost_estimate=cost(0, 7 * 1024 * 1024),
         name="total",
     )(st, st_all, acc)
     got = exchange_rows(hidden_part, "vocab")
@@ -472,6 +500,7 @@
         in_specs=[VMEM] * (2 + len(exps)),
         out_specs=[VMEM] * len(exps),
         compiler_params=params(),
+        cost_estimate=cost(0, 7 * 1024 * 1024),
         name="logit_grad",
     )(coef, tgt, *exps)
     grads_dp = [gather_swaps(g, "dp") for g in grads]
@@ -483,6 +512,7 @@
         in_specs=[pl.BlockSpec((rows, LANES), lambda j: (0, last // LANES - 1))] * n_dp,
         out_specs=whole((8, LANES)),
         compiler_params=params(),
+        cost_estimate=cost(0, 7 * 1024 * 1024),
         name="loss",
     )(*grads_dp[-1])
     mean_loss = loss[0, 0]
@@ -493,18 +523,20 @@
         in_specs=[VMEM] * 3,
         out_specs=[VMEM, VMEM],
         compiler_params=params(),
+        cost_estimate=cost(0, 7 * 1024 * 1024),
         name="gate",
     )(got, mixed, gain)
     inner_all = gather_ring(inner, "seq")
     mixed_grad = pl.pallas_call(
         functools.partial(mixed_grad_kernel, n_seq, full_width),
-        out_shape=sds((own_rows, width), bf16),
+        out_shape=sds((rows, width), bf16),
         in_specs=[SMEM] + [VMEM] * (3 + n_seq),
         out_specs=VMEM,
         compiler_params=params(),
+        cost_estimate=cost(0, 7 * 1024 * 1024),
         name="mixed_grad",
     )(scal, gated, mixed, coef, *inner_all)
-    mg = gather_rows(mixed_grad, "vocab")
+    mg = exchange_rows(mixed_grad, "vocab")
 
     ftile = min(256, features)
     back_part = pl.pallas_call(
@@ -514,6 +546,7 @@
         in_specs=[whole((rows, width)), pl.BlockSpec((ftile, width), lambda j: (j, 0))],
         out_specs=pl.BlockSpec((rows, ftile), lambda j: (0, j)),
         compiler_params=params(),
+        cost_estimate=cost(0, 7 * 1024 * 1024),
         name="back_project",
     )(mg, out_proj)
     back_all = gather_ring(back_part, "seq")
@@ -523,6 +556,7 @@
         in_specs=[SMEM] + [VMEM] * (n_seq + 5),
         out_specs=[VMEM, VMEM],
         compiler_params=params(),
+        cost_estimate=cost(0, 7 * 1024 * 1024),
         name="attend_back",
     )(scal, *back_all, q_all, enc_keys, enc_values, att, lse)
 
@@ -531,13 +565,16 @@
         prev = [head] if c else []
         head = pl.pallas_call(
             functools.partial(head_kernel, n_dp),
-            grid=(n,),
+            grid=(n // 2,),
             out_shape=sds((cols, width), bf16),
             in_specs=[whole((rows, width + LANES))] * n_dp
-            + [pl.BlockSpec((rows, TILE), lambda j: (0, j))] * n_dp
+            + [pl.BlockSpec((rows, HEAD_TILE), lambda j: (0, j))] * n_dp
             + [pl.BlockSpec(memory_space=pl.ANY)] * len(prev),
-            out_specs=pl.BlockSpec((TILE, width), lambda j, t=tile0: (t + j, 0)),
-            scratch_shapes=[pltpu.VMEM((n_dp * rows, width), bf16)],
+            out_specs=pl.BlockSpec((HEAD_TILE, width), lambda j, t=tile0: (t // 2 + j, 0)),
+            scratch_shapes=[
+                pltpu.VMEM((n_dp * rows, width), bf16),
+                pltpu.VMEM((HEAD_TILE, n_dp * rows), bf16),
+            ],
             input_output_aliases={2 * n_dp: 0} if c else {},
             compiler_params=params(),
             cost_estimate=cost(2 * n_dp * rows * width * n * TILE, 2 * width * n * TILE),

time: 184 us -> 170 us (0.924)
  blocking collectives: 41.7 us -> 19.3 us
  waiting for transfers between devices: 22.2 us -> 28.9 us
  starting transfers between devices: 30.1 us -> 33.6 us
    all_gather x3 -> x0, blocking collectives: 41.7 us -> none  [gather_rows(): return lax.all_gather(x, axis, axis=0, tiled=True)]
    all_to_all x0 -> x2, blocking collectives: none -> 19.3 us  [exchange_rows(): return lax.all_to_all(x, axis, split_axis=0, concat_axis=0, tiled=True)]
    ppermute x12, waiting for transfers between devices: 5.42 us -> 15.1 us  [swap(): return lax.ppermute(x, axis, [(i, i ^ bit) for i in range(n)])]
    ppermute x11 -> x10, waiting for transfers between devices: 12.5 us -> 7 us  [from_ahead(): return lax.ppermute(x, axis, [((i + k) % n, i) for i in range(n)])]
    all_to_all x2 -> x3, starting transfers between devices: 8.8 us -> 12.4 us  [exchange_rows(): return lax.all_to_all(x, axis, split_axis=0, concat_axis=0, tiled=True)]
    all_to_all x2 -> x3, waiting for transfers between devices: 4.26 us -> 6.77 us  [exchange_rows(): return lax.all_to_all(x, axis, split_axis=0, concat_axis=0, tiled=True)]
    ppermute x11 -> x10, starting transfers between devices: 16 us -> 14.4 us  [from_ahead(): return lax.ppermute(x, axis, [((i + k) % n, i) for i in range(n)])]
    unnamed x24 -> x30, local copies, waits for them, and re-layouts: 9.69 us -> 9.15 us
  transfers between devices with their start and end apart: 25 -> 25, of which waited for: 9 -> 7; matrix products, arithmetic and copies ran while one was open for 1% -> 0% of each run, Pallas kernels for 27% -> 30%
where the time goes in v3:
time: 170 us; the launch traced here: 169 us
  Pallas kernels  75.6 us (44%)
  starting transfers between devices  33.6 us (20%)
  waiting for transfers between devices  28.9 us (17%)
  blocking collectives  19.3 us (11%)
  local copies, waits for them, and re-layouts  10.5 us (6%)
    pallas_call x3, Pallas kernels, body(): pl.pallas_call(functools.partial(logits_kernel, tile0 * TILE, cols), grid...  21.9 us
    pallas_call x3, Pallas kernels, body(): pl.pallas_call(functools.partial(hidden_kernel, c, tile0 * TILE, cols, n_...  20.9 us
    pallas_call x3, Pallas kernels, body(): pl.pallas_call(functools.partial(head_kernel, n_dp), grid=(n // 2,), out_...  20.1 us
    all_to_all x2, blocking collectives, exchange_rows(): return lax.all_to_all(x, axis, split_axis=0, concat_axis=0, tiled=True)  19.3 us
    ppermute x12, waiting for transfers between devices, swap(): return lax.ppermute(x, axis, [(i, i ^ bit) for i in range(n)])  15.1 us
    ppermute x10, starting transfers between devices, from_ahead(): return lax.ppermute(x, axis, [((i + k) % n, i) for i in range(n)])  14.4 us
    all_to_all x3, starting transfers between devices, exchange_rows(): return lax.all_to_all(x, axis, split_axis=0, concat_axis=0, tiled=True)  12.4 us
    unnamed x30, local copies, waits for them, and re-layouts  9.15 us
  transfers between devices with their start and end apart: 25, of which 7 were waited for; matrix products, arithmetic and copies ran while one was open for 0% of the time, Pallas kernels for 30%

profile of v3, /device:TPU:0, one launch (start us, length us, event | category | flops | bytes accessed | tf_op | source)
XLA Modules:
  0.0 169.3 jit_solution(3083113721953600516)
XLA Ops:
  0.6 3.0 %collective-permute-start = (bf16[1,32,1024]{2,1,0:T(8,128)(2,1)}, bf16[1,32,1024]{2,1,0:T(8,128)(2,1)S(1)}, u32[]{:S(2)}, u32[]{:S(2)}) collective-permute-start(bf16[1,32,1024]{2,1,0:T(8,128)(2,1)} %refs_0_.1), channel_id=1, source_target_pairs={{4,0},{0,4},{5,1},{1,5},{6,2},{2,6},{7,3},{3,7},{12,8},{8,12},{13,... | collective-permute-start | bytes 196616 | tf_op jit(solution)/shard_map/ppermute | solution.py:46
  4.4 1.7 %collective-permute-done.refs_1_ = bf16[1,32,1024]{2,1,0:T(8,128)(2,1)S(1)} collective-permute-done((bf16[1,32,1024]{2,1,0:T(8,128)(2,1)}, bf16[1,32,1024]{2,1,0:T(8,128)(2,1)S(1)}, u32[]{:S(2)}, u32[]{:S(2)}) %collective-permute-start) | collective-permute-done | bytes 65568 | tf_op jit(solution)/shard_map/ppermute | solution.py:46
  9.6 1.6 attend.1
  11.9 2.0 %collective-permute-start.1 = (bf16[64,1152]{1,0:T(8,128)(2,1)S(1)}, bf16[64,1152]{1,0:T(8,128)(2,1)S(1)}, u32[]{:S(2)}, u32[]{:S(2)}) collective-permute-start(bf16[64,1152]{1,0:T(8,128)(2,1)S(1)} %get-tuple-element.36.refs_0_), channel_id=1, source_target_pairs={{4,0},{0,4},{5,1},{1,5},{6,2},{2,6},{7,3},{3,7},{12,8},{8,12},{13,... | collective-permute-start | bytes 442376 | tf_op jit(solution)/shard_map/ppermute | solution.py:46
  13.9 3.1 %collective-permute-done.1.refs_1_ = bf16[64,1152]{1,0:T(8,128)(2,1)S(1)} collective-permute-done((bf16[64,1152]{1,0:T(8,128)(2,1)S(1)}, bf16[64,1152]{1,0:T(8,128)(2,1)S(1)}, u32[]{:S(2)}, u32[]{:S(2)}) %collective-permute-start.1) | collective-permute-done | bytes 147488 | tf_op jit(solution)/shard_map/ppermute | solution.py:46
  17.0 2.2 %copy-done.2 = bf16[1024,2048]{1,0:T(8,128)(2,1)S(1)} copy-done((bf16[1024,2048]{1,0:T(8,128)(2,1)S(1)}, bf16[1024,2048]{1,0:T(8,128)(2,1)}, u32[]{:S(2)}) %copy-start.2) | copy-done | bytes 4194328
  19.2 3.2 %project.1 = (bf16[64,2048]{1,0:T(8,128)(2,1)}, bf16[64,1024]{1,0:T(8,128)(2,1)S(1)}, f32[64,128]{1,0:T(8,128)S(1)}, s32[64,128]{1,0:T(8,128)S(1)}) custom-call(s32[5]{0:T(128)S(1)} %stack.23.scal, bf16[64,1152]{1,0:T(8,128)(2,1)S(1)} %get-tuple-element.36.refs_0_, bf16[64,1152]{1,0:T(8,128)(2,1)S(1)} %collective-permute-done.1.refs_1_, ...), custom_call_target="tpu_custom_call" | custom-call | bytes 7340032 | tf_op jit(solution)/shard_map/project/pallas_call | solution.py:408
  23.1 5.4 %all-to-all-start = ((bf16[4,16,2048]{2,1,0:T(8,128)(2,1)}), bf16[4,16,2048]{2,1,0:T(8,128)(2,1)S(1)}, u32[]{:S(2)}, u32[]{:S(2)}) async-start(bf16[4,16,2048]{2,1,0:T(8,128)(2,1)} %bitcast.7), calls=%async_computation | async-start | bytes 524288 | tf_op jit(solution)/shard_map/all_to_all | solution.py:54
  28.4 6.8 %all-to-all-done = bf16[4,16,2048]{2,1,0:T(8,128)(2,1)S(1)} async-done(((bf16[4,16,2048]{2,1,0:T(8,128)(2,1)}), bf16[4,16,2048]{2,1,0:T(8,128)(2,1)S(1)}, u32[]{:S(2)}, u32[]{:S(2)}) %all-to-all-start) | async-done | bytes 262176 | tf_op jit(solution)/shard_map/all_to_all | solution.py:54
  36.0 11.0 %all_to_all.55 = bf16[4,16,2176]{2,1,0:T(8,128)(2,1)S(1)} all-to-all(bf16[4,16,2176]{2,1,0:T(8,128)(2,1)S(1)} %bitcast.37), channel_id=1, replica_groups=mesh['dp'=4,'seq'=2,'vocab'=4] {'vocab'}, dimensions={0} | all-to-all | bytes 557056 | tf_op jit(solution)/shard_map/all_to_all | solution.py:54
  47.0 8.1 %logits.5 = (s16[64,3072]{1,0:T(8,128)(2,1)S(1)}, f32[64,128]{1,0:T(8,128)S(1)}) custom-call(bf16[64,2176]{1,0:T(8,128)(2,1)S(1)} %bitcast.24, bf16[8032,2048]{1,0:T(8,128)(2,1)} %bitcast.40, bf16[8032,2048]{1,0:T(8,128)(2,1)} %bitcast.41, bf16[8032,2048]{1,0:T(8,128)(2,1)} %bitcast.42, bf16[8032,2048]{1,0:T(8,128)(2,1)} %bitcast.43), custom_call_target="tpu_custom_call" | custom-call | flops 3221225472 | bytes 12582912 | tf_op jit(solution)/shard_map/logits/pallas_call | solution.py:447
  55.1 1.6 collective-permute-start.6
  57.2 8.1 %logits.4 = (s16[64,3072]{1,0:T(8,128)(2,1)S(1)}, f32[64,128]{1,0:T(8,128)S(1)}) custom-call(bf16[64,2176]{1,0:T(8,128)(2,1)S(1)} %bitcast.25, bf16[8032,2048]{1,0:T(8,128)(2,1)} %bitcast.44, bf16[8032,2048]{1,0:T(8,128)(2,1)} %bitcast.45, bf16[8032,2048]{1,0:T(8,128)(2,1)} %bitcast.46, bf16[8032,2048]{1,0:T(8,128)(2,1)} %bitcast.47), custom_call_target="tpu_custom_call" | custom-call | flops 3221225472 | bytes 12582912 | tf_op jit(solution)/shard_map/logits/pallas_call | solution.py:447
  65.3 1.6 collective-permute-start.4
  66.9 5.6 %logits.3 = (s16[64,2048]{1,0:T(8,128)(2,1)S(1)}, f32[64,128]{1,0:T(8,128)S(1)}) custom-call(bf16[64,2176]{1,0:T(8,128)(2,1)S(1)} %bitcast.26, bf16[8032,2048]{1,0:T(8,128)(2,1)} %bitcast.51, bf16[8032,2048]{1,0:T(8,128)(2,1)} %bitcast.49, bf16[8032,2048]{1,0:T(8,128)(2,1)} %bitcast.50, bf16[8032,2048]{1,0:T(8,128)(2,1)} %bitcast.48), custom_call_target="tpu_custom_call" | custom-call | flops 2147483648 | bytes 8388608 | tf_op jit(solution)/shard_map/logits/pallas_call | solution.py:447
  75.1 7.7 %hidden.3 = (f32[128,2048]{1,0:T(8,128)S(1)}, bf16[64,3072]{1,0:T(8,128)(2,1)S(1)}, f32[64,128]{1,0:T(8,128)S(1)}) custom-call(s32[5]{0:T(128)S(1)} %stack.23.scal, s16[64,3072]{1,0:T(8,128)(2,1)S(1)} %get-tuple-element.44.refs_0_, s16[64,3072]{1,0:T(8,128)(2,1)S(1)} %collective-permute-done.6.refs_1_, f32[64,128]{1,0:T(8,128)S(1)} %get-tuple-element.45.refs_2_, ...), custom_call_target="tpu_custom_call" | custom-call | flops 3221225472 | bytes 12582912 | tf_op jit(solution)/shard_map/hidden/pallas_call | solution.py:467
  82.9 7.8 %hidden.4 = (f32[128,2048]{1,0:T(8,128)S(1)}, bf16[64,3072]{1,0:T(8,128)(2,1)S(1)}, f32[64,128]{1,0:T(8,128)S(1)}) custom-call(s32[5]{0:T(128)S(1)} %stack.23.scal, s16[64,3072]{1,0:T(8,128)(2,1)S(1)} %get-tuple-element.42.refs_0_, s16[64,3072]{1,0:T(8,128)(2,1)S(1)} %collective-permute-done.4.refs_1_, f32[64,128]{1,0:T(8,128)S(1)} %get-tuple-element.43.refs_2_, ...), custom_call_target="tpu_custom_call" | custom-call | flops 3221225472 | bytes 12582912 | tf_op jit(solution)/shard_map/hidden/pallas_call | solution.py:467
  90.7 5.4 %hidden.5 = (f32[128,2048]{1,0:T(8,128)S(1)}, bf16[64,2048]{1,0:T(8,128)(2,1)S(1)}, f32[256,128]{1,0:T(8,128)S(1)}) custom-call(s32[5]{0:T(128)S(1)} %stack.23.scal, s16[64,2048]{1,0:T(8,128)(2,1)S(1)} %get-tuple-element.39.refs_0_, s16[64,2048]{1,0:T(8,128)(2,1)S(1)} %collective-permute-done.2.refs_1_, f32[64,128]{1,0:T(8,128)S(1)} %get-tuple-element.40.refs_2_, ...), custom_call_target="tpu_custom_call" | custom-call | flops 2147483648 | bytes 8388608 | tf_op jit(solution)/shard_map/hidden/pallas_call | solution.py:467
  96.1 8.3 %all_to_all.56 = f32[4,64,128]{2,1,0:T(8,128)S(1)} all-to-all(f32[4,64,128]{2,1,0:T(8,128)S(1)} %bitcast.35), channel_id=1, replica_groups=mesh['dp'=4,'seq'=2,'vocab'=4] {'vocab'}, dimensions={0} | all-to-all | bytes 262144 | tf_op jit(solution)/shard_map/all_to_all | solution.py:54
  109.9 3.4 %all-to-all-start.3 = ((bf16[4,16,2048]{2,1,0:T(8,128)(2,1)}), bf16[4,16,2048]{2,1,0:T(8,128)(2,1)S(1)}, u32[]{:S(2)}, u32[]{:S(2)}) async-start(bf16[4,16,2048]{2,1,0:T(8,128)(2,1)} %bitcast.18), calls=%async_computation.3 | async-start | bytes 524288 | tf_op jit(solution)/shard_map/all_to_all | solution.py:54
  113.3 9.2 %collective-permute-done.11.refs_1_ = bf16[64,2176]{1,0:T(8,128)(2,1)S(1)} collective-permute-done((bf16[64,2176]{1,0:T(8,128)(2,1)S(1)}, bf16[64,2176]{1,0:T(8,128)(2,1)S(1)}, u32[]{:S(2)}, u32[]{:S(2)}) %collective-permute-start.11) | collective-permute-done | bytes 278560 | tf_op jit(solution)/shard_map/ppermute | solution.py:59
  124.4 2.3 %collective-permute-done.8.refs_1_.refs_5_ = bf16[64,2048]{1,0:T(8,128)(2,1)S(1)} collective-permute-done((bf16[64,2048]{1,0:T(8,128)(2,1)S(1)}, bf16[64,2048]{1,0:T(8,128)(2,1)S(1)}, u32[]{:S(2)}, u32[]{:S(2)}) %collective-permute-start.8) | collective-permute-done | bytes 262176 | tf_op jit(solution)/shard_map/ppermute | solution.py:59
  127.3 3.7 %collective-permute-done.14.refs_5_ = bf16[64,3072]{1,0:T(8,128)(2,1)} collective-permute-done((bf16[64,3072]{1,0:T(8,128)(2,1)S(1)}, bf16[64,3072]{1,0:T(8,128)(2,1)}, u32[]{:S(2)}, u32[]{:S(2)}) %collective-permute-start.14) | collective-permute-done | bytes 393248 | tf_op jit(solution)/shard_map/ppermute | solution.py:59
  132.5 2.1 %collective-permute-done.20.refs_1_ = f32[16,128]{1,0:T(8,128)S(1)} collective-permute-done((f32[16,128]{1,0:T(8,128)S(1)}, f32[16,128]{1,0:T(8,128)S(1)}, u32[]{:S(2)}, u32[]{:S(2)}) %collective-permute-start.20) | collective-permute-done | bytes 8224 | tf_op jit(solution)/shard_map/ppermute | solution.py:46
  136.5 3.6 %all-to-all-start.4 = ((bf16[4,16,2048]{2,1,0:T(8,128)(2,1)}), bf16[4,16,2048]{2,1,0:T(8,128)(2,1)S(1)}, u32[]{:S(2)}, u32[]{:S(2)}) async-start(bf16[4,16,2048]{2,1,0:T(8,128)(2,1)} %bitcast.20), calls=%async_computation.4 | async-start | bytes 524288 | tf_op jit(solution)/shard_map/all_to_all | solution.py:54
  140.8 7.7 %head_grad.3.refs_8_ = bf16[8032,2048]{1,0:T(8,128)(2,1)} custom-call(bf16[64,2176]{1,0:T(8,128)(2,1)S(1)} %bitcast.29, bf16[64,2176]{1,0:T(8,128)(2,1)S(1)} %collective-permute-done.11.refs_1_, bf16[64,2176]{1,0:T(8,128)(2,1)S(1)} %collective-permute-done.12.refs_2_, bf16[64,2176]{1,0:T(8,128)(2,1)S(1)} %collective-permute-done.13.refs_3_, ...), custom_call_target="tpu_custom_call" | custom-call | flops 3221225472 | bytes 12582912 | tf_op jit(solution)/shard_map/head_grad/pallas_call | solution.py:566
  148.6 7.7 %head_grad.4.refs_8_ = bf16[8032,2048]{1,0:T(8,128)(2,1)} custom-call(bf16[64,2176]{1,0:T(8,128)(2,1)S(1)} %bitcast.30, bf16[64,2176]{1,0:T(8,128)(2,1)S(1)} %collective-permute-done.11.refs_1_, bf16[64,2176]{1,0:T(8,128)(2,1)S(1)} %collective-permute-done.12.refs_2_, ...), custom_call_target="tpu_custom_call", output_to_operand_aliasing={{}: (8, {})} | custom-call | flops 3221225472 | bytes 12582912 | tf_op jit(solution)/shard_map/head_grad/pallas_call | solution.py:566
  156.4 2.2 %copy-done.3 = bf16[1024,2048]{1,0:T(8,128)(2,1)S(1)} copy-done((bf16[1024,2048]{1,0:T(8,128)(2,1)S(1)}, bf16[1024,2048]{1,0:T(8,128)(2,1)}, u32[]{:S(2)}) %copy-start.3) | copy-done | bytes 4194328
  158.5 1.8 %back_project.1.refs_0_ = bf16[64,1024]{1,0:T(8,128)(2,1)S(1)} custom-call(bf16[64,2048]{1,0:T(8,128)(2,1)S(1)} %bitcast.32, bf16[1024,2048]{1,0:T(8,128)(2,1)S(1)} %copy-done.3), custom_call_target="tpu_custom_call" | custom-call | bytes 7340032 | tf_op jit(solution)/shard_map/back_project/pallas_call | solution.py:542
  160.4 1.6 collective-permute-start.21
  162.0 4.7 %head_grad.5 = bf16[8032,2048]{1,0:T(8,128)(2,1)} custom-call(bf16[64,2176]{1,0:T(8,128)(2,1)S(1)} %bitcast.31, bf16[64,2176]{1,0:T(8,128)(2,1)S(1)} %collective-permute-done.11.refs_1_, bf16[64,2176]{1,0:T(8,128)(2,1)S(1)} %collective-permute-done.12.refs_2_, bf16[64,2176]{1,0:T(8,128)(2,1)S(1)} %collective-permute-done.13.refs_3_, ...), custom_call_target="tpu_custom_call", output_to_operand_aliasing={{}: (8, {})} | custom-call | flops 2147483648 | bytes 8388608 | tf_op jit(solution)/shard_map/head_grad/pallas_call | solution.py:566
  166.7 2.6 %attend_back.1 = (f32[1,128,1024]{2,1,0:T(8,128)}, f32[1,128,1024]{2,1,0:T(8,128)}) custom-call(s32[5]{0:T(128)S(1)} %stack.23.scal, bf16[64,1024]{1,0:T(8,128)(2,1)S(1)} %back_project.1.refs_0_, bf16[64,1024]{1,0:T(8,128)(2,1)S(1)} %collective-permute-done.21.refs_1_, bf16[64,1024]{1,0:T(8,128)(2,1)S(1)} %copy-done.9, bf16[1,128,1024]{2,1,0:T(8,128)(2,1)S(1)} %copy-done.5, ...), custom_call_target="tpu_custom_call" | custom-call | bytes 7340032 | tf_op jit(solution)/shard_map/attend_back/pallas_call | solution.py:553
  (73 shorter events, 21.0 us)
Async XLA Ops:
  0.6 27.8 %copy-start = (bf16[1,64,2048]{2,1,0:T(8,128)(2,1)S(1)}, bf16[1,64,2048]{2,1,0:T(8,128)(2,1)}, u32[]{:S(2)}) copy-start(bf16[1,64,2048]{2,1,0:T(8,128)(2,1)} %param.14) | copy-start | bytes 786436
  0.6 5.5 %collective-permute-start = (bf16[1,32,1024]{2,1,0:T(8,128)(2,1)}, bf16[1,32,1024]{2,1,0:T(8,128)(2,1)S(1)}, u32[]{:S(2)}, u32[]{:S(2)}) collective-permute-start(bf16[1,32,1024]{2,1,0:T(8,128)(2,1)} %refs_0_.1), channel_id=1, source_target_pairs={{4,0},{0,4},{5,1},{1,5},{6,2},{2,6},{7,3},{3,7},{12,8},{8,12},{13,... | collective-permute-start | bytes 196616 | tf_op jit(solution)/shard_map/ppermute | solution.py:46
  11.9 5.1 %collective-permute-start.1 = (bf16[64,1152]{1,0:T(8,128)(2,1)S(1)}, bf16[64,1152]{1,0:T(8,128)(2,1)S(1)}, u32[]{:S(2)}, u32[]{:S(2)}) collective-permute-start(bf16[64,1152]{1,0:T(8,128)(2,1)S(1)} %get-tuple-element.36.refs_0_), channel_id=1, source_target_pairs={{4,0},{0,4},{5,1},{1,5},{6,2},{2,6},{7,3},{3,7},{12,8},{8,12},{13,... | collective-permute-start | bytes 442376 | tf_op jit(solution)/shard_map/ppermute | solution.py:46
  23.1 12.1 %all-to-all-start = ((bf16[4,16,2048]{2,1,0:T(8,128)(2,1)}), bf16[4,16,2048]{2,1,0:T(8,128)(2,1)S(1)}, u32[]{:S(2)}, u32[]{:S(2)}) async-start(bf16[4,16,2048]{2,1,0:T(8,128)(2,1)} %bitcast.7), calls=%async_computation | async-start | bytes 524288 | tf_op jit(solution)/shard_map/all_to_all | solution.py:54
  55.1 20.0 %collective-permute-start.6 = (s16[64,3072]{1,0:T(8,128)(2,1)S(1)}, s16[64,3072]{1,0:T(8,128)(2,1)S(1)}, u32[]{:S(2)}, u32[]{:S(2)}) collective-permute-start(s16[64,3072]{1,0:T(8,128)(2,1)S(1)} %get-tuple-element.44.refs_0_), channel_id=1, source_target_pairs={{4,0},{0,4},{5,1},{1,5},{6,2},{2,6},{7,3},{3,7},{12,8},{8,12},{13,... | collective-permute-start | bytes 1179656 | tf_op jit(solution)/shard_map/ppermute | solution.py:46
  56.7 18.0 %collective-permute-start.7 = (f32[64,128]{1,0:T(8,128)S(1)}, f32[64,128]{1,0:T(8,128)S(1)}, u32[]{:S(2)}, u32[]{:S(2)}) collective-permute-start(f32[64,128]{1,0:T(8,128)S(1)} %get-tuple-element.45.refs_2_), channel_id=1, source_target_pairs={{4,0},{0,4},{5,1},{1,5},{6,2},{2,6},{7,3},{3,7},{12,8},{8,12},{13,... | collective-permute-start | bytes 98312 | tf_op jit(solution)/shard_map/ppermute | solution.py:46
  65.3 17.5 %collective-permute-start.4 = (s16[64,3072]{1,0:T(8,128)(2,1)S(1)}, s16[64,3072]{1,0:T(8,128)(2,1)S(1)}, u32[]{:S(2)}, u32[]{:S(2)}) collective-permute-start(s16[64,3072]{1,0:T(8,128)(2,1)S(1)} %get-tuple-element.42.refs_0_), channel_id=1, source_target_pairs={{4,0},{0,4},{5,1},{1,5},{6,2},{2,6},{7,3},{3,7},{12,8},{8,12},{13,... | collective-permute-start | bytes 1179656 | tf_op jit(solution)/shard_map/ppermute | solution.py:46
  72.5 10.3 %collective-permute-start.5 = (f32[64,128]{1,0:T(8,128)S(1)}, f32[64,128]{1,0:T(8,128)S(1)}, u32[]{:S(2)}, u32[]{:S(2)}) collective-permute-start(f32[64,128]{1,0:T(8,128)S(1)} %get-tuple-element.43.refs_2_), channel_id=1, source_target_pairs={{4,0},{0,4},{5,1},{1,5},{6,2},{2,6},{7,3},{3,7},{12,8},{8,12},{13,... | collective-permute-start | bytes 98312 | tf_op jit(solution)/shard_map/ppermute | solution.py:46
  73.1 17.6 %collective-permute-start.2 = (s16[64,2048]{1,0:T(8,128)(2,1)S(1)}, s16[64,2048]{1,0:T(8,128)(2,1)S(1)}, u32[]{:S(2)}, u32[]{:S(2)}) collective-permute-start(s16[64,2048]{1,0:T(8,128)(2,1)S(1)} %get-tuple-element.39.refs_0_), channel_id=1, source_target_pairs={{4,0},{0,4},{5,1},{1,5},{6,2},{2,6},{7,3},{3,7},{12,8},{8,12},{13,... | collective-permute-start | bytes 786440 | tf_op jit(solution)/shard_map/ppermute | solution.py:46
  74.6 16.0 %collective-permute-start.3 = (f32[64,128]{1,0:T(8,128)S(1)}, f32[64,128]{1,0:T(8,128)S(1)}, u32[]{:S(2)}, u32[]{:S(2)}) collective-permute-start(f32[64,128]{1,0:T(8,128)S(1)} %get-tuple-element.40.refs_2_), channel_id=1, source_target_pairs={{4,0},{0,4},{5,1},{1,5},{6,2},{2,6},{7,3},{3,7},{12,8},{8,12},{13,... | collective-permute-start | bytes 98312 | tf_op jit(solution)/shard_map/ppermute | solution.py:46
  90.7 36.5 %copy-start.14 = (f32[2048]{0:T(1024)S(1)}, f32[2048]{0:T(1024)}, u32[]{:S(2)}) copy-start(f32[2048]{0:T(1024)} %param.15) | copy-start | bytes 24580
  106.0 17.9 %collective-permute-start.17 = (bf16[64,3072]{1,0:T(8,128)(2,1)S(1)}, bf16[64,3072]{1,0:T(8,128)(2,1)}, u32[]{:S(2)}, u32[]{:S(2)}) collective-permute-start(bf16[64,3072]{1,0:T(8,128)(2,1)S(1)} %get-tuple-element.58.refs_4_), channel_id=1, source_target_pairs={{0,16},{8,24},{16,0},{24,8},{1,17},{9,25},{17,1},{25,9},{2,18},{10... | collective-permute-start | bytes 1179656 | tf_op jit(solution)/shard_map/ppermute | solution.py:59
  107.6 14.8 %collective-permute-start.11 = (bf16[64,2176]{1,0:T(8,128)(2,1)S(1)}, bf16[64,2176]{1,0:T(8,128)(2,1)S(1)}, u32[]{:S(2)}, u32[]{:S(2)}) collective-permute-start(bf16[64,2176]{1,0:T(8,128)(2,1)S(1)} %bitcast.27), channel_id=1, source_target_pairs={{0,16},{8,24},{16,0},{24,8},{1,17},{9,25},{17,1},{25,9},{2,18},{10... | collective-permute-start | bytes 835592 | tf_op jit(solution)/shard_map/ppermute | solution.py:59
  108.1 15.8 %collective-permute-start.12 = (bf16[64,2176]{1,0:T(8,128)(2,1)S(1)}, bf16[64,2176]{1,0:T(8,128)(2,1)S(1)}, u32[]{:S(2)}, u32[]{:S(2)}) collective-permute-start(bf16[64,2176]{1,0:T(8,128)(2,1)S(1)} %bitcast.28), channel_id=1, source_target_pairs={{0,8},{8,0},{16,24},{24,16},{1,9},{9,1},{17,25},{25,17},{2,10},{10... | collective-permute-start | bytes 835592 | tf_op jit(solution)/shard_map/ppermute | solution.py:59
  108.1 18.6 %collective-permute-start.8 = (bf16[64,2048]{1,0:T(8,128)(2,1)S(1)}, bf16[64,2048]{1,0:T(8,128)(2,1)S(1)}, u32[]{:S(2)}, u32[]{:S(2)}) collective-permute-start(bf16[64,2048]{1,0:T(8,128)(2,1)S(1)} %get-tuple-element.56.refs_0_.refs_4_), channel_id=1, source_target_pairs={{0,16},{8,24},{16,0},{24,8},{1,17},{9,25},{17,1},{25,9},{2,18},{10... | collective-permute-start | bytes 786440 | tf_op jit(solution)/shard_map/ppermute | solution.py:59
  109.6 17.1 %collective-permute-start.9 = (bf16[64,2048]{1,0:T(8,128)(2,1)S(1)}, bf16[64,2048]{1,0:T(8,128)(2,1)S(1)}, u32[]{:S(2)}, u32[]{:S(2)}) collective-permute-start(bf16[64,2048]{1,0:T(8,128)(2,1)S(1)} %get-tuple-element.56.refs_0_.refs_4_), channel_id=1, source_target_pairs={{0,8},{8,0},{16,24},{24,16},{1,9},{9,1},{17,25},{25,17},{2,10},{10... | collective-permute-start | bytes 786440 | tf_op jit(solution)/shard_map/ppermute | solution.py:59
  109.9 17.4 %all-to-all-start.3 = ((bf16[4,16,2048]{2,1,0:T(8,128)(2,1)}), bf16[4,16,2048]{2,1,0:T(8,128)(2,1)S(1)}, u32[]{:S(2)}, u32[]{:S(2)}) async-start(bf16[4,16,2048]{2,1,0:T(8,128)(2,1)} %bitcast.18), calls=%async_computation.3 | async-start | bytes 524288 | tf_op jit(solution)/shard_map/all_to_all | solution.py:54
  122.4 8.6 %collective-permute-start.14 = (bf16[64,3072]{1,0:T(8,128)(2,1)S(1)}, bf16[64,3072]{1,0:T(8,128)(2,1)}, u32[]{:S(2)}, u32[]{:S(2)}) collective-permute-start(bf16[64,3072]{1,0:T(8,128)(2,1)S(1)} %get-tuple-element.57.refs_4_), channel_id=1, source_target_pairs={{0,16},{8,24},{16,0},{24,8},{1,17},{9,25},{17,1},{25,9},{2,18},{10... | collective-permute-start | bytes 1179656 | tf_op jit(solution)/shard_map/ppermute | solution.py:59
  123.9 16.9 %collective-permute-start.18 = (bf16[64,3072]{1,0:T(8,128)(2,1)S(1)}, bf16[64,3072]{1,0:T(8,128)(2,1)}, u32[]{:S(2)}, u32[]{:S(2)}) collective-permute-start(bf16[64,3072]{1,0:T(8,128)(2,1)S(1)} %get-tuple-element.58.refs_4_), channel_id=1, source_target_pairs={{0,8},{8,0},{16,24},{24,16},{1,9},{9,1},{17,25},{25,17},{2,10},{10... | collective-permute-start | bytes 1179656 | tf_op jit(solution)/shard_map/ppermute | solution.py:59
  123.9 16.9 %collective-permute-start.19 = (bf16[64,3072]{1,0:T(8,128)(2,1)}, bf16[64,3072]{1,0:T(8,128)(2,1)}, u32[]{:S(2)}, u32[]{:S(2)}) collective-permute-start(bf16[64,3072]{1,0:T(8,128)(2,1)} %collective-permute-done.17.refs_5_), channel_id=1, source_target_pairs={{0,8},{8,0},{16,24},{24,16},{1,9},{9,1},{17,25},{25,17},{2,10},{10... | collective-permute-start | bytes 1179656 | tf_op jit(solution)/shard_map/ppermute | solution.py:59
  126.7 8.0 %collective-permute-start.10 = (bf16[64,2048]{1,0:T(8,128)(2,1)S(1)}, bf16[64,2048]{1,0:T(8,128)(2,1)S(1)}, u32[]{:S(2)}, u32[]{:S(2)}) collective-permute-start(bf16[64,2048]{1,0:T(8,128)(2,1)S(1)} %collective-permute-done.8.refs_1_.refs_5_), channel_id=1, source_target_pairs={{0,8},{8,0},{16,24},{24,16},{1,9},{9,1},{17,25},{25,17},{2,10},{10... | collective-permute-start | bytes 786440 | tf_op jit(solution)/shard_map/ppermute | solution.py:59
  126.7 14.1 %collective-permute-start.13 = (bf16[64,2176]{1,0:T(8,128)(2,1)S(1)}, bf16[64,2176]{1,0:T(8,128)(2,1)S(1)}, u32[]{:S(2)}, u32[]{:S(2)}) collective-permute-start(bf16[64,2176]{1,0:T(8,128)(2,1)S(1)} %collective-permute-done.11.refs_1_), channel_id=1, source_target_pairs={{0,8},{8,0},{16,24},{24,16},{1,9},{9,1},{17,25},{25,17},{2,10},{10... | collective-permute-start | bytes 835592 | tf_op jit(solution)/shard_map/ppermute | solution.py:59
  131.0 3.7 %collective-permute-start.20 = (f32[16,128]{1,0:T(8,128)S(1)}, f32[16,128]{1,0:T(8,128)S(1)}, u32[]{:S(2)}, u32[]{:S(2)}) collective-permute-start(f32[16,128]{1,0:T(8,128)S(1)} %get-tuple-element.62.refs_0_), channel_id=1, source_target_pairs={{4,0},{0,4},{5,1},{1,5},{6,2},{2,6},{7,3},{3,7},{12,8},{8,12},{13,... | collective-permute-start | bytes 24584 | tf_op jit(solution)/shard_map/ppermute | solution.py:46
  134.7 13.9 %collective-permute-start.15 = (bf16[64,3072]{1,0:T(8,128)(2,1)S(1)}, bf16[64,3072]{1,0:T(8,128)(2,1)}, u32[]{:S(2)}, u32[]{:S(2)}) collective-permute-start(bf16[64,3072]{1,0:T(8,128)(2,1)S(1)} %get-tuple-element.57.refs_4_), channel_id=1, source_target_pairs={{0,8},{8,0},{16,24},{24,16},{1,9},{9,1},{17,25},{25,17},{2,10},{10... | collective-permute-start | bytes 1179656 | tf_op jit(solution)/shard_map/ppermute | solution.py:59
  134.7 13.9 %collective-permute-start.16 = (bf16[64,3072]{1,0:T(8,128)(2,1)}, bf16[64,3072]{1,0:T(8,128)(2,1)}, u32[]{:S(2)}, u32[]{:S(2)}) collective-permute-start(bf16[64,3072]{1,0:T(8,128)(2,1)} %collective-permute-done.14.refs_5_), channel_id=1, source_target_pairs={{0,8},{8,0},{16,24},{24,16},{1,9},{9,1},{17,25},{25,17},{2,10},{10... | collective-permute-start | bytes 1179656 | tf_op jit(solution)/shard_map/ppermute | solution.py:59
  136.5 19.8 %all-to-all-start.4 = ((bf16[4,16,2048]{2,1,0:T(8,128)(2,1)}), bf16[4,16,2048]{2,1,0:T(8,128)(2,1)S(1)}, u32[]{:S(2)}, u32[]{:S(2)}) async-start(bf16[4,16,2048]{2,1,0:T(8,128)(2,1)} %bitcast.20), calls=%async_computation.4 | async-start | bytes 524288 | tf_op jit(solution)/shard_map/all_to_all | solution.py:54
  158.5 10.8 %copy-start.1 = (bf16[1,64,2048]{2,1,0:T(8,128)(2,1)S(1)}, bf16[1,64,2048]{2,1,0:T(8,128)(2,1)}, u32[]{:S(2)}) copy-start(bf16[1,64,2048]{2,1,0:T(8,128)(2,1)} %param.14) | copy-start | bytes 786436
  160.4 6.3 %copy-start.5 = (bf16[1,128,1024]{2,1,0:T(8,128)(2,1)S(1)}, bf16[1,128,1024]{2,1,0:T(8,128)(2,1)}, u32[]{:S(2)}) copy-start(bf16[1,128,1024]{2,1,0:T(8,128)(2,1)} %refs_3_.3) | copy-start | bytes 786436
  160.4 6.3 %copy-start.7 = (bf16[1,128,1024]{2,1,0:T(8,128)(2,1)S(1)}, bf16[1,128,1024]{2,1,0:T(8,128)(2,1)}, u32[]{:S(2)}) copy-start(bf16[1,128,1024]{2,1,0:T(8,128)(2,1)} %refs_4_.3) | copy-start | bytes 786436
  160.4 6.3 %copy-start.9 = (bf16[64,1024]{1,0:T(8,128)(2,1)S(1)}, bf16[64,1024]{1,0:T(8,128)(2,1)}, u32[]{:S(2)}) copy-start(bf16[64,1024]{1,0:T(8,128)(2,1)} %copy-done.8) | copy-start | bytes 393220
  160.4 6.3 %copy-start.11 = (bf16[64,1024]{1,0:T(8,128)(2,1)S(1)}, bf16[64,1024]{1,0:T(8,128)(2,1)}, u32[]{:S(2)}) copy-start(bf16[64,1024]{1,0:T(8,128)(2,1)} %copy-done.10) | copy-start | bytes 393220
  160.4 6.2 %collective-permute-start.21 = (bf16[64,1024]{1,0:T(8,128)(2,1)S(1)}, bf16[64,1024]{1,0:T(8,128)(2,1)S(1)}, u32[]{:S(2)}, u32[]{:S(2)}) collective-permute-start(bf16[64,1024]{1,0:T(8,128)(2,1)S(1)} %back_project.1.refs_0_), channel_id=1, source_target_pairs={{4,0},{0,4},{5,1},{1,5},{6,2},{2,6},{7,3},{3,7},{12,8},{8,12},{13,... | collective-permute-start | bytes 393224 | tf_op jit(solution)/shard_map/ppermute | solution.py:46
  (8 other events, 9.1 us)

commit v4 on v1

v4 whole, which is shorter than its diff:
```python
import functools
import jax
import jax.numpy as jnp
from jax import lax
from jax.experimental import pallas as pl
from jax.experimental.pallas import tpu as pltpu
from jax.sharding import PartitionSpec as P

HDIM = 256
LANES = 128
TILE = 512
PARTS = 4
PART = TILE // PARTS
HEAD_TILE = 2 * TILE
MAX_CHUNKS = 3
GROUPS = 1
LOW = -1e30
CODE_TOP = 32767.0

zloss_weight = 0.0001
norm_epsilon = 1e-06
score_scale = HDIM ** (-0.5)
f32, bf16, i32 = jnp.float32, jnp.bfloat16, jnp.int32

VMEM = pl.BlockSpec(memory_space=pltpu.VMEM)
SMEM = pl.BlockSpec(memory_space=pltpu.SMEM)


def sds(shape, dtype):
    return jax.ShapeDtypeStruct(shape, dtype)


def params(mib=40):
    return pltpu.CompilerParams(vmem_limit_bytes=mib * 1024 * 1024)


def cost(flops, nbytes):
    return pl.CostEstimate(flops=int(flops), bytes_accessed=int(nbytes), transcendentals=0)


def dot(a, b, ca, cb):
    return lax.dot_general(a, b, (((ca,), (cb,)), ((), ())), preferred_element_type=f32)


def from_ahead(x, axis, k):
    n = lax.axis_size(axis)
    return lax.ppermute(x, axis, [((i + k) % n, i) for i in range(n)])


def gather_ring(x, axis):
    return [x] + [from_ahead(x, axis, k) for k in range(1, lax.axis_size(axis))]


def scatter_ring(x, axis, rows):
    n = lax.axis_size(axis)
    return [
        lax.ppermute(x[k * rows : (k + 1) * rows], axis, [(i, (i + k) % n) for i in range(n)])
        for k in range(1, n)
    ]


def swap(x, axis, bit):
    n = lax.axis_size(axis)
    return lax.ppermute(x, axis, [(i, i ^ bit) for i in range(n)])


def gather_swaps(x, axis):
    held = [x]
    bit = lax.axis_size(axis) // 2
    while bit:
        held = held + [swap(h, axis, bit) for h in held]
        bit //= 2
    return held


def tree(terms, op=jnp.add):
    while len(terms) > 1:
        half = len(terms) // 2
        rest = terms[2 * half :]
        terms = [op(terms[i], terms[i + half]) for i in range(half)] + rest
    return terms[0]


def three_parts(x):
    hi = x.astype(bf16).astype(f32)
    mid = (x - hi).astype(bf16).astype(f32)
    return hi, mid, x - hi - mid


def lanes(rows):
    return lax.broadcasted_iota(i32, (rows, LANES), 1)


def attend_kernel(n_seq, scal, *refs):
    q_refs = refs[:n_seq]
    tgt_ref, k_ref, v_ref, o_ref, q_out, q_twice, t_twice = refs[n_seq:]
    tgt_rows = q_refs[0].shape[1]
    rows = tgt_rows * n_seq
    enc, features = k_ref.shape[1:]
    for i, r in enumerate(q_refs):
        for at in (i * tgt_rows, rows + i * tgt_rows):
            q_twice[at : at + tgt_rows, :] = r[0]
    q = q_twice[pl.ds(pl.multiple_of(scal[0], 16), rows), :]
    q_out[...] = q
    valid = lax.broadcasted_iota(i32, (rows, enc), 1) < scal[1]
    lane = lanes(rows)
    corner = (tgt_rows, tgt_rows)
    same = lax.broadcasted_iota(i32, corner, 0) == lax.broadcasted_iota(i32, corner, 1)
    here = lanes(tgt_rows)
    digits = jnp.zeros((tgt_rows, LANES), f32)
    ids = jnp.broadcast_to(tgt_ref[...], corner)
    for at, digit in ((LANES - 2, ids >> 8), (LANES - 1, ids & 255)):
        column = jnp.sum(jnp.where(same, digit.astype(f32), 0.0), axis=1, keepdims=True)
        digits = jnp.where(here == at, column, digits)
    t_twice[...] = jnp.zeros_like(t_twice)
    t_twice[:tgt_rows, :] = digits
    t_twice[rows : rows + tgt_rows, :] = digits
    stat = t_twice[pl.ds(pl.multiple_of(scal[0], 16), rows), :]
    for h in range(features // HDIM):
        at = slice(h * HDIM, (h + 1) * HDIM)
        scores = dot(q[:, at], k_ref[0, :, at], 1, 1) * score_scale
        scores = jnp.where(valid, scores, LOW)
        peak = jnp.max(scores, axis=1, keepdims=True)
        e = jnp.where(valid, jnp.exp(scores - peak), 0.0)
        total = jnp.sum(e, axis=1, keepdims=True)
        some = total > 0.0
        safe = jnp.where(some, total, 1.0)
        o = dot(e.astype(bf16), v_ref[0, :, at], 1, 0) / safe
        o_ref[:, at] = o.astype(bf16)
        lse = jnp.where(some, peak + jnp.log(safe), LOW)
        for i, part in enumerate(three_parts(lse)):
            stat = jnp.where(lane == 3 * h + i, part, stat)
    o_ref[:, features:] = stat.astype(bf16)


def project_kernel(n_seq, own_rows, ptile, scal, *refs):
    o_refs = refs[:n_seq]
    p_ref, mixed_ref, own_ref, att_ref, lse_ref, tgt_ref, p_buf, sems = refs[n_seq:]
    rows, features = att_ref.shape
    columns = [pl.ds(at, ptile) for at in range(0, p_buf.shape[1], ptile)]
    copies = [
        pltpu.make_async_copy(p_ref.at[:, c], p_buf.at[:, c], sems.at[i])
        for i, c in enumerate(columns)
    ]
    for c in copies:
        c.start()
    stats = [r[:, features:].astype(f32) for r in o_refs]
    lane = lanes(rows)
    lse_all = jnp.zeros((rows, LANES), f32)
    for h in range(features // HDIM):
        at = slice(h * HDIM, (h + 1) * HDIM)
        lses = [
            s[:, 3 * h : 3 * h + 1] + s[:, 3 * h + 1 : 3 * h + 2] + s[:, 3 * h + 2 : 3 * h + 3]
            for s in stats
        ]
        top = tree(lses, jnp.maximum)
        lse = top + jnp.log(tree([jnp.exp(x - top) for x in lses]))
        o = tree([jnp.exp(x - lse) * r[:, at].astype(f32) for x, r in zip(lses, o_refs)])
        att_ref[:, at] = o.astype(bf16)
        lse_all = jnp.where(lane == h, lse, lse_all)
    lse_ref[...] = lse_all
    ids = tree([s[:, LANES - 2 : LANES - 1] * 256.0 + s[:, LANES - 1 :] for s in stats])
    tgt_ref[...] = jnp.broadcast_to(ids.astype(i32), (rows, LANES)) - scal[2]
    for c, copy in zip(columns, copies):
        copy.wait()
        part = dot(att_ref[...], p_buf[:, c], 1, 0)
        mixed_ref[:, c] = part.astype(bf16)
        own_ref[:, c] = part[:own_rows]


def norm_kernel(n_got, *refs):
    own_ref, got_refs = refs[0], refs[1 : 1 + n_got]
    residual_ref, gain_ref, mixed_ref, ng_ref = refs[1 + n_got :]
    rows, width = mixed_ref.shape
    mixed = own_ref[...] + residual_ref[...].astype(f32)
    for r in got_refs:
        mixed = mixed + r[...].astype(f32)
    mixed_ref[...] = mixed
    ng_ref[:, :width] = (mixed * gain_ref[...]).astype(bf16)
    square = jnp.sum(mixed * mixed, axis=1, keepdims=True)
    lane = lanes(rows)
    stat = jnp.zeros((rows, LANES), f32)
    for i, part in enumerate(three_parts(square)):
        stat = jnp.where(lane == i, part, stat)
    ng_ref[:, width:] = stat.astype(bf16)


def start_weights(first, cols, w_ref, edge_ref, buf, sems):
    copies = []
    for i in range(buf.shape[0] // PART):
        at = first + i * PART
        n = PART if at + PART <= cols else cols - at
        if n == PART or (n > 0 and cols % 16 == 0):
            here = buf.at[i * PART : i * PART + n]
            copies.append(pltpu.make_async_copy(w_ref.at[at : at + n], here, sems.at[i]))
    for c in copies:
        c.start()
    for i in range(buf.shape[0] // PART):
        n = min(max(cols - first - i * PART, 0), PART)
        if n == PART:
            continue
        if i < len(copies):
            buf[i * PART + n : (i + 1) * PART, :] = jnp.zeros((PART - n, buf.shape[1]), bf16)
        elif n:
            rows = lax.broadcasted_iota(i32, (PART, 1), 0)
            edge = edge_ref[...]
            buf[i * PART : (i + 1) * PART, :] = jnp.where(rows < n, edge, jnp.zeros_like(edge))
        else:
            buf[i * PART : (i + 1) * PART, :] = jnp.zeros((PART, buf.shape[1]), bf16)
    return copies


def wait_tile(copies, t):
    for c in copies[t * PARTS : (t + 1) * PARTS]:
        c.wait()


def logits_kernel(first, cols, n_vocab, *refs):
    ng_refs, (w_ref, edge_ref) = refs[:n_vocab], refs[n_vocab : n_vocab + 2]
    outs = refs[n_vocab + 2 :]
    code_ref, stat_ref = outs[:2]
    z, buf, sems = outs[-3:]
    width = buf.shape[1]
    copies = start_weights(first, cols, w_ref, edge_ref, buf, sems)
    ng = jnp.concatenate([r[...] for r in ng_refs], axis=0)
    if len(outs) > 5:
        outs[2][...] = ng[:, :width]
    for t in range(z.shape[1] // TILE):
        wait_tile(copies, t)
        at = slice(t * TILE, (t + 1) * TILE)
        z[:, at] = dot(buf[at, :], ng[:, :width], 1, 1).T
    val = z[...]
    peak = jnp.maximum(jnp.max(jnp.abs(val), axis=1, keepdims=True), 1e-30)
    code_ref[...] = jnp.round(val * (CODE_TOP / peak)).astype(i32).astype(jnp.int16)
    s = ng[:, width:].astype(f32)
    square = s[:, 0:1] + s[:, 1:2] + s[:, 2:3]
    lane = lanes(z.shape[0])
    stat_ref[...] = jnp.where(lane == 0, peak / CODE_TOP, jnp.where(lane == 1, square, 0.0))


def exp_rows(chunk, first, cols, n_seq, features, refs, e_ref, st_ref, lhs):
    code_refs, sc_refs, tgt_ref = refs[:n_seq], refs[n_seq : 2 * n_seq], refs[2 * n_seq]
    rows, size = e_ref.shape
    z = tree([c[...].astype(i32).astype(f32) * s[:, 0:1] for c, s in zip(code_refs, sc_refs)])
    square = tree([s[:, 1:2] for s in sc_refs])
    inv = lax.rsqrt(square / features + norm_epsilon)
    z = z * inv
    at = first + lax.broadcasted_iota(i32, (rows, size), 1)
    hit = at == tgt_ref[:, 0:1]
    if first + size > cols:
        z = jnp.where(at < cols, z, LOW)
        hit = hit & (at < cols)
    here = jnp.sum(jnp.where(hit, z, 0.0), axis=1, keepdims=True)
    peak = jnp.max(z, axis=1, keepdims=True)
    if chunk:
        old = refs[2 * n_seq + 1][...]
        peak = jnp.maximum(peak, old[:, 0:1])
        fade = jnp.exp(old[:, 0:1] - peak)
    else:
        old = jnp.zeros((rows, LANES), f32)
        fade = jnp.zeros((rows, 1), f32)
    e = jnp.exp(z - peak)
    total = jnp.sum(e, axis=1, keepdims=True) + old[:, 1:2] * fade
    eh = e.astype(bf16)
    e_ref[...] = eh
    lhs[:rows, :] = eh
    lhs[rows:, :] = hit.astype(f32).astype(bf16)
    lane = lanes(rows)
    st = jnp.where(lane == 0, peak, old)
    st = jnp.where(lane == 1, total, st)
    st = jnp.where(lane == 2, here + old[:, 2:3], st)
    st = jnp.where(lane == 3, inv, st)
    st_ref[...] = jnp.where(lane == 8 + chunk, peak, st)
    return fade


def hidden_sum(chunk, copies, buf, lhs, acc_prev, fade, acc_ref):
    rows = acc_ref.shape[0] // 2
    if chunk:
        acc_ref[:rows, :] = acc_prev[:rows, :] * fade
        acc_ref[rows:, :] = acc_prev[rows:, :]
    for t in range(buf.shape[0] // TILE):
        wait_tile(copies, t)
        at = slice(t * TILE, (t + 1) * TILE)
        part = dot(lhs[:, at], buf[at, :], 1, 0)
        if chunk or t:
            acc_ref[...] += part
        else:
            acc_ref[...] = part


def hidden_kernel(chunk, first, cols, n_seq, features, *refs):
    n = 2 * n_seq + 1 + (1 if chunk else 0)
    ins, refs = refs[:n], refs[n:]
    acc_prev = None
    if chunk:
        acc_prev, refs = refs[0], refs[1:]
    w_ref, edge_ref, acc_ref, e_ref, st_ref, lhs, buf, sems = refs
    copies = start_weights(first, cols, w_ref, edge_ref, buf, sems)
    fade = exp_rows(chunk, first, cols, n_seq, features, ins, e_ref, st_ref, lhs)
    hidden_sum(chunk, copies, buf, lhs, acc_prev, fade, acc_ref)


def last_exp_kernel(chunk, first, cols, n_seq, features, *refs):
    ins, (e_ref, st_ref, lhs_ref) = refs[:-3], refs[-3:]
    exp_rows(chunk, first, cols, n_seq, features, ins, e_ref, st_ref, lhs_ref)


def last_hidden_kernel(
    chunk, first, cols, st_prev, st_ref, lhs_ref, acc_prev, w_ref, edge_ref, acc_ref, buf, sems
):
    copies = start_weights(first, cols, w_ref, edge_ref, buf, sems)
    fade = jnp.exp(st_prev[:, 0:1] - st_ref[:, 0:1])
    hidden_sum(chunk, copies, buf, lhs_ref, acc_prev, fade, acc_ref)


def total_kernel(n_vocab, own_rows, *refs):
    st_refs = refs[:n_vocab]
    acc_ref, part_ref, own_ref, coef_ref = refs[n_vocab:]
    rows = coef_ref.shape[0]
    mine = st_refs[0][...]
    stats = [mine]
    for k in range(1, n_vocab):
        s = st_refs[k][...]
        cut = rows - k * own_rows
        stats.append(jnp.concatenate([s[cut:], s[:cut]], axis=0))
    top = tree([s[:, 0:1] for s in stats], jnp.maximum)
    total = tree([s[:, 1:2] * jnp.exp(s[:, 0:1] - top) for s in stats])
    hit_logit = tree([s[:, 2:3] for s in stats])
    log_total = top + jnp.log(total)
    loss = log_total - hit_logit + zloss_weight * log_total * log_total
    lift = 1.0 + 2.0 * zloss_weight * log_total
    inv = mine[:, 3:4]
    lane = lanes(rows)
    coef = jnp.exp(jnp.minimum(mine - log_total, 30.0)) * lift * inv
    coef = jnp.where(lane >= 8, coef, inv)
    coef_ref[...] = jnp.where(lane == 1, loss, coef)
    scale = jnp.exp(mine[:, 0:1] - log_total) * lift
    part = acc_ref[:rows, :] * scale - acc_ref[rows:, :]
    part_ref[...] = part.astype(bf16)
    own_ref[...] = part[:own_rows]


def grad_kernel(firsts, n_out, coef_ref, tgt_ref, *refs):
    n = len(firsts)
    outs = refs[n : n + n_out]
    inv = coef_ref[:, 0:1]
    for c, first in enumerate(firsts):
        e_ref = refs[c]
        for off in range(0, e_ref.shape[1], TILE):
            e = e_ref[:, off : off + TILE]
            at = first + off + lax.broadcasted_iota(i32, e.shape, 1)
            hit = at == tgt_ref[:, 0:1]
            g = e.astype(f32) * coef_ref[:, 8 + c : 9 + c] - jnp.where(hit, inv, 0.0)
            group, place = divmod(first + off, outs[0].shape[1])
            outs[group][:, place : place + TILE] = g.astype(bf16)
    last = refs[-1]
    rows, size = last.shape
    lane = lanes(rows)
    stat = last[:, size - LANES :].astype(f32)
    for i, part in enumerate(three_parts(coef_ref[:, 1:2])):
        stat = jnp.where(lane == LANES - 3 + i, part, stat)
    last[:, size - LANES :] = stat.astype(bf16)


def loss_kernel(rows_all, *refs):
    sums = []
    for r in refs[:-1]:
        s = r[...].astype(f32)
        sums.append(jnp.sum(s[:, -3:-2] + s[:, -2:-1] + s[:, -1:], axis=0, keepdims=True))
    refs[-1][...] = jnp.broadcast_to(tree(sums) / rows_all, refs[-1].shape)


def head_kernel(n_dp, *refs):
    ng_refs, g_refs = refs[:n_dp], refs[n_dp : 2 * n_dp]
    out_ref, ng, turned = refs[-3:]
    rows, width = ng_refs[0].shape[0], out_ref.shape[1]

    @pl.when(pl.program_id(0) == 0)
    def _():
        for i, r in enumerate(ng_refs):
            ng[i * rows : (i + 1) * rows, :] = r[:, :width]

    turned[...] = jnp.concatenate([r[...] for r in g_refs], axis=0).T
    for at in range(0, width, 256):
        out_ref[:, at : at + 256] = dot(turned[...], ng[:, at : at + 256], 1, 0).astype(bf16)


def gate_kernel(n_got, *refs):
    own_ref, got_refs = refs[0], refs[1 : 1 + n_got]
    mixed_ref, gain_ref, gated_ref, dot_ref = refs[1 + n_got :]
    total = own_ref[...]
    for r in got_refs:
        total = total + r[...].astype(f32)
    gated = total * gain_ref[...]
    gated_ref[...] = gated
    inner = jnp.sum(gated * mixed_ref[...], axis=1, keepdims=True)
    dot_ref[...] = jnp.broadcast_to(inner, dot_ref.shape)


def mixed_grad_kernel(n_seq, features, gated_ref, mixed_ref, coef_ref, *refs):
    dot_refs, out_ref = refs[:n_seq], refs[n_seq]
    inner = tree([r[:, 0:1] for r in dot_refs])
    inv = coef_ref[: out_ref.shape[0], 0:1]
    out = gated_ref[...] * inv - mixed_ref[...] * (inv * inv * inv * inner / features)
    out_ref[...] = out.astype(bf16)


def back_project_kernel(*refs):
    mg_refs, p_ref, out_ref = refs[:-2], refs[-2], refs[-1]
    mg = jnp.concatenate([r[...] for r in mg_refs], axis=0)
    out_ref[...] = dot(mg, p_ref[...], 1, 1).astype(bf16)


def attend_back_kernel(n_seq, scal, *refs):
    a_refs = refs[:n_seq]
    q_ref, k_ref, v_ref, att_ref, lse_ref, kg_ref, vg_ref = refs[n_seq:]
    enc, features = k_ref.shape[1:]
    rows = q_ref.shape[0]
    valid = lax.broadcasted_iota(i32, (rows, enc), 1) < scal[1]
    for h in range(features // HDIM):
        at = slice(h * HDIM, (h + 1) * HDIM)
        grad = tree([r[:, at].astype(f32) for r in a_refs]).astype(bf16)
        q = q_ref[:, at]
        scores = dot(q, k_ref[0, :, at], 1, 1) * score_scale
        w = jnp.where(valid, jnp.exp(jnp.minimum(scores - lse_ref[:, h : h + 1], 0.5)), 0.0)
        prob_grad = dot(grad, v_ref[0, :, at], 1, 1)
        inner = jnp.sum(grad.astype(f32) * att_ref[:, at].astype(f32), axis=1, keepdims=True)
        sg = (w * (prob_grad - inner) * score_scale).astype(bf16)
        vg_ref[0, :, at] = dot(w.astype(bf16), grad, 0, 0)
        kg_ref[0, :, at] = dot(sg, q, 0, 0)


def body(
    queries, enc_keys, enc_values, enc_lengths, out_proj, residual, norm_gain, head_weight, targets
):
    n_seq, n_vocab, n_dp = lax.axis_size("seq"), lax.axis_size("vocab"), lax.axis_size("dp")
    seq, voc = lax.axis_index("seq"), lax.axis_index("vocab")
    tgt_rows, features = queries.shape[1:]
    enc = enc_keys.shape[1]
    rows = tgt_rows * n_seq
    own_rows = rows // n_vocab
    width, cols = head_weight.shape
    full_width = width * n_seq
    tiles = -(-cols // TILE)
    per = 2 * -(-tiles // (2 * MAX_CHUNKS))
    assert tiles % 2 == 0
    chunks = [(t, min(per, tiles - t)) for t in range(0, tiles, per)]
    firsts = [t * TILE for t, _ in chunks]
    gain = norm_gain.reshape(1, width)
    weight = head_weight.T

    start = lax.rem(voc * own_rows - seq * tgt_rows + rows, rows).astype(i32)
    scal = jnp.stack([start, enc_lengths[0] - seq * enc, voc * cols]).astype(i32)

    q_parts = gather_ring(queries, "seq")
    res_own = lax.dynamic_slice(residual[0], (voc * own_rows, 0), (own_rows, width))
    o_part, q_all = pl.pallas_call(
        functools.partial(attend_kernel, n_seq),
        out_shape=[sds((rows, features + LANES), bf16), sds((rows, features), bf16)],
        in_specs=[SMEM] + [VMEM] * (n_seq + 3),
        out_specs=[VMEM, VMEM],
        scratch_shapes=[
            pltpu.VMEM((2 * rows, features), bf16),
            pltpu.VMEM((2 * rows, LANES), f32),
        ],
        compiler_params=params(),
        cost_estimate=cost(0, 7 * 1024 * 1024),
        name="attend",
    )(scal, *q_parts, targets, enc_keys, enc_values)

    o_all = gather_ring(o_part, "seq")
    ptile = min(TILE, width)
    whole = lambda shape: pl.BlockSpec(shape, lambda j: (0, 0))
    anywhere = pl.BlockSpec(memory_space=pl.ANY)
    mixed_part, mixed_own, att, lse, tgt = pl.pallas_call(
        functools.partial(project_kernel, n_seq, own_rows, ptile),
        out_shape=[
            sds((rows, width), bf16),
            sds((own_rows, width), f32),
            sds((rows, features), bf16),
            sds((rows, LANES), f32),
            sds((rows, LANES), i32),
        ],
        in_specs=[SMEM] + [VMEM] * n_seq + [anywhere],
        out_specs=[VMEM] * 5,
        scratch_shapes=[
            pltpu.VMEM((features, width), bf16),
            pltpu.SemaphoreType.DMA((width // ptile,)),
        ],
        compiler_params=params(),
        cost_estimate=cost(0, 7 * 1024 * 1024),
        name="project",
    )(scal, *o_all, out_proj)

    got = scatter_ring(mixed_part, "vocab", own_rows)
    mixed, ng_own = pl.pallas_call(
        functools.partial(norm_kernel, len(got)),
        out_shape=[sds((own_rows, width), f32), sds((own_rows, width + LANES), bf16)],
        in_specs=[VMEM] * (3 + len(got)),
        out_specs=[VMEM, VMEM],
        compiler_params=params(),
        cost_estimate=cost(0, 7 * 1024 * 1024),
        name="norm",
    )(mixed_own, *got, res_own, gain)
    ng_parts = gather_ring(ng_own, "vocab")

    last_part = pl.BlockSpec((PART, width), lambda j: (-(-cols // PART) - 1, 0))

    def in_vmem(shapes, odd):
        if not odd:
            return [VMEM] * len(shapes)
        return [pl.BlockSpec(x.shape, lambda j: (0, 0)) for x in shapes]

    weights = [weight, weight]
    codes, stats = [], []
    for c, (tile0, n) in enumerate(chunks):
        size = n * TILE
        odd = tile0 * TILE + size > cols and cols % 16 != 0
        edge = last_part if odd else anywhere
        stacked = [] if c else [sds((rows, width), bf16)]
        shapes = [sds((rows, size), jnp.int16), sds((rows, LANES), f32)] + stacked
        outs = pl.pallas_call(
            functools.partial(logits_kernel, tile0 * TILE, cols, n_vocab),
            grid=(1,) if odd else (),
            out_shape=shapes,
            in_specs=in_vmem(ng_parts, odd) + [anywhere, edge],
            out_specs=in_vmem(shapes, odd),
            scratch_shapes=[
                pltpu.VMEM((rows, size), f32),
                pltpu.VMEM((size, width), bf16),
                pltpu.SemaphoreType.DMA((size // PART,)),
            ],
            compiler_params=params(),
            cost_estimate=cost(2 * 256 * width * size, 2 * width * size),
            name="logits",
        )(*ng_parts, *weights)
        codes.append(gather_ring(outs[0], "seq"))
        stats.append(gather_ring(outs[1], "seq"))
        if stacked:
            ng_dp = gather_swaps(outs[2], "dp")

    if len(chunks) > 1:
        codes[1], ng_dp = lax.optimization_barrier((codes[1], ng_dp))
    acc = st = None
    exps = []
    for c, (tile0, n) in enumerate(chunks):
        size = n * TILE
        first = tile0 * TILE
        odd = first + size > cols and cols % 16 != 0
        edge = last_part if odd else anywhere
        estimate = cost(2 * 256 * width * size, 2 * width * size)
        acc_shape, e_shape = sds((2 * rows, width), f32), sds((rows, size), bf16)
        st_shape = sds((rows, LANES), f32)
        buffers = [
            pltpu.VMEM((size, width), bf16),
            pltpu.SemaphoreType.DMA((size // PART,)),
        ]
        prev = [st] if c else []
        ins = [*codes[c], *stats[c], tgt, *prev]
        if c == 0 or c < len(chunks) - 1:
            acc, e, st = pl.pallas_call(
                functools.partial(hidden_kernel, c, first, cols, n_seq, full_width),
                grid=(1,) if odd else (),
                out_shape=[acc_shape, e_shape, st_shape],
                in_specs=in_vmem(ins + ([acc] if c else []), odd) + [anywhere, edge],
                out_specs=in_vmem([acc_shape, e_shape, st_shape], odd),
                scratch_shapes=[pltpu.VMEM((2 * rows, size), bf16)] + buffers,
                compiler_params=params(),
                cost_estimate=estimate,
                name="hidden",
            )(*ins, *([acc] if c else []), *weights)
            st_all = gather_ring(st, "vocab") if c == len(chunks) - 1 else None
        else:
            before = st
            e, st, left = pl.pallas_call(
                functools.partial(last_exp_kernel, c, first, cols, n_seq, full_width),
                out_shape=[e_shape, st_shape, sds((2 * rows, size), bf16)],
                in_specs=[VMEM] * len(ins),
                out_specs=[VMEM] * 3,
                compiler_params=params(),
                cost_estimate=cost(0, 4 * 1024 * 1024),
                name="last_exp",
            )(*ins)
            st_all = gather_ring(st, "vocab")
            acc = pl.pallas_call(
                functools.partial(last_hidden_kernel, c, first, cols),
                grid=(1,) if odd else (),
                out_shape=acc_shape,
                in_specs=in_vmem([before, st, left, acc], odd) + [anywhere, edge],
                out_specs=in_vmem([acc_shape], odd)[0],
                scratch_shapes=buffers,
                compiler_params=params(),
                cost_estimate=estimate,
                name="last_hidden",
            )(before, st, left, acc, *weights)
        exps.append(e)

    hidden_part, hidden_own, coef = pl.pallas_call(
        functools.partial(total_kernel, n_vocab, own_rows),
        out_shape=[
            sds((rows, width), bf16),
            sds((own_rows, width), f32),
            sds((rows, LANES), f32),
        ],
        in_specs=[VMEM] * (n_vocab + 1),
        out_specs=[VMEM] * 3,
        compiler_params=params(),
        cost_estimate=cost(0, 7 * 1024 * 1024),
        name="total",
    )(*st_all, acc)
    got = scatter_ring(hidden_part, "vocab", own_rows)
    got, coef_later = lax.optimization_barrier((got, coef))

    group = tiles * TILE // GROUPS
    assert cols + 3 <= tiles * TILE and group % HEAD_TILE == 0
    grads = pl.pallas_call(
        functools.partial(grad_kernel, firsts, GROUPS),
        out_shape=[sds((rows, group), bf16)] * GROUPS,
        in_specs=[VMEM] * (2 + len(exps)),
        out_specs=[VMEM] * GROUPS,
        compiler_params=params(),
        cost_estimate=cost(0, 7 * 1024 * 1024),
        name="logit_grad",
    )(coef_later, tgt, *exps)
    bit = n_dp // 2
    across = [swap(g, "dp", bit) for g in grads] if bit else []
    gated, inner = pl.pallas_call(
        functools.partial(gate_kernel, len(got)),
        out_shape=[sds((own_rows, width), f32), sds((own_rows, LANES), f32)],
        in_specs=[VMEM] * (3 + len(got)),
        out_specs=[VMEM, VMEM],
        compiler_params=params(),
        cost_estimate=cost(0, 7 * 1024 * 1024),
        name="gate",
    )(hidden_own, *got, mixed, gain)
    inner_all = gather_ring(inner, "seq")
    mixed_grad = pl.pallas_call(
        functools.partial(mixed_grad_kernel, n_seq, full_width),
        out_shape=sds((own_rows, width), bf16),
        in_specs=[VMEM] * (3 + n_seq),
        out_specs=VMEM,
        compiler_params=params(),
        cost_estimate=cost(0, 7 * 1024 * 1024),
        name="mixed_grad",
    )(gated, mixed, coef, *inner_all)
    mg_parts = gather_ring(mixed_grad, "vocab")

    ftile = min(256, features)
    back_part = pl.pallas_call(
        back_project_kernel,
        grid=(features // ftile,),
        out_shape=sds((rows, features), bf16),
        in_specs=[whole((own_rows, width))] * n_vocab
        + [pl.BlockSpec((ftile, width), lambda j: (j, 0))],
        out_specs=pl.BlockSpec((rows, ftile), lambda j: (0, j)),
        compiler_params=params(),
        cost_estimate=cost(0, 7 * 1024 * 1024),
        name="back_project",
    )(*mg_parts, out_proj)
    back_all = gather_ring(back_part, "seq")
    back_all, across = lax.optimization_barrier((back_all, across))
    grads_dp = []
    for i, g in enumerate(grads):
        held, bit = ([g, across[i]] if across else [g]), n_dp // 4
        while bit:
            held = held + [swap(h, "dp", bit) for h in held]
            bit //= 2
        grads_dp.append(held)
    key_grad, value_grad = pl.pallas_call(
        functools.partial(attend_back_kernel, n_seq),
        out_shape=[sds(enc_keys.shape, f32), sds(enc_values.shape, f32)],
        in_specs=[SMEM] + [VMEM] * (n_seq + 5),
        out_specs=[VMEM, VMEM],
        compiler_params=params(),
        cost_estimate=cost(0, 7 * 1024 * 1024),
        name="attend_back",
    )(scal, *back_all, q_all, enc_keys, enc_values, att, lse)

    loss = pl.pallas_call(
        functools.partial(loss_kernel, n_dp * rows),
        grid=(1,),
        out_shape=sds((8, LANES), f32),
        in_specs=[pl.BlockSpec((rows, LANES), lambda j: (0, group // LANES - 1))] * n_dp,
        out_specs=whole((8, LANES)),
        compiler_params=params(),
        cost_estimate=cost(0, 7 * 1024 * 1024),
        name="loss",
    )(*grads_dp[-1])
    mean_loss = loss[0, 0]

    head = None
    for c in range(GROUPS):
        prev = [head] if c else []
        steps = group // HEAD_TILE
        head = pl.pallas_call(
            functools.partial(head_kernel, n_dp),
            grid=(steps,),
            out_shape=sds((cols, width), bf16),
            in_specs=[whole((rows, width))] * n_dp
            + [pl.BlockSpec((rows, HEAD_TILE), lambda j: (0, j))] * n_dp
            + [anywhere] * len(prev),
            out_specs=pl.BlockSpec((HEAD_TILE, width), lambda j, t=c * steps: (t + j, 0)),
            scratch_shapes=[
                pltpu.VMEM((n_dp * rows, width), bf16),
                pltpu.VMEM((HEAD_TILE, n_dp * rows), bf16),
            ],
            input_output_aliases={2 * n_dp: 0} if c else {},
            compiler_params=params(),
            cost_estimate=cost(2 * n_dp * rows * width * group, 2 * width * group),
            name="head_grad",
        )(*ng_dp, *grads_dp[c], *prev)
    return (mean_loss, head.T, key_grad, value_grad)


def solution(mesh):
    placed = (
        P("dp", "seq", "vocab"),
        P("dp", "seq", "vocab"),
        P("dp", "seq", "vocab"),
        P("dp"),
        P("vocab", "seq"),
        P("dp", None, "seq"),
        P("seq"),
        P("seq", "vocab"),
        P("dp", "seq"),
    )
    return jax.shard_map(
        body,
        mesh=mesh,
        in_specs=placed,
        out_specs=(P(), P("seq", "vocab"), P("dp", "seq", "vocab"), P("dp", "seq", "vocab")),
        check_vma=False,
    )
```

time: 244 us -> 145 us (0.59)
  local copies, waits for them, and re-layouts: 88.5 us -> 6.87 us
  Pallas kernels: 75.9 us -> 65.8 us
  starting transfers between devices: 46.2 us -> 37.3 us
  waiting for transfers between devices: 25.5 us -> 32.7 us
    unnamed x22 -> x24, local copies, waits for them, and re-layouts: 86.3 us -> 6.31 us
    ppermute x22 -> x19, waiting for transfers between devices: 10.5 us -> 21.5 us  [from_ahead(): return lax.ppermute(x, axis, [((i + k) % n, i) for i in range(n)])]
    pallas_call x14 -> x11, Pallas kernels: 68.6 us -> 59.1 us  [the longest x3 25.8 us: body(): pl.pallas_call(functools.partial(logits_kernel, tile0 * TILE, cols, n_voc...]
    ppermute x17 -> x6, starting transfers between devices: 9.95 us -> 2.17 us  [swap(): return lax.ppermute(x, axis, [(i, i ^ bit) for i in range(n)])]
    ppermute x17 -> x6, waiting for transfers between devices: 8.09 us -> 3.9 us  [swap(): return lax.ppermute(x, axis, [(i, i ^ bit) for i in range(n)])]
    ppermute x22 -> x19, starting transfers between devices: 26.4 us -> 24.2 us  [from_ahead(): return lax.ppermute(x, axis, [((i + k) % n, i) for i in range(n)])]
  transfers between devices with their start and end apart: 45 -> 31, of which waited for: 16 -> 16; matrix products, arithmetic and copies ran while one was open for 17% -> 0% of each run, Pallas kernels for 22% -> 25%
where the time goes in v4:
time: 145 us; the launch traced here: 144 us
  Pallas kernels  65.8 us (45%)
  starting transfers between devices  37.3 us (26%)
  waiting for transfers between devices  32.7 us (23%)
  local copies, waits for them, and re-layouts  6.87 us (5%)
  between operations  1.52 us (1%)
    pallas_call x3, Pallas kernels, body(): pl.pallas_call(functools.partial(logits_kernel, tile0 * TILE, cols, n_voc...  25.8 us
    ppermute x19, starting transfers between devices, from_ahead(): return lax.ppermute(x, axis, [((i + k) % n, i) for i in range(n)])  24.2 us
    ppermute x19, waiting for transfers between devices, from_ahead(): return lax.ppermute(x, axis, [((i + k) % n, i) for i in range(n)])  21.5 us
    pallas_call x1, Pallas kernels, body(): pl.pallas_call(functools.partial(head_kernel, n_dp), grid=(steps,), out_s...  14.6 us
    pallas_call x2, Pallas kernels, body(): pl.pallas_call(functools.partial(hidden_kernel, c, first, cols, n_seq, fu...  10.9 us
    ppermute x6, starting transfers between devices, scatter_ring(): lax.ppermute(x[k * rows:(k + 1) * rows], axis, [(i, (i + k) % n) for i in...  10.8 us
    ppermute x6, waiting for transfers between devices, scatter_ring(): lax.ppermute(x[k * rows:(k + 1) * rows], axis, [(i, (i + k) % n) for i in...  7.23 us
    unnamed x24, local copies, waits for them, and re-layouts  6.31 us
  transfers between devices with their start and end apart: 31, of which 16 were waited for; matrix products, arithmetic and copies ran while one was open for 0% of the time, Pallas kernels for 25%

profile of v4, /device:TPU:0, one launch (start us, length us, event | category | flops | bytes accessed | tf_op | source)
XLA Modules:
  0.0 144.2 jit_solution(7921422773898589669)
XLA Ops:
  0.6 3.0 %collective-permute-start = (bf16[1,32,1024]{2,1,0:T(8,128)(2,1)}, bf16[1,32,1024]{2,1,0:T(8,128)(2,1)S(1)}, u32[]{:S(2)}, u32[]{:S(2)}) collective-permute-start(bf16[1,32,1024]{2,1,0:T(8,128)(2,1)} %refs_0_.1), channel_id=1, source_target_pairs={{4,0},{0,4},{5,1},{1,5},{6,2},{2,6},{7,3},{3,7},{12,8},{8,12},{13,... | collective-permute-start | bytes 196616 | tf_op jit(solution)/shard_map/ppermute | solution.py:47
  4.4 1.7 %collective-permute-done.refs_1_ = bf16[1,32,1024]{2,1,0:T(8,128)(2,1)S(1)} collective-permute-done((bf16[1,32,1024]{2,1,0:T(8,128)(2,1)}, bf16[1,32,1024]{2,1,0:T(8,128)(2,1)S(1)}, u32[]{:S(2)}, u32[]{:S(2)}) %collective-permute-start) | collective-permute-done | bytes 65568 | tf_op jit(solution)/shard_map/ppermute | solution.py:47
  9.5 1.6 %attend.1 = (bf16[64,1152]{1,0:T(8,128)(2,1)S(1)}, bf16[64,1024]{1,0:T(8,128)(2,1)S(1)}) custom-call(s32[3]{0:T(128)S(1)} %pad_add_fusion.scal, bf16[1,32,1024]{2,1,0:T(8,128)(2,1)S(1)} %copy-done.8, bf16[1,32,1024]{2,1,0:T(8,128)(2,1)S(1)} %collective-permute-done.refs_1_, s32[1,32]{1,0:T(1,128)S(1)} %copy-done.11, bf16[1,128,1024]{2,1,0:T(8,128)(2,1)S(1)} %copy-done.4, ...), custom_call_target="tpu_custom_call" | custom-call | bytes 7340032 | tf_op jit(solution)/shard_map/attend/pallas_call | solution.py:458
  11.2 2.1 %collective-permute-start.1 = (bf16[64,1152]{1,0:T(8,128)(2,1)S(1)}, bf16[64,1152]{1,0:T(8,128)(2,1)S(1)}, u32[]{:S(2)}, u32[]{:S(2)}) collective-permute-start(bf16[64,1152]{1,0:T(8,128)(2,1)S(1)} %get-tuple-element.49.refs_0_), channel_id=1, source_target_pairs={{4,0},{0,4},{5,1},{1,5},{6,2},{2,6},{7,3},{3,7},{12,8},{8,12},{13,... | collective-permute-start | bytes 442376 | tf_op jit(solution)/shard_map/ppermute | solution.py:47
  13.2 3.1 %collective-permute-done.1.refs_1_ = bf16[64,1152]{1,0:T(8,128)(2,1)S(1)} collective-permute-done((bf16[64,1152]{1,0:T(8,128)(2,1)S(1)}, bf16[64,1152]{1,0:T(8,128)(2,1)S(1)}, u32[]{:S(2)}, u32[]{:S(2)}) %collective-permute-start.1) | collective-permute-done | bytes 147488 | tf_op jit(solution)/shard_map/ppermute | solution.py:47
  16.4 2.2 %copy-done.2 = bf16[1024,2048]{1,0:T(8,128)(2,1)S(1)} copy-done((bf16[1024,2048]{1,0:T(8,128)(2,1)S(1)}, bf16[1024,2048]{1,0:T(8,128)(2,1)}, u32[]{:S(2)}) %copy-start.2) | copy-done | bytes 4194328
  18.6 2.6 %project.1 = (bf16[64,2048]{1,0:T(8,128)(2,1)S(1)}, f32[16,2048]{1,0:T(8,128)S(1)}, bf16[64,1024]{1,0:T(8,128)(2,1)S(1)}, f32[64,128]{1,0:T(8,128)S(1)}, s32[64,128]{1,0:T(8,128)S(1)}) custom-call(s32[3]{0:T(128)S(1)} %pad_add_fusion.scal, bf16[64,1152]{1,0:T(8,128)(2,1)S(1)} %get-tuple-element.49.refs_0_, ...), custom_call_target="tpu_custom_call" | custom-call | bytes 7340032 | tf_op jit(solution)/shard_map/project/pallas_call | solution.py:476
  21.2 2.1 %collective-permute-start.2 = (bf16[16,2048]{1,0:T(8,128)(2,1)S(1)}, bf16[16,2048]{1,0:T(8,128)(2,1)S(1)}, u32[]{:S(2)}, u32[]{:S(2)}) collective-permute-start(bf16[16,2048]{1,0:T(8,128)(2,1)S(1)} %get-tuple-element.99), channel_id=1, source_target_pairs={{0,1},{1,2},{2,3},{3,0},{4,5},{5,6},{6,7},{7,4},{8,9},{9,10},{10,1... | collective-permute-start | bytes 196616 | tf_op jit(solution)/shard_map/ppermute | solution.py:57
  23.3 2.6 %collective-permute-start.3 = (bf16[16,2048]{1,0:T(8,128)(2,1)S(1)}, bf16[16,2048]{1,0:T(8,128)(2,1)S(1)}, u32[]{:S(2)}, u32[]{:S(2)}) collective-permute-start(bf16[16,2048]{1,0:T(8,128)(2,1)S(1)} %get-tuple-element.98), channel_id=1, source_target_pairs={{0,2},{1,3},{2,0},{3,1},{4,6},{5,7},{6,4},{7,5},{8,10},{9,11},{10,... | collective-permute-start | bytes 196616 | tf_op jit(solution)/shard_map/ppermute | solution.py:57
  28.5 2.4 %collective-permute-done.4.refs_3_ = bf16[16,2048]{1,0:T(8,128)(2,1)S(1)} collective-permute-done((bf16[16,2048]{1,0:T(8,128)(2,1)S(1)}, bf16[16,2048]{1,0:T(8,128)(2,1)S(1)}, u32[]{:S(2)}, u32[]{:S(2)}) %collective-permute-start.4) | collective-permute-done | bytes 65568 | tf_op jit(solution)/shard_map/ppermute | solution.py:57
  31.7 2.5 %collective-permute-start.5 = (bf16[16,2176]{1,0:T(8,128)(2,1)S(1)}, bf16[16,2176]{1,0:T(8,128)(2,1)S(1)}, u32[]{:S(2)}, u32[]{:S(2)}) collective-permute-start(bf16[16,2176]{1,0:T(8,128)(2,1)S(1)} %get-tuple-element.52.refs_0_), channel_id=1, source_target_pairs={{1,0},{2,1},{3,2},{0,3},{5,4},{6,5},{7,6},{4,7},{9,8},{10,9},{11,1... | collective-permute-start | bytes 208904 | tf_op jit(solution)/shard_map/ppermute | solution.py:47
  36.3 3.0 %collective-permute-done.6.refs_2_ = bf16[16,2176]{1,0:T(8,128)(2,1)S(1)} collective-permute-done((bf16[16,2176]{1,0:T(8,128)(2,1)S(1)}, bf16[16,2176]{1,0:T(8,128)(2,1)S(1)}, u32[]{:S(2)}, u32[]{:S(2)}) %collective-permute-start.6) | collective-permute-done | bytes 69664 | tf_op jit(solution)/shard_map/ppermute | solution.py:47
  40.3 9.5 %logits.5 = (s16[64,3072]{1,0:T(8,128)(2,1)S(1)}, f32[64,128]{1,0:T(8,128)S(1)}, bf16[64,2048]{1,0:T(8,128)(2,1)S(1)}) custom-call(bf16[16,2176]{1,0:T(8,128)(2,1)S(1)} %get-tuple-element.52.refs_0_, bf16[16,2176]{1,0:T(8,128)(2,1)S(1)} %collective-permute-done.5.refs_1_, bf16[16,2176]{1,0:T(8,128)(2,1)S(1)} %collective-permute-done.6.refs_2_, ...), custom_call_target="tpu_custom_call" | custom-call | flops 3221225472 | bytes 12582912 | tf_op jit(solution)/shard_map/logits/pallas_call | solution.py:523
  53.3 9.5 %logits.4 = (s16[64,3072]{1,0:T(8,128)(2,1)S(1)}, f32[64,128]{1,0:T(8,128)S(1)}) custom-call(bf16[16,2176]{1,0:T(8,128)(2,1)S(1)} %get-tuple-element.52.refs_0_, bf16[16,2176]{1,0:T(8,128)(2,1)S(1)} %collective-permute-done.5.refs_1_, bf16[16,2176]{1,0:T(8,128)(2,1)S(1)} %collective-permute-done.6.refs_2_, ...), custom_call_target="tpu_custom_call" | custom-call | flops 3221225472 | bytes 12582912 | tf_op jit(solution)/shard_map/logits/pallas_call | solution.py:523
  62.8 1.6 %collective-permute-start.10 = (s16[64,3072]{1,0:T(8,128)(2,1)S(1)}, s16[64,3072]{1,0:T(8,128)(2,1)S(1)}, u32[]{:S(2)}, u32[]{:S(2)}) collective-permute-start(s16[64,3072]{1,0:T(8,128)(2,1)S(1)} %get-tuple-element.58.refs_0_), channel_id=1, source_target_pairs={{4,0},{0,4},{5,1},{1,5},{6,2},{2,6},{7,3},{3,7},{12,8},{8,12},{13,... | collective-permute-start | bytes 1179656 | tf_op jit(solution)/shard_map/ppermute | solution.py:47
  64.4 6.8 %logits.3 = (s16[64,2048]{1,0:T(8,128)(2,1)S(1)}, f32[64,128]{1,0:T(8,128)S(1)}) custom-call(bf16[16,2176]{1,0:T(8,128)(2,1)S(1)} %get-tuple-element.52.refs_0_, bf16[16,2176]{1,0:T(8,128)(2,1)S(1)} %collective-permute-done.5.refs_1_, bf16[16,2176]{1,0:T(8,128)(2,1)S(1)} %collective-permute-done.6.refs_2_, ...), custom_call_target="tpu_custom_call" | custom-call | flops 2147483648 | bytes 8388608 | tf_op jit(solution)/shard_map/logits/pallas_call | solution.py:523
  73.4 5.3 %hidden.2 = (f32[128,2048]{1,0:T(8,128)S(1)}, bf16[64,3072]{1,0:T(8,128)(2,1)S(1)}, f32[64,128]{1,0:T(8,128)S(1)}) custom-call(s16[64,3072]{1,0:T(8,128)(2,1)S(1)} %get-tuple-element.61.refs_0_, s16[64,3072]{1,0:T(8,128)(2,1)S(1)} %collective-permute-done.15.refs_1_, f32[64,128]{1,0:T(8,128)S(1)} %get-tuple-element.62.refs_2_, ...), custom_call_target="tpu_custom_call" | custom-call | flops 3221225472 | bytes 12582912 | tf_op jit(solution)/shard_map/hidden/pallas_call | solution.py:562
  79.3 5.5 %hidden.3 = (f32[128,2048]{1,0:T(8,128)S(1)}, bf16[64,3072]{1,0:T(8,128)(2,1)S(1)}, f32[64,128]{1,0:T(8,128)S(1)}) custom-call(s16[64,3072]{1,0:T(8,128)(2,1)S(1)} %get-tuple-element.58.refs_0_, s16[64,3072]{1,0:T(8,128)(2,1)S(1)} %collective-permute-done.10.refs_1_, f32[64,128]{1,0:T(8,128)S(1)} %get-tuple-element.60.refs_2_, ...), custom_call_target="tpu_custom_call" | custom-call | flops 3221225472 | bytes 12582912 | tf_op jit(solution)/shard_map/hidden/pallas_call | solution.py:562
  86.6 1.9 %collective-permute-start.19 = (f32[64,128]{1,0:T(8,128)S(1)}, f32[64,128]{1,0:T(8,128)S(1)}, u32[]{:S(2)}, u32[]{:S(2)}) collective-permute-start(f32[64,128]{1,0:T(8,128)S(1)} %get-tuple-element.66.st_ref.refs_0_), channel_id=1, source_target_pairs={{3,0},{0,1},{1,2},{2,3},{7,4},{4,5},{5,6},{6,7},{11,8},{8,9},{9,10... | collective-permute-start | bytes 98312 | tf_op jit(solution)/shard_map/ppermute | solution.py:47
  88.6 3.9 %last_hidden.1.refs_4_ = f32[128,2048]{1,0:T(8,128)S(1)} custom-call(f32[64,128]{1,0:T(8,128)S(1)} %get-tuple-element.65.refs_5_.st_prev, f32[64,128]{1,0:T(8,128)S(1)} %get-tuple-element.66.st_ref.refs_0_, bf16[128,2048]{1,0:T(8,128)(2,1)S(1)} %get-tuple-element.67.lhs_ref, f32[128,2048]{1,0:T(8,128)S(1)} %get-tuple-element.68.acc_prev, ...), custom_call_target="tpu_custom_call" | custom-call | flops 2147483648 | bytes 8388608 | tf_op jit(solution)/shard_map/last_hidden/pallas_call | solution.py:586
  95.4 2.3 %collective-permute-start.22 = (bf16[16,2048]{1,0:T(8,128)(2,1)S(1)}, bf16[16,2048]{1,0:T(8,128)(2,1)S(1)}, u32[]{:S(2)}, u32[]{:S(2)}) collective-permute-start(bf16[16,2048]{1,0:T(8,128)(2,1)S(1)} %get-tuple-element.94), channel_id=1, source_target_pairs={{0,3},{1,0},{2,1},{3,2},{4,7},{5,4},{6,5},{7,6},{8,11},{9,8},{10,9... | collective-permute-start | bytes 196616 | tf_op jit(solution)/shard_map/ppermute | solution.py:57
  97.7 2.0 %collective-permute-done.20.refs_1_ = bf16[16,2048]{1,0:T(8,128)(2,1)S(1)} collective-permute-done((bf16[16,2048]{1,0:T(8,128)(2,1)S(1)}, bf16[16,2048]{1,0:T(8,128)(2,1)S(1)}, u32[]{:S(2)}, u32[]{:S(2)}) %collective-permute-start.20) | collective-permute-done | bytes 65568 | tf_op jit(solution)/shard_map/ppermute | solution.py:57
  99.7 1.7 %collective-permute-done.21.refs_2_ = bf16[16,2048]{1,0:T(8,128)(2,1)S(1)} collective-permute-done((bf16[16,2048]{1,0:T(8,128)(2,1)S(1)}, bf16[16,2048]{1,0:T(8,128)(2,1)S(1)}, u32[]{:S(2)}, u32[]{:S(2)}) %collective-permute-start.21) | collective-permute-done | bytes 65568 | tf_op jit(solution)/shard_map/ppermute | solution.py:57
  104.1 2.1 %collective-permute-done.23.refs_1_ = f32[16,128]{1,0:T(8,128)S(1)} collective-permute-done((f32[16,128]{1,0:T(8,128)S(1)}, f32[16,128]{1,0:T(8,128)S(1)}, u32[]{:S(2)}, u32[]{:S(2)}) %collective-permute-start.23) | collective-permute-done | bytes 8224 | tf_op jit(solution)/shard_map/ppermute | solution.py:47
  106.3 2.8 %collective-permute-start.24 = (bf16[16,2048]{1,0:T(8,128)(2,1)S(1)}, bf16[16,2048]{1,0:T(8,128)(2,1)S(1)}, u32[]{:S(2)}, u32[]{:S(2)}) collective-permute-start(bf16[16,2048]{1,0:T(8,128)(2,1)S(1)} %mixed_grad.1.refs_0_), channel_id=1, source_target_pairs={{1,0},{2,1},{3,2},{0,3},{5,4},{6,5},{7,6},{4,7},{9,8},{10,9},{11,1... | collective-permute-start | bytes 196616 | tf_op jit(solution)/shard_map/ppermute | solution.py:47
  111.2 3.1 %collective-permute-done.25.refs_2_ = bf16[16,2048]{1,0:T(8,128)(2,1)S(1)} collective-permute-done((bf16[16,2048]{1,0:T(8,128)(2,1)S(1)}, bf16[16,2048]{1,0:T(8,128)(2,1)S(1)}, u32[]{:S(2)}, u32[]{:S(2)}) %collective-permute-start.25) | collective-permute-done | bytes 65568 | tf_op jit(solution)/shard_map/ppermute | solution.py:47
  115.4 1.8 %back_project.1.refs_0_ = bf16[64,1024]{1,0:T(8,128)(2,1)S(1)} custom-call(bf16[16,2048]{1,0:T(8,128)(2,1)S(1)} %mixed_grad.1.refs_0_, bf16[16,2048]{1,0:T(8,128)(2,1)S(1)} %collective-permute-done.24.refs_1_, bf16[16,2048]{1,0:T(8,128)(2,1)S(1)} %collective-permute-done.25.refs_2_, bf16[16,2048]{1,0:T(8,128)(2,1)S(1)} %collective-permute-done.26.refs_3_, ...), custom_call_target="tpu_custom_call" | custom-call | bytes 7340032 | tf_op jit(solution)/shard_map/back_project/pallas_call | solution.py:650
  117.3 1.6 %collective-permute-start.27 = (bf16[64,1024]{1,0:T(8,128)(2,1)S(1)}, bf16[64,1024]{1,0:T(8,128)(2,1)S(1)}, u32[]{:S(2)}, u32[]{:S(2)}) collective-permute-start(bf16[64,1024]{1,0:T(8,128)(2,1)S(1)} %back_project.1.refs_0_), channel_id=1, source_target_pairs={{4,0},{0,4},{5,1},{1,5},{6,2},{2,6},{7,3},{3,7},{12,8},{8,12},{13,... | collective-permute-start | bytes 393224 | tf_op jit(solution)/shard_map/ppermute | solution.py:47
  118.9 3.4 %collective-permute-done.27.refs_1_ = bf16[64,1024]{1,0:T(8,128)(2,1)S(1)} collective-permute-done((bf16[64,1024]{1,0:T(8,128)(2,1)S(1)}, bf16[64,1024]{1,0:T(8,128)(2,1)S(1)}, u32[]{:S(2)}, u32[]{:S(2)}) %collective-permute-start.27) | collective-permute-done | bytes 131104 | tf_op jit(solution)/shard_map/ppermute | solution.py:47
  122.3 3.9 %collective-permute-done.28.refs_1_.refs_5_ = bf16[64,8192]{1,0:T(8,128)(2,1)S(1)} collective-permute-done((bf16[64,8192]{1,0:T(8,128)(2,1)S(1)}, bf16[64,8192]{1,0:T(8,128)(2,1)S(1)}, u32[]{:S(2)}, u32[]{:S(2)}) %collective-permute-start.28) | collective-permute-done | bytes 1048608 | tf_op jit(solution)/shard_map/ppermute | solution.py:64
  126.2 2.6 %attend_back.1 = (f32[1,128,1024]{2,1,0:T(8,128)}, f32[1,128,1024]{2,1,0:T(8,128)}) custom-call(s32[3]{0:T(128)S(1)} %pad_add_fusion.scal, bf16[64,1024]{1,0:T(8,128)(2,1)S(1)} %back_project.1.refs_0_, bf16[64,1024]{1,0:T(8,128)(2,1)S(1)} %collective-permute-done.27.refs_1_, bf16[64,1024]{1,0:T(8,128)(2,1)S(1)} %get-tuple-element.89.refs_2_, ...), custom_call_target="tpu_custom_call" | custom-call | bytes 7340032 | tf_op jit(solution)/shard_map/attend_back/pallas_call | solution.py:670
  129.6 14.6 %head_grad.1 = bf16[8032,2048]{1,0:T(8,128)(2,1)} custom-call(bf16[64,2048]{1,0:T(8,128)(2,1)S(1)} %get-tuple-element.83.refs_0_, bf16[64,2048]{1,0:T(8,128)(2,1)S(1)} %collective-permute-done.11.refs_1_, bf16[64,2048]{1,0:T(8,128)(2,1)S(1)} %collective-permute-done.12.refs_2_, bf16[64,2048]{1,0:T(8,128)(2,1)S(1)} %collective-permute-done.13.refs_3_, ...), custom_call_target="tpu_custom_call" | custom-call | flops 8589934592 | bytes 33554432 | tf_op jit(solution)/shard_map/head_grad/pallas_call | solution.py:696
  (77 shorter events, 27.6 us)
Async XLA Ops:
  0.6 5.5 %collective-permute-start = (bf16[1,32,1024]{2,1,0:T(8,128)(2,1)}, bf16[1,32,1024]{2,1,0:T(8,128)(2,1)S(1)}, u32[]{:S(2)}, u32[]{:S(2)}) collective-permute-start(bf16[1,32,1024]{2,1,0:T(8,128)(2,1)} %refs_0_.1), channel_id=1, source_target_pairs={{4,0},{0,4},{5,1},{1,5},{6,2},{2,6},{7,3},{3,7},{12,8},{8,12},{13,... | collective-permute-start | bytes 196616 | tf_op jit(solution)/shard_map/ppermute | solution.py:47
  11.2 5.2 %collective-permute-start.1 = (bf16[64,1152]{1,0:T(8,128)(2,1)S(1)}, bf16[64,1152]{1,0:T(8,128)(2,1)S(1)}, u32[]{:S(2)}, u32[]{:S(2)}) collective-permute-start(bf16[64,1152]{1,0:T(8,128)(2,1)S(1)} %get-tuple-element.49.refs_0_), channel_id=1, source_target_pairs={{4,0},{0,4},{5,1},{1,5},{6,2},{2,6},{7,3},{3,7},{12,8},{8,12},{13,... | collective-permute-start | bytes 442376 | tf_op jit(solution)/shard_map/ppermute | solution.py:47
  21.2 6.4 %collective-permute-start.2 = (bf16[16,2048]{1,0:T(8,128)(2,1)S(1)}, bf16[16,2048]{1,0:T(8,128)(2,1)S(1)}, u32[]{:S(2)}, u32[]{:S(2)}) collective-permute-start(bf16[16,2048]{1,0:T(8,128)(2,1)S(1)} %get-tuple-element.99), channel_id=1, source_target_pairs={{0,1},{1,2},{2,3},{3,0},{4,5},{5,6},{6,7},{7,4},{8,9},{9,10},{10,1... | collective-permute-start | bytes 196616 | tf_op jit(solution)/shard_map/ppermute | solution.py:57
  23.3 5.2 %collective-permute-start.3 = (bf16[16,2048]{1,0:T(8,128)(2,1)S(1)}, bf16[16,2048]{1,0:T(8,128)(2,1)S(1)}, u32[]{:S(2)}, u32[]{:S(2)}) collective-permute-start(bf16[16,2048]{1,0:T(8,128)(2,1)S(1)} %get-tuple-element.98), channel_id=1, source_target_pairs={{0,2},{1,3},{2,0},{3,1},{4,6},{5,7},{6,4},{7,5},{8,10},{9,11},{10,... | collective-permute-start | bytes 196616 | tf_op jit(solution)/shard_map/ppermute | solution.py:57
  25.9 5.0 %collective-permute-start.4 = (bf16[16,2048]{1,0:T(8,128)(2,1)S(1)}, bf16[16,2048]{1,0:T(8,128)(2,1)S(1)}, u32[]{:S(2)}, u32[]{:S(2)}) collective-permute-start(bf16[16,2048]{1,0:T(8,128)(2,1)S(1)} %get-tuple-element.97), channel_id=1, source_target_pairs={{0,3},{1,0},{2,1},{3,2},{4,7},{5,4},{6,5},{7,6},{8,11},{9,8},{10,9... | collective-permute-start | bytes 196616 | tf_op jit(solution)/shard_map/ppermute | solution.py:57
  31.7 4.6 %collective-permute-start.5 = (bf16[16,2176]{1,0:T(8,128)(2,1)S(1)}, bf16[16,2176]{1,0:T(8,128)(2,1)S(1)}, u32[]{:S(2)}, u32[]{:S(2)}) collective-permute-start(bf16[16,2176]{1,0:T(8,128)(2,1)S(1)} %get-tuple-element.52.refs_0_), channel_id=1, source_target_pairs={{1,0},{2,1},{3,2},{0,3},{5,4},{6,5},{7,6},{4,7},{9,8},{10,9},{11,1... | collective-permute-start | bytes 208904 | tf_op jit(solution)/shard_map/ppermute | solution.py:47
  34.2 5.2 %collective-permute-start.6 = (bf16[16,2176]{1,0:T(8,128)(2,1)S(1)}, bf16[16,2176]{1,0:T(8,128)(2,1)S(1)}, u32[]{:S(2)}, u32[]{:S(2)}) collective-permute-start(bf16[16,2176]{1,0:T(8,128)(2,1)S(1)} %get-tuple-element.52.refs_0_), channel_id=1, source_target_pairs={{2,0},{3,1},{0,2},{1,3},{6,4},{7,5},{4,6},{5,7},{10,8},{11,9},{8,1... | collective-permute-start | bytes 208904 | tf_op jit(solution)/shard_map/ppermute | solution.py:47
  34.2 6.1 %collective-permute-start.7 = (bf16[16,2176]{1,0:T(8,128)(2,1)S(1)}, bf16[16,2176]{1,0:T(8,128)(2,1)S(1)}, u32[]{:S(2)}, u32[]{:S(2)}) collective-permute-start(bf16[16,2176]{1,0:T(8,128)(2,1)S(1)} %get-tuple-element.52.refs_0_), channel_id=1, source_target_pairs={{3,0},{0,1},{1,2},{2,3},{7,4},{4,5},{5,6},{6,7},{11,8},{8,9},{9,10... | collective-permute-start | bytes 208904 | tf_op jit(solution)/shard_map/ppermute | solution.py:47
  49.8 22.1 %collective-permute-start.11 = (bf16[64,2048]{1,0:T(8,128)(2,1)S(1)}, bf16[64,2048]{1,0:T(8,128)(2,1)S(1)}, u32[]{:S(2)}, u32[]{:S(2)}) collective-permute-start(bf16[64,2048]{1,0:T(8,128)(2,1)S(1)} %get-tuple-element.83.refs_0_), channel_id=1, source_target_pairs={{0,16},{8,24},{16,0},{24,8},{1,17},{9,25},{17,1},{25,9},{2,18},{10... | collective-permute-start | bytes 786440 | tf_op jit(solution)/shard_map/ppermute | solution.py:64
  51.3 27.4 %collective-permute-start.12 = (bf16[64,2048]{1,0:T(8,128)(2,1)S(1)}, bf16[64,2048]{1,0:T(8,128)(2,1)S(1)}, u32[]{:S(2)}, u32[]{:S(2)}) collective-permute-start(bf16[64,2048]{1,0:T(8,128)(2,1)S(1)} %get-tuple-element.83.refs_0_), channel_id=1, source_target_pairs={{0,8},{8,0},{16,24},{24,16},{1,9},{9,1},{17,25},{25,17},{2,10},{10... | collective-permute-start | bytes 786440 | tf_op jit(solution)/shard_map/ppermute | solution.py:64
  51.3 22.0 %collective-permute-start.15 = (s16[64,3072]{1,0:T(8,128)(2,1)S(1)}, s16[64,3072]{1,0:T(8,128)(2,1)S(1)}, u32[]{:S(2)}, u32[]{:S(2)}) collective-permute-start(s16[64,3072]{1,0:T(8,128)(2,1)S(1)} %get-tuple-element.61.refs_0_), channel_id=1, source_target_pairs={{4,0},{0,4},{5,1},{1,5},{6,2},{2,6},{7,3},{3,7},{12,8},{8,12},{13,... | collective-permute-start | bytes 1179656 | tf_op jit(solution)/shard_map/ppermute | solution.py:47
  52.8 18.4 %collective-permute-start.16 = (f32[64,128]{1,0:T(8,128)S(1)}, f32[64,128]{1,0:T(8,128)S(1)}, u32[]{:S(2)}, u32[]{:S(2)}) collective-permute-start(f32[64,128]{1,0:T(8,128)S(1)} %get-tuple-element.62.refs_2_), channel_id=1, source_target_pairs={{4,0},{0,4},{5,1},{1,5},{6,2},{2,6},{7,3},{3,7},{12,8},{8,12},{13,... | collective-permute-start | bytes 98312 | tf_op jit(solution)/shard_map/ppermute | solution.py:47
  62.8 16.5 %collective-permute-start.10 = (s16[64,3072]{1,0:T(8,128)(2,1)S(1)}, s16[64,3072]{1,0:T(8,128)(2,1)S(1)}, u32[]{:S(2)}, u32[]{:S(2)}) collective-permute-start(s16[64,3072]{1,0:T(8,128)(2,1)S(1)} %get-tuple-element.58.refs_0_), channel_id=1, source_target_pairs={{4,0},{0,4},{5,1},{1,5},{6,2},{2,6},{7,3},{3,7},{12,8},{8,12},{13,... | collective-permute-start | bytes 1179656 | tf_op jit(solution)/shard_map/ppermute | solution.py:47
  71.3 8.0 %collective-permute-start.14 = (f32[64,128]{1,0:T(8,128)S(1)}, f32[64,128]{1,0:T(8,128)S(1)}, u32[]{:S(2)}, u32[]{:S(2)}) collective-permute-start(f32[64,128]{1,0:T(8,128)S(1)} %get-tuple-element.60.refs_2_), channel_id=1, source_target_pairs={{4,0},{0,4},{5,1},{1,5},{6,2},{2,6},{7,3},{3,7},{12,8},{8,12},{13,... | collective-permute-start | bytes 98312 | tf_op jit(solution)/shard_map/ppermute | solution.py:47
  71.8 13.0 %collective-permute-start.8 = (s16[64,2048]{1,0:T(8,128)(2,1)S(1)}, s16[64,2048]{1,0:T(8,128)(2,1)S(1)}, u32[]{:S(2)}, u32[]{:S(2)}) collective-permute-start(s16[64,2048]{1,0:T(8,128)(2,1)S(1)} %get-tuple-element.53.refs_0_), channel_id=1, source_target_pairs={{4,0},{0,4},{5,1},{1,5},{6,2},{2,6},{7,3},{3,7},{12,8},{8,12},{13,... | collective-permute-start | bytes 786440 | tf_op jit(solution)/shard_map/ppermute | solution.py:47
  73.4 5.9 %collective-permute-start.13 = (bf16[64,2048]{1,0:T(8,128)(2,1)S(1)}, bf16[64,2048]{1,0:T(8,128)(2,1)S(1)}, u32[]{:S(2)}, u32[]{:S(2)}) collective-permute-start(bf16[64,2048]{1,0:T(8,128)(2,1)S(1)} %collective-permute-done.11.refs_1_), channel_id=1, source_target_pairs={{0,8},{8,0},{16,24},{24,16},{1,9},{9,1},{17,25},{25,17},{2,10},{10... | collective-permute-start | bytes 786440 | tf_op jit(solution)/shard_map/ppermute | solution.py:64
  78.7 6.1 %collective-permute-start.9 = (f32[64,128]{1,0:T(8,128)S(1)}, f32[64,128]{1,0:T(8,128)S(1)}, u32[]{:S(2)}, u32[]{:S(2)}) collective-permute-start(f32[64,128]{1,0:T(8,128)S(1)} %get-tuple-element.54.refs_2_), channel_id=1, source_target_pairs={{4,0},{0,4},{5,1},{1,5},{6,2},{2,6},{7,3},{3,7},{12,8},{8,12},{13,... | collective-permute-start | bytes 98312 | tf_op jit(solution)/shard_map/ppermute | solution.py:47
  85.4 7.1 %collective-permute-start.17 = (f32[64,128]{1,0:T(8,128)S(1)}, f32[64,128]{1,0:T(8,128)S(1)}, u32[]{:S(2)}, u32[]{:S(2)}) collective-permute-start(f32[64,128]{1,0:T(8,128)S(1)} %get-tuple-element.66.st_ref.refs_0_), channel_id=1, source_target_pairs={{1,0},{2,1},{3,2},{0,3},{5,4},{6,5},{7,6},{4,7},{9,8},{10,9},{11,1... | collective-permute-start | bytes 98312 | tf_op jit(solution)/shard_map/ppermute | solution.py:47
  86.2 6.4 %collective-permute-start.18 = (f32[64,128]{1,0:T(8,128)S(1)}, f32[64,128]{1,0:T(8,128)S(1)}, u32[]{:S(2)}, u32[]{:S(2)}) collective-permute-start(f32[64,128]{1,0:T(8,128)S(1)} %get-tuple-element.66.st_ref.refs_0_), channel_id=1, source_target_pairs={{2,0},{3,1},{0,2},{1,3},{6,4},{7,5},{4,6},{5,7},{10,8},{11,9},{8,1... | collective-permute-start | bytes 98312 | tf_op jit(solution)/shard_map/ppermute | solution.py:47
  86.6 5.9 %collective-permute-start.19 = (f32[64,128]{1,0:T(8,128)S(1)}, f32[64,128]{1,0:T(8,128)S(1)}, u32[]{:S(2)}, u32[]{:S(2)}) collective-permute-start(f32[64,128]{1,0:T(8,128)S(1)} %get-tuple-element.66.st_ref.refs_0_), channel_id=1, source_target_pairs={{3,0},{0,1},{1,2},{2,3},{7,4},{4,5},{5,6},{6,7},{11,8},{8,9},{9,10... | collective-permute-start | bytes 98312 | tf_op jit(solution)/shard_map/ppermute | solution.py:47
  88.6 55.6 %copy-start.1 = (bf16[1,64,2048]{2,1,0:T(8,128)(2,1)S(1)}, bf16[1,64,2048]{2,1,0:T(8,128)(2,1)}, u32[]{:S(2)}) copy-start(bf16[1,64,2048]{2,1,0:T(8,128)(2,1)} %param.14) | copy-start | bytes 786436
  92.9 6.8 %collective-permute-start.20 = (bf16[16,2048]{1,0:T(8,128)(2,1)S(1)}, bf16[16,2048]{1,0:T(8,128)(2,1)S(1)}, u32[]{:S(2)}, u32[]{:S(2)}) collective-permute-start(bf16[16,2048]{1,0:T(8,128)(2,1)S(1)} %get-tuple-element.96), channel_id=1, source_target_pairs={{0,1},{1,2},{2,3},{3,0},{4,5},{5,6},{6,7},{7,4},{8,9},{9,10},{10,1... | collective-permute-start | bytes 196616 | tf_op jit(solution)/shard_map/ppermute | solution.py:57
  94.1 7.3 %collective-permute-start.21 = (bf16[16,2048]{1,0:T(8,128)(2,1)S(1)}, bf16[16,2048]{1,0:T(8,128)(2,1)S(1)}, u32[]{:S(2)}, u32[]{:S(2)}) collective-permute-start(bf16[16,2048]{1,0:T(8,128)(2,1)S(1)} %get-tuple-element.95), channel_id=1, source_target_pairs={{0,2},{1,3},{2,0},{3,1},{4,6},{5,7},{6,4},{7,5},{8,10},{9,11},{10,... | collective-permute-start | bytes 196616 | tf_op jit(solution)/shard_map/ppermute | solution.py:57
  95.4 5.9 %collective-permute-start.22 = (bf16[16,2048]{1,0:T(8,128)(2,1)S(1)}, bf16[16,2048]{1,0:T(8,128)(2,1)S(1)}, u32[]{:S(2)}, u32[]{:S(2)}) collective-permute-start(bf16[16,2048]{1,0:T(8,128)(2,1)S(1)} %get-tuple-element.94), channel_id=1, source_target_pairs={{0,3},{1,0},{2,1},{3,2},{4,7},{5,4},{6,5},{7,6},{8,11},{9,8},{10,9... | collective-permute-start | bytes 196616 | tf_op jit(solution)/shard_map/ppermute | solution.py:57
  101.9 24.3 %collective-permute-start.28 = (bf16[64,8192]{1,0:T(8,128)(2,1)S(1)}, bf16[64,8192]{1,0:T(8,128)(2,1)S(1)}, u32[]{:S(2)}, u32[]{:S(2)}) collective-permute-start(bf16[64,8192]{1,0:T(8,128)(2,1)S(1)} %logit_grad.1.refs_0_.refs_4_), channel_id=1, source_target_pairs={{0,16},{8,24},{16,0},{24,8},{1,17},{9,25},{17,1},{25,9},{2,18},{10... | collective-permute-start | bytes 3145736 | tf_op jit(solution)/shard_map/ppermute | solution.py:64
  102.6 3.7 %collective-permute-start.23 = (f32[16,128]{1,0:T(8,128)S(1)}, f32[16,128]{1,0:T(8,128)S(1)}, u32[]{:S(2)}, u32[]{:S(2)}) collective-permute-start(f32[16,128]{1,0:T(8,128)S(1)} %get-tuple-element.81.refs_0_), channel_id=1, source_target_pairs={{4,0},{0,4},{5,1},{1,5},{6,2},{2,6},{7,3},{3,7},{12,8},{8,12},{13,... | collective-permute-start | bytes 24584 | tf_op jit(solution)/shard_map/ppermute | solution.py:47
  106.3 4.9 %collective-permute-start.24 = (bf16[16,2048]{1,0:T(8,128)(2,1)S(1)}, bf16[16,2048]{1,0:T(8,128)(2,1)S(1)}, u32[]{:S(2)}, u32[]{:S(2)}) collective-permute-start(bf16[16,2048]{1,0:T(8,128)(2,1)S(1)} %mixed_grad.1.refs_0_), channel_id=1, source_target_pairs={{1,0},{2,1},{3,2},{0,3},{5,4},{6,5},{7,6},{4,7},{9,8},{10,9},{11,1... | collective-permute-start | bytes 196616 | tf_op jit(solution)/shard_map/ppermute | solution.py:47
  109.2 5.2 %collective-permute-start.25 = (bf16[16,2048]{1,0:T(8,128)(2,1)S(1)}, bf16[16,2048]{1,0:T(8,128)(2,1)S(1)}, u32[]{:S(2)}, u32[]{:S(2)}) collective-permute-start(bf16[16,2048]{1,0:T(8,128)(2,1)S(1)} %mixed_grad.1.refs_0_), channel_id=1, source_target_pairs={{2,0},{3,1},{0,2},{1,3},{6,4},{7,5},{4,6},{5,7},{10,8},{11,9},{8,1... | collective-permute-start | bytes 196616 | tf_op jit(solution)/shard_map/ppermute | solution.py:47
  109.4 6.1 %collective-permute-start.26 = (bf16[16,2048]{1,0:T(8,128)(2,1)S(1)}, bf16[16,2048]{1,0:T(8,128)(2,1)S(1)}, u32[]{:S(2)}, u32[]{:S(2)}) collective-permute-start(bf16[16,2048]{1,0:T(8,128)(2,1)S(1)} %mixed_grad.1.refs_0_), channel_id=1, source_target_pairs={{3,0},{0,1},{1,2},{2,3},{7,4},{4,5},{5,6},{6,7},{11,8},{8,9},{9,10... | collective-permute-start | bytes 196616 | tf_op jit(solution)/shard_map/ppermute | solution.py:47
  117.3 5.0 %collective-permute-start.27 = (bf16[64,1024]{1,0:T(8,128)(2,1)S(1)}, bf16[64,1024]{1,0:T(8,128)(2,1)S(1)}, u32[]{:S(2)}, u32[]{:S(2)}) collective-permute-start(bf16[64,1024]{1,0:T(8,128)(2,1)S(1)} %back_project.1.refs_0_), channel_id=1, source_target_pairs={{4,0},{0,4},{5,1},{1,5},{6,2},{2,6},{7,3},{3,7},{12,8},{8,12},{13,... | collective-permute-start | bytes 393224 | tf_op jit(solution)/shard_map/ppermute | solution.py:47
  118.9 10.0 %collective-permute-start.29 = (bf16[64,8192]{1,0:T(8,128)(2,1)S(1)}, bf16[64,8192]{1,0:T(8,128)(2,1)S(1)}, u32[]{:S(2)}, u32[]{:S(2)}) collective-permute-start(bf16[64,8192]{1,0:T(8,128)(2,1)S(1)} %logit_grad.1.refs_0_.refs_4_), channel_id=1, source_target_pairs={{0,8},{8,0},{16,24},{24,16},{1,9},{9,1},{17,25},{25,17},{2,10},{10... | collective-permute-start | bytes 3145736 | tf_op jit(solution)/shard_map/ppermute | solution.py:64
  126.2 2.7 %collective-permute-start.30 = (bf16[64,8192]{1,0:T(8,128)(2,1)S(1)}, bf16[64,8192]{1,0:T(8,128)(2,1)S(1)}, u32[]{:S(2)}, u32[]{:S(2)}) collective-permute-start(bf16[64,8192]{1,0:T(8,128)(2,1)S(1)} %collective-permute-done.28.refs_1_.refs_5_), channel_id=1, source_target_pairs={{0,8},{8,0},{16,24},{24,16},{1,9},{9,1},{17,25},{25,17},{2,10},{10... | collective-permute-start | bytes 3145736 | tf_op jit(solution)/shard_map/ppermute | solution.py:64
  (11 other events, 148.9 us)

commit v5 on v4

--- a/solution.py
+++ b/solution.py
@@ -51,22 +51,21 @@
     return [x] + [from_ahead(x, axis, k) for k in range(1, lax.axis_size(axis))]
 
 
-def scatter_ring(x, axis, rows):
-    n = lax.axis_size(axis)
-    return [
-        lax.ppermute(x[k * rows : (k + 1) * rows], axis, [(i, (i + k) % n) for i in range(n)])
-        for k in range(1, n)
-    ]
-
-
 def swap(x, axis, bit):
     n = lax.axis_size(axis)
     return lax.ppermute(x, axis, [(i, i ^ bit) for i in range(n)])
 
 
-def gather_swaps(x, axis):
-    held = [x]
-    bit = lax.axis_size(axis) // 2
+def gather_pairs(x, axis):
+    return [x] + [swap(x, axis, k) for k in range(1, lax.axis_size(axis))]
+
+
+def scatter_pairs(x, axis, rows):
+    n = lax.axis_size(axis)
+    return [swap(x[k * rows : (k + 1) * rows], axis, k) for k in range(1, n)]
+
+
+def spread(held, axis, bit):
     while bit:
         held = held + [swap(h, axis, bit) for h in held]
         bit //= 2
@@ -91,18 +90,19 @@
     return lax.broadcasted_iota(i32, (rows, LANES), 1)
 
 
-def attend_kernel(n_seq, scal, *refs):
+def attend_kernel(n_seq, n_vocab, scal, *refs):
     q_refs = refs[:n_seq]
-    tgt_ref, k_ref, v_ref, o_ref, q_out, q_twice, t_twice = refs[n_seq:]
+    tgt_ref, k_ref, v_ref, o_ref, q_out, q_rows, t_rows = refs[n_seq:]
     tgt_rows = q_refs[0].shape[1]
     rows = tgt_rows * n_seq
     enc, features = k_ref.shape[1:]
     for i, r in enumerate(q_refs):
-        for at in (i * tgt_rows, rows + i * tgt_rows):
-            q_twice[at : at + tgt_rows, :] = r[0]
-    q = q_twice[pl.ds(pl.multiple_of(scal[0], 16), rows), :]
+        q_rows[i * tgt_rows : (i + 1) * tgt_rows, :] = r[0]
+    own_rows = rows // n_vocab
+    blocks = [pl.ds(pl.multiple_of(scal[2 + k], 16), own_rows) for k in range(n_vocab)]
+    q = jnp.concatenate([q_rows[b, :] for b in blocks], axis=0)
     q_out[...] = q
-    valid = lax.broadcasted_iota(i32, (rows, enc), 1) < scal[1]
+    valid = lax.broadcasted_iota(i32, (rows, enc), 1) < scal[0]
     lane = lanes(rows)
     corner = (tgt_rows, tgt_rows)
     same = lax.broadcasted_iota(i32, corner, 0) == lax.broadcasted_iota(i32, corner, 1)
@@ -112,10 +112,9 @@
     for at, digit in ((LANES - 2, ids >> 8), (LANES - 1, ids & 255)):
         column = jnp.sum(jnp.where(same, digit.astype(f32), 0.0), axis=1, keepdims=True)
         digits = jnp.where(here == at, column, digits)
-    t_twice[...] = jnp.zeros_like(t_twice)
-    t_twice[:tgt_rows, :] = digits
-    t_twice[rows : rows + tgt_rows, :] = digits
-    stat = t_twice[pl.ds(pl.multiple_of(scal[0], 16), rows), :]
+    t_rows[...] = jnp.zeros_like(t_rows)
+    t_rows[:tgt_rows, :] = digits
+    stat = jnp.concatenate([t_rows[b, :] for b in blocks], axis=0)
     for h in range(features // HDIM):
         at = slice(h * HDIM, (h + 1) * HDIM)
         scores = dot(q[:, at], k_ref[0, :, at], 1, 1) * score_scale
@@ -160,7 +159,7 @@
         lse_all = jnp.where(lane == h, lse, lse_all)
     lse_ref[...] = lse_all
     ids = tree([s[:, LANES - 2 : LANES - 1] * 256.0 + s[:, LANES - 1 :] for s in stats])
-    tgt_ref[...] = jnp.broadcast_to(ids.astype(i32), (rows, LANES)) - scal[2]
+    tgt_ref[...] = jnp.broadcast_to(ids.astype(i32), (rows, LANES)) - scal[1]
     for c, copy in zip(columns, copies):
         copy.wait()
         part = dot(att_ref[...], p_buf[:, c], 1, 0)
@@ -228,7 +227,7 @@
     for t in range(z.shape[1] // TILE):
         wait_tile(copies, t)
         at = slice(t * TILE, (t + 1) * TILE)
-        z[:, at] = dot(buf[at, :], ng[:, :width], 1, 1).T
+        z[:, at] = dot(ng[:, :width], buf[at, :], 1, 1)
     val = z[...]
     peak = jnp.maximum(jnp.max(jnp.abs(val), axis=1, keepdims=True), 1e-30)
     code_ref[...] = jnp.round(val * (CODE_TOP / peak)).astype(i32).astype(jnp.int16)
@@ -322,8 +321,8 @@
     stats = [mine]
     for k in range(1, n_vocab):
         s = st_refs[k][...]
-        cut = rows - k * own_rows
-        stats.append(jnp.concatenate([s[cut:], s[:cut]], axis=0))
+        places = [(i ^ k) * own_rows for i in range(n_vocab)]
+        stats.append(jnp.concatenate([s[p : p + own_rows] for p in places], axis=0))
     top = tree([s[:, 0:1] for s in stats], jnp.maximum)
     total = tree([s[:, 1:2] * jnp.exp(s[:, 0:1] - top) for s in stats])
     hit_logit = tree([s[:, 2:3] for s in stats])
@@ -367,8 +366,8 @@
     sums = []
     for r in refs[:-1]:
         s = r[...].astype(f32)
-        sums.append(jnp.sum(s[:, -3:-2] + s[:, -2:-1] + s[:, -1:], axis=0, keepdims=True))
-    refs[-1][...] = jnp.broadcast_to(tree(sums) / rows_all, refs[-1].shape)
+        sums.append(jnp.sum(s[:, -3:-2] + s[:, -2:-1] + s[:, -1:]))
+    refs[-1][0, 0] = tree(sums) * (1.0 / rows_all)
 
 
 def head_kernel(n_dp, *refs):
@@ -417,7 +416,7 @@
     q_ref, k_ref, v_ref, att_ref, lse_ref, kg_ref, vg_ref = refs[n_seq:]
     enc, features = k_ref.shape[1:]
     rows = q_ref.shape[0]
-    valid = lax.broadcasted_iota(i32, (rows, enc), 1) < scal[1]
+    valid = lax.broadcasted_iota(i32, (rows, enc), 1) < scal[0]
     for h in range(features // HDIM):
         at = slice(h * HDIM, (h + 1) * HDIM)
         grad = tree([r[:, at].astype(f32) for r in a_refs]).astype(bf16)
@@ -450,19 +449,21 @@
     gain = norm_gain.reshape(1, width)
     weight = head_weight.T
 
-    start = lax.rem(voc * own_rows - seq * tgt_rows + rows, rows).astype(i32)
-    scal = jnp.stack([start, enc_lengths[0] - seq * enc, voc * cols]).astype(i32)
+    starts = [
+        lax.rem((voc ^ k) * own_rows - seq * tgt_rows + rows, rows) for k in range(n_vocab)
+    ]
+    scal = jnp.stack([enc_lengths[0] - seq * enc, voc * cols] + starts).astype(i32)
 
     q_parts = gather_ring(queries, "seq")
     res_own = lax.dynamic_slice(residual[0], (voc * own_rows, 0), (own_rows, width))
     o_part, q_all = pl.pallas_call(
-        functools.partial(attend_kernel, n_seq),
+        functools.partial(attend_kernel, n_seq, n_vocab),
         out_shape=[sds((rows, features + LANES), bf16), sds((rows, features), bf16)],
         in_specs=[SMEM] + [VMEM] * (n_seq + 3),
         out_specs=[VMEM, VMEM],
         scratch_shapes=[
-            pltpu.VMEM((2 * rows, features), bf16),
-            pltpu.VMEM((2 * rows, LANES), f32),
+            pltpu.VMEM((rows, features), bf16),
+            pltpu.VMEM((rows, LANES), f32),
         ],
         compiler_params=params(),
         cost_estimate=cost(0, 7 * 1024 * 1024),
@@ -493,7 +494,7 @@
         name="project",
     )(scal, *o_all, out_proj)
 
-    got = scatter_ring(mixed_part, "vocab", own_rows)
+    got = scatter_pairs(mixed_part, "vocab", own_rows)
     mixed, ng_own = pl.pallas_call(
         functools.partial(norm_kernel, len(got)),
         out_shape=[sds((own_rows, width), f32), sds((own_rows, width + LANES), bf16)],
@@ -503,7 +504,7 @@
         cost_estimate=cost(0, 7 * 1024 * 1024),
         name="norm",
     )(mixed_own, *got, res_own, gain)
-    ng_parts = gather_ring(ng_own, "vocab")
+    ng_parts = gather_pairs(ng_own, "vocab")
 
     last_part = pl.BlockSpec((PART, width), lambda j: (-(-cols // PART) - 1, 0))
 
@@ -538,7 +539,7 @@
         codes.append(gather_ring(outs[0], "seq"))
         stats.append(gather_ring(outs[1], "seq"))
         if stacked:
-            ng_dp = gather_swaps(outs[2], "dp")
+            ng_dp = [outs[2]] + ([swap(outs[2], "dp", n_dp // 2)] if n_dp > 1 else [])
 
     if len(chunks) > 1:
         codes[1], ng_dp = lax.optimization_barrier((codes[1], ng_dp))
@@ -570,7 +571,7 @@
                 cost_estimate=estimate,
                 name="hidden",
             )(*ins, *([acc] if c else []), *weights)
-            st_all = gather_ring(st, "vocab") if c == len(chunks) - 1 else None
+            st_all = gather_pairs(st, "vocab") if c == len(chunks) - 1 else None
         else:
             before = st
             e, st, left = pl.pallas_call(
@@ -582,7 +583,7 @@
                 cost_estimate=cost(0, 4 * 1024 * 1024),
                 name="last_exp",
             )(*ins)
-            st_all = gather_ring(st, "vocab")
+            st_all = gather_pairs(st, "vocab")
             acc = pl.pallas_call(
                 functools.partial(last_hidden_kernel, c, first, cols),
                 grid=(1,) if odd else (),
@@ -609,9 +610,6 @@
         cost_estimate=cost(0, 7 * 1024 * 1024),
         name="total",
     )(*st_all, acc)
-    got = scatter_ring(hidden_part, "vocab", own_rows)
-    got, coef_later = lax.optimization_barrier((got, coef))
-
     group = tiles * TILE // GROUPS
     assert cols + 3 <= tiles * TILE and group % HEAD_TILE == 0
     grads = pl.pallas_call(
@@ -622,7 +620,9 @@
         compiler_params=params(),
         cost_estimate=cost(0, 7 * 1024 * 1024),
         name="logit_grad",
-    )(coef_later, tgt, *exps)
+    )(coef, tgt, *exps)
+    hidden_part, grads = lax.optimization_barrier((hidden_part, grads))
+    got = scatter_pairs(hidden_part, "vocab", own_rows)
     bit = n_dp // 2
     across = [swap(g, "dp", bit) for g in grads] if bit else []
     gated, inner = pl.pallas_call(
@@ -644,7 +644,11 @@
         cost_estimate=cost(0, 7 * 1024 * 1024),
         name="mixed_grad",
     )(gated, mixed, coef, *inner_all)
-    mg_parts = gather_ring(mixed_grad, "vocab")
+    mg_parts = gather_pairs(mixed_grad, "vocab")
+    if n_vocab > 1:
+        mg_parts[1], ng_dp = lax.optimization_barrier((mg_parts[1], ng_dp))
+    ng_dp = spread(ng_dp, "dp", n_dp // 4)
+    mg_parts, ng_dp = lax.optimization_barrier((mg_parts, ng_dp))
 
     ftile = min(256, features)
     back_part = pl.pallas_call(
@@ -662,11 +666,7 @@
     back_all, across = lax.optimization_barrier((back_all, across))
     grads_dp = []
     for i, g in enumerate(grads):
-        held, bit = ([g, across[i]] if across else [g]), n_dp // 4
-        while bit:
-            held = held + [swap(h, "dp", bit) for h in held]
-            bit //= 2
-        grads_dp.append(held)
+        grads_dp.append(spread([g, across[i]] if across else [g], "dp", n_dp // 4))
     key_grad, value_grad = pl.pallas_call(
         functools.partial(attend_back_kernel, n_seq),
         out_shape=[sds(enc_keys.shape, f32), sds(enc_values.shape, f32)],
@@ -680,14 +680,14 @@
     loss = pl.pallas_call(
         functools.partial(loss_kernel, n_dp * rows),
         grid=(1,),
-        out_shape=sds((8, LANES), f32),
+        out_shape=sds((1, 1), f32),
         in_specs=[pl.BlockSpec((rows, LANES), lambda j: (0, group // LANES - 1))] * n_dp,
-        out_specs=whole((8, LANES)),
+        out_specs=SMEM,
         compiler_params=params(),
         cost_estimate=cost(0, 7 * 1024 * 1024),
         name="loss",
     )(*grads_dp[-1])
-    mean_loss = loss[0, 0]
+    mean_loss = loss.reshape(())
 
     head = None
     for c in range(GROUPS):

time: 145 us -> 139 us (0.959)
  Pallas kernels: 65.8 us -> 58.5 us
  waiting for transfers between devices: 32.7 us -> 35 us
    ppermute x6 -> x21, waiting for transfers between devices: 3.9 us -> 24.5 us  [swap(): return lax.ppermute(x, axis, [(i, i ^ bit) for i in range(n)])]
    ppermute x6 -> x21, starting transfers between devices: 2.17 us -> 22.8 us  [swap(): return lax.ppermute(x, axis, [(i, i ^ bit) for i in range(n)])]
    ppermute x19 -> x10, waiting for transfers between devices: 21.5 us -> 10.5 us  [from_ahead(): return lax.ppermute(x, axis, [((i + k) % n, i) for i in range(n)])]
    ppermute x6 -> x0, starting transfers between devices: 10.8 us -> none  [scatter_ring(): lax.ppermute(x[k * rows:(k + 1) * rows], axis, [(i, (i + k) % n) for i in...]
    ppermute x19 -> x10, starting transfers between devices: 24.2 us -> 14.5 us  [from_ahead(): return lax.ppermute(x, axis, [((i + k) % n, i) for i in range(n)])]
    pallas_call x3, Pallas kernels: 25.8 us -> 17.8 us  [body(): pl.pallas_call(functools.partial(logits_kernel, tile0 * TILE, cols, n_voc...]
    ppermute x6 -> x0, waiting for transfers between devices: 7.23 us -> none  [scatter_ring(): lax.ppermute(x[k * rows:(k + 1) * rows], axis, [(i, (i + k) % n) for i in...]
  transfers between devices with their start and end apart: 31 -> 31, of which waited for: 16 -> 13; matrix products, arithmetic and copies ran while one was open for 0% -> 0% of each run, Pallas kernels for 25% -> 22%
where the time goes in v5:
time: 139 us
  Pallas kernels  58.5 us (42%)
  starting transfers between devices  37.3 us (27%)
  waiting for transfers between devices  35 us (25%)
  local copies, waits for them, and re-layouts  6.43 us (5%)
  between operations  1.58 us (1%)
    ppermute x21, waiting for transfers between devices, swap(): return lax.ppermute(x, axis, [(i, i ^ bit) for i in range(n)])  24.5 us
    ppermute x21, starting transfers between devices, swap(): return lax.ppermute(x, axis, [(i, i ^ bit) for i in range(n)])  22.8 us
    pallas_call x3, Pallas kernels, body(): pl.pallas_call(functools.partial(logits_kernel, tile0 * TILE, cols, n_voc...  17.8 us
    pallas_call x1, Pallas kernels, body(): pl.pallas_call(functools.partial(head_kernel, n_dp), grid=(steps,), out_s...  14.7 us
    ppermute x10, starting transfers between devices, from_ahead(): return lax.ppermute(x, axis, [((i + k) % n, i) for i in range(n)])  14.5 us
    pallas_call x2, Pallas kernels, body(): pl.pallas_call(functools.partial(hidden_kernel, c, first, cols, n_seq, fu...  10.9 us
    ppermute x10, waiting for transfers between devices, from_ahead(): return lax.ppermute(x, axis, [((i + k) % n, i) for i in range(n)])  10.5 us
    unnamed x24, local copies, waits for them, and re-layouts  6.31 us
  transfers between devices with their start and end apart: 31, of which 13 were waited for; matrix products, arithmetic and copies ran while one was open for 0% of the time, Pallas kernels for 22%

profile of v5, /device:TPU:0, one launch (start us, length us, event | category | flops | bytes accessed | tf_op | source)
XLA Modules:
  0.0 138.8 jit_solution(13660285631709145298)
XLA Ops:
  0.6 3.0 %collective-permute-start = (bf16[1,32,1024]{2,1,0:T(8,128)(2,1)}, bf16[1,32,1024]{2,1,0:T(8,128)(2,1)S(1)}, u32[]{:S(2)}, u32[]{:S(2)}) collective-permute-start(bf16[1,32,1024]{2,1,0:T(8,128)(2,1)} %refs_0_.1), channel_id=1, source_target_pairs={{4,0},{0,4},{5,1},{1,5},{6,2},{2,6},{7,3},{3,7},{12,8},{8,12},{13,... | collective-permute-start | bytes 196616 | tf_op jit(solution)/shard_map/ppermute | solution.py:47
  4.4 1.7 %collective-permute-done.refs_1_ = bf16[1,32,1024]{2,1,0:T(8,128)(2,1)S(1)} collective-permute-done((bf16[1,32,1024]{2,1,0:T(8,128)(2,1)}, bf16[1,32,1024]{2,1,0:T(8,128)(2,1)S(1)}, u32[]{:S(2)}, u32[]{:S(2)}) %collective-permute-start) | collective-permute-done | bytes 65568 | tf_op jit(solution)/shard_map/ppermute | solution.py:47
  9.5 1.6 %attend.1 = (bf16[64,1152]{1,0:T(8,128)(2,1)S(1)}, bf16[64,1024]{1,0:T(8,128)(2,1)S(1)}) custom-call(s32[6]{0:T(128)S(1)} %stack.27.scal, bf16[1,32,1024]{2,1,0:T(8,128)(2,1)S(1)} %copy-done.8, bf16[1,32,1024]{2,1,0:T(8,128)(2,1)S(1)} %collective-permute-done.refs_1_, s32[1,32]{1,0:T(1,128)S(1)} %copy-done.11, bf16[1,128,1024]{2,1,0:T(8,128)(2,1)S(1)} %copy-done.4, ...), custom_call_target="tpu_custom_call" | custom-call | bytes 7340032 | tf_op jit(solution)/shard_map/attend/pallas_call | solution.py:459
  11.2 2.1 %collective-permute-start.1 = (bf16[64,1152]{1,0:T(8,128)(2,1)S(1)}, bf16[64,1152]{1,0:T(8,128)(2,1)S(1)}, u32[]{:S(2)}, u32[]{:S(2)}) collective-permute-start(bf16[64,1152]{1,0:T(8,128)(2,1)S(1)} %get-tuple-element.56.refs_0_), channel_id=1, source_target_pairs={{4,0},{0,4},{5,1},{1,5},{6,2},{2,6},{7,3},{3,7},{12,8},{8,12},{13,... | collective-permute-start | bytes 442376 | tf_op jit(solution)/shard_map/ppermute | solution.py:47
  13.2 3.1 %collective-permute-done.1.refs_1_ = bf16[64,1152]{1,0:T(8,128)(2,1)S(1)} collective-permute-done((bf16[64,1152]{1,0:T(8,128)(2,1)S(1)}, bf16[64,1152]{1,0:T(8,128)(2,1)S(1)}, u32[]{:S(2)}, u32[]{:S(2)}) %collective-permute-start.1) | collective-permute-done | bytes 147488 | tf_op jit(solution)/shard_map/ppermute | solution.py:47
  16.4 2.2 %copy-done.2 = bf16[1024,2048]{1,0:T(8,128)(2,1)S(1)} copy-done((bf16[1024,2048]{1,0:T(8,128)(2,1)S(1)}, bf16[1024,2048]{1,0:T(8,128)(2,1)}, u32[]{:S(2)}) %copy-start.2) | copy-done | bytes 4194328
  18.6 2.6 %project.1 = (bf16[64,2048]{1,0:T(8,128)(2,1)S(1)}, f32[16,2048]{1,0:T(8,128)S(1)}, bf16[64,1024]{1,0:T(8,128)(2,1)S(1)}, f32[64,128]{1,0:T(8,128)S(1)}, s32[64,128]{1,0:T(8,128)S(1)}) custom-call(s32[6]{0:T(128)S(1)} %stack.27.scal, bf16[64,1152]{1,0:T(8,128)(2,1)S(1)} %get-tuple-element.56.refs_0_, bf16[64,1152]{1,0:T(8,128)(2,1)S(1)} %collective-permute-done.1.refs_1_, ...), custom_call_target="tpu_custom_call" | custom-call | bytes 7340032 | tf_op jit(solution)/shard_map/project/pallas_call | solution.py:477
  21.2 2.1 %collective-permute-start.2 = (bf16[16,2048]{1,0:T(8,128)(2,1)S(1)}, bf16[16,2048]{1,0:T(8,128)(2,1)S(1)}, u32[]{:S(2)}, u32[]{:S(2)}) collective-permute-start(bf16[16,2048]{1,0:T(8,128)(2,1)S(1)} %get-tuple-element.113), channel_id=1, source_target_pairs={{0,1},{1,0},{2,3},{3,2},{4,5},{5,4},{6,7},{7,6},{8,9},{9,8},{10,11... | collective-permute-start | bytes 196616 | tf_op jit(solution)/shard_map/ppermute | solution.py:56
  23.4 2.6 %collective-permute-start.3 = (bf16[16,2048]{1,0:T(8,128)(2,1)S(1)}, bf16[16,2048]{1,0:T(8,128)(2,1)S(1)}, u32[]{:S(2)}, u32[]{:S(2)}) collective-permute-start(bf16[16,2048]{1,0:T(8,128)(2,1)S(1)} %get-tuple-element.112), channel_id=1, source_target_pairs={{0,2},{1,3},{2,0},{3,1},{4,6},{5,7},{6,4},{7,5},{8,10},{9,11},{10,... | collective-permute-start | bytes 196616 | tf_op jit(solution)/shard_map/ppermute | solution.py:56
  26.0 3.7 %collective-permute-done.3.refs_2_ = bf16[16,2048]{1,0:T(8,128)(2,1)S(1)} collective-permute-done((bf16[16,2048]{1,0:T(8,128)(2,1)S(1)}, bf16[16,2048]{1,0:T(8,128)(2,1)S(1)}, u32[]{:S(2)}, u32[]{:S(2)}) %collective-permute-start.3) | collective-permute-done | bytes 65568 | tf_op jit(solution)/shard_map/ppermute | solution.py:56
  29.6 2.9 %collective-permute-done.4.refs_3_ = bf16[16,2048]{1,0:T(8,128)(2,1)S(1)} collective-permute-done((bf16[16,2048]{1,0:T(8,128)(2,1)S(1)}, bf16[16,2048]{1,0:T(8,128)(2,1)S(1)}, u32[]{:S(2)}, u32[]{:S(2)}) %collective-permute-start.4) | collective-permute-done | bytes 65568 | tf_op jit(solution)/shard_map/ppermute | solution.py:56
  34.2 3.5 %collective-permute-start.7 = (bf16[16,2176]{1,0:T(8,128)(2,1)S(1)}, bf16[16,2176]{1,0:T(8,128)(2,1)S(1)}, u32[]{:S(2)}, u32[]{:S(2)}) collective-permute-start(bf16[16,2176]{1,0:T(8,128)(2,1)S(1)} %get-tuple-element.59.refs_0_), channel_id=1, source_target_pairs={{0,3},{1,2},{2,1},{3,0},{4,7},{5,6},{6,5},{7,4},{8,11},{9,10},{10,... | collective-permute-start | bytes 208904 | tf_op jit(solution)/shard_map/ppermute | solution.py:56
  38.7 2.2 %collective-permute-done.7.refs_3_ = bf16[16,2176]{1,0:T(8,128)(2,1)S(1)} collective-permute-done((bf16[16,2176]{1,0:T(8,128)(2,1)S(1)}, bf16[16,2176]{1,0:T(8,128)(2,1)S(1)}, u32[]{:S(2)}, u32[]{:S(2)}) %collective-permute-start.7) | collective-permute-done | bytes 69664 | tf_op jit(solution)/shard_map/ppermute | solution.py:56
  40.9 6.5 %logits.5 = (s16[64,3072]{1,0:T(8,128)(2,1)S(1)}, f32[64,128]{1,0:T(8,128)S(1)}, bf16[64,2048]{1,0:T(8,128)(2,1)S(1)}) custom-call(bf16[16,2176]{1,0:T(8,128)(2,1)S(1)} %get-tuple-element.59.refs_0_, bf16[16,2176]{1,0:T(8,128)(2,1)S(1)} %collective-permute-done.5.refs_1_, bf16[16,2176]{1,0:T(8,128)(2,1)S(1)} %collective-permute-done.6.refs_2_, ...), custom_call_target="tpu_custom_call" | custom-call | flops 3221225472 | bytes 12582912 | tf_op jit(solution)/shard_map/logits/pallas_call | solution.py:524
  47.4 1.6 %collective-permute-start.13 = (s16[64,3072]{1,0:T(8,128)(2,1)S(1)}, s16[64,3072]{1,0:T(8,128)(2,1)S(1)}, u32[]{:S(2)}, u32[]{:S(2)}) collective-permute-start(s16[64,3072]{1,0:T(8,128)(2,1)S(1)} %get-tuple-element.68.refs_0_), channel_id=1, source_target_pairs={{4,0},{0,4},{5,1},{1,5},{6,2},{2,6},{7,3},{3,7},{12,8},{8,12},{13,... | collective-permute-start | bytes 1179656 | tf_op jit(solution)/shard_map/ppermute | solution.py:47
  51.0 6.5 %logits.4 = (s16[64,3072]{1,0:T(8,128)(2,1)S(1)}, f32[64,128]{1,0:T(8,128)S(1)}) custom-call(bf16[16,2176]{1,0:T(8,128)(2,1)S(1)} %get-tuple-element.59.refs_0_, bf16[16,2176]{1,0:T(8,128)(2,1)S(1)} %collective-permute-done.5.refs_1_, bf16[16,2176]{1,0:T(8,128)(2,1)S(1)} %collective-permute-done.6.refs_2_, ...), custom_call_target="tpu_custom_call" | custom-call | flops 3221225472 | bytes 12582912 | tf_op jit(solution)/shard_map/logits/pallas_call | solution.py:524
  59.5 4.8 %logits.3 = (s16[64,2048]{1,0:T(8,128)(2,1)S(1)}, f32[64,128]{1,0:T(8,128)S(1)}) custom-call(bf16[16,2176]{1,0:T(8,128)(2,1)S(1)} %get-tuple-element.59.refs_0_, bf16[16,2176]{1,0:T(8,128)(2,1)S(1)} %collective-permute-done.5.refs_1_, bf16[16,2176]{1,0:T(8,128)(2,1)S(1)} %collective-permute-done.6.refs_2_, ...), custom_call_target="tpu_custom_call" | custom-call | flops 2147483648 | bytes 8388608 | tf_op jit(solution)/shard_map/logits/pallas_call | solution.py:524
  66.5 5.3 %hidden.2 = (f32[128,2048]{1,0:T(8,128)S(1)}, bf16[64,3072]{1,0:T(8,128)(2,1)S(1)}, f32[64,128]{1,0:T(8,128)S(1)}) custom-call(s16[64,3072]{1,0:T(8,128)(2,1)S(1)} %get-tuple-element.68.refs_0_, s16[64,3072]{1,0:T(8,128)(2,1)S(1)} %collective-permute-done.13.refs_1_, f32[64,128]{1,0:T(8,128)S(1)} %get-tuple-element.69.refs_2_, ...), custom_call_target="tpu_custom_call" | custom-call | flops 3221225472 | bytes 12582912 | tf_op jit(solution)/shard_map/hidden/pallas_call | solution.py:563
  71.8 5.5 %hidden.3 = (f32[128,2048]{1,0:T(8,128)S(1)}, bf16[64,3072]{1,0:T(8,128)(2,1)S(1)}, f32[64,128]{1,0:T(8,128)S(1)}) custom-call(s16[64,3072]{1,0:T(8,128)(2,1)S(1)} %get-tuple-element.65.refs_0_, s16[64,3072]{1,0:T(8,128)(2,1)S(1)} %collective-permute-done.10.refs_1_, f32[64,128]{1,0:T(8,128)S(1)} %get-tuple-element.67.refs_2_, ...), custom_call_target="tpu_custom_call" | custom-call | flops 3221225472 | bytes 12582912 | tf_op jit(solution)/shard_map/hidden/pallas_call | solution.py:563
  78.0 3.5 %collective-permute-start.16 = (f32[64,128]{1,0:T(8,128)S(1)}, f32[64,128]{1,0:T(8,128)S(1)}, u32[]{:S(2)}, u32[]{:S(2)}) collective-permute-start(f32[64,128]{1,0:T(8,128)S(1)} %get-tuple-element.73.st_ref.refs_0_), channel_id=1, source_target_pairs={{0,2},{1,3},{2,0},{3,1},{4,6},{5,7},{6,4},{7,5},{8,10},{9,11},{10,... | collective-permute-start | bytes 98312 | tf_op jit(solution)/shard_map/ppermute | solution.py:56
  82.4 3.9 %last_hidden.1.refs_4_ = f32[128,2048]{1,0:T(8,128)S(1)} custom-call(f32[64,128]{1,0:T(8,128)S(1)} %get-tuple-element.72.refs_5_.st_prev, f32[64,128]{1,0:T(8,128)S(1)} %get-tuple-element.73.st_ref.refs_0_, bf16[128,2048]{1,0:T(8,128)(2,1)S(1)} %get-tuple-element.74.lhs_ref, f32[128,2048]{1,0:T(8,128)S(1)} %get-tuple-element.75.acc_prev, ...), custom_call_target="tpu_custom_call" | custom-call | flops 2147483648 | bytes 8388608 | tf_op jit(solution)/shard_map/last_hidden/pallas_call | solution.py:587
  88.8 2.6 %collective-permute-start.19 = (bf16[16,2048]{1,0:T(8,128)(2,1)S(1)}, bf16[16,2048]{1,0:T(8,128)(2,1)S(1)}, u32[]{:S(2)}, u32[]{:S(2)}) collective-permute-start(bf16[16,2048]{1,0:T(8,128)(2,1)S(1)} %get-tuple-element.109), channel_id=1, source_target_pairs={{0,2},{1,3},{2,0},{3,1},{4,6},{5,7},{6,4},{7,5},{8,10},{9,11},{10,... | collective-permute-start | bytes 196616 | tf_op jit(solution)/shard_map/ppermute | solution.py:56
  91.5 1.7 %collective-permute-start.20 = (bf16[16,2048]{1,0:T(8,128)(2,1)S(1)}, bf16[16,2048]{1,0:T(8,128)(2,1)S(1)}, u32[]{:S(2)}, u32[]{:S(2)}) collective-permute-start(bf16[16,2048]{1,0:T(8,128)(2,1)S(1)} %get-tuple-element.108), channel_id=1, source_target_pairs={{0,3},{1,2},{2,1},{3,0},{4,7},{5,6},{6,5},{7,4},{8,11},{9,10},{10,... | collective-permute-start | bytes 196616 | tf_op jit(solution)/shard_map/ppermute | solution.py:56
  94.1 3.4 %collective-permute-done.20.refs_3_ = bf16[16,2048]{1,0:T(8,128)(2,1)S(1)} collective-permute-done((bf16[16,2048]{1,0:T(8,128)(2,1)S(1)}, bf16[16,2048]{1,0:T(8,128)(2,1)S(1)}, u32[]{:S(2)}, u32[]{:S(2)}) %collective-permute-start.20) | collective-permute-done | bytes 65568 | tf_op jit(solution)/shard_map/ppermute | solution.py:56
  99.2 2.1 %collective-permute-done.21.refs_1_ = f32[16,128]{1,0:T(8,128)S(1)} collective-permute-done((f32[16,128]{1,0:T(8,128)S(1)}, f32[16,128]{1,0:T(8,128)S(1)}, u32[]{:S(2)}, u32[]{:S(2)}) %collective-permute-start.21) | collective-permute-done | bytes 8224 | tf_op jit(solution)/shard_map/ppermute | solution.py:47
  101.5 4.3 %collective-permute-done.22.refs_1_ = bf16[16,2048]{1,0:T(8,128)(2,1)S(1)} collective-permute-done((bf16[16,2048]{1,0:T(8,128)(2,1)S(1)}, bf16[16,2048]{1,0:T(8,128)(2,1)S(1)}, u32[]{:S(2)}, u32[]{:S(2)}) %collective-permute-start.22) | collective-permute-done | bytes 65568 | tf_op jit(solution)/shard_map/ppermute | solution.py:56
  106.5 2.1 %collective-permute-start.24 = (bf16[16,2048]{1,0:T(8,128)(2,1)S(1)}, bf16[16,2048]{1,0:T(8,128)(2,1)S(1)}, u32[]{:S(2)}, u32[]{:S(2)}) collective-permute-start(bf16[16,2048]{1,0:T(8,128)(2,1)S(1)} %mixed_grad.1.refs_0_), channel_id=1, source_target_pairs={{0,3},{1,2},{2,1},{3,0},{4,7},{5,6},{6,5},{7,4},{8,11},{9,10},{10,... | collective-permute-start | bytes 196616 | tf_op jit(solution)/shard_map/ppermute | solution.py:56
  108.6 5.0 %collective-permute-done.23.refs_2_ = bf16[16,2048]{1,0:T(8,128)(2,1)S(1)} collective-permute-done((bf16[16,2048]{1,0:T(8,128)(2,1)S(1)}, bf16[16,2048]{1,0:T(8,128)(2,1)S(1)}, u32[]{:S(2)}, u32[]{:S(2)}) %collective-permute-start.23) | collective-permute-done | bytes 65568 | tf_op jit(solution)/shard_map/ppermute | solution.py:56
  113.7 1.9 %back_project.1.refs_0_ = bf16[64,1024]{1,0:T(8,128)(2,1)S(1)} custom-call(bf16[16,2048]{1,0:T(8,128)(2,1)S(1)} %mixed_grad.1.refs_0_, bf16[16,2048]{1,0:T(8,128)(2,1)S(1)} %collective-permute-done.22.refs_1_, bf16[16,2048]{1,0:T(8,128)(2,1)S(1)} %collective-permute-done.23.refs_2_, bf16[16,2048]{1,0:T(8,128)(2,1)S(1)} %collective-permute-done.24.refs_3_, ...), custom_call_target="tpu_custom_call" | custom-call | bytes 7340032 | tf_op jit(solution)/shard_map/back_project/pallas_call | solution.py:654
  117.1 3.5 %collective-permute-done.27.refs_1_ = bf16[64,1024]{1,0:T(8,128)(2,1)S(1)} collective-permute-done((bf16[64,1024]{1,0:T(8,128)(2,1)S(1)}, bf16[64,1024]{1,0:T(8,128)(2,1)S(1)}, u32[]{:S(2)}, u32[]{:S(2)}) %collective-permute-start.27) | collective-permute-done | bytes 131104 | tf_op jit(solution)/shard_map/ppermute | solution.py:47
  120.6 2.6 %attend_back.1 = (f32[1,128,1024]{2,1,0:T(8,128)}, f32[1,128,1024]{2,1,0:T(8,128)}) custom-call(s32[6]{0:T(128)S(1)} %stack.27.scal, bf16[64,1024]{1,0:T(8,128)(2,1)S(1)} %back_project.1.refs_0_, bf16[64,1024]{1,0:T(8,128)(2,1)S(1)} %collective-permute-done.27.refs_1_, bf16[64,1024]{1,0:T(8,128)(2,1)S(1)} %get-tuple-element.103.refs_2_, ...), custom_call_target="tpu_custom_call" | custom-call | bytes 7340032 | tf_op jit(solution)/shard_map/attend_back/pallas_call | solution.py:670
  124.1 14.7 %head_grad.1 = bf16[8032,2048]{1,0:T(8,128)(2,1)} custom-call(bf16[64,2048]{1,0:T(8,128)(2,1)S(1)} %get-tuple-element.97.refs_0_, bf16[64,2048]{1,0:T(8,128)(2,1)S(1)} %collective-permute-done.11.refs_1_, bf16[64,2048]{1,0:T(8,128)(2,1)S(1)} %collective-permute-done.25.refs_2_, bf16[64,2048]{1,0:T(8,128)(2,1)S(1)} %collective-permute-done.26.refs_3_, ...), custom_call_target="tpu_custom_call" | custom-call | flops 8589934592 | bytes 33554432 | tf_op jit(solution)/shard_map/head_grad/pallas_call | solution.py:696
  (76 shorter events, 22.2 us)
Async XLA Ops:
  0.6 5.5 %collective-permute-start = (bf16[1,32,1024]{2,1,0:T(8,128)(2,1)}, bf16[1,32,1024]{2,1,0:T(8,128)(2,1)S(1)}, u32[]{:S(2)}, u32[]{:S(2)}) collective-permute-start(bf16[1,32,1024]{2,1,0:T(8,128)(2,1)} %refs_0_.1), channel_id=1, source_target_pairs={{4,0},{0,4},{5,1},{1,5},{6,2},{2,6},{7,3},{3,7},{12,8},{8,12},{13,... | collective-permute-start | bytes 196616 | tf_op jit(solution)/shard_map/ppermute | solution.py:47
  11.2 5.2 %collective-permute-start.1 = (bf16[64,1152]{1,0:T(8,128)(2,1)S(1)}, bf16[64,1152]{1,0:T(8,128)(2,1)S(1)}, u32[]{:S(2)}, u32[]{:S(2)}) collective-permute-start(bf16[64,1152]{1,0:T(8,128)(2,1)S(1)} %get-tuple-element.56.refs_0_), channel_id=1, source_target_pairs={{4,0},{0,4},{5,1},{1,5},{6,2},{2,6},{7,3},{3,7},{12,8},{8,12},{13,... | collective-permute-start | bytes 442376 | tf_op jit(solution)/shard_map/ppermute | solution.py:47
  21.2 4.7 %collective-permute-start.2 = (bf16[16,2048]{1,0:T(8,128)(2,1)S(1)}, bf16[16,2048]{1,0:T(8,128)(2,1)S(1)}, u32[]{:S(2)}, u32[]{:S(2)}) collective-permute-start(bf16[16,2048]{1,0:T(8,128)(2,1)S(1)} %get-tuple-element.113), channel_id=1, source_target_pairs={{0,1},{1,0},{2,3},{3,2},{4,5},{5,4},{6,7},{7,6},{8,9},{9,8},{10,11... | collective-permute-start | bytes 196616 | tf_op jit(solution)/shard_map/ppermute | solution.py:56
  23.4 6.3 %collective-permute-start.3 = (bf16[16,2048]{1,0:T(8,128)(2,1)S(1)}, bf16[16,2048]{1,0:T(8,128)(2,1)S(1)}, u32[]{:S(2)}, u32[]{:S(2)}) collective-permute-start(bf16[16,2048]{1,0:T(8,128)(2,1)S(1)} %get-tuple-element.112), channel_id=1, source_target_pairs={{0,2},{1,3},{2,0},{3,1},{4,6},{5,7},{6,4},{7,5},{8,10},{9,11},{10,... | collective-permute-start | bytes 196616 | tf_op jit(solution)/shard_map/ppermute | solution.py:56
  25.9 6.6 %collective-permute-start.4 = (bf16[16,2048]{1,0:T(8,128)(2,1)S(1)}, bf16[16,2048]{1,0:T(8,128)(2,1)S(1)}, u32[]{:S(2)}, u32[]{:S(2)}) collective-permute-start(bf16[16,2048]{1,0:T(8,128)(2,1)S(1)} %get-tuple-element.111), channel_id=1, source_target_pairs={{0,3},{1,2},{2,1},{3,0},{4,7},{5,6},{6,5},{7,4},{8,11},{9,10},{10,... | collective-permute-start | bytes 196616 | tf_op jit(solution)/shard_map/ppermute | solution.py:56
  33.4 4.4 %collective-permute-start.5 = (bf16[16,2176]{1,0:T(8,128)(2,1)S(1)}, bf16[16,2176]{1,0:T(8,128)(2,1)S(1)}, u32[]{:S(2)}, u32[]{:S(2)}) collective-permute-start(bf16[16,2176]{1,0:T(8,128)(2,1)S(1)} %get-tuple-element.59.refs_0_), channel_id=1, source_target_pairs={{0,1},{1,0},{2,3},{3,2},{4,5},{5,4},{6,7},{7,6},{8,9},{9,8},{10,11... | collective-permute-start | bytes 208904 | tf_op jit(solution)/shard_map/ppermute | solution.py:56
  33.4 5.3 %collective-permute-start.6 = (bf16[16,2176]{1,0:T(8,128)(2,1)S(1)}, bf16[16,2176]{1,0:T(8,128)(2,1)S(1)}, u32[]{:S(2)}, u32[]{:S(2)}) collective-permute-start(bf16[16,2176]{1,0:T(8,128)(2,1)S(1)} %get-tuple-element.59.refs_0_), channel_id=1, source_target_pairs={{0,2},{1,3},{2,0},{3,1},{4,6},{5,7},{6,4},{7,5},{8,10},{9,11},{10,... | collective-permute-start | bytes 208904 | tf_op jit(solution)/shard_map/ppermute | solution.py:56
  34.2 6.7 %collective-permute-start.7 = (bf16[16,2176]{1,0:T(8,128)(2,1)S(1)}, bf16[16,2176]{1,0:T(8,128)(2,1)S(1)}, u32[]{:S(2)}, u32[]{:S(2)}) collective-permute-start(bf16[16,2176]{1,0:T(8,128)(2,1)S(1)} %get-tuple-element.59.refs_0_), channel_id=1, source_target_pairs={{0,3},{1,2},{2,1},{3,0},{4,7},{5,6},{6,5},{7,4},{8,11},{9,10},{10,... | collective-permute-start | bytes 208904 | tf_op jit(solution)/shard_map/ppermute | solution.py:56
  47.4 18.6 %collective-permute-start.13 = (s16[64,3072]{1,0:T(8,128)(2,1)S(1)}, s16[64,3072]{1,0:T(8,128)(2,1)S(1)}, u32[]{:S(2)}, u32[]{:S(2)}) collective-permute-start(s16[64,3072]{1,0:T(8,128)(2,1)S(1)} %get-tuple-element.68.refs_0_), channel_id=1, source_target_pairs={{4,0},{0,4},{5,1},{1,5},{6,2},{2,6},{7,3},{3,7},{12,8},{8,12},{13,... | collective-permute-start | bytes 1179656 | tf_op jit(solution)/shard_map/ppermute | solution.py:47
  49.0 15.4 %collective-permute-start.14 = (f32[64,128]{1,0:T(8,128)S(1)}, f32[64,128]{1,0:T(8,128)S(1)}, u32[]{:S(2)}, u32[]{:S(2)}) collective-permute-start(f32[64,128]{1,0:T(8,128)S(1)} %get-tuple-element.69.refs_2_), channel_id=1, source_target_pairs={{4,0},{0,4},{5,1},{1,5},{6,2},{2,6},{7,3},{3,7},{12,8},{8,12},{13,... | collective-permute-start | bytes 98312 | tf_op jit(solution)/shard_map/ppermute | solution.py:47
  49.5 22.4 %collective-permute-start.11 = (bf16[64,2048]{1,0:T(8,128)(2,1)S(1)}, bf16[64,2048]{1,0:T(8,128)(2,1)S(1)}, u32[]{:S(2)}, u32[]{:S(2)}) collective-permute-start(bf16[64,2048]{1,0:T(8,128)(2,1)S(1)} %get-tuple-element.97.refs_0_), channel_id=1, source_target_pairs={{0,16},{8,24},{16,0},{24,8},{1,17},{9,25},{17,1},{25,9},{2,18},{10... | collective-permute-start | bytes 786440 | tf_op jit(solution)/shard_map/ppermute | solution.py:56
  57.4 14.4 %collective-permute-start.10 = (s16[64,3072]{1,0:T(8,128)(2,1)S(1)}, s16[64,3072]{1,0:T(8,128)(2,1)S(1)}, u32[]{:S(2)}, u32[]{:S(2)}) collective-permute-start(s16[64,3072]{1,0:T(8,128)(2,1)S(1)} %get-tuple-element.65.refs_0_), channel_id=1, source_target_pairs={{4,0},{0,4},{5,1},{1,5},{6,2},{2,6},{7,3},{3,7},{12,8},{8,12},{13,... | collective-permute-start | bytes 1179656 | tf_op jit(solution)/shard_map/ppermute | solution.py:47
  59.0 12.8 %collective-permute-start.12 = (f32[64,128]{1,0:T(8,128)S(1)}, f32[64,128]{1,0:T(8,128)S(1)}, u32[]{:S(2)}, u32[]{:S(2)}) collective-permute-start(f32[64,128]{1,0:T(8,128)S(1)} %get-tuple-element.67.refs_2_), channel_id=1, source_target_pairs={{4,0},{0,4},{5,1},{1,5},{6,2},{2,6},{7,3},{3,7},{12,8},{8,12},{13,... | collective-permute-start | bytes 98312 | tf_op jit(solution)/shard_map/ppermute | solution.py:47
  64.4 13.0 %collective-permute-start.8 = (s16[64,2048]{1,0:T(8,128)(2,1)S(1)}, s16[64,2048]{1,0:T(8,128)(2,1)S(1)}, u32[]{:S(2)}, u32[]{:S(2)}) collective-permute-start(s16[64,2048]{1,0:T(8,128)(2,1)S(1)} %get-tuple-element.60.refs_0_), channel_id=1, source_target_pairs={{4,0},{0,4},{5,1},{1,5},{6,2},{2,6},{7,3},{3,7},{12,8},{8,12},{13,... | collective-permute-start | bytes 786440 | tf_op jit(solution)/shard_map/ppermute | solution.py:47
  66.0 11.4 %collective-permute-start.9 = (f32[64,128]{1,0:T(8,128)S(1)}, f32[64,128]{1,0:T(8,128)S(1)}, u32[]{:S(2)}, u32[]{:S(2)}) collective-permute-start(f32[64,128]{1,0:T(8,128)S(1)} %get-tuple-element.61.refs_2_), channel_id=1, source_target_pairs={{4,0},{0,4},{5,1},{1,5},{6,2},{2,6},{7,3},{3,7},{12,8},{8,12},{13,... | collective-permute-start | bytes 98312 | tf_op jit(solution)/shard_map/ppermute | solution.py:47
  78.0 8.4 %collective-permute-start.15 = (f32[64,128]{1,0:T(8,128)S(1)}, f32[64,128]{1,0:T(8,128)S(1)}, u32[]{:S(2)}, u32[]{:S(2)}) collective-permute-start(f32[64,128]{1,0:T(8,128)S(1)} %get-tuple-element.73.st_ref.refs_0_), channel_id=1, source_target_pairs={{0,1},{1,0},{2,3},{3,2},{4,5},{5,4},{6,7},{7,6},{8,9},{9,8},{10,11... | collective-permute-start | bytes 98312 | tf_op jit(solution)/shard_map/ppermute | solution.py:56
  78.0 8.3 %collective-permute-start.16 = (f32[64,128]{1,0:T(8,128)S(1)}, f32[64,128]{1,0:T(8,128)S(1)}, u32[]{:S(2)}, u32[]{:S(2)}) collective-permute-start(f32[64,128]{1,0:T(8,128)S(1)} %get-tuple-element.73.st_ref.refs_0_), channel_id=1, source_target_pairs={{0,2},{1,3},{2,0},{3,1},{4,6},{5,7},{6,4},{7,5},{8,10},{9,11},{10,... | collective-permute-start | bytes 98312 | tf_op jit(solution)/shard_map/ppermute | solution.py:56
  81.5 6.0 %collective-permute-start.17 = (f32[64,128]{1,0:T(8,128)S(1)}, f32[64,128]{1,0:T(8,128)S(1)}, u32[]{:S(2)}, u32[]{:S(2)}) collective-permute-start(f32[64,128]{1,0:T(8,128)S(1)} %get-tuple-element.73.st_ref.refs_0_), channel_id=1, source_target_pairs={{0,3},{1,2},{2,1},{3,0},{4,7},{5,6},{6,5},{7,4},{8,11},{9,10},{10,... | collective-permute-start | bytes 98312 | tf_op jit(solution)/shard_map/ppermute | solution.py:56
  82.4 56.4 %copy-start.1 = (bf16[1,64,2048]{2,1,0:T(8,128)(2,1)S(1)}, bf16[1,64,2048]{2,1,0:T(8,128)(2,1)}, u32[]{:S(2)}) copy-start(bf16[1,64,2048]{2,1,0:T(8,128)(2,1)} %param.14) | copy-start | bytes 786436
  88.4 32.2 %collective-permute-start.28 = (bf16[64,8192]{1,0:T(8,128)(2,1)S(1)}, bf16[64,8192]{1,0:T(8,128)(2,1)S(1)}, u32[]{:S(2)}, u32[]{:S(2)}) collective-permute-start(bf16[64,8192]{1,0:T(8,128)(2,1)S(1)} %logit_grad.1.refs_0_.refs_4_), channel_id=1, source_target_pairs={{0,16},{8,24},{16,0},{24,8},{1,17},{9,25},{17,1},{25,9},{2,18},{10... | collective-permute-start | bytes 3145736 | tf_op jit(solution)/shard_map/ppermute | solution.py:56
  88.7 4.5 %collective-permute-start.18 = (bf16[16,2048]{1,0:T(8,128)(2,1)S(1)}, bf16[16,2048]{1,0:T(8,128)(2,1)S(1)}, u32[]{:S(2)}, u32[]{:S(2)}) collective-permute-start(bf16[16,2048]{1,0:T(8,128)(2,1)S(1)} %get-tuple-element.110), channel_id=1, source_target_pairs={{0,1},{1,0},{2,3},{3,2},{4,5},{5,4},{6,7},{7,6},{8,9},{9,8},{10,11... | collective-permute-start | bytes 196616 | tf_op jit(solution)/shard_map/ppermute | solution.py:56
  88.8 5.3 %collective-permute-start.19 = (bf16[16,2048]{1,0:T(8,128)(2,1)S(1)}, bf16[16,2048]{1,0:T(8,128)(2,1)S(1)}, u32[]{:S(2)}, u32[]{:S(2)}) collective-permute-start(bf16[16,2048]{1,0:T(8,128)(2,1)S(1)} %get-tuple-element.109), channel_id=1, source_target_pairs={{0,2},{1,3},{2,0},{3,1},{4,6},{5,7},{6,4},{7,5},{8,10},{9,11},{10,... | collective-permute-start | bytes 196616 | tf_op jit(solution)/shard_map/ppermute | solution.py:56
  91.5 6.1 %collective-permute-start.20 = (bf16[16,2048]{1,0:T(8,128)(2,1)S(1)}, bf16[16,2048]{1,0:T(8,128)(2,1)S(1)}, u32[]{:S(2)}, u32[]{:S(2)}) collective-permute-start(bf16[16,2048]{1,0:T(8,128)(2,1)S(1)} %get-tuple-element.108), channel_id=1, source_target_pairs={{0,3},{1,2},{2,1},{3,0},{4,7},{5,6},{6,5},{7,4},{8,11},{9,10},{10,... | collective-permute-start | bytes 196616 | tf_op jit(solution)/shard_map/ppermute | solution.py:56
  97.7 3.7 %collective-permute-start.21 = (f32[16,128]{1,0:T(8,128)S(1)}, f32[16,128]{1,0:T(8,128)S(1)}, u32[]{:S(2)}, u32[]{:S(2)}) collective-permute-start(f32[16,128]{1,0:T(8,128)S(1)} %get-tuple-element.86.refs_0_), channel_id=1, source_target_pairs={{4,0},{0,4},{5,1},{1,5},{6,2},{2,6},{7,3},{3,7},{12,8},{8,12},{13,... | collective-permute-start | bytes 24584 | tf_op jit(solution)/shard_map/ppermute | solution.py:47
  101.4 4.3 %collective-permute-start.22 = (bf16[16,2048]{1,0:T(8,128)(2,1)S(1)}, bf16[16,2048]{1,0:T(8,128)(2,1)S(1)}, u32[]{:S(2)}, u32[]{:S(2)}) collective-permute-start(bf16[16,2048]{1,0:T(8,128)(2,1)S(1)} %mixed_grad.1.refs_0_), channel_id=1, source_target_pairs={{0,1},{1,0},{2,3},{3,2},{4,5},{5,4},{6,7},{7,6},{8,9},{9,8},{10,11... | collective-permute-start | bytes 196616 | tf_op jit(solution)/shard_map/ppermute | solution.py:56
  105.7 7.9 %collective-permute-start.25 = (bf16[64,2048]{1,0:T(8,128)(2,1)S(1)}, bf16[64,2048]{1,0:T(8,128)(2,1)S(1)}, u32[]{:S(2)}, u32[]{:S(2)}) collective-permute-start(bf16[64,2048]{1,0:T(8,128)(2,1)S(1)} %get-tuple-element.97.refs_0_), channel_id=1, source_target_pairs={{0,8},{8,0},{16,24},{24,16},{1,9},{9,1},{17,25},{25,17},{2,10},{10... | collective-permute-start | bytes 786440 | tf_op jit(solution)/shard_map/ppermute | solution.py:56
  105.7 7.9 %collective-permute-start.26 = (bf16[64,2048]{1,0:T(8,128)(2,1)S(1)}, bf16[64,2048]{1,0:T(8,128)(2,1)S(1)}, u32[]{:S(2)}, u32[]{:S(2)}) collective-permute-start(bf16[64,2048]{1,0:T(8,128)(2,1)S(1)} %collective-permute-done.11.refs_1_), channel_id=1, source_target_pairs={{0,8},{8,0},{16,24},{24,16},{1,9},{9,1},{17,25},{25,17},{2,10},{10... | collective-permute-start | bytes 786440 | tf_op jit(solution)/shard_map/ppermute | solution.py:56
  106.2 7.4 %collective-permute-start.23 = (bf16[16,2048]{1,0:T(8,128)(2,1)S(1)}, bf16[16,2048]{1,0:T(8,128)(2,1)S(1)}, u32[]{:S(2)}, u32[]{:S(2)}) collective-permute-start(bf16[16,2048]{1,0:T(8,128)(2,1)S(1)} %mixed_grad.1.refs_0_), channel_id=1, source_target_pairs={{0,2},{1,3},{2,0},{3,1},{4,6},{5,7},{6,4},{7,5},{8,10},{9,11},{10,... | collective-permute-start | bytes 196616 | tf_op jit(solution)/shard_map/ppermute | solution.py:56
  106.5 7.1 %collective-permute-start.24 = (bf16[16,2048]{1,0:T(8,128)(2,1)S(1)}, bf16[16,2048]{1,0:T(8,128)(2,1)S(1)}, u32[]{:S(2)}, u32[]{:S(2)}) collective-permute-start(bf16[16,2048]{1,0:T(8,128)(2,1)S(1)} %mixed_grad.1.refs_0_), channel_id=1, source_target_pairs={{0,3},{1,2},{2,1},{3,0},{4,7},{5,6},{6,5},{7,4},{8,11},{9,10},{10,... | collective-permute-start | bytes 196616 | tf_op jit(solution)/shard_map/ppermute | solution.py:56
  115.5 5.1 %collective-permute-start.27 = (bf16[64,1024]{1,0:T(8,128)(2,1)S(1)}, bf16[64,1024]{1,0:T(8,128)(2,1)S(1)}, u32[]{:S(2)}, u32[]{:S(2)}) collective-permute-start(bf16[64,1024]{1,0:T(8,128)(2,1)S(1)} %back_project.1.refs_0_), channel_id=1, source_target_pairs={{4,0},{0,4},{5,1},{1,5},{6,2},{2,6},{7,3},{3,7},{12,8},{8,12},{13,... | collective-permute-start | bytes 393224 | tf_op jit(solution)/shard_map/ppermute | solution.py:47
  117.1 6.1 %collective-permute-start.29 = (bf16[64,8192]{1,0:T(8,128)(2,1)S(1)}, bf16[64,8192]{1,0:T(8,128)(2,1)S(1)}, u32[]{:S(2)}, u32[]{:S(2)}) collective-permute-start(bf16[64,8192]{1,0:T(8,128)(2,1)S(1)} %logit_grad.1.refs_0_.refs_4_), channel_id=1, source_target_pairs={{0,8},{8,0},{16,24},{24,16},{1,9},{9,1},{17,25},{25,17},{2,10},{10... | collective-permute-start | bytes 3145736 | tf_op jit(solution)/shard_map/ppermute | solution.py:56
  120.6 2.7 %collective-permute-start.30 = (bf16[64,8192]{1,0:T(8,128)(2,1)S(1)}, bf16[64,8192]{1,0:T(8,128)(2,1)S(1)}, u32[]{:S(2)}, u32[]{:S(2)}) collective-permute-start(bf16[64,8192]{1,0:T(8,128)(2,1)S(1)} %collective-permute-done.28.refs_1_.refs_5_), channel_id=1, source_target_pairs={{0,8},{8,0},{16,24},{24,16},{1,9},{9,1},{17,25},{25,17},{2,10},{10... | collective-permute-start | bytes 3145736 | tf_op jit(solution)/shard_map/ppermute | solution.py:56
  (11 other events, 154.4 us)

commit v6 on v4

--- a/solution.py
+++ b/solution.py
@@ -16,6 +16,8 @@
 GROUPS = 1
 LOW = -1e30
 CODE_TOP = 32767.0
+LOG_STEPS = 256.0
+FINE_STEPS = 1e7
 
 zloss_weight = 0.0001
 norm_epsilon = 1e-06
@@ -64,9 +66,7 @@
     return lax.ppermute(x, axis, [(i, i ^ bit) for i in range(n)])
 
 
-def gather_swaps(x, axis):
-    held = [x]
-    bit = lax.axis_size(axis) // 2
+def spread(held, axis, bit):
     while bit:
         held = held + [swap(h, axis, bit) for h in held]
         bit //= 2
@@ -93,7 +93,7 @@
 
 def attend_kernel(n_seq, scal, *refs):
     q_refs = refs[:n_seq]
-    tgt_ref, k_ref, v_ref, o_ref, q_out, q_twice, t_twice = refs[n_seq:]
+    k_ref, v_ref, o_ref, q_out, q_twice, t_twice = refs[n_seq:]
     tgt_rows = q_refs[0].shape[1]
     rows = tgt_rows * n_seq
     enc, features = k_ref.shape[1:]
@@ -104,14 +104,13 @@
     q_out[...] = q
     valid = lax.broadcasted_iota(i32, (rows, enc), 1) < scal[1]
     lane = lanes(rows)
-    corner = (tgt_rows, tgt_rows)
-    same = lax.broadcasted_iota(i32, corner, 0) == lax.broadcasted_iota(i32, corner, 1)
     here = lanes(tgt_rows)
-    digits = jnp.zeros((tgt_rows, LANES), f32)
-    ids = jnp.broadcast_to(tgt_ref[...], corner)
-    for at, digit in ((LANES - 2, ids >> 8), (LANES - 1, ids & 255)):
-        column = jnp.sum(jnp.where(same, digit.astype(f32), 0.0), axis=1, keepdims=True)
-        digits = jnp.where(here == at, column, digits)
+    row = lax.broadcasted_iota(i32, here.shape, 0)
+    ids = jnp.zeros(here.shape, i32)
+    for i in range(tgt_rows):
+        ids = jnp.where(row == i, scal[3 + i], ids)
+    digits = jnp.where(here == LANES - 2, ids >> 8, jnp.where(here == LANES - 1, ids & 255, 0))
+    digits = digits.astype(f32)
     t_twice[...] = jnp.zeros_like(t_twice)
     t_twice[:tgt_rows, :] = digits
     t_twice[rows : rows + tgt_rows, :] = digits
@@ -170,13 +169,13 @@
 
 def norm_kernel(n_got, *refs):
     own_ref, got_refs = refs[0], refs[1 : 1 + n_got]
-    residual_ref, gain_ref, mixed_ref, ng_ref = refs[1 + n_got :]
+    packed_ref, mixed_ref, ng_ref = refs[1 + n_got :]
     rows, width = mixed_ref.shape
-    mixed = own_ref[...] + residual_ref[...].astype(f32)
+    mixed = own_ref[...] + packed_ref[:rows, :]
     for r in got_refs:
         mixed = mixed + r[...].astype(f32)
     mixed_ref[...] = mixed
-    ng_ref[:, :width] = (mixed * gain_ref[...]).astype(bf16)
+    ng_ref[:, :width] = (mixed * packed_ref[rows : rows + 1, :]).astype(bf16)
     square = jnp.sum(mixed * mixed, axis=1, keepdims=True)
     lane = lanes(rows)
     stat = jnp.zeros((rows, LANES), f32)
@@ -218,31 +217,48 @@
 def logits_kernel(first, cols, n_vocab, *refs):
     ng_refs, (w_ref, edge_ref) = refs[:n_vocab], refs[n_vocab : n_vocab + 2]
     outs = refs[n_vocab + 2 :]
-    code_ref, stat_ref = outs[:2]
+    code_ref = outs[0]
     z, buf, sems = outs[-3:]
     width = buf.shape[1]
     copies = start_weights(first, cols, w_ref, edge_ref, buf, sems)
     ng = jnp.concatenate([r[...] for r in ng_refs], axis=0)
-    if len(outs) > 5:
-        outs[2][...] = ng[:, :width]
+    if len(outs) > 4:
+        outs[1][...] = ng[:, :width]
     for t in range(z.shape[1] // TILE):
         wait_tile(copies, t)
         at = slice(t * TILE, (t + 1) * TILE)
-        z[:, at] = dot(buf[at, :], ng[:, :width], 1, 1).T
+        z[:, at] = dot(ng[:, :width], buf[at, :], 1, 1)
     val = z[...]
     peak = jnp.maximum(jnp.max(jnp.abs(val), axis=1, keepdims=True), 1e-30)
-    code_ref[...] = jnp.round(val * (CODE_TOP / peak)).astype(i32).astype(jnp.int16)
     s = ng[:, width:].astype(f32)
-    square = s[:, 0:1] + s[:, 1:2] + s[:, 2:3]
+    square = jnp.maximum(s[:, 0:1] + s[:, 1:2] + s[:, 2:3], 1e-30)
+    mark = jnp.floor(jnp.log(peak) * LOG_STEPS) + 2.0
+    coarse = jnp.round(jnp.log(square) * LOG_STEPS)
+    fine = jnp.round((square / jnp.exp(coarse / LOG_STEPS) - 1.0) * FINE_STEPS)
+    size = z.shape[1]
+    code = jnp.round(val / code_step(mark))
+    code_ref[:, :size] = code.astype(i32).astype(jnp.int16)
     lane = lanes(z.shape[0])
-    stat_ref[...] = jnp.where(lane == 0, peak / CODE_TOP, jnp.where(lane == 1, square, 0.0))
+    stat = jnp.where(lane == 0, mark, jnp.where(lane == 1, coarse, jnp.where(lane == 2, fine, 0.0)))
+    code_ref[:, size:] = stat.astype(i32).astype(jnp.int16)
+
+
+def code_step(mark):
+    return jnp.exp(mark / LOG_STEPS) / CODE_TOP
+
+
+def decode(code_ref, size):
+    stat = code_ref[:, size:].astype(i32).astype(f32)
+    square = jnp.exp(stat[:, 1:2] / LOG_STEPS) * (1.0 + stat[:, 2:3] / FINE_STEPS)
+    return code_ref[:, :size].astype(i32).astype(f32) * code_step(stat[:, 0:1]), square
 
 
 def exp_rows(chunk, first, cols, n_seq, features, refs, e_ref, st_ref, lhs):
-    code_refs, sc_refs, tgt_ref = refs[:n_seq], refs[n_seq : 2 * n_seq], refs[2 * n_seq]
+    tgt_ref = refs[n_seq]
     rows, size = e_ref.shape
-    z = tree([c[...].astype(i32).astype(f32) * s[:, 0:1] for c, s in zip(code_refs, sc_refs)])
-    square = tree([s[:, 1:2] for s in sc_refs])
+    members = [decode(r, size) for r in refs[:n_seq]]
+    z = tree([m[0] for m in members])
+    square = tree([m[1] for m in members])
     inv = lax.rsqrt(square / features + norm_epsilon)
     z = z * inv
     at = first + lax.broadcasted_iota(i32, (rows, size), 1)
@@ -253,7 +269,7 @@
     here = jnp.sum(jnp.where(hit, z, 0.0), axis=1, keepdims=True)
     peak = jnp.max(z, axis=1, keepdims=True)
     if chunk:
-        old = refs[2 * n_seq + 1][...]
+        old = refs[n_seq + 1][...]
         peak = jnp.maximum(peak, old[:, 0:1])
         fade = jnp.exp(old[:, 0:1] - peak)
     else:
@@ -290,7 +306,7 @@
 
 
 def hidden_kernel(chunk, first, cols, n_seq, features, *refs):
-    n = 2 * n_seq + 1 + (1 if chunk else 0)
+    n = n_seq + 1 + (1 if chunk else 0)
     ins, refs = refs[:n], refs[n:]
     acc_prev = None
     if chunk:
@@ -363,17 +379,9 @@
     last[:, size - LANES :] = stat.astype(bf16)
 
 
-def loss_kernel(rows_all, *refs):
-    sums = []
-    for r in refs[:-1]:
-        s = r[...].astype(f32)
-        sums.append(jnp.sum(s[:, -3:-2] + s[:, -2:-1] + s[:, -1:], axis=0, keepdims=True))
-    refs[-1][...] = jnp.broadcast_to(tree(sums) / rows_all, refs[-1].shape)
-
-
-def head_kernel(n_dp, *refs):
+def head_kernel(n_dp, rows_all, *refs):
     ng_refs, g_refs = refs[:n_dp], refs[n_dp : 2 * n_dp]
-    out_ref, ng, turned = refs[-3:]
+    out_ref, loss_ref, ng, turned = refs[-4:]
     rows, width = ng_refs[0].shape[0], out_ref.shape[1]
 
     @pl.when(pl.program_id(0) == 0)
@@ -385,14 +393,23 @@
     for at in range(0, width, 256):
         out_ref[:, at : at + 256] = dot(turned[...], ng[:, at : at + 256], 1, 0).astype(bf16)
 
+    @pl.when(pl.program_id(0) == pl.num_programs(0) - 1)
+    def _():
+        sums = []
+        for r in g_refs:
+            s = r[:, HEAD_TILE - LANES :].astype(f32)
+            sums.append(jnp.sum(s[:, -3:-2] + s[:, -2:-1] + s[:, -1:]))
+        loss_ref[0, 0] = tree(sums) * (1.0 / rows_all)
+
 
 def gate_kernel(n_got, *refs):
     own_ref, got_refs = refs[0], refs[1 : 1 + n_got]
-    mixed_ref, gain_ref, gated_ref, dot_ref = refs[1 + n_got :]
+    mixed_ref, packed_ref, gated_ref, dot_ref = refs[1 + n_got :]
     total = own_ref[...]
     for r in got_refs:
         total = total + r[...].astype(f32)
-    gated = total * gain_ref[...]
+    rows = mixed_ref.shape[0]
+    gated = total * packed_ref[rows : rows + 1, :]
     gated_ref[...] = gated
     inner = jnp.sum(gated * mixed_ref[...], axis=1, keepdims=True)
     dot_ref[...] = jnp.broadcast_to(inner, dot_ref.shape)
@@ -452,13 +469,15 @@
 
     start = lax.rem(voc * own_rows - seq * tgt_rows + rows, rows).astype(i32)
     scal = jnp.stack([start, enc_lengths[0] - seq * enc, voc * cols]).astype(i32)
+    scal = jnp.concatenate([scal, targets[0]])
 
     q_parts = gather_ring(queries, "seq")
-    res_own = lax.dynamic_slice(residual[0], (voc * own_rows, 0), (own_rows, width))
+    res_own = lax.dynamic_slice(residual[0], (voc * own_rows, 0), (own_rows, width)).astype(f32)
+    packed = jnp.concatenate([res_own, jnp.broadcast_to(gain, (8, width))], axis=0)
     o_part, q_all = pl.pallas_call(
         functools.partial(attend_kernel, n_seq),
         out_shape=[sds((rows, features + LANES), bf16), sds((rows, features), bf16)],
-        in_specs=[SMEM] + [VMEM] * (n_seq + 3),
+        in_specs=[SMEM] + [VMEM] * (n_seq + 2),
         out_specs=[VMEM, VMEM],
         scratch_shapes=[
             pltpu.VMEM((2 * rows, features), bf16),
@@ -467,7 +486,7 @@
         compiler_params=params(),
         cost_estimate=cost(0, 7 * 1024 * 1024),
         name="attend",
-    )(scal, *q_parts, targets, enc_keys, enc_values)
+    )(scal, *q_parts, enc_keys, enc_values)
 
     o_all = gather_ring(o_part, "seq")
     ptile = min(TILE, width)
@@ -497,12 +516,12 @@
     mixed, ng_own = pl.pallas_call(
         functools.partial(norm_kernel, len(got)),
         out_shape=[sds((own_rows, width), f32), sds((own_rows, width + LANES), bf16)],
-        in_specs=[VMEM] * (3 + len(got)),
+        in_specs=[VMEM] * (2 + len(got)),
         out_specs=[VMEM, VMEM],
         compiler_params=params(),
         cost_estimate=cost(0, 7 * 1024 * 1024),
         name="norm",
-    )(mixed_own, *got, res_own, gain)
+    )(mixed_own, *got, packed)
     ng_parts = gather_ring(ng_own, "vocab")
 
     last_part = pl.BlockSpec((PART, width), lambda j: (-(-cols // PART) - 1, 0))
@@ -513,13 +532,13 @@
         return [pl.BlockSpec(x.shape, lambda j: (0, 0)) for x in shapes]
 
     weights = [weight, weight]
-    codes, stats = [], []
+    codes = []
     for c, (tile0, n) in enumerate(chunks):
         size = n * TILE
         odd = tile0 * TILE + size > cols and cols % 16 != 0
         edge = last_part if odd else anywhere
         stacked = [] if c else [sds((rows, width), bf16)]
-        shapes = [sds((rows, size), jnp.int16), sds((rows, LANES), f32)] + stacked
+        shapes = [sds((rows, size + LANES), jnp.int16)] + stacked
         outs = pl.pallas_call(
             functools.partial(logits_kernel, tile0 * TILE, cols, n_vocab),
             grid=(1,) if odd else (),
@@ -536,12 +555,10 @@
             name="logits",
         )(*ng_parts, *weights)
         codes.append(gather_ring(outs[0], "seq"))
-        stats.append(gather_ring(outs[1], "seq"))
         if stacked:
-            ng_dp = gather_swaps(outs[2], "dp")
-
-    if len(chunks) > 1:
-        codes[1], ng_dp = lax.optimization_barrier((codes[1], ng_dp))
+            ng_dp = [outs[1]] + ([swap(outs[1], "dp", n_dp // 2)] if n_dp > 1 else [])
+
+    codes[-1], ng_dp = lax.optimization_barrier((codes[-1], ng_dp))
     acc = st = None
     exps = []
     for c, (tile0, n) in enumerate(chunks):
@@ -557,7 +574,7 @@
             pltpu.SemaphoreType.DMA((size // PART,)),
         ]
         prev = [st] if c else []
-        ins = [*codes[c], *stats[c], tgt, *prev]
+        ins = [*codes[c], tgt, *prev]
         if c == 0 or c < len(chunks) - 1:
             acc, e, st = pl.pallas_call(
                 functools.partial(hidden_kernel, c, first, cols, n_seq, full_width),
@@ -609,9 +626,6 @@
         cost_estimate=cost(0, 7 * 1024 * 1024),
         name="total",
     )(*st_all, acc)
-    got = scatter_ring(hidden_part, "vocab", own_rows)
-    got, coef_later = lax.optimization_barrier((got, coef))
-
     group = tiles * TILE // GROUPS
     assert cols + 3 <= tiles * TILE and group % HEAD_TILE == 0
     grads = pl.pallas_call(
@@ -622,7 +636,9 @@
         compiler_params=params(),
         cost_estimate=cost(0, 7 * 1024 * 1024),
         name="logit_grad",
-    )(coef_later, tgt, *exps)
+    )(coef, tgt, *exps)
+    hidden_part, grads = lax.optimization_barrier((hidden_part, grads))
+    got = scatter_ring(hidden_part, "vocab", own_rows)
     bit = n_dp // 2
     across = [swap(g, "dp", bit) for g in grads] if bit else []
     gated, inner = pl.pallas_call(
@@ -633,7 +649,7 @@
         compiler_params=params(),
         cost_estimate=cost(0, 7 * 1024 * 1024),
         name="gate",
-    )(hidden_own, *got, mixed, gain)
+    )(hidden_own, *got, mixed, packed)
     inner_all = gather_ring(inner, "seq")
     mixed_grad = pl.pallas_call(
         functools.partial(mixed_grad_kernel, n_seq, full_width),
@@ -658,15 +674,13 @@
         cost_estimate=cost(0, 7 * 1024 * 1024),
         name="back_project",
     )(*mg_parts, out_proj)
+    back_part, ng_dp = lax.optimization_barrier((back_part, ng_dp))
     back_all = gather_ring(back_part, "seq")
+    ng_dp = spread(ng_dp, "dp", n_dp // 4)
     back_all, across = lax.optimization_barrier((back_all, across))
     grads_dp = []
     for i, g in enumerate(grads):
-        held, bit = ([g, across[i]] if across else [g]), n_dp // 4
-        while bit:
-            held = held + [swap(h, "dp", bit) for h in held]
-            bit //= 2
-        grads_dp.append(held)
+        grads_dp.append(spread([g, across[i]] if across else [g], "dp", n_dp // 4))
     key_grad, value_grad = pl.pallas_call(
         functools.partial(attend_back_kernel, n_seq),
         out_shape=[sds(enc_keys.shape, f32), sds(enc_values.shape, f32)],
@@ -677,30 +691,21 @@
         name="attend_back",
     )(scal, *back_all, q_all, enc_keys, enc_values, att, lse)
 
-    loss = pl.pallas_call(
-        functools.partial(loss_kernel, n_dp * rows),
-        grid=(1,),
-        out_shape=sds((8, LANES), f32),
-        in_specs=[pl.BlockSpec((rows, LANES), lambda j: (0, group // LANES - 1))] * n_dp,
-        out_specs=whole((8, LANES)),
-        compiler_params=params(),
-        cost_estimate=cost(0, 7 * 1024 * 1024),
-        name="loss",
-    )(*grads_dp[-1])
-    mean_loss = loss[0, 0]
-
     head = None
     for c in range(GROUPS):
         prev = [head] if c else []
         steps = group // HEAD_TILE
-        head = pl.pallas_call(
-            functools.partial(head_kernel, n_dp),
+        head, loss = pl.pallas_call(
+            functools.partial(head_kernel, n_dp, n_dp * rows),
             grid=(steps,),
-            out_shape=sds((cols, width), bf16),
+            out_shape=[sds((cols, width), bf16), sds((1, 1), f32)],
             in_specs=[whole((rows, width))] * n_dp
             + [pl.BlockSpec((rows, HEAD_TILE), lambda j: (0, j))] * n_dp
             + [anywhere] * len(prev),
-            out_specs=pl.BlockSpec((HEAD_TILE, width), lambda j, t=c * steps: (t + j, 0)),
+            out_specs=[
+                pl.BlockSpec((HEAD_TILE, width), lambda j, t=c * steps: (t + j, 0)),
+                SMEM,
+            ],
             scratch_shapes=[
                 pltpu.VMEM((n_dp * rows, width), bf16),
                 pltpu.VMEM((HEAD_TILE, n_dp * rows), bf16),
@@ -710,7 +715,7 @@
             cost_estimate=cost(2 * n_dp * rows * width * group, 2 * width * group),
             name="head_grad",
         )(*ng_dp, *grads_dp[c], *prev)
-    return (mean_loss, head.T, key_grad, value_grad)
+    return (loss.reshape(()), head.T, key_grad, value_grad)
 
 
 def solution(mesh):

time: 145 us -> 131 us (0.903)
  Pallas kernels: 65.8 us -> 58.6 us
  waiting for transfers between devices: 32.7 us -> 26.7 us
  other arithmetic: 0.08 us -> 1.6 us
    pallas_call x3, Pallas kernels: 25.8 us -> 17.9 us  [body(): pl.pallas_call(functools.partial(logits_kernel, tile0 * TILE, cols, n_voc...]
    ppermute x6, waiting for transfers between devices: 3.9 us -> 0.26 us  [swap(): return lax.ppermute(x, axis, [(i, i ^ bit) for i in range(n)])]
    ppermute x6, waiting for transfers between devices: 7.23 us -> 4.98 us  [scatter_ring(): lax.ppermute(x[k * rows:(k + 1) * rows], axis, [(i, (i + k) % n) for i in...]
    ppermute x19 -> x16, starting transfers between devices: 24.2 us -> 22.4 us  [from_ahead(): return lax.ppermute(x, axis, [((i + k) % n, i) for i in range(n)])]
    unnamed x24 -> x14, local copies, waits for them, and re-layouts: 6.31 us -> 4.94 us
    pallas_call x2 -> x1, Pallas kernels: 14.8 us -> 14.9 us  [body(): pl.pallas_call(functools.partial(head_kernel, n_dp, n_dp * rows), grid=(s...]
    ppermute x19 -> x16, waiting for transfers between devices: 21.5 us -> 21.5 us  [from_ahead(): return lax.ppermute(x, axis, [((i + k) % n, i) for i in range(n)])]
  transfers between devices with their start and end apart: 31 -> 28, of which waited for: 16 -> 17; matrix products, arithmetic and copies ran while one was open for 0% -> 2% of each run, Pallas kernels for 25% -> 20%
where the time goes in v6:
time: 131 us; the launch traced here: 130 us
  Pallas kernels  58.6 us (45%)
  starting transfers between devices  36.2 us (28%)
  waiting for transfers between devices  26.7 us (20%)
  local copies, waits for them, and re-layouts  5.67 us (4%)
  other arithmetic  1.6 us (1%)
  between operations  1.46 us (1%)
    ppermute x16, starting transfers between devices, from_ahead(): return lax.ppermute(x, axis, [((i + k) % n, i) for i in range(n)])  22.4 us
    ppermute x16, waiting for transfers between devices, from_ahead(): return lax.ppermute(x, axis, [((i + k) % n, i) for i in range(n)])  21.5 us
    pallas_call x3, Pallas kernels, body(): pl.pallas_call(functools.partial(logits_kernel, tile0 * TILE, cols, n_voc...  17.9 us
    pallas_call x1, Pallas kernels, body(): pl.pallas_call(functools.partial(head_kernel, n_dp, n_dp * rows), grid=(s...  14.9 us
    pallas_call x2, Pallas kernels, body(): pl.pallas_call(functools.partial(hidden_kernel, c, first, cols, n_seq, fu...  11.3 us
    ppermute x6, starting transfers between devices, scatter_ring(): lax.ppermute(x[k * rows:(k + 1) * rows], axis, [(i, (i + k) % n) for i in...  10.8 us
    ppermute x6, waiting for transfers between devices, scatter_ring(): lax.ppermute(x[k * rows:(k + 1) * rows], axis, [(i, (i + k) % n) for i in...  4.98 us
    unnamed x14, local copies, waits for them, and re-layouts  4.94 us
  transfers between devices with their start and end apart: 28, of which 17 were waited for; matrix products, arithmetic and copies ran while one was open for 2% of the time, Pallas kernels for 20%

profile of v6, /device:TPU:0, one launch (start us, length us, event | category | flops | bytes accessed | tf_op | source)
XLA Modules:
  0.0 130.3 jit_solution(6602344203925312535)
XLA Ops:
  0.6 3.0 %collective-permute-start = (bf16[1,32,1024]{2,1,0:T(8,128)(2,1)}, bf16[1,32,1024]{2,1,0:T(8,128)(2,1)S(1)}, u32[]{:S(2)}, u32[]{:S(2)}) collective-permute-start(bf16[1,32,1024]{2,1,0:T(8,128)(2,1)} %refs_0_.1), channel_id=1, source_target_pairs={{4,0},{0,4},{5,1},{1,5},{6,2},{2,6},{7,3},{3,7},{12,8},{8,12},{13,... | collective-permute-start | bytes 196616 | tf_op jit(solution)/shard_map/ppermute | solution.py:49
  8.9 1.6 %attend.1 = (bf16[64,1152]{1,0:T(8,128)(2,1)S(1)}, bf16[64,1024]{1,0:T(8,128)(2,1)S(1)}) custom-call(s32[35]{0:T(128)S(1)} %pad_add_fusion.scal, bf16[1,32,1024]{2,1,0:T(8,128)(2,1)S(1)} %copy-done.6, bf16[1,32,1024]{2,1,0:T(8,128)(2,1)S(1)} %collective-permute-done.refs_1_, bf16[1,128,1024]{2,1,0:T(8,128)(2,1)S(1)} %copy-done.2, ...), custom_call_target="tpu_custom_call" | custom-call | bytes 7340032 | tf_op jit(solution)/shard_map/attend/pallas_call | solution.py:477
  10.5 2.1 %collective-permute-start.1 = (bf16[64,1152]{1,0:T(8,128)(2,1)S(1)}, bf16[64,1152]{1,0:T(8,128)(2,1)S(1)}, u32[]{:S(2)}, u32[]{:S(2)}) collective-permute-start(bf16[64,1152]{1,0:T(8,128)(2,1)S(1)} %get-tuple-element.45.refs_0_), channel_id=1, source_target_pairs={{4,0},{0,4},{5,1},{1,5},{6,2},{2,6},{7,3},{3,7},{12,8},{8,12},{13,... | collective-permute-start | bytes 442376 | tf_op jit(solution)/shard_map/ppermute | solution.py:49
  13.4 2.3 %collective-permute-done.1.refs_1_ = bf16[64,1152]{1,0:T(8,128)(2,1)S(1)} collective-permute-done((bf16[64,1152]{1,0:T(8,128)(2,1)S(1)}, bf16[64,1152]{1,0:T(8,128)(2,1)S(1)}, u32[]{:S(2)}, u32[]{:S(2)}) %collective-permute-start.1) | collective-permute-done | bytes 147488 | tf_op jit(solution)/shard_map/ppermute | solution.py:49
  15.7 2.2 %copy-done = bf16[1024,2048]{1,0:T(8,128)(2,1)S(1)} copy-done((bf16[1024,2048]{1,0:T(8,128)(2,1)S(1)}, bf16[1024,2048]{1,0:T(8,128)(2,1)}, u32[]{:S(2)}) %copy-start) | copy-done | bytes 4194328
  17.9 2.6 %project.1 = (bf16[64,2048]{1,0:T(8,128)(2,1)S(1)}, f32[16,2048]{1,0:T(8,128)S(1)}, bf16[64,1024]{1,0:T(8,128)(2,1)S(1)}, f32[64,128]{1,0:T(8,128)S(1)}, s32[64,128]{1,0:T(8,128)S(1)}) custom-call(s32[35]{0:T(128)S(1)} %pad_add_fusion.scal, bf16[64,1152]{1,0:T(8,128)(2,1)S(1)} %get-tuple-element.45.refs_0_, ...), custom_call_target="tpu_custom_call" | custom-call | bytes 7340032 | tf_op jit(solution)/shard_map/project/pallas_call | solution.py:495
  20.5 2.1 %collective-permute-start.2 = (bf16[16,2048]{1,0:T(8,128)(2,1)S(1)}, bf16[16,2048]{1,0:T(8,128)(2,1)S(1)}, u32[]{:S(2)}, u32[]{:S(2)}) collective-permute-start(bf16[16,2048]{1,0:T(8,128)(2,1)S(1)} %get-tuple-element.91), channel_id=1, source_target_pairs={{0,1},{1,2},{2,3},{3,0},{4,5},{5,6},{6,7},{7,4},{8,9},{9,10},{10,1... | collective-permute-start | bytes 196616 | tf_op jit(solution)/shard_map/ppermute | solution.py:59
  22.7 2.6 %collective-permute-start.3 = (bf16[16,2048]{1,0:T(8,128)(2,1)S(1)}, bf16[16,2048]{1,0:T(8,128)(2,1)S(1)}, u32[]{:S(2)}, u32[]{:S(2)}) collective-permute-start(bf16[16,2048]{1,0:T(8,128)(2,1)S(1)} %get-tuple-element.90), channel_id=1, source_target_pairs={{0,2},{1,3},{2,0},{3,1},{4,6},{5,7},{6,4},{7,5},{8,10},{9,11},{10,... | collective-permute-start | bytes 196616 | tf_op jit(solution)/shard_map/ppermute | solution.py:59
  27.8 1.7 %collective-permute-done.4.refs_3_ = bf16[16,2048]{1,0:T(8,128)(2,1)S(1)} collective-permute-done((bf16[16,2048]{1,0:T(8,128)(2,1)S(1)}, bf16[16,2048]{1,0:T(8,128)(2,1)S(1)}, u32[]{:S(2)}, u32[]{:S(2)}) %collective-permute-start.4) | collective-permute-done | bytes 65568 | tf_op jit(solution)/shard_map/ppermute | solution.py:59
  29.6 3.2 %collective-permute-start.5 = (bf16[16,2176]{1,0:T(8,128)(2,1)S(1)}, bf16[16,2176]{1,0:T(8,128)(2,1)S(1)}, u32[]{:S(2)}, u32[]{:S(2)}) collective-permute-start(bf16[16,2176]{1,0:T(8,128)(2,1)S(1)} %get-tuple-element.48.refs_0_), channel_id=1, source_target_pairs={{1,0},{2,1},{3,2},{0,3},{5,4},{6,5},{7,6},{4,7},{9,8},{10,9},{11,1... | collective-permute-start | bytes 208904 | tf_op jit(solution)/shard_map/ppermute | solution.py:49
  34.7 3.3 %collective-permute-done.6.refs_2_ = bf16[16,2176]{1,0:T(8,128)(2,1)S(1)} collective-permute-done((bf16[16,2176]{1,0:T(8,128)(2,1)S(1)}, bf16[16,2176]{1,0:T(8,128)(2,1)S(1)}, u32[]{:S(2)}, u32[]{:S(2)}) %collective-permute-start.6) | collective-permute-done | bytes 69664 | tf_op jit(solution)/shard_map/ppermute | solution.py:49
  38.9 6.5 %logits.4 = (s16[64,3200]{1,0:T(8,128)(2,1)S(1)}, bf16[64,2048]{1,0:T(8,128)(2,1)S(1)}) custom-call(bf16[16,2176]{1,0:T(8,128)(2,1)S(1)} %get-tuple-element.48.refs_0_, bf16[16,2176]{1,0:T(8,128)(2,1)S(1)} %collective-permute-done.5.refs_1_, bf16[16,2176]{1,0:T(8,128)(2,1)S(1)} %collective-permute-done.6.refs_2_, ...), custom_call_target="tpu_custom_call" | custom-call | flops 3221225472 | bytes 12582912 | tf_op jit(solution)/shard_map/logits/pallas_call | solution.py:542
  45.4 1.6 %collective-permute-start.11 = (s16[64,3200]{1,0:T(8,128)(2,1)S(1)}, s16[64,3200]{1,0:T(8,128)(2,1)S(1)}, u32[]{:S(2)}, u32[]{:S(2)}) collective-permute-start(s16[64,3200]{1,0:T(8,128)(2,1)S(1)} %get-tuple-element.53.refs_0_), channel_id=1, source_target_pairs={{4,0},{0,4},{5,1},{1,5},{6,2},{2,6},{7,3},{3,7},{12,8},{8,12},{13,... | collective-permute-start | bytes 1228808 | tf_op jit(solution)/shard_map/ppermute | solution.py:49
  47.0 1.5 %collective-permute-start.9 = (bf16[64,2048]{1,0:T(8,128)(2,1)S(1)}, bf16[64,2048]{1,0:T(8,128)(2,1)S(1)}, u32[]{:S(2)}, u32[]{:S(2)}) collective-permute-start(bf16[64,2048]{1,0:T(8,128)(2,1)S(1)} %get-tuple-element.72.refs_0_), channel_id=1, source_target_pairs={{0,16},{8,24},{16,0},{24,8},{1,17},{9,25},{17,1},{25,9},{2,18},{10... | collective-permute-start | bytes 786440 | tf_op jit(solution)/shard_map/ppermute | solution.py:66
  48.5 4.9 %logits.3.refs_0_ = s16[64,2176]{1,0:T(8,128)(2,1)S(1)} custom-call(bf16[16,2176]{1,0:T(8,128)(2,1)S(1)} %get-tuple-element.48.refs_0_, bf16[16,2176]{1,0:T(8,128)(2,1)S(1)} %collective-permute-done.5.refs_1_, bf16[16,2176]{1,0:T(8,128)(2,1)S(1)} %collective-permute-done.6.refs_2_, bf16[16,2176]{1,0:T(8,128)(2,1)S(1)} %collective-permute-done.7.refs_3_, ...), custom_call_target="tpu_custom_call" | custom-call | flops 2147483648 | bytes 8388608 | tf_op jit(solution)/shard_map/logits/pallas_call | solution.py:542
  53.9 6.5 %logits.5.refs_0_ = s16[64,3200]{1,0:T(8,128)(2,1)S(1)} custom-call(bf16[16,2176]{1,0:T(8,128)(2,1)S(1)} %get-tuple-element.48.refs_0_, bf16[16,2176]{1,0:T(8,128)(2,1)S(1)} %collective-permute-done.5.refs_1_, bf16[16,2176]{1,0:T(8,128)(2,1)S(1)} %collective-permute-done.6.refs_2_, bf16[16,2176]{1,0:T(8,128)(2,1)S(1)} %collective-permute-done.7.refs_3_, ...), custom_call_target="tpu_custom_call" | custom-call | flops 3221225472 | bytes 12582912 | tf_op jit(solution)/shard_map/logits/pallas_call | solution.py:542
  60.4 1.6 %collective-permute-start.10 = (s16[64,3200]{1,0:T(8,128)(2,1)S(1)}, s16[64,3200]{1,0:T(8,128)(2,1)S(1)}, u32[]{:S(2)}, u32[]{:S(2)}) collective-permute-start(s16[64,3200]{1,0:T(8,128)(2,1)S(1)} %logits.5.refs_0_), channel_id=1, source_target_pairs={{4,0},{0,4},{5,1},{1,5},{6,2},{2,6},{7,3},{3,7},{12,8},{8,12},{13,... | collective-permute-start | bytes 1228808 | tf_op jit(solution)/shard_map/ppermute | solution.py:49
  62.7 5.6 %hidden.2 = (f32[128,2048]{1,0:T(8,128)S(1)}, bf16[64,3072]{1,0:T(8,128)(2,1)S(1)}, f32[64,128]{1,0:T(8,128)S(1)}) custom-call(s16[64,3200]{1,0:T(8,128)(2,1)S(1)} %get-tuple-element.53.refs_0_, s16[64,3200]{1,0:T(8,128)(2,1)S(1)} %collective-permute-done.11.refs_1_, s32[64,128]{1,0:T(8,128)S(1)} %get-tuple-element.52.refs_2_.tgt_ref, ...), custom_call_target="tpu_custom_call" | custom-call | flops 3221225472 | bytes 12582912 | tf_op jit(solution)/shard_map/hidden/pallas_call | solution.py:579
  68.8 5.7 %hidden.3 = (f32[128,2048]{1,0:T(8,128)S(1)}, bf16[64,3072]{1,0:T(8,128)(2,1)S(1)}, f32[64,128]{1,0:T(8,128)S(1)}) custom-call(s16[64,3200]{1,0:T(8,128)(2,1)S(1)} %logits.5.refs_0_, s16[64,3200]{1,0:T(8,128)(2,1)S(1)} %collective-permute-done.10.refs_1_, s32[64,128]{1,0:T(8,128)S(1)} %get-tuple-element.52.refs_2_.tgt_ref, ...), custom_call_target="tpu_custom_call" | custom-call | flops 3221225472 | bytes 12582912 | tf_op jit(solution)/shard_map/hidden/pallas_call | solution.py:579
  76.5 1.9 %collective-permute-start.14 = (f32[64,128]{1,0:T(8,128)S(1)}, f32[64,128]{1,0:T(8,128)S(1)}, u32[]{:S(2)}, u32[]{:S(2)}) collective-permute-start(f32[64,128]{1,0:T(8,128)S(1)} %get-tuple-element.57.st_ref.refs_0_), channel_id=1, source_target_pairs={{3,0},{0,1},{1,2},{2,3},{7,4},{4,5},{5,6},{6,7},{11,8},{8,9},{9,10... | collective-permute-start | bytes 98312 | tf_op jit(solution)/shard_map/ppermute | solution.py:49
  78.4 3.9 %last_hidden.1.refs_4_ = f32[128,2048]{1,0:T(8,128)S(1)} custom-call(f32[64,128]{1,0:T(8,128)S(1)} %get-tuple-element.56.refs_3_.st_prev, f32[64,128]{1,0:T(8,128)S(1)} %get-tuple-element.57.st_ref.refs_0_, bf16[128,2048]{1,0:T(8,128)(2,1)S(1)} %get-tuple-element.58.lhs_ref, f32[128,2048]{1,0:T(8,128)S(1)} %get-tuple-element.59.acc_prev, ...), custom_call_target="tpu_custom_call" | custom-call | flops 2147483648 | bytes 8388608 | tf_op jit(solution)/shard_map/last_hidden/pallas_call | solution.py:603
  85.4 1.4 %collective-permute-start.16 = (bf16[16,2048]{1,0:T(8,128)(2,1)S(1)}, bf16[16,2048]{1,0:T(8,128)(2,1)S(1)}, u32[]{:S(2)}, u32[]{:S(2)}) collective-permute-start(bf16[16,2048]{1,0:T(8,128)(2,1)S(1)} %get-tuple-element.87), channel_id=1, source_target_pairs={{0,2},{1,3},{2,0},{3,1},{4,6},{5,7},{6,4},{7,5},{8,10},{9,11},{10,... | collective-permute-start | bytes 196616 | tf_op jit(solution)/shard_map/ppermute | solution.py:59
  86.7 2.3 %collective-permute-start.17 = (bf16[16,2048]{1,0:T(8,128)(2,1)S(1)}, bf16[16,2048]{1,0:T(8,128)(2,1)S(1)}, u32[]{:S(2)}, u32[]{:S(2)}) collective-permute-start(bf16[16,2048]{1,0:T(8,128)(2,1)S(1)} %get-tuple-element.86), channel_id=1, source_target_pairs={{0,3},{1,0},{2,1},{3,2},{4,7},{5,4},{6,5},{7,6},{8,11},{9,8},{10,9... | collective-permute-start | bytes 196616 | tf_op jit(solution)/shard_map/ppermute | solution.py:59
  89.0 1.4 %collective-permute-done.15.refs_1_ = bf16[16,2048]{1,0:T(8,128)(2,1)S(1)} collective-permute-done((bf16[16,2048]{1,0:T(8,128)(2,1)S(1)}, bf16[16,2048]{1,0:T(8,128)(2,1)S(1)}, u32[]{:S(2)}, u32[]{:S(2)}) %collective-permute-start.15) | collective-permute-done | bytes 65568 | tf_op jit(solution)/shard_map/ppermute | solution.py:59
  90.4 1.4 %collective-permute-done.16.refs_2_ = bf16[16,2048]{1,0:T(8,128)(2,1)S(1)} collective-permute-done((bf16[16,2048]{1,0:T(8,128)(2,1)S(1)}, bf16[16,2048]{1,0:T(8,128)(2,1)S(1)}, u32[]{:S(2)}, u32[]{:S(2)}) %collective-permute-start.16) | collective-permute-done | bytes 65568 | tf_op jit(solution)/shard_map/ppermute | solution.py:59
  93.3 2.3 %collective-permute-done.18.refs_1_ = f32[16,128]{1,0:T(8,128)S(1)} collective-permute-done((f32[16,128]{1,0:T(8,128)S(1)}, f32[16,128]{1,0:T(8,128)S(1)}, u32[]{:S(2)}, u32[]{:S(2)}) %collective-permute-start.18) | collective-permute-done | bytes 8224 | tf_op jit(solution)/shard_map/ppermute | solution.py:49
  95.7 3.3 %collective-permute-start.19 = (bf16[16,2048]{1,0:T(8,128)(2,1)S(1)}, bf16[16,2048]{1,0:T(8,128)(2,1)S(1)}, u32[]{:S(2)}, u32[]{:S(2)}) collective-permute-start(bf16[16,2048]{1,0:T(8,128)(2,1)S(1)} %mixed_grad.1.refs_0_), channel_id=1, source_target_pairs={{1,0},{2,1},{3,2},{0,3},{5,4},{6,5},{7,6},{4,7},{9,8},{10,9},{11,1... | collective-permute-start | bytes 196616 | tf_op jit(solution)/shard_map/ppermute | solution.py:49
  100.9 3.3 %collective-permute-done.20.refs_2_ = bf16[16,2048]{1,0:T(8,128)(2,1)S(1)} collective-permute-done((bf16[16,2048]{1,0:T(8,128)(2,1)S(1)}, bf16[16,2048]{1,0:T(8,128)(2,1)S(1)}, u32[]{:S(2)}, u32[]{:S(2)}) %collective-permute-start.20) | collective-permute-done | bytes 65568 | tf_op jit(solution)/shard_map/ppermute | solution.py:49
  105.1 1.8 %back_project.1.refs_0_ = bf16[64,1024]{1,0:T(8,128)(2,1)S(1)} custom-call(bf16[16,2048]{1,0:T(8,128)(2,1)S(1)} %mixed_grad.1.refs_0_, bf16[16,2048]{1,0:T(8,128)(2,1)S(1)} %collective-permute-done.19.refs_1_, bf16[16,2048]{1,0:T(8,128)(2,1)S(1)} %collective-permute-done.20.refs_2_, bf16[16,2048]{1,0:T(8,128)(2,1)S(1)} %collective-permute-done.21.refs_3_, ...), custom_call_target="tpu_custom_call" | custom-call | bytes 7340032 | tf_op jit(solution)/shard_map/back_project/pallas_call | solution.py:666
  108.1 3.8 %collective-permute-done.24.refs_1_ = bf16[64,1024]{1,0:T(8,128)(2,1)S(1)} collective-permute-done((bf16[64,1024]{1,0:T(8,128)(2,1)S(1)}, bf16[64,1024]{1,0:T(8,128)(2,1)S(1)}, u32[]{:S(2)}, u32[]{:S(2)}) %collective-permute-start.24) | collective-permute-done | bytes 131104 | tf_op jit(solution)/shard_map/ppermute | solution.py:49
  112.5 2.6 %attend_back.1 = (f32[1,128,1024]{2,1,0:T(8,128)}, f32[1,128,1024]{2,1,0:T(8,128)}) custom-call(s32[35]{0:T(128)S(1)} %pad_add_fusion.scal, bf16[64,1024]{1,0:T(8,128)(2,1)S(1)} %back_project.1.refs_0_, bf16[64,1024]{1,0:T(8,128)(2,1)S(1)} %collective-permute-done.24.refs_1_, bf16[64,1024]{1,0:T(8,128)(2,1)S(1)} %get-tuple-element.81.refs_2_, ...), custom_call_target="tpu_custom_call" | custom-call | bytes 7340032 | tf_op jit(solution)/shard_map/attend_back/pallas_call | solution.py:684
  115.4 14.9 %head_grad.1 = (bf16[8032,2048]{1,0:T(8,128)(2,1)}, f32[1,1]{1,0:T(1,128)}) custom-call(bf16[64,2048]{1,0:T(8,128)(2,1)S(1)} %get-tuple-element.72.refs_0_, bf16[64,2048]{1,0:T(8,128)(2,1)S(1)} %collective-permute-done.9.refs_1_, bf16[64,2048]{1,0:T(8,128)(2,1)S(1)} %collective-permute-done.22.refs_2_, bf16[64,2048]{1,0:T(8,128)(2,1)S(1)} %collective-permute-done.23.refs_3_, ...), custom_call_target="tpu_custom_call" | custom-call | flops 8589934592 | bytes 33554432 | tf_op jit(solution)/shard_map/head_grad/pallas_call | solution.py:698
  (61 shorter events, 24.0 us)
Async XLA Ops:
  0.6 5.5 %collective-permute-start = (bf16[1,32,1024]{2,1,0:T(8,128)(2,1)}, bf16[1,32,1024]{2,1,0:T(8,128)(2,1)S(1)}, u32[]{:S(2)}, u32[]{:S(2)}) collective-permute-start(bf16[1,32,1024]{2,1,0:T(8,128)(2,1)} %refs_0_.1), channel_id=1, source_target_pairs={{4,0},{0,4},{5,1},{1,5},{6,2},{2,6},{7,3},{3,7},{12,8},{8,12},{13,... | collective-permute-start | bytes 196616 | tf_op jit(solution)/shard_map/ppermute | solution.py:49
  10.5 5.2 %collective-permute-start.1 = (bf16[64,1152]{1,0:T(8,128)(2,1)S(1)}, bf16[64,1152]{1,0:T(8,128)(2,1)S(1)}, u32[]{:S(2)}, u32[]{:S(2)}) collective-permute-start(bf16[64,1152]{1,0:T(8,128)(2,1)S(1)} %get-tuple-element.45.refs_0_), channel_id=1, source_target_pairs={{4,0},{0,4},{5,1},{1,5},{6,2},{2,6},{7,3},{3,7},{12,8},{8,12},{13,... | collective-permute-start | bytes 442376 | tf_op jit(solution)/shard_map/ppermute | solution.py:49
  15.7 2.2 %copy-start = (bf16[1024,2048]{1,0:T(8,128)(2,1)S(1)}, bf16[1024,2048]{1,0:T(8,128)(2,1)}, u32[]{:S(2)}) copy-start(bf16[1024,2048]{1,0:T(8,128)(2,1)} %refs_4_.2) | copy-start | bytes 12582916
  20.5 6.8 %collective-permute-start.2 = (bf16[16,2048]{1,0:T(8,128)(2,1)S(1)}, bf16[16,2048]{1,0:T(8,128)(2,1)S(1)}, u32[]{:S(2)}, u32[]{:S(2)}) collective-permute-start(bf16[16,2048]{1,0:T(8,128)(2,1)S(1)} %get-tuple-element.91), channel_id=1, source_target_pairs={{0,1},{1,2},{2,3},{3,0},{4,5},{5,6},{6,7},{7,4},{8,9},{9,10},{10,1... | collective-permute-start | bytes 196616 | tf_op jit(solution)/shard_map/ppermute | solution.py:59
  22.7 5.2 %collective-permute-start.3 = (bf16[16,2048]{1,0:T(8,128)(2,1)S(1)}, bf16[16,2048]{1,0:T(8,128)(2,1)S(1)}, u32[]{:S(2)}, u32[]{:S(2)}) collective-permute-start(bf16[16,2048]{1,0:T(8,128)(2,1)S(1)} %get-tuple-element.90), channel_id=1, source_target_pairs={{0,2},{1,3},{2,0},{3,1},{4,6},{5,7},{6,4},{7,5},{8,10},{9,11},{10,... | collective-permute-start | bytes 196616 | tf_op jit(solution)/shard_map/ppermute | solution.py:59
  25.2 4.3 %collective-permute-start.4 = (bf16[16,2048]{1,0:T(8,128)(2,1)S(1)}, bf16[16,2048]{1,0:T(8,128)(2,1)S(1)}, u32[]{:S(2)}, u32[]{:S(2)}) collective-permute-start(bf16[16,2048]{1,0:T(8,128)(2,1)S(1)} %get-tuple-element.89), channel_id=1, source_target_pairs={{0,3},{1,0},{2,1},{3,2},{4,7},{5,4},{6,5},{7,6},{8,11},{9,8},{10,9... | collective-permute-start | bytes 196616 | tf_op jit(solution)/shard_map/ppermute | solution.py:59
  29.6 5.1 %collective-permute-start.5 = (bf16[16,2176]{1,0:T(8,128)(2,1)S(1)}, bf16[16,2176]{1,0:T(8,128)(2,1)S(1)}, u32[]{:S(2)}, u32[]{:S(2)}) collective-permute-start(bf16[16,2176]{1,0:T(8,128)(2,1)S(1)} %get-tuple-element.48.refs_0_), channel_id=1, source_target_pairs={{1,0},{2,1},{3,2},{0,3},{5,4},{6,5},{7,6},{4,7},{9,8},{10,9},{11,1... | collective-permute-start | bytes 208904 | tf_op jit(solution)/shard_map/ppermute | solution.py:49
  32.8 5.2 %collective-permute-start.6 = (bf16[16,2176]{1,0:T(8,128)(2,1)S(1)}, bf16[16,2176]{1,0:T(8,128)(2,1)S(1)}, u32[]{:S(2)}, u32[]{:S(2)}) collective-permute-start(bf16[16,2176]{1,0:T(8,128)(2,1)S(1)} %get-tuple-element.48.refs_0_), channel_id=1, source_target_pairs={{2,0},{3,1},{0,2},{1,3},{6,4},{7,5},{4,6},{5,7},{10,8},{11,9},{8,1... | collective-permute-start | bytes 208904 | tf_op jit(solution)/shard_map/ppermute | solution.py:49
  32.8 6.1 %collective-permute-start.7 = (bf16[16,2176]{1,0:T(8,128)(2,1)S(1)}, bf16[16,2176]{1,0:T(8,128)(2,1)S(1)}, u32[]{:S(2)}, u32[]{:S(2)}) collective-permute-start(bf16[16,2176]{1,0:T(8,128)(2,1)S(1)} %get-tuple-element.48.refs_0_), channel_id=1, source_target_pairs={{3,0},{0,1},{1,2},{2,3},{7,4},{4,5},{5,6},{6,7},{11,8},{8,9},{9,10... | collective-permute-start | bytes 208904 | tf_op jit(solution)/shard_map/ppermute | solution.py:49
  45.4 17.2 %collective-permute-start.11 = (s16[64,3200]{1,0:T(8,128)(2,1)S(1)}, s16[64,3200]{1,0:T(8,128)(2,1)S(1)}, u32[]{:S(2)}, u32[]{:S(2)}) collective-permute-start(s16[64,3200]{1,0:T(8,128)(2,1)S(1)} %get-tuple-element.53.refs_0_), channel_id=1, source_target_pairs={{4,0},{0,4},{5,1},{1,5},{6,2},{2,6},{7,3},{3,7},{12,8},{8,12},{13,... | collective-permute-start | bytes 1228808 | tf_op jit(solution)/shard_map/ppermute | solution.py:49
  47.0 15.0 %collective-permute-start.9 = (bf16[64,2048]{1,0:T(8,128)(2,1)S(1)}, bf16[64,2048]{1,0:T(8,128)(2,1)S(1)}, u32[]{:S(2)}, u32[]{:S(2)}) collective-permute-start(bf16[64,2048]{1,0:T(8,128)(2,1)S(1)} %get-tuple-element.72.refs_0_), channel_id=1, source_target_pairs={{0,16},{8,24},{16,0},{24,8},{1,17},{9,25},{17,1},{25,9},{2,18},{10... | collective-permute-start | bytes 786440 | tf_op jit(solution)/shard_map/ppermute | solution.py:66
  53.4 9.3 %collective-permute-start.8 = (s16[64,2176]{1,0:T(8,128)(2,1)S(1)}, s16[64,2176]{1,0:T(8,128)(2,1)S(1)}, u32[]{:S(2)}, u32[]{:S(2)}) collective-permute-start(s16[64,2176]{1,0:T(8,128)(2,1)S(1)} %logits.3.refs_0_), channel_id=1, source_target_pairs={{4,0},{0,4},{5,1},{1,5},{6,2},{2,6},{7,3},{3,7},{12,8},{8,12},{13,... | collective-permute-start | bytes 835592 | tf_op jit(solution)/shard_map/ppermute | solution.py:49
  60.4 8.3 %collective-permute-start.10 = (s16[64,3200]{1,0:T(8,128)(2,1)S(1)}, s16[64,3200]{1,0:T(8,128)(2,1)S(1)}, u32[]{:S(2)}, u32[]{:S(2)}) collective-permute-start(s16[64,3200]{1,0:T(8,128)(2,1)S(1)} %logits.5.refs_0_), channel_id=1, source_target_pairs={{4,0},{0,4},{5,1},{1,5},{6,2},{2,6},{7,3},{3,7},{12,8},{8,12},{13,... | collective-permute-start | bytes 1228808 | tf_op jit(solution)/shard_map/ppermute | solution.py:49
  75.2 7.1 %collective-permute-start.12 = (f32[64,128]{1,0:T(8,128)S(1)}, f32[64,128]{1,0:T(8,128)S(1)}, u32[]{:S(2)}, u32[]{:S(2)}) collective-permute-start(f32[64,128]{1,0:T(8,128)S(1)} %get-tuple-element.57.st_ref.refs_0_), channel_id=1, source_target_pairs={{1,0},{2,1},{3,2},{0,3},{5,4},{6,5},{7,6},{4,7},{9,8},{10,9},{11,1... | collective-permute-start | bytes 98312 | tf_op jit(solution)/shard_map/ppermute | solution.py:49
  76.0 6.4 %collective-permute-start.13 = (f32[64,128]{1,0:T(8,128)S(1)}, f32[64,128]{1,0:T(8,128)S(1)}, u32[]{:S(2)}, u32[]{:S(2)}) collective-permute-start(f32[64,128]{1,0:T(8,128)S(1)} %get-tuple-element.57.st_ref.refs_0_), channel_id=1, source_target_pairs={{2,0},{3,1},{0,2},{1,3},{6,4},{7,5},{4,6},{5,7},{10,8},{11,9},{8,1... | collective-permute-start | bytes 98312 | tf_op jit(solution)/shard_map/ppermute | solution.py:49
  76.5 5.9 %collective-permute-start.14 = (f32[64,128]{1,0:T(8,128)S(1)}, f32[64,128]{1,0:T(8,128)S(1)}, u32[]{:S(2)}, u32[]{:S(2)}) collective-permute-start(f32[64,128]{1,0:T(8,128)S(1)} %get-tuple-element.57.st_ref.refs_0_), channel_id=1, source_target_pairs={{3,0},{0,1},{1,2},{2,3},{7,4},{4,5},{5,6},{6,7},{11,8},{8,9},{9,10... | collective-permute-start | bytes 98312 | tf_op jit(solution)/shard_map/ppermute | solution.py:49
  78.4 26.6 %copy-start.1 = (bf16[1024,2048]{1,0:T(8,128)(2,1)S(1)}, bf16[1024,2048]{1,0:T(8,128)(2,1)}, u32[]{:S(2)}) copy-start(bf16[1024,2048]{1,0:T(8,128)(2,1)} %refs_4_.2) | copy-start | bytes 12582916
  78.4 34.0 %copy-start.3 = (bf16[1,128,1024]{2,1,0:T(8,128)(2,1)S(1)}, bf16[1,128,1024]{2,1,0:T(8,128)(2,1)}, u32[]{:S(2)}) copy-start(bf16[1,128,1024]{2,1,0:T(8,128)(2,1)} %refs_3_.3) | copy-start | bytes 786436
  78.4 34.0 %copy-start.5 = (bf16[1,128,1024]{2,1,0:T(8,128)(2,1)S(1)}, bf16[1,128,1024]{2,1,0:T(8,128)(2,1)}, u32[]{:S(2)}) copy-start(bf16[1,128,1024]{2,1,0:T(8,128)(2,1)} %refs_4_.3) | copy-start | bytes 786436
  83.2 28.7 %collective-permute-start.25 = (bf16[64,8192]{1,0:T(8,128)(2,1)S(1)}, bf16[64,8192]{1,0:T(8,128)(2,1)S(1)}, u32[]{:S(2)}, u32[]{:S(2)}) collective-permute-start(bf16[64,8192]{1,0:T(8,128)(2,1)S(1)} %logit_grad.1.refs_4_), channel_id=1, source_target_pairs={{0,16},{8,24},{16,0},{24,8},{1,17},{9,25},{17,1},{25,9},{2,18},{10... | collective-permute-start | bytes 3145736 | tf_op jit(solution)/shard_map/ppermute | solution.py:66
  84.2 6.2 %collective-permute-start.15 = (bf16[16,2048]{1,0:T(8,128)(2,1)S(1)}, bf16[16,2048]{1,0:T(8,128)(2,1)S(1)}, u32[]{:S(2)}, u32[]{:S(2)}) collective-permute-start(bf16[16,2048]{1,0:T(8,128)(2,1)S(1)} %get-tuple-element.88), channel_id=1, source_target_pairs={{0,1},{1,2},{2,3},{3,0},{4,5},{5,6},{6,7},{7,4},{8,9},{9,10},{10,1... | collective-permute-start | bytes 196616 | tf_op jit(solution)/shard_map/ppermute | solution.py:59
  85.4 6.4 %collective-permute-start.16 = (bf16[16,2048]{1,0:T(8,128)(2,1)S(1)}, bf16[16,2048]{1,0:T(8,128)(2,1)S(1)}, u32[]{:S(2)}, u32[]{:S(2)}) collective-permute-start(bf16[16,2048]{1,0:T(8,128)(2,1)S(1)} %get-tuple-element.87), channel_id=1, source_target_pairs={{0,2},{1,3},{2,0},{3,1},{4,6},{5,7},{6,4},{7,5},{8,10},{9,11},{10,... | collective-permute-start | bytes 196616 | tf_op jit(solution)/shard_map/ppermute | solution.py:59
  86.7 5.1 %collective-permute-start.17 = (bf16[16,2048]{1,0:T(8,128)(2,1)S(1)}, bf16[16,2048]{1,0:T(8,128)(2,1)S(1)}, u32[]{:S(2)}, u32[]{:S(2)}) collective-permute-start(bf16[16,2048]{1,0:T(8,128)(2,1)S(1)} %get-tuple-element.86), channel_id=1, source_target_pairs={{0,3},{1,0},{2,1},{3,2},{4,7},{5,4},{6,5},{7,6},{8,11},{9,8},{10,9... | collective-permute-start | bytes 196616 | tf_op jit(solution)/shard_map/ppermute | solution.py:59
  91.9 3.7 %collective-permute-start.18 = (f32[16,128]{1,0:T(8,128)S(1)}, f32[16,128]{1,0:T(8,128)S(1)}, u32[]{:S(2)}, u32[]{:S(2)}) collective-permute-start(f32[16,128]{1,0:T(8,128)S(1)} %get-tuple-element.69.refs_0_), channel_id=1, source_target_pairs={{4,0},{0,4},{5,1},{1,5},{6,2},{2,6},{7,3},{3,7},{12,8},{8,12},{13,... | collective-permute-start | bytes 24584 | tf_op jit(solution)/shard_map/ppermute | solution.py:49
  95.7 5.2 %collective-permute-start.19 = (bf16[16,2048]{1,0:T(8,128)(2,1)S(1)}, bf16[16,2048]{1,0:T(8,128)(2,1)S(1)}, u32[]{:S(2)}, u32[]{:S(2)}) collective-permute-start(bf16[16,2048]{1,0:T(8,128)(2,1)S(1)} %mixed_grad.1.refs_0_), channel_id=1, source_target_pairs={{1,0},{2,1},{3,2},{0,3},{5,4},{6,5},{7,6},{4,7},{9,8},{10,9},{11,1... | collective-permute-start | bytes 196616 | tf_op jit(solution)/shard_map/ppermute | solution.py:49
  99.0 5.2 %collective-permute-start.20 = (bf16[16,2048]{1,0:T(8,128)(2,1)S(1)}, bf16[16,2048]{1,0:T(8,128)(2,1)S(1)}, u32[]{:S(2)}, u32[]{:S(2)}) collective-permute-start(bf16[16,2048]{1,0:T(8,128)(2,1)S(1)} %mixed_grad.1.refs_0_), channel_id=1, source_target_pairs={{2,0},{3,1},{0,2},{1,3},{6,4},{7,5},{4,6},{5,7},{10,8},{11,9},{8,1... | collective-permute-start | bytes 196616 | tf_op jit(solution)/shard_map/ppermute | solution.py:49
  99.0 6.1 %collective-permute-start.21 = (bf16[16,2048]{1,0:T(8,128)(2,1)S(1)}, bf16[16,2048]{1,0:T(8,128)(2,1)S(1)}, u32[]{:S(2)}, u32[]{:S(2)}) collective-permute-start(bf16[16,2048]{1,0:T(8,128)(2,1)S(1)} %mixed_grad.1.refs_0_), channel_id=1, source_target_pairs={{3,0},{0,1},{1,2},{2,3},{7,4},{4,5},{5,6},{6,7},{11,8},{8,9},{9,10... | collective-permute-start | bytes 196616 | tf_op jit(solution)/shard_map/ppermute | solution.py:49
  106.9 5.0 %collective-permute-start.24 = (bf16[64,1024]{1,0:T(8,128)(2,1)S(1)}, bf16[64,1024]{1,0:T(8,128)(2,1)S(1)}, u32[]{:S(2)}, u32[]{:S(2)}) collective-permute-start(bf16[64,1024]{1,0:T(8,128)(2,1)S(1)} %back_project.1.refs_0_), channel_id=1, source_target_pairs={{4,0},{0,4},{5,1},{1,5},{6,2},{2,6},{7,3},{3,7},{12,8},{8,12},{13,... | collective-permute-start | bytes 393224 | tf_op jit(solution)/shard_map/ppermute | solution.py:49
  108.1 7.2 %collective-permute-start.26 = (bf16[64,8192]{1,0:T(8,128)(2,1)S(1)}, bf16[64,8192]{1,0:T(8,128)(2,1)S(1)}, u32[]{:S(2)}, u32[]{:S(2)}) collective-permute-start(bf16[64,8192]{1,0:T(8,128)(2,1)S(1)} %logit_grad.1.refs_4_), channel_id=1, source_target_pairs={{0,8},{8,0},{16,24},{24,16},{1,9},{9,1},{17,25},{25,17},{2,10},{10... | collective-permute-start | bytes 3145736 | tf_op jit(solution)/shard_map/ppermute | solution.py:66
  112.0 3.4 %collective-permute-start.27 = (bf16[64,8192]{1,0:T(8,128)(2,1)S(1)}, bf16[64,8192]{1,0:T(8,128)(2,1)S(1)}, u32[]{:S(2)}, u32[]{:S(2)}) collective-permute-start(bf16[64,8192]{1,0:T(8,128)(2,1)S(1)} %collective-permute-done.25.refs_5_), channel_id=1, source_target_pairs={{0,8},{8,0},{16,24},{24,16},{1,9},{9,1},{17,25},{25,17},{2,10},{10... | collective-permute-start | bytes 3145736 | tf_op jit(solution)/shard_map/ppermute | solution.py:66
  112.0 3.2 %collective-permute-start.22 = (bf16[64,2048]{1,0:T(8,128)(2,1)S(1)}, bf16[64,2048]{1,0:T(8,128)(2,1)S(1)}, u32[]{:S(2)}, u32[]{:S(2)}) collective-permute-start(bf16[64,2048]{1,0:T(8,128)(2,1)S(1)} %get-tuple-element.72.refs_0_), channel_id=1, source_target_pairs={{0,8},{8,0},{16,24},{24,16},{1,9},{9,1},{17,25},{25,17},{2,10},{10... | collective-permute-start | bytes 786440 | tf_op jit(solution)/shard_map/ppermute | solution.py:66
  112.5 2.9 %collective-permute-start.23 = (bf16[64,2048]{1,0:T(8,128)(2,1)S(1)}, bf16[64,2048]{1,0:T(8,128)(2,1)S(1)}, u32[]{:S(2)}, u32[]{:S(2)}) collective-permute-start(bf16[64,2048]{1,0:T(8,128)(2,1)S(1)} %collective-permute-done.9.refs_1_), channel_id=1, source_target_pairs={{0,8},{8,0},{16,24},{24,16},{1,9},{9,1},{17,25},{25,17},{2,10},{10... | collective-permute-start | bytes 786440 | tf_op jit(solution)/shard_map/ppermute | solution.py:66
  (3 other events, 2.7 us)

commit v7 on v6

--- a/solution.py
+++ b/solution.py
@@ -117,7 +117,7 @@
     stat = t_twice[pl.ds(pl.multiple_of(scal[0], 16), rows), :]
     for h in range(features // HDIM):
         at = slice(h * HDIM, (h + 1) * HDIM)
-        scores = dot(q[:, at], k_ref[0, :, at], 1, 1) * score_scale
+        scores = dot(q[:, at], k_ref[0, :, at], 1, 1)
         scores = jnp.where(valid, scores, LOW)
         peak = jnp.max(scores, axis=1, keepdims=True)
         e = jnp.where(valid, jnp.exp(scores - peak), 0.0)
@@ -134,15 +134,8 @@
 
 def project_kernel(n_seq, own_rows, ptile, scal, *refs):
     o_refs = refs[:n_seq]
-    p_ref, mixed_ref, own_ref, att_ref, lse_ref, tgt_ref, p_buf, sems = refs[n_seq:]
+    p_ref, mixed_ref, own_ref, att_ref, lse_ref, tgt_ref = refs[n_seq:]
     rows, features = att_ref.shape
-    columns = [pl.ds(at, ptile) for at in range(0, p_buf.shape[1], ptile)]
-    copies = [
-        pltpu.make_async_copy(p_ref.at[:, c], p_buf.at[:, c], sems.at[i])
-        for i, c in enumerate(columns)
-    ]
-    for c in copies:
-        c.start()
     stats = [r[:, features:].astype(f32) for r in o_refs]
     lane = lanes(rows)
     lse_all = jnp.zeros((rows, LANES), f32)
@@ -160,9 +153,9 @@
     lse_ref[...] = lse_all
     ids = tree([s[:, LANES - 2 : LANES - 1] * 256.0 + s[:, LANES - 1 :] for s in stats])
     tgt_ref[...] = jnp.broadcast_to(ids.astype(i32), (rows, LANES)) - scal[2]
-    for c, copy in zip(columns, copies):
-        copy.wait()
-        part = dot(att_ref[...], p_buf[:, c], 1, 0)
+    for at in range(0, mixed_ref.shape[1], ptile):
+        c = slice(at, at + ptile)
+        part = dot(att_ref[...], p_ref[:, c], 1, 0)
         mixed_ref[:, c] = part.astype(bf16)
         own_ref[:, c] = part[:own_rows]
 
@@ -426,7 +419,9 @@
 def back_project_kernel(*refs):
     mg_refs, p_ref, out_ref = refs[:-2], refs[-2], refs[-1]
     mg = jnp.concatenate([r[...] for r in mg_refs], axis=0)
-    out_ref[...] = dot(mg, p_ref[...], 1, 1).astype(bf16)
+    for at in range(0, out_ref.shape[1], HDIM):
+        part = dot(mg, p_ref[at : at + HDIM, :], 1, 1)
+        out_ref[:, at : at + HDIM] = part.astype(bf16)
 
 
 def attend_back_kernel(n_seq, scal, *refs):
@@ -439,7 +434,7 @@
         at = slice(h * HDIM, (h + 1) * HDIM)
         grad = tree([r[:, at].astype(f32) for r in a_refs]).astype(bf16)
         q = q_ref[:, at]
-        scores = dot(q, k_ref[0, :, at], 1, 1) * score_scale
+        scores = dot(q, k_ref[0, :, at], 1, 1)
         w = jnp.where(valid, jnp.exp(jnp.minimum(scores - lse_ref[:, h : h + 1], 0.5)), 0.0)
         prob_grad = dot(grad, v_ref[0, :, at], 1, 1)
         inner = jnp.sum(grad.astype(f32) * att_ref[:, at].astype(f32), axis=1, keepdims=True)
@@ -472,6 +467,7 @@
     scal = jnp.concatenate([scal, targets[0]])
 
     q_parts = gather_ring(queries, "seq")
+    keys = enc_keys * jnp.asarray(score_scale, bf16)
     res_own = lax.dynamic_slice(residual[0], (voc * own_rows, 0), (own_rows, width)).astype(f32)
     packed = jnp.concatenate([res_own, jnp.broadcast_to(gain, (8, width))], axis=0)
     o_part, q_all = pl.pallas_call(
@@ -486,7 +482,7 @@
         compiler_params=params(),
         cost_estimate=cost(0, 7 * 1024 * 1024),
         name="attend",
-    )(scal, *q_parts, enc_keys, enc_values)
+    )(scal, *q_parts, keys, enc_values)
 
     o_all = gather_ring(o_part, "seq")
     ptile = min(TILE, width)
@@ -501,12 +497,8 @@
             sds((rows, LANES), f32),
             sds((rows, LANES), i32),
         ],
-        in_specs=[SMEM] + [VMEM] * n_seq + [anywhere],
+        in_specs=[SMEM] + [VMEM] * (n_seq + 1),
         out_specs=[VMEM] * 5,
-        scratch_shapes=[
-            pltpu.VMEM((features, width), bf16),
-            pltpu.SemaphoreType.DMA((width // ptile,)),
-        ],
         compiler_params=params(),
         cost_estimate=cost(0, 7 * 1024 * 1024),
         name="project",
@@ -662,14 +654,11 @@
     )(gated, mixed, coef, *inner_all)
     mg_parts = gather_ring(mixed_grad, "vocab")
 
-    ftile = min(256, features)
     back_part = pl.pallas_call(
         back_project_kernel,
-        grid=(features // ftile,),
         out_shape=sds((rows, features), bf16),
-        in_specs=[whole((own_rows, width))] * n_vocab
-        + [pl.BlockSpec((ftile, width), lambda j: (j, 0))],
-        out_specs=pl.BlockSpec((rows, ftile), lambda j: (0, j)),
+        in_specs=[VMEM] * (n_vocab + 1),
+        out_specs=VMEM,
         compiler_params=params(),
         cost_estimate=cost(0, 7 * 1024 * 1024),
         name="back_project",
@@ -689,7 +678,7 @@
         compiler_params=params(),
         cost_estimate=cost(0, 7 * 1024 * 1024),
         name="attend_back",
-    )(scal, *back_all, q_all, enc_keys, enc_values, att, lse)
+    )(scal, *back_all, q_all, keys, enc_values, att, lse)
 
     head = None
     for c in range(GROUPS):

time: 131 us -> 128 us (0.977)
  Pallas kernels: 58.6 us -> 57.1 us
    ppermute x16, waiting for transfers between devices: 21.5 us -> 20.2 us  [from_ahead(): return lax.ppermute(x, axis, [((i + k) % n, i) for i in range(n)])]
    unnamed x14 -> x10, local copies, waits for them, and re-layouts: 4.94 us -> 3.98 us
  transfers between devices with their start and end apart: 28 -> 28, of which waited for: 17 -> 17; matrix products, arithmetic and copies ran while one was open for 2% -> 3% of each run, Pallas kernels for 20% -> 20%
where the time goes in v7:
time: 128 us
  Pallas kernels  57.1 us (45%)
  starting transfers between devices  36 us (28%)
  waiting for transfers between devices  26 us (20%)
  local copies, waits for them, and re-layouts  4.71 us (4%)
  other arithmetic  2.58 us (2%)
  between operations  1.45 us (1%)
    ppermute x16, starting transfers between devices, from_ahead(): return lax.ppermute(x, axis, [((i + k) % n, i) for i in range(n)])  22.3 us
    ppermute x16, waiting for transfers between devices, from_ahead(): return lax.ppermute(x, axis, [((i + k) % n, i) for i in range(n)])  20.2 us
    pallas_call x3, Pallas kernels, body(): pl.pallas_call(functools.partial(logits_kernel, tile0 * TILE, cols, n_voc...  17.9 us
    pallas_call x1, Pallas kernels, body(): pl.pallas_call(functools.partial(head_kernel, n_dp, n_dp * rows), grid=(s...  14.9 us
    pallas_call x2, Pallas kernels, body(): pl.pallas_call(functools.partial(hidden_kernel, c, first, cols, n_seq, fu...  11.3 us
    ppermute x6, starting transfers between devices, scatter_ring(): lax.ppermute(x[k * rows:(k + 1) * rows], axis, [(i, (i + k) % n) for i in...  10.8 us
    ppermute x6, waiting for transfers between devices, scatter_ring(): lax.ppermute(x[k * rows:(k + 1) * rows], axis, [(i, (i + k) % n) for i in...  5.53 us
    unnamed x10, local copies, waits for them, and re-layouts  3.98 us
  transfers between devices with their start and end apart: 28, of which 17 were waited for; matrix products, arithmetic and copies ran while one was open for 3% of the time, Pallas kernels for 20%

profile of v7, /device:TPU:0, one launch (start us, length us, event | category | flops | bytes accessed | tf_op | source)
XLA Modules:
  0.0 127.8 jit_solution(8931166425852311059)
XLA Ops:
  0.6 3.0 %collective-permute-start = (bf16[1,32,1024]{2,1,0:T(8,128)(2,1)}, bf16[1,32,1024]{2,1,0:T(8,128)(2,1)S(1)}, u32[]{:S(2)}, u32[]{:S(2)}) collective-permute-start(bf16[1,32,1024]{2,1,0:T(8,128)(2,1)} %refs_0_.1), channel_id=1, source_target_pairs={{4,0},{0,4},{5,1},{1,5},{6,2},{2,6},{7,3},{3,7},{12,8},{8,12},{13,... | collective-permute-start | bytes 196616 | tf_op jit(solution)/shard_map/ppermute | solution.py:49
  7.9 1.6 %attend.1 = (bf16[64,1152]{1,0:T(8,128)(2,1)S(1)}, bf16[64,1024]{1,0:T(8,128)(2,1)S(1)}) custom-call(s32[35]{0:T(128)S(1)} %pad_add_fusion.scal, bf16[1,32,1024]{2,1,0:T(8,128)(2,1)S(1)} %copy-done.4, bf16[1,32,1024]{2,1,0:T(8,128)(2,1)S(1)} %collective-permute-done.refs_1_, bf16[1,128,1024]{2,1,0:T(8,128)(2,1)S(1)} %broadcast_multiply_fusion.refs_2_.refs_3_, ...), custom_call_target="tpu_custom_call" | custom-call | bytes 7340032 | tf_op jit(solution)/shard_map/attend/pallas_call | solution.py:473
  9.5 2.1 %collective-permute-start.1 = (bf16[64,1152]{1,0:T(8,128)(2,1)S(1)}, bf16[64,1152]{1,0:T(8,128)(2,1)S(1)}, u32[]{:S(2)}, u32[]{:S(2)}) collective-permute-start(bf16[64,1152]{1,0:T(8,128)(2,1)S(1)} %get-tuple-element.45.refs_0_), channel_id=1, source_target_pairs={{4,0},{0,4},{5,1},{1,5},{6,2},{2,6},{7,3},{3,7},{12,8},{8,12},{13,... | collective-permute-start | bytes 442376 | tf_op jit(solution)/shard_map/ppermute | solution.py:49
  12.5 2.4 %collective-permute-done.1.refs_1_ = bf16[64,1152]{1,0:T(8,128)(2,1)S(1)} collective-permute-done((bf16[64,1152]{1,0:T(8,128)(2,1)S(1)}, bf16[64,1152]{1,0:T(8,128)(2,1)S(1)}, u32[]{:S(2)}, u32[]{:S(2)}) %collective-permute-start.1) | collective-permute-done | bytes 147488 | tf_op jit(solution)/shard_map/ppermute | solution.py:49
  14.8 2.2 %copy-done = bf16[1024,2048]{1,0:T(8,128)(2,1)S(1)} copy-done((bf16[1024,2048]{1,0:T(8,128)(2,1)S(1)}, bf16[1024,2048]{1,0:T(8,128)(2,1)}, u32[]{:S(2)}) %copy-start) | copy-done | bytes 4194328
  17.0 1.5 %project.1 = (bf16[64,2048]{1,0:T(8,128)(2,1)S(1)}, f32[16,2048]{1,0:T(8,128)S(1)}, bf16[64,1024]{1,0:T(8,128)(2,1)S(1)}, f32[64,128]{1,0:T(8,128)S(1)}, s32[64,128]{1,0:T(8,128)S(1)}) custom-call(s32[35]{0:T(128)S(1)} %pad_add_fusion.scal, bf16[64,1152]{1,0:T(8,128)(2,1)S(1)} %get-tuple-element.45.refs_0_, ...), custom_call_target="tpu_custom_call" | custom-call | bytes 7340032 | tf_op jit(solution)/shard_map/project/pallas_call | solution.py:491
  18.6 2.0 %collective-permute-start.2 = (bf16[16,2048]{1,0:T(8,128)(2,1)S(1)}, bf16[16,2048]{1,0:T(8,128)(2,1)S(1)}, u32[]{:S(2)}, u32[]{:S(2)}) collective-permute-start(bf16[16,2048]{1,0:T(8,128)(2,1)S(1)} %get-tuple-element.91), channel_id=1, source_target_pairs={{0,1},{1,2},{2,3},{3,0},{4,5},{5,6},{6,7},{7,4},{8,9},{9,10},{10,1... | collective-permute-start | bytes 196616 | tf_op jit(solution)/shard_map/ppermute | solution.py:59
  20.6 2.6 %collective-permute-start.3 = (bf16[16,2048]{1,0:T(8,128)(2,1)S(1)}, bf16[16,2048]{1,0:T(8,128)(2,1)S(1)}, u32[]{:S(2)}, u32[]{:S(2)}) collective-permute-start(bf16[16,2048]{1,0:T(8,128)(2,1)S(1)} %get-tuple-element.90), channel_id=1, source_target_pairs={{0,2},{1,3},{2,0},{3,1},{4,6},{5,7},{6,4},{7,5},{8,10},{9,11},{10,... | collective-permute-start | bytes 196616 | tf_op jit(solution)/shard_map/ppermute | solution.py:59
  25.8 2.2 %collective-permute-done.4.refs_3_ = bf16[16,2048]{1,0:T(8,128)(2,1)S(1)} collective-permute-done((bf16[16,2048]{1,0:T(8,128)(2,1)S(1)}, bf16[16,2048]{1,0:T(8,128)(2,1)S(1)}, u32[]{:S(2)}, u32[]{:S(2)}) %collective-permute-start.4) | collective-permute-done | bytes 65568 | tf_op jit(solution)/shard_map/ppermute | solution.py:59
  28.1 2.6 %collective-permute-start.5 = (bf16[16,2176]{1,0:T(8,128)(2,1)S(1)}, bf16[16,2176]{1,0:T(8,128)(2,1)S(1)}, u32[]{:S(2)}, u32[]{:S(2)}) collective-permute-start(bf16[16,2176]{1,0:T(8,128)(2,1)S(1)} %get-tuple-element.48.refs_0_), channel_id=1, source_target_pairs={{1,0},{2,1},{3,2},{0,3},{5,4},{6,5},{7,6},{4,7},{9,8},{10,9},{11,1... | collective-permute-start | bytes 208904 | tf_op jit(solution)/shard_map/ppermute | solution.py:49
  31.4 1.8 %collective-permute-done.5.refs_1_ = bf16[16,2176]{1,0:T(8,128)(2,1)S(1)} collective-permute-done((bf16[16,2176]{1,0:T(8,128)(2,1)S(1)}, bf16[16,2176]{1,0:T(8,128)(2,1)S(1)}, u32[]{:S(2)}, u32[]{:S(2)}) %collective-permute-start.5) | collective-permute-done | bytes 69664 | tf_op jit(solution)/shard_map/ppermute | solution.py:49
  33.2 2.8 %collective-permute-done.6.refs_2_ = bf16[16,2176]{1,0:T(8,128)(2,1)S(1)} collective-permute-done((bf16[16,2176]{1,0:T(8,128)(2,1)S(1)}, bf16[16,2176]{1,0:T(8,128)(2,1)S(1)}, u32[]{:S(2)}, u32[]{:S(2)}) %collective-permute-start.6) | collective-permute-done | bytes 69664 | tf_op jit(solution)/shard_map/ppermute | solution.py:49
  36.9 6.5 %logits.4 = (s16[64,3200]{1,0:T(8,128)(2,1)S(1)}, bf16[64,2048]{1,0:T(8,128)(2,1)S(1)}) custom-call(bf16[16,2176]{1,0:T(8,128)(2,1)S(1)} %get-tuple-element.48.refs_0_, bf16[16,2176]{1,0:T(8,128)(2,1)S(1)} %collective-permute-done.5.refs_1_, bf16[16,2176]{1,0:T(8,128)(2,1)S(1)} %collective-permute-done.6.refs_2_, ...), custom_call_target="tpu_custom_call" | custom-call | flops 3221225472 | bytes 12582912 | tf_op jit(solution)/shard_map/logits/pallas_call | solution.py:534
  43.4 1.6 %collective-permute-start.11 = (s16[64,3200]{1,0:T(8,128)(2,1)S(1)}, s16[64,3200]{1,0:T(8,128)(2,1)S(1)}, u32[]{:S(2)}, u32[]{:S(2)}) collective-permute-start(s16[64,3200]{1,0:T(8,128)(2,1)S(1)} %get-tuple-element.53.refs_0_), channel_id=1, source_target_pairs={{4,0},{0,4},{5,1},{1,5},{6,2},{2,6},{7,3},{3,7},{12,8},{8,12},{13,... | collective-permute-start | bytes 1228808 | tf_op jit(solution)/shard_map/ppermute | solution.py:49
  44.9 1.5 %collective-permute-start.9 = (bf16[64,2048]{1,0:T(8,128)(2,1)S(1)}, bf16[64,2048]{1,0:T(8,128)(2,1)S(1)}, u32[]{:S(2)}, u32[]{:S(2)}) collective-permute-start(bf16[64,2048]{1,0:T(8,128)(2,1)S(1)} %get-tuple-element.72.refs_0_), channel_id=1, source_target_pairs={{0,16},{8,24},{16,0},{24,8},{1,17},{9,25},{17,1},{25,9},{2,18},{10... | collective-permute-start | bytes 786440 | tf_op jit(solution)/shard_map/ppermute | solution.py:66
  46.4 4.9 %logits.3.refs_0_ = s16[64,2176]{1,0:T(8,128)(2,1)S(1)} custom-call(bf16[16,2176]{1,0:T(8,128)(2,1)S(1)} %get-tuple-element.48.refs_0_, bf16[16,2176]{1,0:T(8,128)(2,1)S(1)} %collective-permute-done.5.refs_1_, bf16[16,2176]{1,0:T(8,128)(2,1)S(1)} %collective-permute-done.6.refs_2_, bf16[16,2176]{1,0:T(8,128)(2,1)S(1)} %collective-permute-done.7.refs_3_, ...), custom_call_target="tpu_custom_call" | custom-call | flops 2147483648 | bytes 8388608 | tf_op jit(solution)/shard_map/logits/pallas_call | solution.py:534
  51.9 6.5 %logits.5.refs_0_ = s16[64,3200]{1,0:T(8,128)(2,1)S(1)} custom-call(bf16[16,2176]{1,0:T(8,128)(2,1)S(1)} %get-tuple-element.48.refs_0_, bf16[16,2176]{1,0:T(8,128)(2,1)S(1)} %collective-permute-done.5.refs_1_, bf16[16,2176]{1,0:T(8,128)(2,1)S(1)} %collective-permute-done.6.refs_2_, bf16[16,2176]{1,0:T(8,128)(2,1)S(1)} %collective-permute-done.7.refs_3_, ...), custom_call_target="tpu_custom_call" | custom-call | flops 3221225472 | bytes 12582912 | tf_op jit(solution)/shard_map/logits/pallas_call | solution.py:534
  58.4 1.6 %collective-permute-start.10 = (s16[64,3200]{1,0:T(8,128)(2,1)S(1)}, s16[64,3200]{1,0:T(8,128)(2,1)S(1)}, u32[]{:S(2)}, u32[]{:S(2)}) collective-permute-start(s16[64,3200]{1,0:T(8,128)(2,1)S(1)} %logits.5.refs_0_), channel_id=1, source_target_pairs={{4,0},{0,4},{5,1},{1,5},{6,2},{2,6},{7,3},{3,7},{12,8},{8,12},{13,... | collective-permute-start | bytes 1228808 | tf_op jit(solution)/shard_map/ppermute | solution.py:49
  60.3 5.6 %hidden.2 = (f32[128,2048]{1,0:T(8,128)S(1)}, bf16[64,3072]{1,0:T(8,128)(2,1)S(1)}, f32[64,128]{1,0:T(8,128)S(1)}) custom-call(s16[64,3200]{1,0:T(8,128)(2,1)S(1)} %get-tuple-element.53.refs_0_, s16[64,3200]{1,0:T(8,128)(2,1)S(1)} %collective-permute-done.11.refs_1_, s32[64,128]{1,0:T(8,128)S(1)} %get-tuple-element.52.refs_2_.tgt_ref, ...), custom_call_target="tpu_custom_call" | custom-call | flops 3221225472 | bytes 12582912 | tf_op jit(solution)/shard_map/hidden/pallas_call | solution.py:571
  66.7 5.7 %hidden.3 = (f32[128,2048]{1,0:T(8,128)S(1)}, bf16[64,3072]{1,0:T(8,128)(2,1)S(1)}, f32[64,128]{1,0:T(8,128)S(1)}) custom-call(s16[64,3200]{1,0:T(8,128)(2,1)S(1)} %logits.5.refs_0_, s16[64,3200]{1,0:T(8,128)(2,1)S(1)} %collective-permute-done.10.refs_1_, s32[64,128]{1,0:T(8,128)S(1)} %get-tuple-element.52.refs_2_.tgt_ref, ...), custom_call_target="tpu_custom_call" | custom-call | flops 3221225472 | bytes 12582912 | tf_op jit(solution)/shard_map/hidden/pallas_call | solution.py:571
  74.4 1.9 %collective-permute-start.14 = (f32[64,128]{1,0:T(8,128)S(1)}, f32[64,128]{1,0:T(8,128)S(1)}, u32[]{:S(2)}, u32[]{:S(2)}) collective-permute-start(f32[64,128]{1,0:T(8,128)S(1)} %get-tuple-element.57.st_ref.refs_0_), channel_id=1, source_target_pairs={{3,0},{0,1},{1,2},{2,3},{7,4},{4,5},{5,6},{6,7},{11,8},{8,9},{9,10... | collective-permute-start | bytes 98312 | tf_op jit(solution)/shard_map/ppermute | solution.py:49
  76.3 3.9 %last_hidden.1.refs_4_ = f32[128,2048]{1,0:T(8,128)S(1)} custom-call(f32[64,128]{1,0:T(8,128)S(1)} %get-tuple-element.56.refs_3_.st_prev, f32[64,128]{1,0:T(8,128)S(1)} %get-tuple-element.57.st_ref.refs_0_, bf16[128,2048]{1,0:T(8,128)(2,1)S(1)} %get-tuple-element.58.lhs_ref, f32[128,2048]{1,0:T(8,128)S(1)} %get-tuple-element.59.acc_prev, ...), custom_call_target="tpu_custom_call" | custom-call | flops 2147483648 | bytes 8388608 | tf_op jit(solution)/shard_map/last_hidden/pallas_call | solution.py:595
  84.6 2.3 %collective-permute-start.17 = (bf16[16,2048]{1,0:T(8,128)(2,1)S(1)}, bf16[16,2048]{1,0:T(8,128)(2,1)S(1)}, u32[]{:S(2)}, u32[]{:S(2)}) collective-permute-start(bf16[16,2048]{1,0:T(8,128)(2,1)S(1)} %get-tuple-element.86), channel_id=1, source_target_pairs={{0,3},{1,0},{2,1},{3,2},{4,7},{5,4},{6,5},{7,6},{8,11},{9,8},{10,9... | collective-permute-start | bytes 196616 | tf_op jit(solution)/shard_map/ppermute | solution.py:59
  86.9 1.4 %collective-permute-done.15.refs_1_ = bf16[16,2048]{1,0:T(8,128)(2,1)S(1)} collective-permute-done((bf16[16,2048]{1,0:T(8,128)(2,1)S(1)}, bf16[16,2048]{1,0:T(8,128)(2,1)S(1)}, u32[]{:S(2)}, u32[]{:S(2)}) %collective-permute-start.15) | collective-permute-done | bytes 65568 | tf_op jit(solution)/shard_map/ppermute | solution.py:59
  89.8 1.5 %collective-permute-start.18 = (f32[16,128]{1,0:T(8,128)S(1)}, f32[16,128]{1,0:T(8,128)S(1)}, u32[]{:S(2)}, u32[]{:S(2)}) collective-permute-start(f32[16,128]{1,0:T(8,128)S(1)} %get-tuple-element.69.refs_0_), channel_id=1, source_target_pairs={{4,0},{0,4},{5,1},{1,5},{6,2},{2,6},{7,3},{3,7},{12,8},{8,12},{13,... | collective-permute-start | bytes 24584 | tf_op jit(solution)/shard_map/ppermute | solution.py:49
  91.3 2.2 %collective-permute-done.18.refs_1_ = f32[16,128]{1,0:T(8,128)S(1)} collective-permute-done((f32[16,128]{1,0:T(8,128)S(1)}, f32[16,128]{1,0:T(8,128)S(1)}, u32[]{:S(2)}, u32[]{:S(2)}) %collective-permute-start.18) | collective-permute-done | bytes 8224 | tf_op jit(solution)/shard_map/ppermute | solution.py:49
  93.6 3.3 %collective-permute-start.19 = (bf16[16,2048]{1,0:T(8,128)(2,1)S(1)}, bf16[16,2048]{1,0:T(8,128)(2,1)S(1)}, u32[]{:S(2)}, u32[]{:S(2)}) collective-permute-start(bf16[16,2048]{1,0:T(8,128)(2,1)S(1)} %mixed_grad.1.refs_0_), channel_id=1, source_target_pairs={{1,0},{2,1},{3,2},{0,3},{5,4},{6,5},{7,6},{4,7},{9,8},{10,9},{11,1... | collective-permute-start | bytes 196616 | tf_op jit(solution)/shard_map/ppermute | solution.py:49
  98.8 3.3 %collective-permute-done.20.refs_2_ = bf16[16,2048]{1,0:T(8,128)(2,1)S(1)} collective-permute-done((bf16[16,2048]{1,0:T(8,128)(2,1)S(1)}, bf16[16,2048]{1,0:T(8,128)(2,1)S(1)}, u32[]{:S(2)}, u32[]{:S(2)}) %collective-permute-start.20) | collective-permute-done | bytes 65568 | tf_op jit(solution)/shard_map/ppermute | solution.py:49
  104.4 1.5 %collective-permute-start.24 = (bf16[64,1024]{1,0:T(8,128)(2,1)S(1)}, bf16[64,1024]{1,0:T(8,128)(2,1)S(1)}, u32[]{:S(2)}, u32[]{:S(2)}) collective-permute-start(bf16[64,1024]{1,0:T(8,128)(2,1)S(1)} %back_project.1.refs_0_), channel_id=1, source_target_pairs={{4,0},{0,4},{5,1},{1,5},{6,2},{2,6},{7,3},{3,7},{12,8},{8,12},{13,... | collective-permute-start | bytes 393224 | tf_op jit(solution)/shard_map/ppermute | solution.py:49
  105.9 3.5 %collective-permute-done.24.refs_1_ = bf16[64,1024]{1,0:T(8,128)(2,1)S(1)} collective-permute-done((bf16[64,1024]{1,0:T(8,128)(2,1)S(1)}, bf16[64,1024]{1,0:T(8,128)(2,1)S(1)}, u32[]{:S(2)}, u32[]{:S(2)}) %collective-permute-start.24) | collective-permute-done | bytes 131104 | tf_op jit(solution)/shard_map/ppermute | solution.py:49
  109.9 2.6 %attend_back.1 = (f32[1,128,1024]{2,1,0:T(8,128)}, f32[1,128,1024]{2,1,0:T(8,128)}) custom-call(s32[35]{0:T(128)S(1)} %pad_add_fusion.scal, bf16[64,1024]{1,0:T(8,128)(2,1)S(1)} %back_project.1.refs_0_, bf16[64,1024]{1,0:T(8,128)(2,1)S(1)} %collective-permute-done.24.refs_1_, bf16[64,1024]{1,0:T(8,128)(2,1)S(1)} %get-tuple-element.81.refs_2_, ...), custom_call_target="tpu_custom_call" | custom-call | bytes 7340032 | tf_op jit(solution)/shard_map/attend_back/pallas_call | solution.py:673
  112.8 14.9 %head_grad.1 = (bf16[8032,2048]{1,0:T(8,128)(2,1)}, f32[1,1]{1,0:T(1,128)}) custom-call(bf16[64,2048]{1,0:T(8,128)(2,1)S(1)} %get-tuple-element.72.refs_0_, bf16[64,2048]{1,0:T(8,128)(2,1)S(1)} %collective-permute-done.9.refs_1_, bf16[64,2048]{1,0:T(8,128)(2,1)S(1)} %collective-permute-done.22.refs_2_, bf16[64,2048]{1,0:T(8,128)(2,1)S(1)} %collective-permute-done.23.refs_3_, ...), custom_call_target="tpu_custom_call" | custom-call | flops 8589934592 | bytes 33554432 | tf_op jit(solution)/shard_map/head_grad/pallas_call | solution.py:687
  (58 shorter events, 23.3 us)
Async XLA Ops:
  0.6 5.5 %collective-permute-start = (bf16[1,32,1024]{2,1,0:T(8,128)(2,1)}, bf16[1,32,1024]{2,1,0:T(8,128)(2,1)S(1)}, u32[]{:S(2)}, u32[]{:S(2)}) collective-permute-start(bf16[1,32,1024]{2,1,0:T(8,128)(2,1)} %refs_0_.1), channel_id=1, source_target_pairs={{4,0},{0,4},{5,1},{1,5},{6,2},{2,6},{7,3},{3,7},{12,8},{8,12},{13,... | collective-permute-start | bytes 196616 | tf_op jit(solution)/shard_map/ppermute | solution.py:49
  6.1 1.0 copy-start.2
  9.5 5.3 %collective-permute-start.1 = (bf16[64,1152]{1,0:T(8,128)(2,1)S(1)}, bf16[64,1152]{1,0:T(8,128)(2,1)S(1)}, u32[]{:S(2)}, u32[]{:S(2)}) collective-permute-start(bf16[64,1152]{1,0:T(8,128)(2,1)S(1)} %get-tuple-element.45.refs_0_), channel_id=1, source_target_pairs={{4,0},{0,4},{5,1},{1,5},{6,2},{2,6},{7,3},{3,7},{12,8},{8,12},{13,... | collective-permute-start | bytes 442376 | tf_op jit(solution)/shard_map/ppermute | solution.py:49
  14.8 2.2 %copy-start = (bf16[1024,2048]{1,0:T(8,128)(2,1)S(1)}, bf16[1024,2048]{1,0:T(8,128)(2,1)}, u32[]{:S(2)}) copy-start(bf16[1024,2048]{1,0:T(8,128)(2,1)} %refs_4_.2) | copy-start | bytes 12582916
  18.6 6.7 %collective-permute-start.2 = (bf16[16,2048]{1,0:T(8,128)(2,1)S(1)}, bf16[16,2048]{1,0:T(8,128)(2,1)S(1)}, u32[]{:S(2)}, u32[]{:S(2)}) collective-permute-start(bf16[16,2048]{1,0:T(8,128)(2,1)S(1)} %get-tuple-element.91), channel_id=1, source_target_pairs={{0,1},{1,2},{2,3},{3,0},{4,5},{5,6},{6,7},{7,4},{8,9},{9,10},{10,1... | collective-permute-start | bytes 196616 | tf_op jit(solution)/shard_map/ppermute | solution.py:59
  20.6 5.2 %collective-permute-start.3 = (bf16[16,2048]{1,0:T(8,128)(2,1)S(1)}, bf16[16,2048]{1,0:T(8,128)(2,1)S(1)}, u32[]{:S(2)}, u32[]{:S(2)}) collective-permute-start(bf16[16,2048]{1,0:T(8,128)(2,1)S(1)} %get-tuple-element.90), channel_id=1, source_target_pairs={{0,2},{1,3},{2,0},{3,1},{4,6},{5,7},{6,4},{7,5},{8,10},{9,11},{10,... | collective-permute-start | bytes 196616 | tf_op jit(solution)/shard_map/ppermute | solution.py:59
  23.2 4.8 %collective-permute-start.4 = (bf16[16,2048]{1,0:T(8,128)(2,1)S(1)}, bf16[16,2048]{1,0:T(8,128)(2,1)S(1)}, u32[]{:S(2)}, u32[]{:S(2)}) collective-permute-start(bf16[16,2048]{1,0:T(8,128)(2,1)S(1)} %get-tuple-element.89), channel_id=1, source_target_pairs={{0,3},{1,0},{2,1},{3,2},{4,7},{5,4},{6,5},{7,6},{8,11},{9,8},{10,9... | collective-permute-start | bytes 196616 | tf_op jit(solution)/shard_map/ppermute | solution.py:59
  28.1 5.0 %collective-permute-start.5 = (bf16[16,2176]{1,0:T(8,128)(2,1)S(1)}, bf16[16,2176]{1,0:T(8,128)(2,1)S(1)}, u32[]{:S(2)}, u32[]{:S(2)}) collective-permute-start(bf16[16,2176]{1,0:T(8,128)(2,1)S(1)} %get-tuple-element.48.refs_0_), channel_id=1, source_target_pairs={{1,0},{2,1},{3,2},{0,3},{5,4},{6,5},{7,6},{4,7},{9,8},{10,9},{11,1... | collective-permute-start | bytes 208904 | tf_op jit(solution)/shard_map/ppermute | solution.py:49
  30.7 5.2 %collective-permute-start.6 = (bf16[16,2176]{1,0:T(8,128)(2,1)S(1)}, bf16[16,2176]{1,0:T(8,128)(2,1)S(1)}, u32[]{:S(2)}, u32[]{:S(2)}) collective-permute-start(bf16[16,2176]{1,0:T(8,128)(2,1)S(1)} %get-tuple-element.48.refs_0_), channel_id=1, source_target_pairs={{2,0},{3,1},{0,2},{1,3},{6,4},{7,5},{4,6},{5,7},{10,8},{11,9},{8,1... | collective-permute-start | bytes 208904 | tf_op jit(solution)/shard_map/ppermute | solution.py:49
  30.7 6.1 %collective-permute-start.7 = (bf16[16,2176]{1,0:T(8,128)(2,1)S(1)}, bf16[16,2176]{1,0:T(8,128)(2,1)S(1)}, u32[]{:S(2)}, u32[]{:S(2)}) collective-permute-start(bf16[16,2176]{1,0:T(8,128)(2,1)S(1)} %get-tuple-element.48.refs_0_), channel_id=1, source_target_pairs={{3,0},{0,1},{1,2},{2,3},{7,4},{4,5},{5,6},{6,7},{11,8},{8,9},{9,10... | collective-permute-start | bytes 208904 | tf_op jit(solution)/shard_map/ppermute | solution.py:49
  43.4 16.9 %collective-permute-start.11 = (s16[64,3200]{1,0:T(8,128)(2,1)S(1)}, s16[64,3200]{1,0:T(8,128)(2,1)S(1)}, u32[]{:S(2)}, u32[]{:S(2)}) collective-permute-start(s16[64,3200]{1,0:T(8,128)(2,1)S(1)} %get-tuple-element.53.refs_0_), channel_id=1, source_target_pairs={{4,0},{0,4},{5,1},{1,5},{6,2},{2,6},{7,3},{3,7},{12,8},{8,12},{13,... | collective-permute-start | bytes 1228808 | tf_op jit(solution)/shard_map/ppermute | solution.py:49
  44.9 15.0 %collective-permute-start.9 = (bf16[64,2048]{1,0:T(8,128)(2,1)S(1)}, bf16[64,2048]{1,0:T(8,128)(2,1)S(1)}, u32[]{:S(2)}, u32[]{:S(2)}) collective-permute-start(bf16[64,2048]{1,0:T(8,128)(2,1)S(1)} %get-tuple-element.72.refs_0_), channel_id=1, source_target_pairs={{0,16},{8,24},{16,0},{24,8},{1,17},{9,25},{17,1},{25,9},{2,18},{10... | collective-permute-start | bytes 786440 | tf_op jit(solution)/shard_map/ppermute | solution.py:66
  51.3 9.0 %collective-permute-start.8 = (s16[64,2176]{1,0:T(8,128)(2,1)S(1)}, s16[64,2176]{1,0:T(8,128)(2,1)S(1)}, u32[]{:S(2)}, u32[]{:S(2)}) collective-permute-start(s16[64,2176]{1,0:T(8,128)(2,1)S(1)} %logits.3.refs_0_), channel_id=1, source_target_pairs={{4,0},{0,4},{5,1},{1,5},{6,2},{2,6},{7,3},{3,7},{12,8},{8,12},{13,... | collective-permute-start | bytes 835592 | tf_op jit(solution)/shard_map/ppermute | solution.py:49
  58.4 8.3 %collective-permute-start.10 = (s16[64,3200]{1,0:T(8,128)(2,1)S(1)}, s16[64,3200]{1,0:T(8,128)(2,1)S(1)}, u32[]{:S(2)}, u32[]{:S(2)}) collective-permute-start(s16[64,3200]{1,0:T(8,128)(2,1)S(1)} %logits.5.refs_0_), channel_id=1, source_target_pairs={{4,0},{0,4},{5,1},{1,5},{6,2},{2,6},{7,3},{3,7},{12,8},{8,12},{13,... | collective-permute-start | bytes 1228808 | tf_op jit(solution)/shard_map/ppermute | solution.py:49
  73.1 7.1 %collective-permute-start.12 = (f32[64,128]{1,0:T(8,128)S(1)}, f32[64,128]{1,0:T(8,128)S(1)}, u32[]{:S(2)}, u32[]{:S(2)}) collective-permute-start(f32[64,128]{1,0:T(8,128)S(1)} %get-tuple-element.57.st_ref.refs_0_), channel_id=1, source_target_pairs={{1,0},{2,1},{3,2},{0,3},{5,4},{6,5},{7,6},{4,7},{9,8},{10,9},{11,1... | collective-permute-start | bytes 98312 | tf_op jit(solution)/shard_map/ppermute | solution.py:49
  73.9 6.3 %collective-permute-start.13 = (f32[64,128]{1,0:T(8,128)S(1)}, f32[64,128]{1,0:T(8,128)S(1)}, u32[]{:S(2)}, u32[]{:S(2)}) collective-permute-start(f32[64,128]{1,0:T(8,128)S(1)} %get-tuple-element.57.st_ref.refs_0_), channel_id=1, source_target_pairs={{2,0},{3,1},{0,2},{1,3},{6,4},{7,5},{4,6},{5,7},{10,8},{11,9},{8,1... | collective-permute-start | bytes 98312 | tf_op jit(solution)/shard_map/ppermute | solution.py:49
  74.4 5.9 %collective-permute-start.14 = (f32[64,128]{1,0:T(8,128)S(1)}, f32[64,128]{1,0:T(8,128)S(1)}, u32[]{:S(2)}, u32[]{:S(2)}) collective-permute-start(f32[64,128]{1,0:T(8,128)S(1)} %get-tuple-element.57.st_ref.refs_0_), channel_id=1, source_target_pairs={{3,0},{0,1},{1,2},{2,3},{7,4},{4,5},{5,6},{6,7},{11,8},{8,9},{9,10... | collective-permute-start | bytes 98312 | tf_op jit(solution)/shard_map/ppermute | solution.py:49
  76.3 26.6 %copy-start.1 = (bf16[1024,2048]{1,0:T(8,128)(2,1)S(1)}, bf16[1024,2048]{1,0:T(8,128)(2,1)}, u32[]{:S(2)}) copy-start(bf16[1024,2048]{1,0:T(8,128)(2,1)} %refs_4_.2) | copy-start | bytes 12582916
  76.3 33.6 %copy-start.3 = (bf16[1,128,1024]{2,1,0:T(8,128)(2,1)S(1)}, bf16[1,128,1024]{2,1,0:T(8,128)(2,1)}, u32[]{:S(2)}) copy-start(bf16[1,128,1024]{2,1,0:T(8,128)(2,1)} %refs_4_.3) | copy-start | bytes 786436
  81.2 28.2 %collective-permute-start.25 = (bf16[64,8192]{1,0:T(8,128)(2,1)S(1)}, bf16[64,8192]{1,0:T(8,128)(2,1)S(1)}, u32[]{:S(2)}, u32[]{:S(2)}) collective-permute-start(bf16[64,8192]{1,0:T(8,128)(2,1)S(1)} %logit_grad.1.refs_4_), channel_id=1, source_target_pairs={{0,16},{8,24},{16,0},{24,8},{1,17},{9,25},{17,1},{25,9},{2,18},{10... | collective-permute-start | bytes 3145736 | tf_op jit(solution)/shard_map/ppermute | solution.py:66
  82.1 6.2 %collective-permute-start.15 = (bf16[16,2048]{1,0:T(8,128)(2,1)S(1)}, bf16[16,2048]{1,0:T(8,128)(2,1)S(1)}, u32[]{:S(2)}, u32[]{:S(2)}) collective-permute-start(bf16[16,2048]{1,0:T(8,128)(2,1)S(1)} %get-tuple-element.88), channel_id=1, source_target_pairs={{0,1},{1,2},{2,3},{3,0},{4,5},{5,6},{6,7},{7,4},{8,9},{9,10},{10,1... | collective-permute-start | bytes 196616 | tf_op jit(solution)/shard_map/ppermute | solution.py:59
  83.3 6.4 %collective-permute-start.16 = (bf16[16,2048]{1,0:T(8,128)(2,1)S(1)}, bf16[16,2048]{1,0:T(8,128)(2,1)S(1)}, u32[]{:S(2)}, u32[]{:S(2)}) collective-permute-start(bf16[16,2048]{1,0:T(8,128)(2,1)S(1)} %get-tuple-element.87), channel_id=1, source_target_pairs={{0,2},{1,3},{2,0},{3,1},{4,6},{5,7},{6,4},{7,5},{8,10},{9,11},{10,... | collective-permute-start | bytes 196616 | tf_op jit(solution)/shard_map/ppermute | solution.py:59
  84.6 5.1 %collective-permute-start.17 = (bf16[16,2048]{1,0:T(8,128)(2,1)S(1)}, bf16[16,2048]{1,0:T(8,128)(2,1)S(1)}, u32[]{:S(2)}, u32[]{:S(2)}) collective-permute-start(bf16[16,2048]{1,0:T(8,128)(2,1)S(1)} %get-tuple-element.86), channel_id=1, source_target_pairs={{0,3},{1,0},{2,1},{3,2},{4,7},{5,4},{6,5},{7,6},{8,11},{9,8},{10,9... | collective-permute-start | bytes 196616 | tf_op jit(solution)/shard_map/ppermute | solution.py:59
  89.8 3.7 %collective-permute-start.18 = (f32[16,128]{1,0:T(8,128)S(1)}, f32[16,128]{1,0:T(8,128)S(1)}, u32[]{:S(2)}, u32[]{:S(2)}) collective-permute-start(f32[16,128]{1,0:T(8,128)S(1)} %get-tuple-element.69.refs_0_), channel_id=1, source_target_pairs={{4,0},{0,4},{5,1},{1,5},{6,2},{2,6},{7,3},{3,7},{12,8},{8,12},{13,... | collective-permute-start | bytes 24584 | tf_op jit(solution)/shard_map/ppermute | solution.py:49
  93.6 5.2 %collective-permute-start.19 = (bf16[16,2048]{1,0:T(8,128)(2,1)S(1)}, bf16[16,2048]{1,0:T(8,128)(2,1)S(1)}, u32[]{:S(2)}, u32[]{:S(2)}) collective-permute-start(bf16[16,2048]{1,0:T(8,128)(2,1)S(1)} %mixed_grad.1.refs_0_), channel_id=1, source_target_pairs={{1,0},{2,1},{3,2},{0,3},{5,4},{6,5},{7,6},{4,7},{9,8},{10,9},{11,1... | collective-permute-start | bytes 196616 | tf_op jit(solution)/shard_map/ppermute | solution.py:49
  96.9 5.2 %collective-permute-start.20 = (bf16[16,2048]{1,0:T(8,128)(2,1)S(1)}, bf16[16,2048]{1,0:T(8,128)(2,1)S(1)}, u32[]{:S(2)}, u32[]{:S(2)}) collective-permute-start(bf16[16,2048]{1,0:T(8,128)(2,1)S(1)} %mixed_grad.1.refs_0_), channel_id=1, source_target_pairs={{2,0},{3,1},{0,2},{1,3},{6,4},{7,5},{4,6},{5,7},{10,8},{11,9},{8,1... | collective-permute-start | bytes 196616 | tf_op jit(solution)/shard_map/ppermute | solution.py:49
  96.9 6.1 %collective-permute-start.21 = (bf16[16,2048]{1,0:T(8,128)(2,1)S(1)}, bf16[16,2048]{1,0:T(8,128)(2,1)S(1)}, u32[]{:S(2)}, u32[]{:S(2)}) collective-permute-start(bf16[16,2048]{1,0:T(8,128)(2,1)S(1)} %mixed_grad.1.refs_0_), channel_id=1, source_target_pairs={{3,0},{0,1},{1,2},{2,3},{7,4},{4,5},{5,6},{6,7},{11,8},{8,9},{9,10... | collective-permute-start | bytes 196616 | tf_op jit(solution)/shard_map/ppermute | solution.py:49
  104.4 5.0 %collective-permute-start.24 = (bf16[64,1024]{1,0:T(8,128)(2,1)S(1)}, bf16[64,1024]{1,0:T(8,128)(2,1)S(1)}, u32[]{:S(2)}, u32[]{:S(2)}) collective-permute-start(bf16[64,1024]{1,0:T(8,128)(2,1)S(1)} %back_project.1.refs_0_), channel_id=1, source_target_pairs={{4,0},{0,4},{5,1},{1,5},{6,2},{2,6},{7,3},{3,7},{12,8},{8,12},{13,... | collective-permute-start | bytes 393224 | tf_op jit(solution)/shard_map/ppermute | solution.py:49
  105.9 6.9 %collective-permute-start.26 = (bf16[64,8192]{1,0:T(8,128)(2,1)S(1)}, bf16[64,8192]{1,0:T(8,128)(2,1)S(1)}, u32[]{:S(2)}, u32[]{:S(2)}) collective-permute-start(bf16[64,8192]{1,0:T(8,128)(2,1)S(1)} %logit_grad.1.refs_4_), channel_id=1, source_target_pairs={{0,8},{8,0},{16,24},{24,16},{1,9},{9,1},{17,25},{25,17},{2,10},{10... | collective-permute-start | bytes 3145736 | tf_op jit(solution)/shard_map/ppermute | solution.py:66
  109.4 3.4 %collective-permute-start.27 = (bf16[64,8192]{1,0:T(8,128)(2,1)S(1)}, bf16[64,8192]{1,0:T(8,128)(2,1)S(1)}, u32[]{:S(2)}, u32[]{:S(2)}) collective-permute-start(bf16[64,8192]{1,0:T(8,128)(2,1)S(1)} %collective-permute-done.25.refs_5_), channel_id=1, source_target_pairs={{0,8},{8,0},{16,24},{24,16},{1,9},{9,1},{17,25},{25,17},{2,10},{10... | collective-permute-start | bytes 3145736 | tf_op jit(solution)/shard_map/ppermute | solution.py:66
  109.4 3.2 %collective-permute-start.22 = (bf16[64,2048]{1,0:T(8,128)(2,1)S(1)}, bf16[64,2048]{1,0:T(8,128)(2,1)S(1)}, u32[]{:S(2)}, u32[]{:S(2)}) collective-permute-start(bf16[64,2048]{1,0:T(8,128)(2,1)S(1)} %get-tuple-element.72.refs_0_), channel_id=1, source_target_pairs={{0,8},{8,0},{16,24},{24,16},{1,9},{9,1},{17,25},{25,17},{2,10},{10... | collective-permute-start | bytes 786440 | tf_op jit(solution)/shard_map/ppermute | solution.py:66
  109.9 2.9 %collective-permute-start.23 = (bf16[64,2048]{1,0:T(8,128)(2,1)S(1)}, bf16[64,2048]{1,0:T(8,128)(2,1)S(1)}, u32[]{:S(2)}, u32[]{:S(2)}) collective-permute-start(bf16[64,2048]{1,0:T(8,128)(2,1)S(1)} %collective-permute-done.9.refs_1_), channel_id=1, source_target_pairs={{0,8},{8,0},{16,24},{24,16},{1,9},{9,1},{17,25},{25,17},{2,10},{10... | collective-permute-start | bytes 786440 | tf_op jit(solution)/shard_map/ppermute | solution.py:66
  (1 other events, 0.8 us)
